TPU v7x, 32 devices: a whole 2x2x4 slice. The times are simulated.
32 devices in a mesh: dp: 2 (over y), expert: 16 (over z, x, core).
Axes of the slice: x: 2, y: 2, z: 4, core: 2. Of those that a mesh axis runs over, the one named last changes fastest.
Arguments:
- tokens: bfloat16 [2, 32, 64, 768], P(None, ('dp', 'expert')), may hold values from -6 to 6
- attn_weight: bfloat16 [768, 3072], P(None, ('dp', 'expert'))
- gain_attn: bfloat16 [768], replicated, may hold values from 0.5 to 1.5
- gain_expert: bfloat16 [768], replicated, may hold values from 0.5 to 1.5
- bias_table: bfloat16 [32, 12], replicated, may hold values from -5 to 5
- router_weight: bfloat16 [768, 16], replicated, may hold values from -0.15625 to 0.15625
- expert_in: bfloat16 [16, 768, 3072], P('expert', 'dp'), may hold values from -0.21875 to 0.21875
- expert_out: bfloat16 [16, 3072, 768], P('expert', None, 'dp'), may hold values from -2 to 2
- routes: int32 [2, 32, 64], P(None, ('dp', 'expert')), may hold values from 0 to 15, as said below
- slots: int32 [2, 32, 64], P(None, ('dp', 'expert')), may hold values from 0 to 5, as said below
- buckets: int32 [64, 64], replicated, may hold values from 0 to 31, as said below
- cotangent: bfloat16 [2, 32, 64, 768], P(None, ('dp', 'expert')), may hold values from -6 to 6
Outputs:
- output: bfloat16 [2, 32, 64, 768], P(None, ('dp', 'expert'))
- token_grad: float32 [2, 32, 64, 768], P(None, ('dp', 'expert'))
- attn_weight_grad: float32 [768, 3072], P(None, ('dp', 'expert'))
- gain_attn_grad: float32 [768], replicated
- gain_expert_grad: float32 [768], replicated
- bias_grad: float32 [32, 12], replicated
- router_grad: float32 [768, 16], replicated
- expert_in_grad: float32 [16, 768, 3072], P('expert', 'dp')
- expert_out_grad: float32 [16, 3072, 768], P('expert', None, 'dp')
Inputs may be any that keep to these rules, and one draw needn't show every extreme that they name: `routes`: an expert index for each token; in each micro-batch one expert is named by at least 6 tokens of every sequence, so some of its tokens are dropped. `slots`: the number of earlier tokens of the same sequence with the same route, or 5 where that number is 5 or more (the token is dropped). buckets[a, b] depends only on b - a.
All inputs are finite; a program needn't handle non-finite values.
Results may differ from a plain program's by a relative error of at most 0.012.
The roundings to bfloat16 on the way count: a program that leaves them out, or rounds other values in their place, can miss the bound.
Values may be sent and summed in bfloat16 or wider, within the bound.
No kernel may reach another device: no remote copies, remote signals or barrier semaphores. Data moves between devices by JAX's collectives and lax.ppermute only.
A program may use at most 128 MiB of HBM per device.

v0:
```python
import jax
import jax.numpy as jnp
from jax import lax
from jax.sharding import PartitionSpec as P

EPSILON = 1e-06
HIGH = lax.Precision.HIGHEST


def smooth_gate(values):
    return jax.nn.gelu(values, approximate=True)


def rms_scale(values):
    return lax.rsqrt(jnp.mean(values * values, axis=-1, keepdims=True) + EPSILON)


def body(
    tokens,
    attn_weight,
    gain_attn,
    gain_expert,
    bias_table,
    router_weight,
    expert_in,
    expert_out,
    routes,
    slots,
    buckets,
    cotangent,
):
    micro = tokens.shape[0]
    seq_len = tokens.shape[2]
    width = tokens.shape[3]
    heads = bias_table.shape[1]
    head_size = width // heads
    bucket_count = bias_table.shape[0]
    local_experts = expert_in.shape[0]
    expert_devices = lax.axis_size("expert")
    total_experts = local_experts * expert_devices
    capacity = (5 * seq_len + 4 * total_experts - 1) // (4 * total_experts)
    slot_total = total_experts * capacity
    gain_one = gain_attn.astype(jnp.float32)
    gain_two = gain_expert.astype(jnp.float32)
    router_full = router_weight.astype(jnp.float32)
    bucket_hot = (buckets[:, :, None] == jnp.arange(bucket_count)).astype(jnp.float32)
    bias_term = jnp.einsum(
        "ijb,bh->hij", bucket_hot, bias_table.astype(jnp.float32), precision=HIGH
    )

    def to_experts(tensor):
        tensor = tensor.reshape(expert_devices, local_experts, capacity, width)
        return jnp.transpose(tensor, (1, 0, 2, 3)).reshape(
            local_experts, expert_devices * capacity, width
        )

    def from_experts(tensor):
        tensor = tensor.reshape(local_experts, expert_devices, capacity, width)
        return jnp.transpose(tensor, (1, 0, 2, 3)).reshape(total_experts, capacity, width)

    gain_one_total = jnp.zeros((width,), jnp.float32)
    gain_two_total = jnp.zeros((width,), jnp.float32)
    bias_total = jnp.zeros((bucket_count, heads), jnp.float32)
    router_total = jnp.zeros((width, total_experts), jnp.float32)
    results = []
    token_grads = []
    kept_rows = []
    kept_hidden = []
    kept_dmade = []
    kept_dpre = []
    kept_mixed = []
    kept_dattn = []
    kept_normed = []
    kept_dqkv = []
    for micro_index in range(micro):
        inputs = tokens[micro_index, 0].astype(jnp.float32)
        full_attn = lax.all_gather(attn_weight, ("dp", "expert"), axis=1, tiled=True)
        scale_one = rms_scale(inputs)
        n1hat = inputs * scale_one
        n1b = (n1hat * gain_one).astype(jnp.bfloat16)
        qkv = jnp.dot(n1b, full_attn[:, : 3 * width], preferred_element_type=jnp.float32).astype(
            jnp.bfloat16
        )
        query = qkv[:, :width].reshape(seq_len, heads, head_size)
        key_part = qkv[:, width : 2 * width].reshape(seq_len, heads, head_size)
        value_part = qkv[:, 2 * width :].reshape(seq_len, heads, head_size)
        scores = (
            jnp.einsum("ihd,jhd->hij", query, key_part, preferred_element_type=jnp.float32)
            + bias_term
        )
        log_total = jax.nn.logsumexp(scores, axis=-1, keepdims=True)
        probs_b = jnp.exp(scores - log_total).astype(jnp.bfloat16)
        mixed = jnp.einsum("hij,jhd->ihd", probs_b, value_part, preferred_element_type=jnp.float32)
        mixed_b = mixed.reshape(seq_len, width).astype(jnp.bfloat16)
        resid = inputs + jnp.dot(
            mixed_b, full_attn[:, 3 * width :], preferred_element_type=jnp.float32
        )
        scale_two = rms_scale(resid)
        n2hat = resid * scale_two
        n2b = (n2hat * gain_two).astype(jnp.bfloat16)
        logits = jnp.dot(n2b, router_weight, preferred_element_type=jnp.float32)
        router_probs = jax.nn.softmax(logits, axis=-1)
        route_ids = routes[micro_index, 0]
        slot_ids = slots[micro_index, 0]
        picked = (route_ids[:, None] == jnp.arange(total_experts)).astype(jnp.float32)
        gate = jnp.sum(router_probs * picked, axis=-1)
        flat = route_ids * capacity + slot_ids
        dispatch = (
            (flat[:, None] == jnp.arange(slot_total)) & (slot_ids[:, None] < capacity)
        ).astype(jnp.bfloat16)
        outgoing = jnp.einsum(
            "sk,sd->kd", dispatch, n2b, preferred_element_type=jnp.float32
        ).astype(jnp.bfloat16)
        arrived = lax.all_to_all(
            outgoing.reshape(total_experts, capacity, width),
            "expert",
            split_axis=0,
            concat_axis=0,
            tiled=True,
        )
        expert_rows = to_experts(arrived)
        full_in, full_out = (
            lax.all_gather(expert_in, "dp", axis=1, tiled=True),
            lax.all_gather(expert_out, "dp", axis=2, tiled=True),
        )
        hidden_pre = jnp.einsum(
            "erd,edf->erf", expert_rows, full_in, preferred_element_type=jnp.float32
        )
        hidden = smooth_gate(hidden_pre).astype(jnp.bfloat16)
        made = jnp.einsum(
            "erf,efd->erd", hidden, full_out, preferred_element_type=jnp.float32
        ).astype(jnp.bfloat16)
        kept_rows.append(expert_rows)
        kept_hidden.append(hidden)
        came_back = lax.all_to_all(
            from_experts(made), "expert", split_axis=0, concat_axis=0, tiled=True
        )
        returned = jnp.einsum(
            "sk,kd->sd",
            dispatch,
            came_back.reshape(slot_total, width),
            preferred_element_type=jnp.float32,
        )
        results.append((resid + gate[:, None] * returned).astype(jnp.bfloat16))
        upstream = cotangent[micro_index, 0].astype(jnp.float32)
        dgate = jnp.sum(upstream * returned, axis=-1)
        dreturned = (gate[:, None] * upstream).astype(jnp.bfloat16)
        dslots = jnp.einsum(
            "sk,sd->kd", dispatch, dreturned, preferred_element_type=jnp.float32
        ).astype(jnp.bfloat16)
        dmade = to_experts(
            lax.all_to_all(
                dslots.reshape(total_experts, capacity, width),
                "expert",
                split_axis=0,
                concat_axis=0,
                tiled=True,
            )
        )
        back_attn = lax.all_gather(attn_weight, ("dp", "expert"), axis=1, tiled=True)
        back_in, back_out = (
            lax.all_gather(expert_in, "dp", axis=1, tiled=True),
            lax.all_gather(expert_out, "dp", axis=2, tiled=True),
        )
        dhidden = jnp.einsum("erd,efd->erf", dmade, back_out, preferred_element_type=jnp.float32)
        dpre = jax.vjp(smooth_gate, hidden_pre)[1](dhidden)[0].astype(jnp.bfloat16)
        kept_dmade.append(dmade)
        kept_dpre.append(dpre)
        drows = jnp.einsum(
            "erf,edf->erd", dpre, back_in, preferred_element_type=jnp.float32
        ).astype(jnp.bfloat16)
        drows_home = lax.all_to_all(
            from_experts(drows), "expert", split_axis=0, concat_axis=0, tiled=True
        )
        dnormed = jnp.einsum(
            "sk,kd->sd",
            dispatch,
            drows_home.reshape(slot_total, width),
            preferred_element_type=jnp.float32,
        )
        dpick = picked * dgate[:, None]
        dlogits = router_probs * (dpick - jnp.sum(router_probs * dpick, axis=-1, keepdims=True))
        router_total = router_total + jnp.dot(n2b.astype(jnp.float32).T, dlogits, precision=HIGH)
        dnormed = dnormed + jnp.dot(dlogits, router_full.T, precision=HIGH)
        gain_two_total = gain_two_total + jnp.sum(dnormed * n2hat, axis=0)
        dhat_two = dnormed * gain_two
        dresid = upstream + scale_two * (
            dhat_two - n2hat * jnp.mean(dhat_two * n2hat, axis=-1, keepdims=True)
        )
        dattn = dresid.astype(jnp.bfloat16)
        dmixed = jnp.einsum(
            "se,de->sd", dattn, back_attn[:, 3 * width :], preferred_element_type=jnp.float32
        )
        dmixed = dmixed.astype(jnp.bfloat16).reshape(seq_len, heads, head_size)
        again_scores = (
            jnp.einsum("ihd,jhd->hij", query, key_part, preferred_element_type=jnp.float32)
            + bias_term
        )
        probs = jnp.exp(again_scores - log_total)
        again_b = probs.astype(jnp.bfloat16)
        dvalue = jnp.einsum("hij,ihd->jhd", again_b, dmixed, preferred_element_type=jnp.float32)
        dprobs = jnp.einsum("ihd,jhd->hij", dmixed, value_part, preferred_element_type=jnp.float32)
        dscores = probs * (dprobs - jnp.sum(probs * dprobs, axis=-1, keepdims=True))
        bias_total = bias_total + jnp.einsum("hij,ijb->bh", dscores, bucket_hot, precision=HIGH)
        dscores_b = dscores.astype(jnp.bfloat16)
        dquery = jnp.einsum("hij,jhd->ihd", dscores_b, key_part, preferred_element_type=jnp.float32)
        dkey = jnp.einsum("hij,ihd->jhd", dscores_b, query, preferred_element_type=jnp.float32)
        dqkv = jnp.concatenate(
            [
                dquery.reshape(seq_len, width),
                dkey.reshape(seq_len, width),
                dvalue.reshape(seq_len, width),
            ],
            axis=1,
        ).astype(jnp.bfloat16)
        kept_mixed.append(mixed_b)
        kept_dattn.append(dattn)
        kept_normed.append(n1b)
        kept_dqkv.append(dqkv)
        dnormed_one = jnp.einsum(
            "se,de->sd", dqkv, back_attn[:, : 3 * width], preferred_element_type=jnp.float32
        )
        gain_one_total = gain_one_total + jnp.sum(dnormed_one * n1hat, axis=0)
        dhat_one = dnormed_one * gain_one
        token_grads.append(
            dresid
            + scale_one * (dhat_one - n1hat * jnp.mean(dhat_one * n1hat, axis=-1, keepdims=True))
        )
    normed_all = jnp.concatenate(kept_normed, axis=0)
    dqkv_all = jnp.concatenate(kept_dqkv, axis=0)
    mixed_all = jnp.concatenate(kept_mixed, axis=0)
    dattn_all = jnp.concatenate(kept_dattn, axis=0)
    dqkv_proj = jnp.einsum("sd,se->de", normed_all, dqkv_all, preferred_element_type=jnp.float32)
    dout_proj = jnp.einsum("sd,se->de", mixed_all, dattn_all, preferred_element_type=jnp.float32)
    attn_total = jnp.concatenate([dqkv_proj, dout_proj], axis=1)
    attn_share = lax.psum_scatter(attn_total, ("dp", "expert"), scatter_dimension=1, tiled=True)
    rows_all = jnp.concatenate(kept_rows, axis=1)
    hidden_all = jnp.concatenate(kept_hidden, axis=1)
    dmade_cat = jnp.concatenate(kept_dmade, axis=1)
    dpre_all = jnp.concatenate(kept_dpre, axis=1)
    in_total = jnp.einsum("erd,erf->edf", rows_all, dpre_all, preferred_element_type=jnp.float32)
    out_turned_total = jnp.einsum(
        "erd,erf->edf", dmade_cat, hidden_all, preferred_element_type=jnp.float32
    )
    in_share, out_turned_share = (
        lax.psum_scatter(
            in_total.astype(jnp.bfloat16), "dp", scatter_dimension=1, tiled=True
        ).astype(jnp.float32),
        lax.psum_scatter(
            out_turned_total.astype(jnp.bfloat16), "dp", scatter_dimension=1, tiled=True
        ).astype(jnp.float32),
    )
    out_share = jnp.transpose(out_turned_share, (0, 2, 1))
    gain_one_sum, gain_two_sum, bias_sum, router_sum = lax.psum(
        (gain_one_total, gain_two_total, bias_total, router_total), ("dp", "expert")
    )
    output = jnp.stack(results)[:, None]
    token_grad = jnp.stack(token_grads)[:, None]
    return (
        output,
        token_grad,
        attn_share,
        gain_one_sum,
        gain_two_sum,
        bias_sum,
        router_sum,
        in_share,
        out_share,
    )


def solution(mesh):
    placed = (
        P(None, ("dp", "expert"), None, None),
        P(None, ("dp", "expert")),
        P(),
        P(),
        P(),
        P(),
        P("expert", "dp", None),
        P("expert", None, "dp"),
        P(None, ("dp", "expert"), None),
        P(None, ("dp", "expert"), None),
        P(),
        P(None, ("dp", "expert"), None, None),
    )
    return jax.shard_map(
        body,
        mesh=mesh,
        in_specs=placed,
        out_specs=(
            P(None, ("dp", "expert"), None, None),
            P(None, ("dp", "expert"), None, None),
            P(None, ("dp", "expert")),
            P(),
            P(),
            P(),
            P(),
            P("expert", "dp", None),
            P("expert", None, "dp"),
        ),
        check_vma=False,
    )
```

profile of v0, /device:TPU:0, one launch (start us, length us, event | category | flops | bytes accessed | tf_op | source)
XLA Modules:
  0.0 543.7 jit_solution(12372844576048235892)
XLA Ops:
  11.1 66.2 %all-gather.4.cloned.1.call-done = bf16[768,3072]{0,1:T(8,128)(2,1)} async-done(((bf16[768,96]{0,1:T(8,128)(2,1)}), bf16[768,3072]{0,1:T(8,128)(2,1)}) %all-gather.4.cloned.1.call-update) | async-done | bytes 4718608 | tf_op jit(solution)/shard_map/all_gather | solution.py:77
  77.3 3.2 convolution_convert_fusion.3
  81.4 3.2 convolution_convert_fusion.2
  85.9 2.2 multiply_reduce_fusion.7
  88.4 2.1 multiply_reduce_fusion.6
  91.7 4.4 all-to-all-start.2
  98.7 6.4 %all-to-all-done.2 = bf16[16,5,768]{2,1,0:T(8,128)(2,1)S(1)} async-done(((bf16[16,5,768]{2,1,0:T(8,128)(2,1)}), bf16[16,5,768]{2,1,0:T(8,128)(2,1)S(1)}, u32[]{:S(2)}, u32[]{:S(2)}) %all-to-all-start.2) | async-done | bytes 122912 | tf_op jit(solution)/shard_map/all_to_all | solution.py:114
  105.1 3.5 all-to-all-start
  108.7 31.6 %all-gather.6.cloned.1.call-done = bf16[1,768,3072]{2,1,0:T(8,128)(2,1)} async-done(((bf16[1,384,3072]{2,1,0:T(8,128)(2,1)}), bf16[1,768,3072]{2,1,0:T(8,128)(2,1)}) %all-gather.6.cloned.1.call-update) | async-done | bytes 4718608 | tf_op jit(solution)/shard_map/all_gather | solution.py:123
  140.3 3.3 fusion.12
  143.7 1.1 fusion.234
  144.7 59.8 %all-gather.8.cloned.1.call-done = bf16[1,3072,768]{2,1,0:T(8,128)(2,1)} async-done(((bf16[1,3072,384]{2,1,0:T(8,128)(2,1)}), bf16[1,3072,768]{2,1,0:T(8,128)(2,1)}) %all-gather.8.cloned.1.call-update) | async-done | bytes 4718608 | tf_op jit(solution)/shard_map/all_gather | solution.py:124
  204.6 3.4 fusion.33
  208.7 5.7 %all-to-all-start.3 = ((bf16[16,5,768]{2,1,0:T(8,128)(2,1)}), bf16[16,5,768]{2,1,0:T(8,128)(2,1)}, u32[]{:S(2)}, u32[]{:S(2)}) async-start(bf16[16,5,768]{2,1,0:T(8,128)(2,1)} %reshape_transpose_reshape.25), calls=%async_computation.3 | async-start | bytes 393216 | tf_op jit(solution)/shard_map/all_to_all | solution.py:135
  214.4 3.5 fusion.14
  218.2 1.0 fusion.30
  220.0 3.4 all-to-all-done.3
  223.4 4.2 all-to-all-start.1
  227.6 1.0 reshape.360
  228.6 0.9 fusion.166
  229.5 7.1 %all-to-all-done.1 = bf16[16,5,768]{2,1,0:T(8,128)(2,1)} async-done(((bf16[16,5,768]{2,1,0:T(8,128)(2,1)}), bf16[16,5,768]{2,1,0:T(8,128)(2,1)}, u32[]{:S(2)}, u32[]{:S(2)}) %all-to-all-start.1) | async-done | bytes 122912 | tf_op jit(solution)/shard_map/all_to_all | solution.py:135
  236.6 1.0 reshape.354
  237.6 2.3 fusion.120
  239.9 1.2 fusion.187
  241.7 1.0 convolution_convert_fusion.12
  243.4 3.5 all-to-all-start.6
  247.0 1.2 fusion.185
  248.8 1.0 convolution_convert_fusion.13
  250.5 5.5 %all-to-all-done.6 = bf16[16,5,768]{2,1,0:T(8,128)(2,1)S(1)} async-done(((bf16[16,5,768]{2,1,0:T(8,128)(2,1)}), bf16[16,5,768]{2,1,0:T(8,128)(2,1)S(1)}, u32[]{:S(2)}, u32[]{:S(2)}) %all-to-all-start.6) | async-done | bytes 122912 | tf_op jit(solution)/shard_map/all_to_all | solution.py:152
  255.9 3.5 all-to-all-start.4
  259.7 1.1 fusion.233
  260.8 7.6 %all-to-all-done.4 = bf16[16,5,768]{2,1,0:T(8,128)(2,1)S(1)} async-done(((bf16[16,5,768]{2,1,0:T(8,128)(2,1)}), bf16[16,5,768]{2,1,0:T(8,128)(2,1)S(1)}, u32[]{:S(2)}, u32[]{:S(2)}) %all-to-all-start.4) | async-done | bytes 122912 | tf_op jit(solution)/shard_map/all_to_all | solution.py:152
  269.1 4.9 fusion.17
  274.1 1.7 reshape_transpose_reshape.29
  275.8 1.7 reshape_transpose_reshape.28
  277.4 1.7 reshape.369
  279.1 1.6 reshape.362
  280.8 4.2 fusion.51
  285.1 1.7 fusion.44
  286.8 3.6 fusion.16
  290.4 1.0 copy-done.58
  291.5 4.0 fusion.27
  296.4 3.5 all-to-all-start.7
  299.9 4.1 fusion.24
  304.8 4.1 all-to-all-done.7
  308.9 3.5 all-to-all-start.5
  313.5 7.9 %all-to-all-done.5 = bf16[16,5,768]{2,1,0:T(8,128)(2,1)S(1)} async-done(((bf16[16,5,768]{2,1,0:T(8,128)(2,1)}), bf16[16,5,768]{2,1,0:T(8,128)(2,1)S(1)}, u32[]{:S(2)}, u32[]{:S(2)}) %all-to-all-start.5) | async-done | bytes 122912 | tf_op jit(solution)/shard_map/all_to_all | solution.py:172
  322.2 0.8 fusion.231
  323.0 1.7 convolution_convert_fusion.16
  324.9 1.6 convolution_convert_fusion.17
  326.7 3.2 fusion.126
  331.8 1.3 convolution_convert_fusion.7
  333.8 4.0 fusion.74
  337.8 8.7 %pad_maximum_fusion = f32[768,3072]{1,0:T(8,128)} fusion(f32[768,768]{1,0:T(8,128)S(1)} %copy-done.3, f32[768,2304]{1,0:T(8,128)} %fusion.74), kind=kLoop, calls=%fused_computation | loop fusion | flops 2359296 | bytes 18874368 | tf_op jit(solution)/shard_map/concatenate | solution.py:235
  346.5 9.8 %copy.126 = f32[768,3072]{0,1:T(8,128)} copy(f32[768,3072]{1,0:T(8,128)} %pad_maximum_fusion) | data formatting | bytes 18874368
  357.5 0.8 convolution_add_fusion.6
  358.9 3.0 fusion.18
  362.5 0.8 fusion.109
  364.7 38.4 %all-reduce = (f32[768]{0:T(1024)}, f32[768]{0:T(1024)}, f32[32,12]{0,1:T(8,128)}, f32[768,16]{0,1:T(8,128)}) all-reduce(f32[768]{0:T(1024)S(1)} %add.172, f32[768]{0:T(1024)S(1)} %add.173, f32[32,12]{0,1:T(8,128)S(1)} %fusion.36, f32[768,16]{0,1:T(8,128)S(1)} %copy-done.68), channel_id=1, replica_groups=mesh['dp'=2,'expert'=16] {'dp','expert'}, use_global_device_ids=true, to_apply=%region_27.0 | all-reduce | flops 14208 | bytes 113664 | tf_op jit(solution)/shard_map/psum | solution.py:254
  404.1 1.1 fusion.116
  405.9 4.5 convert_bitcast_fusion
  410.5 6.2 %copy.116 = f32[1,3072,384]{2,1,0:T(8,128)} copy(f32[1,3072,384]{1,2,0:T(8,128)} %convert_bitcast_fusion) | data formatting | bytes 9437184
  416.7 4.5 convert_element_type.233
  421.2 115.6 %reduce-scatter.10.cloned.1.call-done = f32[96,768]{1,0:T(8,128)} async-done(((f32[3072,768]{1,0:T(8,128)}), f32[96,768]{1,0:T(8,128)}) %reduce-scatter.10.cloned.1.call-update) | async-done | bytes 294928
  (369 shorter events, 26.1 us)
Async XLA Ops:
  7.2 88.9 %copy-start = (bf16[768,16]{0,1:T(8,128)(2,1)S(1)}, bf16[768,16]{0,1:T(8,128)(2,1)}, u32[]{:S(2)}) copy-start(bf16[768,16]{0,1:T(8,128)(2,1)} %param.17) | copy-start | bytes 73732
  7.3 70.0 %all-gather.4.cloned.1.call-start = ((), (), s32[]{:S(2)}) async-start(), calls=%async_computation.11 | async-start | bytes 4866048 | tf_op jit(solution)/shard_map/all_gather | solution.py:77
  8.0 132.3 %all-gather.6.cloned.1.call-start = ((), (), s32[]{:S(2)}) async-start(), calls=%async_computation.12 | async-start | bytes 7077888 | tf_op jit(solution)/shard_map/all_gather | solution.py:123
  8.8 195.8 %all-gather.8.cloned.1.call-start = ((), (), s32[]{:S(2)}) async-start(), calls=%async_computation.13 | async-start | bytes 7077888 | tf_op jit(solution)/shard_map/all_gather | solution.py:124
  9.5 81.2 %copy-start.88 = (pred[64]{0:T(512)(128)(4,1)}, pred[64]{0:T(512)(128)(4,1)S(1)}, u32[]{:S(2)}) copy-start(pred[64]{0:T(512)(128)(4,1)S(1)} %get-tuple-element.80) | copy-start | bytes 196
  9.5 86.7 %copy-start.78 = (pred[64]{0:T(512)(128)(4,1)}, pred[64]{0:T(512)(128)(4,1)S(1)}, u32[]{:S(2)}) copy-start(pred[64]{0:T(512)(128)(4,1)S(1)} %get-tuple-element.79) | copy-start | bytes 196
  9.6 81.1 %copy-start.90 = (s32[64]{0:T(128)}, s32[64]{0:T(128)S(1)}, u32[]{:S(2)}) copy-start(s32[64]{0:T(128)S(1)} %get-tuple-element.76) | copy-start | bytes 772
  9.6 86.7 %copy-start.80 = (s32[64]{0:T(128)}, s32[64]{0:T(128)S(1)}, u32[]{:S(2)}) copy-start(s32[64]{0:T(128)S(1)} %get-tuple-element.75) | copy-start | bytes 772
  10.2 67.1 %copy-start.76 = (f32[768]{0:T(1024)}, f32[768]{0:T(1024)S(1)}, u32[]{:S(2)}) copy-start(f32[768]{0:T(1024)S(1)} %convert_element_type.185) | copy-start | bytes 9220
  10.9 79.7 %copy-start.70 = (f32[768]{0:T(1024)}, f32[768]{0:T(1024)S(1)}, u32[]{:S(2)}) copy-start(f32[768]{0:T(1024)S(1)} %convert_element_type.192) | copy-start | bytes 9220
  10.9 66.4 %copy-start.119 = (f32[64]{0:T(128)}, f32[64]{0:T(128)S(1)}, u32[]{:S(2)}) copy-start(f32[64]{0:T(128)S(1)} %get-tuple-element.100) | copy-start | bytes 772
  10.9 66.4 %copy-start.122 = (f32[64]{0:T(128)}, f32[64]{0:T(128)S(1)}, u32[]{:S(2)}) copy-start(f32[64]{0:T(128)S(1)} %get-tuple-element.101) | copy-start | bytes 772
  11.0 73.5 %copy-start.59 = (bf16[64,768]{1,0:T(8,128)(2,1)}, bf16[64,768]{1,0:T(8,128)(2,1)S(1)}, u32[]{:S(2)}) copy-start(bf16[64,768]{1,0:T(8,128)(2,1)S(1)} %get-tuple-element.66) | copy-start | bytes 294916
  11.0 73.5 %copy-start.61 = (bf16[64,768]{1,0:T(8,128)(2,1)}, bf16[64,768]{1,0:T(8,128)(2,1)S(1)}, u32[]{:S(2)}) copy-start(bf16[64,768]{1,0:T(8,128)(2,1)S(1)} %get-tuple-element.67) | copy-start | bytes 294916
  85.9 57.7 %copy-start.42 = (bf16[12,64,64]{2,1,0:T(8,128)(2,1)}, bf16[12,64,64]{2,1,0:T(8,128)(2,1)S(1)}, u32[]{:S(2)}) copy-start(bf16[12,64,64]{2,1,0:T(8,128)(2,1)S(1)} %convolution_convert_fusion.11) | copy-start | bytes 294916
  88.4 20.3 %copy-start.43 = (bf16[12,64,64]{2,1,0:T(8,128)(2,1)}, bf16[12,64,64]{2,1,0:T(8,128)(2,1)S(1)}, u32[]{:S(2)}) copy-start(bf16[12,64,64]{2,1,0:T(8,128)(2,1)S(1)} %convolution_convert_fusion.10) | copy-start | bytes 294916
  90.5 18.2 %copy-start.6 = (f32[64,768]{1,0:T(8,128)}, f32[64,768]{1,0:T(8,128)S(1)}, u32[]{:S(2)}) copy-start(f32[64,768]{1,0:T(8,128)S(1)} %get-tuple-element.88) | copy-start | bytes 589828
  91.7 13.4 %all-to-all-start.2 = ((bf16[16,5,768]{2,1,0:T(8,128)(2,1)}), bf16[16,5,768]{2,1,0:T(8,128)(2,1)S(1)}, u32[]{:S(2)}, u32[]{:S(2)}) async-start(bf16[16,5,768]{2,1,0:T(8,128)(2,1)} %reshape.358), calls=%async_computation.2 | async-start | bytes 393216 | tf_op jit(solution)/shard_map/all_to_all | solution.py:114
  96.8 150.2 %copy-start.65 = (f32[64,16]{0,1:T(8,128)}, f32[64,16]{0,1:T(8,128)S(1)}, u32[]{:S(2)}) copy-start(f32[64,16]{0,1:T(8,128)S(1)} %get-tuple-element.91) | copy-start | bytes 12292
  105.1 102.9 %copy-start.22 = (bf16[16,5,768]{2,1,0:T(8,128)(2,1)}, bf16[16,5,768]{2,1,0:T(8,128)(2,1)S(1)}, u32[]{:S(2)}) copy-start(bf16[16,5,768]{2,1,0:T(8,128)(2,1)S(1)} %all-to-all-done.2) | copy-start | bytes 368644
  105.1 103.6 %all-to-all-start = ((bf16[16,5,768]{2,1,0:T(8,128)(2,1)}), bf16[16,5,768]{2,1,0:T(8,128)(2,1)S(1)}, u32[]{:S(2)}, u32[]{:S(2)}) async-start(bf16[16,5,768]{2,1,0:T(8,128)(2,1)} %reshape.350), calls=%async_computation | async-start | bytes 393216 | tf_op jit(solution)/shard_map/all_to_all | solution.py:114
  208.7 14.7 %all-to-all-start.3 = ((bf16[16,5,768]{2,1,0:T(8,128)(2,1)}), bf16[16,5,768]{2,1,0:T(8,128)(2,1)}, u32[]{:S(2)}, u32[]{:S(2)}) async-start(bf16[16,5,768]{2,1,0:T(8,128)(2,1)} %reshape_transpose_reshape.25), calls=%async_computation.3 | async-start | bytes 393216 | tf_op jit(solution)/shard_map/all_to_all | solution.py:135
  218.2 19.4 %copy-start.11 = (bf16[2,1,64,768]{3,2,1,0:T(8,128)(2,1)S(1)}, bf16[2,1,64,768]{3,2,1,0:T(8,128)(2,1)}, u32[]{:S(2)}) copy-start(bf16[2,1,64,768]{3,2,1,0:T(8,128)(2,1)} %param.23) | copy-start | bytes 589828
  223.4 13.2 %all-to-all-start.1 = ((bf16[16,5,768]{2,1,0:T(8,128)(2,1)}), bf16[16,5,768]{2,1,0:T(8,128)(2,1)}, u32[]{:S(2)}, u32[]{:S(2)}) async-start(bf16[16,5,768]{2,1,0:T(8,128)(2,1)} %reshape_transpose_reshape.24), calls=%async_computation.1 | async-start | bytes 393216 | tf_op jit(solution)/shard_map/all_to_all | solution.py:135
  243.4 12.5 %all-to-all-start.6 = ((bf16[16,5,768]{2,1,0:T(8,128)(2,1)}), bf16[16,5,768]{2,1,0:T(8,128)(2,1)S(1)}, u32[]{:S(2)}, u32[]{:S(2)}) async-start(bf16[16,5,768]{2,1,0:T(8,128)(2,1)} %reshape.368), calls=%async_computation.6 | async-start | bytes 393216 | tf_op jit(solution)/shard_map/all_to_all | solution.py:152
  255.9 18.1 %copy-start.24 = (bf16[16,5,768]{2,1,0:T(8,128)(2,1)}, bf16[16,5,768]{2,1,0:T(8,128)(2,1)S(1)}, u32[]{:S(2)}) copy-start(bf16[16,5,768]{2,1,0:T(8,128)(2,1)S(1)} %all-to-all-done.6) | copy-start | bytes 368644
  255.9 12.5 %all-to-all-start.4 = ((bf16[16,5,768]{2,1,0:T(8,128)(2,1)}), bf16[16,5,768]{2,1,0:T(8,128)(2,1)S(1)}, u32[]{:S(2)}, u32[]{:S(2)}) async-start(bf16[16,5,768]{2,1,0:T(8,128)(2,1)} %reshape.361), calls=%async_computation.4 | async-start | bytes 393216 | tf_op jit(solution)/shard_map/all_to_all | solution.py:152
  259.5 146.5 %reduce-scatter.8.cloned.1.call-start = ((), (), s32[]{:S(2)}) async-start(), calls=%async_computation.15 | async-start | bytes 7077888 | tf_op jit(solution)/shard_map/reduce_scatter | solution.py:249
  274.0 142.7 %reduce-scatter.6.cloned.1.call-start = ((), (), s32[]{:S(2)}) async-start(), calls=%async_computation.14 | async-start | bytes 7077888 | tf_op jit(solution)/shard_map/reduce_scatter | solution.py:246
  291.4 21.3 %copy-start.83 = (f32[64]{0:T(128)S(1)}, f32[64]{0:T(128)}, u32[]{:S(2)}) copy-start(f32[64]{0:T(128)} %copy-done.82) | copy-start | bytes 772
  291.4 21.3 %copy-start.99 = (f32[64]{0:T(128)S(1)}, f32[64]{0:T(128)}, u32[]{:S(2)}) copy-start(f32[64]{0:T(128)} %copy-done.98) | copy-start | bytes 772
  291.4 21.3 %copy-start.103 = (f32[64]{0:T(128)S(1)}, f32[64]{0:T(128)}, u32[]{:S(2)}) copy-start(f32[64]{0:T(128)} %fusion.192) | copy-start | bytes 772
  291.4 21.3 %copy-start.107 = (s32[64]{0:T(128)S(1)}, s32[64]{0:T(128)}, u32[]{:S(2)}) copy-start(s32[64]{0:T(128)} %get-tuple-element.78) | copy-start | bytes 772
  291.4 21.3 %copy-start.113 = (f32[64]{0:T(128)S(1)}, f32[64]{0:T(128)}, u32[]{:S(2)}) copy-start(f32[64]{0:T(128)} %get-tuple-element.52) | copy-start | bytes 772
  295.5 17.6 %copy-start.66 = (f32[64,16]{0,1:T(8,128)S(1)}, f32[64,16]{0,1:T(8,128)}, u32[]{:S(2)}) copy-start(f32[64,16]{0,1:T(8,128)} %copy-done.65) | copy-start | bytes 12292
  295.5 25.9 %copy-start.89 = (pred[64]{0:T(512)(128)(4,1)S(1)}, pred[64]{0:T(512)(128)(4,1)}, u32[]{:S(2)}) copy-start(pred[64]{0:T(512)(128)(4,1)} %copy-done.88) | copy-start | bytes 196
  295.6 25.9 %copy-start.91 = (s32[64]{0:T(128)S(1)}, s32[64]{0:T(128)}, u32[]{:S(2)}) copy-start(s32[64]{0:T(128)} %copy-done.90) | copy-start | bytes 772
  295.6 26.2 %copy-start.7 = (f32[64,768]{1,0:T(8,128)S(1)}, f32[64,768]{1,0:T(8,128)}, u32[]{:S(2)}) copy-start(f32[64,768]{1,0:T(8,128)} %copy-done.6) | copy-start | bytes 589828
  295.6 26.2 %copy-start.71 = (f32[768]{0:T(1024)S(1)}, f32[768]{0:T(1024)}, u32[]{:S(2)}) copy-start(f32[768]{0:T(1024)} %copy-done.70) | copy-start | bytes 9220
  295.6 26.2 %copy-start.79 = (pred[64]{0:T(512)(128)(4,1)S(1)}, pred[64]{0:T(512)(128)(4,1)}, u32[]{:S(2)}) copy-start(pred[64]{0:T(512)(128)(4,1)} %copy-done.78) | copy-start | bytes 196
  295.6 26.2 %copy-start.81 = (s32[64]{0:T(128)S(1)}, s32[64]{0:T(128)}, u32[]{:S(2)}) copy-start(s32[64]{0:T(128)} %copy-done.80) | copy-start | bytes 772
  295.6 26.2 %copy-start.93 = (f32[64]{0:T(128)S(1)}, f32[64]{0:T(128)}, u32[]{:S(2)}) copy-start(f32[64]{0:T(128)} %copy-done.92) | copy-start | bytes 772
  295.6 26.2 %copy-start.96 = (f32[64]{0:T(128)S(1)}, f32[64]{0:T(128)}, u32[]{:S(2)}) copy-start(f32[64]{0:T(128)} %copy-done.95) | copy-start | bytes 772
  295.6 26.6 %copy-start.12 = (bf16[2,1,64,768]{3,2,1,0:T(8,128)(2,1)S(1)}, bf16[2,1,64,768]{3,2,1,0:T(8,128)(2,1)}, u32[]{:S(2)}) copy-start(bf16[2,1,64,768]{3,2,1,0:T(8,128)(2,1)} %param.23) | copy-start | bytes 589828
  295.6 26.6 %copy-start.32 = (f32[64,768]{1,0:T(8,128)S(1)}, f32[64,768]{1,0:T(8,128)}, u32[]{:S(2)}) copy-start(f32[64,768]{1,0:T(8,128)} %copy-done.31) | copy-start | bytes 589828
  295.6 26.6 %copy-start.118 = (f32[64]{0:T(128)S(1)}, f32[64]{0:T(128)}, u32[]{:S(2)}) copy-start(f32[64]{0:T(128)} %copy-done.117) | copy-start | bytes 772
  296.4 12.5 %all-to-all-start.7 = ((bf16[16,5,768]{2,1,0:T(8,128)(2,1)}), bf16[16,5,768]{2,1,0:T(8,128)(2,1)S(1)}, u32[]{:S(2)}, u32[]{:S(2)}) async-start(bf16[16,5,768]{2,1,0:T(8,128)(2,1)} %reshape_transpose_reshape.27), calls=%async_computation.7 | async-start | bytes 393216 | tf_op jit(solution)/shard_map/all_to_all | solution.py:172
  308.9 12.5 %all-to-all-start.5 = ((bf16[16,5,768]{2,1,0:T(8,128)(2,1)}), bf16[16,5,768]{2,1,0:T(8,128)(2,1)S(1)}, u32[]{:S(2)}, u32[]{:S(2)}) async-start(bf16[16,5,768]{2,1,0:T(8,128)(2,1)} %reshape_transpose_reshape.26), calls=%async_computation.5 | async-start | bytes 393216 | tf_op jit(solution)/shard_map/all_to_all | solution.py:172
  312.4 224.4 %reduce-scatter.10.cloned.1.call-start = ((), (), s32[]{:S(2)}) async-start(), calls=%async_computation.16 | async-start | bytes 9732096
  362.3 40.8 %copy-start.13 = (bf16[2,1,64,768]{3,2,1,0:T(8,128)(2,1)S(1)}, bf16[2,1,64,768]{3,2,1,0:T(8,128)(2,1)}, u32[]{:S(2)}) copy-start(bf16[2,1,64,768]{3,2,1,0:T(8,128)(2,1)} %param.23) | copy-start | bytes 589828
  362.3 40.8 %copy-start.28 = (f32[64,768]{1,0:T(8,128)S(1)}, f32[64,768]{1,0:T(8,128)}, u32[]{:S(2)}) copy-start(f32[64,768]{1,0:T(8,128)} %copy-done.27) | copy-start | bytes 589828
  362.3 40.8 %copy-start.41 = (f32[64,768]{1,0:T(8,128)S(1)}, f32[64,768]{1,0:T(8,128)}, u32[]{:S(2)}) copy-start(f32[64,768]{1,0:T(8,128)} %get-tuple-element.89) | copy-start | bytes 589828
  362.3 40.8 %copy-start.72 = (f32[768]{0:T(1024)S(1)}, f32[768]{0:T(1024)}, u32[]{:S(2)}) copy-start(f32[768]{0:T(1024)} %copy-done.70) | copy-start | bytes 9220
  362.4 40.8 %copy-start.97 = (f32[64]{0:T(128)S(1)}, f32[64]{0:T(128)}, u32[]{:S(2)}) copy-start(f32[64]{0:T(128)} %copy-done.95) | copy-start | bytes 772
  362.4 40.8 %copy-start.112 = (f32[64]{0:T(128)S(1)}, f32[64]{0:T(128)}, u32[]{:S(2)}) copy-start(f32[64]{0:T(128)} %copy-done.111) | copy-start | bytes 772
  362.4 40.8 %copy-start.124 = (f32[64]{0:T(128)S(1)}, f32[64]{0:T(128)}, u32[]{:S(2)}) copy-start(f32[64]{0:T(128)} %copy-done.122) | copy-start | bytes 772
  362.4 40.8 %copy-start.131 = (f32[64]{0:T(128)S(1)}, f32[64]{0:T(128)}, u32[]{:S(2)}) copy-start(f32[64]{0:T(128)} %copy-done.130) | copy-start | bytes 772
  362.4 40.9 %copy-start.63 = (bf16[1,64,768]{2,1,0:T(8,128)(2,1)S(1)}, bf16[1,64,768]{2,1,0:T(8,128)(2,1)}, u32[]{:S(2)}) copy-start(bf16[1,64,768]{2,1,0:T(8,128)(2,1)} %get-tuple-element.68) | copy-start | bytes 294916
  362.4 41.6 %copy-start.8 = (f32[64,768]{1,0:T(8,128)S(1)}, f32[64,768]{1,0:T(8,128)}, u32[]{:S(2)}) copy-start(f32[64,768]{1,0:T(8,128)} %copy-done.6) | copy-start | bytes 589828
  362.4 41.6 %copy-start.10 = (f32[64,768]{1,0:T(8,128)S(1)}, f32[64,768]{1,0:T(8,128)}, u32[]{:S(2)}) copy-start(f32[64,768]{1,0:T(8,128)} %copy-done.9) | copy-start | bytes 589828
  362.4 41.6 %copy-start.94 = (f32[64]{0:T(128)S(1)}, f32[64]{0:T(128)}, u32[]{:S(2)}) copy-start(f32[64]{0:T(128)} %copy-done.92) | copy-start | bytes 772
  362.4 41.6 %copy-start.121 = (f32[64]{0:T(128)S(1)}, f32[64]{0:T(128)}, u32[]{:S(2)}) copy-start(f32[64]{0:T(128)} %copy-done.119) | copy-start | bytes 772
  362.4 41.6 %copy-start.129 = (f32[64]{0:T(128)S(1)}, f32[64]{0:T(128)}, u32[]{:S(2)}) copy-start(f32[64]{0:T(128)} %copy-done.128) | copy-start | bytes 772
  410.5 126.4 %copy-start.1 = (bf16[768,16]{0,1:T(8,128)(2,1)S(1)}, bf16[768,16]{0,1:T(8,128)(2,1)}, u32[]{:S(2)}) copy-start(bf16[768,16]{0,1:T(8,128)(2,1)} %param.17) | copy-start | bytes 73732
  (87 other events, 437.0 us)
Sparse Core Ops, SparseCore 0:
  11.0 66.2 all-gather.3
  78.8 61.4 all-gather.5
  141.9 62.6 all-gather.7
  274.1 56.9 reduce-scatter.7
  334.0 60.8 reduce-scatter.5
  401.2 135.6 reduce-scatter.9
where the time goes:
time: 546 us; the launch traced here: 544 us
  waiting for transfers between devices  317 us (58%)
  matrix products  72.2 us (13%)
  local copies, waits for them, and re-layouts  39 us (7%)
  blocking collectives  38.4 us (7%)
  starting transfers between devices  32.4 us (6%)
  other arithmetic  27.9 us (5%)
  between operations  16.4 us (3%)
    unnamed x7, waiting for transfers between devices  118 us
    all_gather x1, waiting for transfers between devices, body(): lax.all_gather(attn_weight, ('dp', 'expert'), axis=1, tiled=True)  66.2 us
    all_gather x1, waiting for transfers between devices, body(): lax.all_gather(expert_out, 'dp', axis=2, tiled=True)  59.8 us
    psum x1, blocking collectives, body(): lax.psum((gain_one_total, gain_two_total, bias_total, router_total), ('dp...  38.4 us
    all_gather x1, waiting for transfers between devices, body(): lax.all_gather(expert_in, 'dp', axis=1, tiled=True)  31.6 us
    unnamed x276, local copies, waits for them, and re-layouts  20.7 us
    all_to_all x2, waiting for transfers between devices, body(): lax.all_to_all(dslots.reshape(total_experts, capacity, width), 'expert',...  13 us
    all_to_all x2, waiting for transfers between devices, body(): lax.all_to_all(from_experts(drows), 'expert', split_axis=0, concat_axis=0...  12 us
  transfers between devices with their start and end apart: 14, of which 11 were waited for; matrix products, arithmetic and copies ran while one was open for 23% of the time, Pallas kernels for 0%

commit v1 on v0

--- a/solution.py
+++ b/solution.py
@@ -269,7 +269,302 @@
     )
 
 
+BOTH = ("dp", "expert")
+
+
+def flip(tensor, bit):
+    if bit == "y":
+        return lax.ppermute(tensor, "dp", [(0, 1), (1, 0)])
+    count = lax.axis_size("expert")
+    return lax.ppermute(tensor, "expert", [(i, i ^ bit) for i in range(count)])
+
+
+def own_bit(bit):
+    if bit == "y":
+        return lax.axis_index("dp")
+    return (lax.axis_index("expert") // bit) % 2
+
+
+ORDERS = ((8, 4, "y", 2), (2, 8, 4, "y"), ("y", 2, 8, 4))
+RS_ORDERS = ((2, "y", 8, 4), ("y", 8, 4, 2), (8, 4, 2, "y"))
+PLACE = {"y": 0, 8: 1, 4: 2, 2: 3, 1: 4}
+
+
+def gather_rows(shard):
+    rows, width = shard.shape
+    third = width // 3
+    pieces = [
+        shard[:, i * third : (i + 1) * third].reshape(1, 1, 1, 1, 1, rows, third) for i in range(3)
+    ]
+
+    def grow(piece, bit):
+        got = flip(piece, bit)
+        low = own_bit(bit) == 0
+        return jnp.concatenate(
+            [jnp.where(low, piece, got), jnp.where(low, got, piece)], axis=PLACE[bit]
+        )
+
+    for step in range(5):
+        pieces = [
+            grow(piece, (ORDERS[i] + (1,))[step]) for i, piece in enumerate(pieces)
+        ]
+    return jnp.concatenate(pieces, axis=-1).reshape(32 * rows, width)
+
+
+def reduce_step(total, bit):
+    mine = own_bit(bit)
+    axis = PLACE[bit]
+    send = lax.dynamic_index_in_dim(total, 1 - mine, axis, keepdims=True).astype(jnp.bfloat16)
+    keep = lax.dynamic_index_in_dim(total, mine, axis, keepdims=True)
+    return keep + flip(send, bit).astype(jnp.float32)
+
+
+def scatter_rows(total):
+    third = total.shape[-1] // 3
+    pieces = [total[..., i * third : (i + 1) * third] for i in range(3)]
+    for step in range(4):
+        pieces = [reduce_step(piece, RS_ORDERS[i][step]) for i, piece in enumerate(pieces)]
+    whole = jnp.concatenate(pieces, axis=-1)
+    return whole.reshape(whole.shape[-2], whole.shape[-1])
+
+
+def sum_all(tensor):
+    for bit in (1, 2, "y", 4, 8):
+        tensor = tensor + flip(tensor, bit)
+    return tensor
+
+
+def dot(left, right, dims, **more):
+    return lax.dot_general(
+        left, right, (dims, ((), ())), preferred_element_type=jnp.float32, **more
+    )
+
+
+def paired_body(
+    tokens,
+    attn_weight,
+    gain_attn,
+    gain_expert,
+    bias_table,
+    router_weight,
+    expert_in,
+    expert_out,
+    routes,
+    slots,
+    buckets,
+    cotangent,
+):
+    f32, bf16 = jnp.float32, jnp.bfloat16
+    micro, _, seq_len, width = tokens.shape
+    count = micro * seq_len
+    heads = bias_table.shape[1]
+    head_size = width // heads
+    bucket_count = bias_table.shape[0]
+    experts = lax.axis_size("expert")
+    capacity = (5 * seq_len + 4 * experts - 1) // (4 * experts)
+    places = micro * capacity
+    hidden_half = expert_in.shape[2] // 2
+    width_half = width // 2
+    dp_at, expert_at = lax.axis_index("dp"), lax.axis_index("expert")
+    core = expert_at % 2
+    home = core == dp_at
+    host = expert_at - core + dp_at
+    gain_one, gain_two = gain_attn.astype(f32), gain_expert.astype(f32)
+
+    away = [
+        (dp * experts + e, (1 - dp) * experts + (e ^ 1))
+        for dp in range(2)
+        for e in range(experts)
+        if e % 2 != dp
+    ]
+    groups = [
+        [dp * experts + 2 * pair + side for dp in range(2) for pair in range(experts // 2)]
+        for side in range(2)
+    ]
+
+    def to_chips(tensor):
+        return lax.all_to_all(
+            tensor, BOTH, split_axis=0, concat_axis=0, tiled=True, axis_index_groups=groups
+        )
+
+    wt = gather_rows(attn_weight.T)
+
+    route_ids, slot_ids = routes[:, 0], slots[:, 0]
+    chip = (route_ids % 2) * (experts // 2) + route_ids // 2
+    flat = chip * places + jnp.arange(micro)[:, None] * capacity + slot_ids
+    dispatch = (
+        (flat[..., None] == jnp.arange(experts * places)) & (slot_ids[..., None] < capacity)
+    ).astype(bf16).reshape(count, experts * places)
+    upstream_b = cotangent.reshape(count, width)
+    upstream = upstream_b.astype(f32)
+    dy_rows = to_chips(dot(dispatch, upstream_b, ((0,), (0,))).astype(bf16))
+    dy_rows = jnp.concatenate([dy_rows, flip(dy_rows, 1)], axis=0)
+
+    def settle(local):
+        return jnp.where(home, local, lax.ppermute(local, BOTH, away))
+
+    in_rows = settle(expert_in[0])
+    out_columns = settle(expert_out[0])
+    in_keep = lax.dynamic_slice_in_dim(in_rows, core * hidden_half, hidden_half, 1)
+    in_got = flip(lax.dynamic_slice_in_dim(in_rows, (1 - core) * hidden_half, hidden_half, 1), 1)
+    out_keep = lax.dynamic_slice_in_dim(out_columns, core * hidden_half, hidden_half, 0)
+    out_got = flip(
+        lax.dynamic_slice_in_dim(out_columns, (1 - core) * hidden_half, hidden_half, 0), 1
+    )
+
+    def halves(tensor):
+        return (
+            lax.dynamic_slice_in_dim(tensor, core * width_half, width_half, 1),
+            lax.dynamic_slice_in_dim(tensor, (1 - core) * width_half, width_half, 1),
+        )
+
+    def whole(keep, got, axis):
+        low = core == 0
+        return jnp.concatenate(
+            [jnp.where(low, keep, got), jnp.where(low, got, keep)], axis=axis
+        )
+
+    bucket_hot = (buckets[:, :, None] == jnp.arange(bucket_count)).astype(f32)
+    bias_term = jnp.einsum("ijb,bh->hij", bucket_hot, bias_table.astype(f32), precision=HIGH)
+
+    inputs = tokens.reshape(count, width).astype(f32)
+    scale_one = rms_scale(inputs)
+    n1hat = inputs * scale_one
+    n1b = (n1hat * gain_one).astype(bf16)
+    qkv = dot(n1b, wt[: 3 * width], ((1,), (1,))).astype(bf16)
+    qkv = qkv.reshape(micro, seq_len, 3, heads, head_size)
+    query, key_part, value_part = qkv[:, :, 0], qkv[:, :, 1], qkv[:, :, 2]
+    scores = (
+        jnp.einsum("mihd,mjhd->mhij", query, key_part, preferred_element_type=f32) + bias_term
+    )
+    probs = jax.nn.softmax(scores, axis=-1)
+    probs_b = probs.astype(bf16)
+    mixed_b = (
+        jnp.einsum("mhij,mjhd->mihd", probs_b, value_part, preferred_element_type=f32)
+        .reshape(count, width)
+        .astype(bf16)
+    )
+    resid = inputs + dot(mixed_b, wt[3 * width :], ((1,), (1,)))
+    scale_two = rms_scale(resid)
+    n2hat = resid * scale_two
+    n2b = (n2hat * gain_two).astype(bf16)
+
+    own_rows = to_chips(dot(dispatch, n2b, ((0,), (0,))).astype(bf16))
+    rows = jnp.concatenate([own_rows, flip(own_rows, 1)], axis=0)
+    row_count = own_rows.shape[0]
+
+    row_probs = jax.nn.softmax(dot(rows, router_weight, ((1,), (0,))), axis=-1)
+    chosen = (jnp.arange(experts) == host).astype(f32)
+    row_gate = jnp.sum(row_probs * chosen, axis=-1, keepdims=True)
+    dmade = (row_gate * dy_rows.astype(f32)).astype(bf16)
+
+    rows_keep, rows_got = halves(rows)
+    dmade_keep, dmade_got = halves(dmade)
+    upre = dot(rows_keep, in_keep, ((1,), (0,))) + dot(rows_got, in_got, ((1,), (0,)))
+    hidden = smooth_gate(upre).astype(bf16)
+    dhidden = dot(dmade_keep, out_keep, ((1,), (1,))) + dot(dmade_got, out_got, ((1,), (1,)))
+    du = jax.vjp(smooth_gate, upre)[1](dhidden)[0].astype(bf16)
+    made_part = whole(
+        dot(hidden, out_keep, ((1,), (0,))), dot(hidden, out_got, ((1,), (0,))), 1
+    )
+    drows_part = whole(dot(du, in_keep, ((1,), (1,))), dot(du, in_got, ((1,), (1,))), 1)
+    parts = jnp.stack([made_part, drows_part])
+    parts = parts[:, :row_count] + flip(parts[:, row_count:], 1)
+    made = parts[0].astype(bf16)
+    drows = parts[1].astype(bf16)
+    dgate = jnp.sum(dy_rows[:row_count].astype(f32) * made.astype(f32), axis=-1, keepdims=True)
+    dlogits = row_probs[:row_count] * dgate * (chosen - row_gate[:row_count])
+    router_part = dot(own_rows.astype(f32), dlogits, ((0,), (0,)), precision=HIGH)
+    dn2_rows = drows.astype(f32) + dot(
+        dlogits, router_weight.astype(f32), ((1,), (1,)), precision=HIGH
+    )
+    dn2_home = to_chips(dn2_rows.astype(bf16))
+    made_home = to_chips(made)
+
+    in_mine = dot(rows_keep, du, ((0,), (0,)))
+    in_other = flip(dot(rows_got, du, ((0,), (0,))).astype(bf16), 1).astype(f32)
+    out_mine = dot(hidden, dmade_keep, ((0,), (0,)))
+    out_other = flip(dot(hidden, dmade_got, ((0,), (0,))).astype(bf16), 1).astype(f32)
+    in_total = whole(in_mine, in_other, 1)
+    out_total = whole(out_mine, out_other, 0)
+    in_share = jnp.where(
+        home, in_total, lax.ppermute(in_total.astype(bf16), BOTH, away).astype(f32)
+    )
+    out_share = jnp.where(
+        home, out_total, lax.ppermute(out_total.astype(bf16), BOTH, away).astype(f32)
+    )
+
+    dn2 = dot(dispatch, dn2_home, ((1,), (0,)))
+    gain_two_part = jnp.sum(dn2 * n2hat, axis=0)
+    dhat_two = dn2 * gain_two
+    dresid = upstream + scale_two * (
+        dhat_two - n2hat * jnp.mean(dhat_two * n2hat, axis=-1, keepdims=True)
+    )
+    dattn = dresid.astype(bf16)
+    dmixed = dot(dattn, wt[3 * width :], ((1,), (0,))).astype(bf16)
+    dmixed = dmixed.reshape(micro, seq_len, heads, head_size)
+    dvalue = jnp.einsum("mhij,mihd->mjhd", probs_b, dmixed, preferred_element_type=f32)
+    dprobs = jnp.einsum("mihd,mjhd->mhij", dmixed, value_part, preferred_element_type=f32)
+    dscores = probs * (dprobs - jnp.sum(probs * dprobs, axis=-1, keepdims=True))
+    bias_part = jnp.einsum("hij,ijb->bh", jnp.sum(dscores, axis=0), bucket_hot, precision=HIGH)
+    dscores_b = dscores.astype(bf16)
+    dquery = jnp.einsum("mhij,mjhd->mihd", dscores_b, key_part, preferred_element_type=f32)
+    dkey = jnp.einsum("mhij,mihd->mjhd", dscores_b, query, preferred_element_type=f32)
+    dqkv = jnp.concatenate(
+        [part.reshape(count, width).astype(bf16) for part in (dquery, dkey, dvalue)], axis=1
+    )
+
+    def core_step(gradient, values):
+        block = width * 4 // 32
+        columns = gradient.T.reshape(-1, 2, block, count)
+
+        def product(side):
+            picked = lax.dynamic_index_in_dim(columns, side, 1, keepdims=False)
+            return dot(picked.reshape(-1, count), values, ((1,), (0,)))
+
+        got = flip(product(1 - core).astype(bf16), 1)
+        return product(core) + got.astype(f32)
+
+    o_total = core_step(dattn, mixed_b)
+    qkv_total = core_step(dqkv, n1b)
+    total = jnp.concatenate([qkv_total, o_total], axis=0)
+    attn_share = scatter_rows(total.reshape(2, 2, 2, 2, 1, -1, width)).T
+
+    dn1 = dot(dqkv, wt[: 3 * width], ((1,), (0,)))
+    gain_one_part = jnp.sum(dn1 * n1hat, axis=0)
+    dhat_one = dn1 * gain_one
+    token_grad = dresid + scale_one * (
+        dhat_one - n1hat * jnp.mean(dhat_one * n1hat, axis=-1, keepdims=True)
+    )
+
+    router_probs = jax.nn.softmax(dot(n2b, router_weight, ((1,), (0,))), axis=-1)
+    picked = (route_ids.reshape(count, 1) == jnp.arange(experts)).astype(f32)
+    gate = jnp.sum(router_probs * picked, axis=-1, keepdims=True)
+    returned = dot(dispatch, made_home, ((1,), (0,)))
+    output = (resid + gate * returned).astype(bf16)
+
+    early = sum_all(
+        jnp.concatenate([gain_two_part[None], router_part.T], axis=0)
+    )
+    late = sum_all(
+        jnp.concatenate([gain_one_part, bias_part.reshape(-1)]).reshape(1, -1)
+    )[0]
+    return (
+        output.reshape(tokens.shape),
+        token_grad.reshape(tokens.shape),
+        attn_share,
+        late[:width],
+        early[0],
+        late[width:].reshape(bucket_count, heads),
+        early[1:].T,
+        in_share[None],
+        out_share[None],
+    )
+
+
 def solution(mesh):
+    paired = mesh.shape["dp"] == 2 and mesh.shape["expert"] == 16
+    chosen = paired_body if paired else body
     placed = (
         P(None, ("dp", "expert"), None, None),
         P(None, ("dp", "expert")),
@@ -285,7 +580,7 @@
         P(None, ("dp", "expert"), None, None),
     )
     return jax.shard_map(
-        body,
+        chosen,
         mesh=mesh,
         in_specs=placed,
         out_specs=(

time: 546 us -> 293 us (0.54)
  waiting for transfers between devices: 317 us -> 95.2 us
  blocking collectives: 38.4 us -> 0 us
  starting transfers between devices: 32.4 us -> 68.1 us
  matrix products: 72.2 us -> 43.6 us
  between operations: 16.4 us -> 2.14 us
  local copies, waits for them, and re-layouts: 39 us -> 48.4 us
  other arithmetic: 27.9 us -> 33.4 us
    all_gather x3 -> x0, waiting for transfers between devices: 158 us -> none  [the longest x1 66.2 us: body(): lax.all_gather(attn_weight, ('dp', 'expert'), axis=1, tiled=True)]
    unnamed x7 -> x0, waiting for transfers between devices: 118 us -> none
    ppermute x0 -> x50, waiting for transfers between devices: none -> 67.2 us  [the longest x38 47.7 us: flip(): return lax.ppermute(tensor, 'expert', [(i, i ^ bit) for i in range(count)])]
    ppermute x0 -> x50, starting transfers between devices: none -> 47.1 us  [the longest x38 30.7 us: flip(): return lax.ppermute(tensor, 'expert', [(i, i ^ bit) for i in range(count)])]
    psum x1 -> x0, blocking collectives: 38.4 us -> none  [body(): lax.psum((gain_one_total, gain_two_total, bias_total, router_total), ('dp...]
    dot_general x49 -> x36, matrix products: 72.2 us -> 43.6 us  [the longest x28 33.6 us: dot(): lax.dot_general(left, right, (dims, ((), ())), preferred_element_type=jnp...]
    convert_element_type x0 -> x22, local copies, waits for them, and re-layouts: none -> 14.3 us  [the longest x6 12.2 us: paired_body(): part.reshape(count, width).astype(bf16)]
    all_to_all x8 -> x4, waiting for transfers between devices: 42 us -> 27.9 us  [to_chips(): lax.all_to_all(tensor, BOTH, split_axis=0, concat_axis=0, tiled=True, axi...]
  transfers between devices with their start and end apart: 14 -> 54, of which waited for: 11 -> 22; matrix products, arithmetic and copies ran while one was open for 23% -> 36% of each run, Pallas kernels for 0% -> 0%
where the time goes in v1:
time: 293 us; the launch traced here: 291 us
  waiting for transfers between devices  95.2 us (32%)
  starting transfers between devices  68.1 us (23%)
  local copies, waits for them, and re-layouts  48.4 us (17%)
  matrix products  43.6 us (15%)
  other arithmetic  33.4 us (11%)
    ppermute x38, waiting for transfers between devices, flip(): return lax.ppermute(tensor, 'expert', [(i, i ^ bit) for i in range(count)])  47.7 us
    dot_general x28, matrix products, dot(): lax.dot_general(left, right, (dims, ((), ())), preferred_element_type=jnp...  33.6 us
    ppermute x38, starting transfers between devices, flip(): return lax.ppermute(tensor, 'expert', [(i, i ^ bit) for i in range(count)])  30.7 us
    all_to_all x4, waiting for transfers between devices, to_chips(): lax.all_to_all(tensor, BOTH, split_axis=0, concat_axis=0, tiled=True, axi...  27.9 us
    all_to_all x4, starting transfers between devices, to_chips(): lax.all_to_all(tensor, BOTH, split_axis=0, concat_axis=0, tiled=True, axi...  21 us
    ppermute x8, waiting for transfers between devices, flip(): return lax.ppermute(tensor, 'dp', [(0, 1), (1, 0)])  19.5 us
    convert_element_type x6, local copies, waits for them, and re-layouts, paired_body(): part.reshape(count, width).astype(bf16)  12.2 us
    unnamed x91, local copies, waits for them, and re-layouts  10.1 us
  transfers between devices with their start and end apart: 54, of which 22 were waited for; matrix products, arithmetic and copies ran while one was open for 36% of the time, Pallas kernels for 0%

profile of v1, /device:TPU:0, one launch (start us, length us, event | category | flops | bytes accessed | tf_op | source)
XLA Modules:
  0.0 290.7 jit_solution(13647032071560886593)
XLA Ops:
  1.6 4.1 %collective-permute-start = (bf16[1,1,1,1,1,96,256]{6,5,4,3,2,1,0:T(8,128)(2,1)S(1)}, bf16[1,1,1,1,1,96,256]{6,5,4,3,2,1,0:T(8,128)(2,1)S(1)}, u32[]{:S(2)}, u32[]{:S(2)}) collective-permute-start(bf16[1,1,1,1,1,96,256]{6,5,4,3,2,1,0:T(8,128)(2,1)S(1)} %get-tuple-element.98), channel_id=1, source_target_pairs={{0,8},{1,9},{2,10},{3,11},{4,12},{5,13},{6,14},{7,15},{8,0},{9,1},... | collective-permute-start | bytes 147464 | tf_op jit(solution)/shard_map/ppermute | solution.py:279
  8.7 2.0 collective-permute-start.16
  20.3 1.6 collective-permute-start.1
  22.0 5.6 %collective-permute-done.6 = bf16[1,1,1,2,1,96,256]{6,5,4,3,2,1,0:T(8,128)(2,1)S(1)} collective-permute-done((bf16[1,1,1,2,1,96,256]{6,5,4,3,2,1,0:T(8,128)(2,1)S(1)}, bf16[1,1,1,2,1,96,256]{6,5,4,3,2,1,0:T(8,128)(2,1)S(1)}, u32[]{:S(2)}, u32[]{:S(2)}) %collective-permute-start.6) | collective-permute-done | bytes 98336 | tf_op jit(solution)/shard_map/ppermute | solution.py:279
  27.8 1.9 collective-permute-start.12
  29.8 7.5 %collective-permute-done.7 = bf16[1,2,1,2,1,96,256]{6,5,4,3,2,1,0:T(8,128)(2,1)S(1)} collective-permute-done((bf16[1,2,1,2,1,96,256]{6,5,4,3,2,1,0:T(8,128)(2,1)S(1)}, bf16[1,2,1,2,1,96,256]{6,5,4,3,2,1,0:T(8,128)(2,1)S(1)}, u32[]{:S(2)}, u32[]{:S(2)}) %collective-permute-start.7) | collective-permute-done | bytes 196640 | tf_op jit(solution)/shard_map/ppermute | solution.py:279
  37.5 2.1 collective-permute-done.12
  39.7 6.1 %collective-permute-done.2 = bf16[1,2,2,1,1,96,256]{6,5,4,3,2,1,0:T(8,128)(2,1)S(1)} collective-permute-done((bf16[1,2,2,1,1,96,256]{6,5,4,3,2,1,0:T(8,128)(2,1)S(1)}, bf16[1,2,2,1,1,96,256]{6,5,4,3,2,1,0:T(8,128)(2,1)S(1)}, u32[]{:S(2)}, u32[]{:S(2)}) %collective-permute-start.2) | collective-permute-done | bytes 196640 | tf_op jit(solution)/shard_map/ppermute | solution.py:277
  46.6 4.3 %collective-permute-done.8 = bf16[1,2,2,2,1,96,256]{6,5,4,3,2,1,0:T(8,128)(2,1)S(1)} collective-permute-done((bf16[1,2,2,2,1,96,256]{6,5,4,3,2,1,0:T(8,128)(2,1)S(1)}, bf16[1,2,2,2,1,96,256]{6,5,4,3,2,1,0:T(8,128)(2,1)S(1)}, u32[]{:S(2)}, u32[]{:S(2)}) %collective-permute-start.8) | collective-permute-done | bytes 393248 | tf_op jit(solution)/shard_map/ppermute | solution.py:277
  51.8 3.4 %collective-permute-done.3 = bf16[2,2,2,1,1,96,256]{6,5,4,3,2,1,0:T(8,128)(2,1)S(1)} collective-permute-done((bf16[2,2,2,1,1,96,256]{6,5,4,3,2,1,0:T(8,128)(2,1)S(1)}, bf16[2,2,2,1,1,96,256]{6,5,4,3,2,1,0:T(8,128)(2,1)S(1)}, u32[]{:S(2)}, u32[]{:S(2)}) %collective-permute-start.3) | collective-permute-done | bytes 393248 | tf_op jit(solution)/shard_map/ppermute | solution.py:279
  55.7 2.0 collective-permute-done.4
  58.3 2.2 copy-done.12
  67.4 2.0 multiply_reduce_fusion.6
  70.6 5.0 %all-to-all-start = ((bf16[16,10,768]{2,1,0:T(8,128)(2,1)}), bf16[16,10,768]{2,1,0:T(8,128)(2,1)}, u32[]{:S(2)}, u32[]{:S(2)}) async-start(bf16[16,10,768]{2,1,0:T(8,128)(2,1)} %all_to_all.30), calls=%async_computation | async-start | bytes 786432 | tf_op jit(solution)/shard_map/all_to_all | solution.py:386
  75.6 2.1 collective-permute-start.18
  79.0 10.0 %all-to-all-done = bf16[16,10,768]{2,1,0:T(8,128)(2,1)} async-done(((bf16[16,10,768]{2,1,0:T(8,128)(2,1)}), bf16[16,10,768]{2,1,0:T(8,128)(2,1)}, u32[]{:S(2)}, u32[]{:S(2)}) %all-to-all-start) | async-done | bytes 245792 | tf_op jit(solution)/shard_map/all_to_all | solution.py:386
  88.9 3.7 %all-to-all-start.1 = ((bf16[16,10,768]{2,1,0:T(8,128)(2,1)}), bf16[16,10,768]{2,1,0:T(8,128)(2,1)S(1)}, u32[]{:S(2)}, u32[]{:S(2)}) async-start(bf16[16,10,768]{2,1,0:T(8,128)(2,1)} %all_to_all.33), calls=%async_computation.1 | async-start | bytes 786432 | tf_op jit(solution)/shard_map/all_to_all | solution.py:386
  92.7 1.8 all_to_all.32
  95.2 17.6 %all-to-all-done.1 = bf16[16,10,768]{2,1,0:T(8,128)(2,1)S(1)} async-done(((bf16[16,10,768]{2,1,0:T(8,128)(2,1)}), bf16[16,10,768]{2,1,0:T(8,128)(2,1)S(1)}, u32[]{:S(2)}, u32[]{:S(2)}) %all-to-all-start.1) | async-done | bytes 245792 | tf_op jit(solution)/shard_map/all_to_all | solution.py:386
  116.4 2.2 collective-permute-start.17
  118.6 1.9 broadcast_select_fusion
  126.1 1.7 fusion.12
  130.2 1.8 convolution_convert_fusion.3
  132.7 2.0 convolution_convert_fusion.2
  138.8 5.5 %all-to-all-start.3 = ((bf16[16,10,768]{2,1,0:T(8,128)(2,1)}), bf16[16,10,768]{2,1,0:T(8,128)(2,1)}, u32[]{:S(2)}, u32[]{:S(2)}) async-start(bf16[16,10,768]{2,1,0:T(8,128)(2,1)} %all_to_all.38), calls=%async_computation.3 | async-start | bytes 786432 | tf_op jit(solution)/shard_map/all_to_all | solution.py:386
  144.6 2.2 convert_select_fusion.3
  146.8 1.7 fusion.2
  149.0 2.0 collective-permute-start.47
  151.1 2.2 convert_select_fusion.1
  155.5 1.7 fusion.1
  157.6 6.8 %all-to-all-start.2 = ((bf16[16,10,768]{2,1,0:T(8,128)(2,1)}), bf16[16,10,768]{2,1,0:T(8,128)(2,1)}, u32[]{:S(2)}, u32[]{:S(2)}) async-start(bf16[16,10,768]{2,1,0:T(8,128)(2,1)} %convert_element_type.272), calls=%async_computation.2 | async-start | bytes 786432 | tf_op jit(solution)/shard_map/all_to_all | solution.py:386
  166.6 1.6 convolution_convert_fusion.11
  169.4 2.1 copy.82
  171.5 2.6 fusion.18
  174.1 1.8 multiply_reduce_fusion
  180.4 2.1 copy.84
  182.5 1.9 convert_element_type.291
  184.4 2.1 copy.78
  186.6 1.9 convert_element_type.285
  188.5 2.2 copy.81
  190.7 1.9 convert_element_type.288
  192.6 2.0 copy.89
  194.7 1.8 convolution_bitcast_fusion.1
  199.4 2.8 multiply_reduce_fusion.3
  203.9 1.8 convolution_convert_fusion.1
  205.7 2.0 collective-permute-start.37
  209.4 1.9 collective-permute-start.38
  211.3 1.7 collective-permute-done.38
  213.1 1.9 collective-permute-start.39
  218.3 1.8 all_to_all.37
  220.2 2.4 collective-permute-start.40
  225.0 1.9 fusion.20
  226.9 2.0 collective-permute-start.49
  230.2 3.8 %collective-permute-done.44 = f32[17,768]{1,0:T(8,128)S(1)} collective-permute-done((f32[17,768]{1,0:T(8,128)S(1)}, f32[17,768]{1,0:T(8,128)S(1)}, u32[]{:S(2)}, u32[]{:S(2)}) %collective-permute-start.44) | collective-permute-done | bytes 52256 | tf_op jit(solution)/shard_map/ppermute | solution.py:279
  235.3 5.4 %collective-permute-done.45 = f32[17,768]{1,0:T(8,128)S(1)} collective-permute-done((f32[17,768]{1,0:T(8,128)S(1)}, f32[17,768]{1,0:T(8,128)S(1)}, u32[]{:S(2)}, u32[]{:S(2)}) %collective-permute-start.45) | collective-permute-done | bytes 52256 | tf_op jit(solution)/shard_map/ppermute | solution.py:279
  243.5 2.1 convert_add_fusion
  248.1 5.0 %select_bitcast_fusion.1 = f32[1,384,3072]{2,1,0:T(8,128)} fusion(bf16[384,3072]{1,0:T(8,128)(2,1)} %collective-permute-done.47, f32[384,1536]{1,0:T(8,128)S(1)} %copy-done.3, f32[384,1536]{1,0:T(8,128)S(1)} %get-tuple-element.49, pred[]{:T(512)S(6)} %eq.124), kind=kLoop, calls=%fused_computation.6 | loop fusion | flops 3538944 | bytes 11796481 | tf_op jit(solution)/shard_map/broadcast_in_dim | solution.py:560
  253.2 4.4 %select_bitcast_fusion = f32[1,3072,384]{2,1,0:T(8,128)} fusion(bf16[3072,384]{1,0:T(8,128)(2,1)} %collective-permute-done.49, f32[1536,384]{1,0:T(8,128)S(1)} %copy-done.7, f32[1536,384]{1,0:T(8,128)S(1)} %copy-done.5, pred[]{:T(512)S(6)} %eq.124), kind=kLoop, calls=%fused_computation.5 | loop fusion | flops 3538944 | bytes 11796481 | tf_op jit(solution)/shard_map/broadcast_in_dim | solution.py:561
  257.6 7.3 %collective-permute-done.28 = bf16[1,2,2,2,1,96,256]{6,5,4,3,2,1,0:T(8,128)(2,1)S(1)} collective-permute-done((bf16[1,2,2,2,1,96,256]{6,5,4,3,2,1,0:T(8,128)(2,1)S(1)}, bf16[1,2,2,2,1,96,256]{6,5,4,3,2,1,0:T(8,128)(2,1)S(1)}, u32[]{:S(2)}, u32[]{:S(2)}) %collective-permute-start.28) | collective-permute-done | bytes 393248 | tf_op jit(solution)/shard_map/ppermute | solution.py:277
  267.0 1.8 collective-permute-start.25
  268.8 8.3 %collective-permute-done.29 = bf16[1,1,2,2,1,96,256]{6,5,4,3,2,1,0:T(8,128)(2,1)S(1)} collective-permute-done((bf16[1,1,2,2,1,96,256]{6,5,4,3,2,1,0:T(8,128)(2,1)S(1)}, bf16[1,1,2,2,1,96,256]{6,5,4,3,2,1,0:T(8,128)(2,1)S(1)}, u32[]{:S(2)}, u32[]{:S(2)}) %collective-permute-start.29) | collective-permute-done | bytes 196640 | tf_op jit(solution)/shard_map/ppermute | solution.py:279
  278.1 1.8 collective-permute-start.26
  279.9 3.2 %collective-permute-done.30 = bf16[1,1,1,2,1,96,256]{6,5,4,3,2,1,0:T(8,128)(2,1)S(1)} collective-permute-done((bf16[1,1,1,2,1,96,256]{6,5,4,3,2,1,0:T(8,128)(2,1)S(1)}, bf16[1,1,1,2,1,96,256]{6,5,4,3,2,1,0:T(8,128)(2,1)S(1)}, u32[]{:S(2)}, u32[]{:S(2)}) %collective-permute-start.30) | collective-permute-done | bytes 98336 | tf_op jit(solution)/shard_map/ppermute | solution.py:279
  287.5 2.5 collective-permute-done.27
  (318 shorter events, 81.6 us)
Async XLA Ops:
  0.6 115.0 %copy-start = (bf16[768,16]{0,1:T(8,128)(2,1)S(1)}, bf16[768,16]{0,1:T(8,128)(2,1)}, u32[]{:S(2)}) copy-start(bf16[768,16]{0,1:T(8,128)(2,1)} %param.17) | copy-start | bytes 73732
  0.7 18.6 %copy-start.39 = (bf16[768,96]{0,1:T(8,128)(2,1)S(1)}, bf16[768,96]{0,1:T(8,128)(2,1)}, u32[]{:S(2)}) copy-start(bf16[768,96]{0,1:T(8,128)(2,1)} %param.13) | copy-start | bytes 442372
  1.6 17.6 %collective-permute-start = (bf16[1,1,1,1,1,96,256]{6,5,4,3,2,1,0:T(8,128)(2,1)S(1)}, bf16[1,1,1,1,1,96,256]{6,5,4,3,2,1,0:T(8,128)(2,1)S(1)}, u32[]{:S(2)}, u32[]{:S(2)}) collective-permute-start(bf16[1,1,1,1,1,96,256]{6,5,4,3,2,1,0:T(8,128)(2,1)S(1)} %get-tuple-element.98), channel_id=1, source_target_pairs={{0,8},{1,9},{2,10},{3,11},{4,12},{5,13},{6,14},{7,15},{8,0},{9,1},... | collective-permute-start | bytes 147464 | tf_op jit(solution)/shard_map/ppermute | solution.py:279
  5.7 13.5 %collective-permute-start.10 = (bf16[1,1,1,1,1,96,256]{6,5,4,3,2,1,0:T(8,128)(2,1)S(1)}, bf16[1,1,1,1,1,96,256]{6,5,4,3,2,1,0:T(8,128)(2,1)S(1)}, u32[]{:S(2)}, u32[]{:S(2)}) collective-permute-start(bf16[1,1,1,1,1,96,256]{6,5,4,3,2,1,0:T(8,128)(2,1)S(1)} %get-tuple-element.99), channel_id=1, source_target_pairs={{0,16},{16,0},{1,17},{17,1},{2,18},{18,2},{3,19},{19,3},{4,20},{20... | collective-permute-start | bytes 147464 | tf_op jit(solution)/shard_map/ppermute | solution.py:277
  7.2 12.0 %collective-permute-start.5 = (bf16[1,1,1,1,1,96,256]{6,5,4,3,2,1,0:T(8,128)(2,1)S(1)}, bf16[1,1,1,1,1,96,256]{6,5,4,3,2,1,0:T(8,128)(2,1)S(1)}, u32[]{:S(2)}, u32[]{:S(2)}) collective-permute-start(bf16[1,1,1,1,1,96,256]{6,5,4,3,2,1,0:T(8,128)(2,1)S(1)} %get-tuple-element.100), channel_id=1, source_target_pairs={{0,2},{1,3},{2,0},{3,1},{4,6},{5,7},{6,4},{7,5},{8,10},{9,11},{10,... | collective-permute-start | bytes 147464 | tf_op jit(solution)/shard_map/ppermute | solution.py:279
  8.7 107.2 %collective-permute-start.16 = (bf16[384,3072]{1,0:T(8,128)(2,1)}, bf16[384,3072]{1,0:T(8,128)(2,1)}, u32[]{:S(2)}, u32[]{:S(2)}) collective-permute-start(bf16[384,3072]{1,0:T(8,128)(2,1)} %bitcast.165), channel_id=1, source_target_pairs={{1,16},{3,18},{5,20},{7,22},{9,24},{11,26},{13,28},{15,30},{16,1},... | collective-permute-start | bytes 7077896 | tf_op jit(solution)/shard_map/ppermute | solution.py:404
  19.3 8.3 %collective-permute-start.6 = (bf16[1,1,1,2,1,96,256]{6,5,4,3,2,1,0:T(8,128)(2,1)S(1)}, bf16[1,1,1,2,1,96,256]{6,5,4,3,2,1,0:T(8,128)(2,1)S(1)}, u32[]{:S(2)}, u32[]{:S(2)}) collective-permute-start(bf16[1,1,1,2,1,96,256]{6,5,4,3,2,1,0:T(8,128)(2,1)S(1)} %pad_maximum_fusion.14), channel_id=1, source_target_pairs={{0,8},{1,9},{2,10},{3,11},{4,12},{5,13},{6,14},{7,15},{8,0},{9,1},... | collective-permute-start | bytes 294920 | tf_op jit(solution)/shard_map/ppermute | solution.py:279
  19.7 8.0 %collective-permute-start.11 = (bf16[2,1,1,1,1,96,256]{6,5,4,3,2,1,0:T(8,128)(2,1)S(1)}, bf16[2,1,1,1,1,96,256]{6,5,4,3,2,1,0:T(8,128)(2,1)S(1)}, u32[]{:S(2)}, u32[]{:S(2)}) collective-permute-start(bf16[2,1,1,1,1,96,256]{6,5,4,3,2,1,0:T(8,128)(2,1)S(1)} %pad_maximum_fusion.15), channel_id=1, source_target_pairs={{0,2},{1,3},{2,0},{3,1},{4,6},{5,7},{6,4},{7,5},{8,10},{9,11},{10,... | collective-permute-start | bytes 294920 | tf_op jit(solution)/shard_map/ppermute | solution.py:279
  20.3 9.4 %collective-permute-start.1 = (bf16[1,2,1,1,1,96,256]{6,5,4,3,2,1,0:T(8,128)(2,1)S(1)}, bf16[1,2,1,1,1,96,256]{6,5,4,3,2,1,0:T(8,128)(2,1)S(1)}, u32[]{:S(2)}, u32[]{:S(2)}) collective-permute-start(bf16[1,2,1,1,1,96,256]{6,5,4,3,2,1,0:T(8,128)(2,1)S(1)} %pad_maximum_fusion.13), channel_id=1, source_target_pairs={{0,4},{1,5},{2,6},{3,7},{4,0},{5,1},{6,2},{7,3},{8,12},{9,13},{10,... | collective-permute-start | bytes 294920 | tf_op jit(solution)/shard_map/ppermute | solution.py:279
  27.6 9.7 %collective-permute-start.7 = (bf16[1,2,1,2,1,96,256]{6,5,4,3,2,1,0:T(8,128)(2,1)S(1)}, bf16[1,2,1,2,1,96,256]{6,5,4,3,2,1,0:T(8,128)(2,1)S(1)}, u32[]{:S(2)}, u32[]{:S(2)}) collective-permute-start(bf16[1,2,1,2,1,96,256]{6,5,4,3,2,1,0:T(8,128)(2,1)S(1)} %pad_maximum_fusion.11), channel_id=1, source_target_pairs={{0,4},{1,5},{2,6},{3,7},{4,0},{5,1},{6,2},{7,3},{8,12},{9,13},{10,... | collective-permute-start | bytes 589832 | tf_op jit(solution)/shard_map/ppermute | solution.py:279
  27.8 11.7 %collective-permute-start.12 = (bf16[2,1,1,2,1,96,256]{6,5,4,3,2,1,0:T(8,128)(2,1)S(1)}, bf16[2,1,1,2,1,96,256]{6,5,4,3,2,1,0:T(8,128)(2,1)S(1)}, u32[]{:S(2)}, u32[]{:S(2)}) collective-permute-start(bf16[2,1,1,2,1,96,256]{6,5,4,3,2,1,0:T(8,128)(2,1)S(1)} %pad_maximum_fusion.12), channel_id=1, source_target_pairs={{0,8},{1,9},{2,10},{3,11},{4,12},{5,13},{6,14},{7,15},{8,0},{9,1},... | collective-permute-start | bytes 589832 | tf_op jit(solution)/shard_map/ppermute | solution.py:279
  29.7 16.1 %collective-permute-start.2 = (bf16[1,2,2,1,1,96,256]{6,5,4,3,2,1,0:T(8,128)(2,1)S(1)}, bf16[1,2,2,1,1,96,256]{6,5,4,3,2,1,0:T(8,128)(2,1)S(1)}, u32[]{:S(2)}, u32[]{:S(2)}) collective-permute-start(bf16[1,2,2,1,1,96,256]{6,5,4,3,2,1,0:T(8,128)(2,1)S(1)} %pad_maximum_fusion.10), channel_id=1, source_target_pairs={{0,16},{16,0},{1,17},{17,1},{2,18},{18,2},{3,19},{19,3},{4,20},{20... | collective-permute-start | bytes 589832 | tf_op jit(solution)/shard_map/ppermute | solution.py:277
  37.4 13.5 %collective-permute-start.8 = (bf16[1,2,2,2,1,96,256]{6,5,4,3,2,1,0:T(8,128)(2,1)S(1)}, bf16[1,2,2,2,1,96,256]{6,5,4,3,2,1,0:T(8,128)(2,1)S(1)}, u32[]{:S(2)}, u32[]{:S(2)}) collective-permute-start(bf16[1,2,2,2,1,96,256]{6,5,4,3,2,1,0:T(8,128)(2,1)S(1)} %pad_maximum_fusion.8), channel_id=1, source_target_pairs={{0,16},{16,0},{1,17},{17,1},{2,18},{18,2},{3,19},{19,3},{4,20},{20... | collective-permute-start | bytes 1179656 | tf_op jit(solution)/shard_map/ppermute | solution.py:277
  39.6 11.5 %collective-permute-start.13 = (bf16[2,2,1,2,1,96,256]{6,5,4,3,2,1,0:T(8,128)(2,1)S(1)}, bf16[2,2,1,2,1,96,256]{6,5,4,3,2,1,0:T(8,128)(2,1)S(1)}, u32[]{:S(2)}, u32[]{:S(2)}) collective-permute-start(bf16[2,2,1,2,1,96,256]{6,5,4,3,2,1,0:T(8,128)(2,1)S(1)} %pad_maximum_fusion.9), channel_id=1, source_target_pairs={{0,4},{1,5},{2,6},{3,7},{4,0},{5,1},{6,2},{7,3},{8,12},{9,13},{10,... | collective-permute-start | bytes 1179656 | tf_op jit(solution)/shard_map/ppermute | solution.py:279
  45.9 9.3 %collective-permute-start.3 = (bf16[2,2,2,1,1,96,256]{6,5,4,3,2,1,0:T(8,128)(2,1)S(1)}, bf16[2,2,2,1,1,96,256]{6,5,4,3,2,1,0:T(8,128)(2,1)S(1)}, u32[]{:S(2)}, u32[]{:S(2)}) collective-permute-start(bf16[2,2,2,1,1,96,256]{6,5,4,3,2,1,0:T(8,128)(2,1)S(1)} %pad_maximum_fusion.7), channel_id=1, source_target_pairs={{0,2},{1,3},{2,0},{3,1},{4,6},{5,7},{6,4},{7,5},{8,10},{9,11},{10,... | collective-permute-start | bytes 1179656 | tf_op jit(solution)/shard_map/ppermute | solution.py:279
  51.0 4.5 %collective-permute-start.9 = (bf16[2,2,2,2,1,96,256]{6,5,4,3,2,1,0:T(8,128)(2,1)S(1)}, bf16[2,2,2,2,1,96,256]{6,5,4,3,2,1,0:T(8,128)(2,1)S(1)}, u32[]{:S(2)}, u32[]{:S(2)}) collective-permute-start(bf16[2,2,2,2,1,96,256]{6,5,4,3,2,1,0:T(8,128)(2,1)S(1)} %pad_maximum_fusion.5), channel_id=1, source_target_pairs={{0,1},{1,0},{2,3},{3,2},{4,5},{5,4},{6,7},{7,6},{8,9},{9,8},{10,11... | collective-permute-start | bytes 2359304 | tf_op jit(solution)/shard_map/ppermute | solution.py:279
  51.2 4.4 %collective-permute-start.14 = (bf16[2,2,2,2,1,96,256]{6,5,4,3,2,1,0:T(8,128)(2,1)S(1)}, bf16[2,2,2,2,1,96,256]{6,5,4,3,2,1,0:T(8,128)(2,1)S(1)}, u32[]{:S(2)}, u32[]{:S(2)}) collective-permute-start(bf16[2,2,2,2,1,96,256]{6,5,4,3,2,1,0:T(8,128)(2,1)S(1)} %pad_maximum_fusion.6), channel_id=1, source_target_pairs={{0,1},{1,0},{2,3},{3,2},{4,5},{5,4},{6,7},{7,6},{8,9},{9,8},{10,11... | collective-permute-start | bytes 2359304 | tf_op jit(solution)/shard_map/ppermute | solution.py:279
  55.4 2.4 collective-permute-start.4
  69.4 60.4 %copy-start.10 = (f32[128,768]{1,0:T(8,128)}, f32[128,768]{1,0:T(8,128)S(1)}, u32[]{:S(2)}) copy-start(f32[128,768]{1,0:T(8,128)S(1)} %get-tuple-element.104) | copy-start | bytes 1179652
  70.6 18.3 %all-to-all-start = ((bf16[16,10,768]{2,1,0:T(8,128)(2,1)}), bf16[16,10,768]{2,1,0:T(8,128)(2,1)}, u32[]{:S(2)}, u32[]{:S(2)}) async-start(bf16[16,10,768]{2,1,0:T(8,128)(2,1)} %all_to_all.30), calls=%async_computation | async-start | bytes 786432 | tf_op jit(solution)/shard_map/all_to_all | solution.py:386
  75.6 43.0 %collective-permute-start.18 = (bf16[3072,384]{1,0:T(8,128)(2,1)}, bf16[3072,384]{1,0:T(8,128)(2,1)}, u32[]{:S(2)}, u32[]{:S(2)}) collective-permute-start(bf16[3072,384]{1,0:T(8,128)(2,1)} %bitcast.13), channel_id=1, source_target_pairs={{1,16},{3,18},{5,20},{7,22},{9,24},{11,26},{13,28},{15,30},{16,1},... | collective-permute-start | bytes 7077896 | tf_op jit(solution)/shard_map/ppermute | solution.py:404
  79.0 36.9 %copy-start.24 = (bf16[1,384,3072]{2,1,0:T(8,128)(2,1)S(1)}, bf16[1,384,3072]{2,1,0:T(8,128)(2,1)}, u32[]{:S(2)}) copy-start(bf16[1,384,3072]{2,1,0:T(8,128)(2,1)} %param.18) | copy-start | bytes 7077892
  88.9 23.9 %all-to-all-start.1 = ((bf16[16,10,768]{2,1,0:T(8,128)(2,1)}), bf16[16,10,768]{2,1,0:T(8,128)(2,1)S(1)}, u32[]{:S(2)}, u32[]{:S(2)}) async-start(bf16[16,10,768]{2,1,0:T(8,128)(2,1)} %all_to_all.33), calls=%async_computation.1 | async-start | bytes 786432 | tf_op jit(solution)/shard_map/all_to_all | solution.py:386
  94.5 20.2 %collective-permute-start.15 = (bf16[160,768]{1,0:T(8,128)(2,1)}, bf16[160,768]{1,0:T(8,128)(2,1)}, u32[]{:S(2)}, u32[]{:S(2)}) collective-permute-start(bf16[160,768]{1,0:T(8,128)(2,1)} %all_to_all.32), channel_id=1, source_target_pairs={{0,1},{1,0},{2,3},{3,2},{4,5},{5,4},{6,7},{7,6},{8,9},{9,8},{10,11... | collective-permute-start | bytes 737288 | tf_op jit(solution)/shard_map/ppermute | solution.py:279
  113.7 8.0 %collective-permute-start.20 = (bf16[160,768]{1,0:T(8,128)(2,1)}, bf16[160,768]{1,0:T(8,128)(2,1)S(1)}, u32[]{:S(2)}, u32[]{:S(2)}) collective-permute-start(bf16[160,768]{1,0:T(8,128)(2,1)} %all_to_all.35), channel_id=1, source_target_pairs={{0,1},{1,0},{2,3},{3,2},{4,5},{5,4},{6,7},{7,6},{8,9},{9,8},{10,11... | collective-permute-start | bytes 737288 | tf_op jit(solution)/shard_map/ppermute | solution.py:279
  115.6 14.6 %copy-start.13 = (bf16[320,768]{1,0:T(8,128)(2,1)}, bf16[320,768]{1,0:T(8,128)(2,1)S(1)}, u32[]{:S(2)}) copy-start(bf16[320,768]{1,0:T(8,128)(2,1)S(1)} %constant_dynamic-update-slice_fusion) | copy-start | bytes 1474564
  116.4 5.4 %collective-permute-start.17 = (bf16[384,1536]{1,0:T(8,128)(2,1)S(1)}, bf16[384,1536]{1,0:T(8,128)(2,1)S(1)}, u32[]{:S(2)}, u32[]{:S(2)}) collective-permute-start(bf16[384,1536]{1,0:T(8,128)(2,1)S(1)} %constant_dynamic-slice_fusion.5), channel_id=1, source_target_pairs={{0,1},{1,0},{2,3},{3,2},{4,5},{5,4},{6,7},{7,6},{8,9},{9,8},{10,11... | collective-permute-start | bytes 3538952 | tf_op jit(solution)/shard_map/ppermute | solution.py:279
  120.7 3.3 %collective-permute-start.19 = (bf16[1536,384]{1,0:T(8,128)(2,1)S(1)}, bf16[1536,384]{1,0:T(8,128)(2,1)S(1)}, u32[]{:S(2)}, u32[]{:S(2)}) collective-permute-start(bf16[1536,384]{1,0:T(8,128)(2,1)S(1)} %constant_dynamic-slice_fusion.4), channel_id=1, source_target_pairs={{0,1},{1,0},{2,3},{3,2},{4,5},{5,4},{6,7},{7,6},{8,9},{9,8},{10,11... | collective-permute-start | bytes 3538952 | tf_op jit(solution)/shard_map/ppermute | solution.py:279
  129.4 5.7 %collective-permute-start.21 = (f32[2,160,768]{2,1,0:T(8,128)S(1)}, f32[2,160,768]{2,1,0:T(8,128)S(1)}, u32[]{:S(2)}, u32[]{:S(2)}) collective-permute-start(f32[2,160,768]{2,1,0:T(8,128)S(1)} %pad_maximum_fusion.3), channel_id=1, source_target_pairs={{0,1},{1,0},{2,3},{3,2},{4,5},{5,4},{6,7},{7,6},{8,9},{9,8},{10,11... | collective-permute-start | bytes 2949128 | tf_op jit(solution)/shard_map/ppermute | solution.py:279
  132.0 12.6 %collective-permute-start.46 = (bf16[384,1536]{1,0:T(8,128)(2,1)}, bf16[384,1536]{1,0:T(8,128)(2,1)}, u32[]{:S(2)}, u32[]{:S(2)}) collective-permute-start(bf16[384,1536]{1,0:T(8,128)(2,1)} %convolution_convert_fusion.3), channel_id=1, source_target_pairs={{0,1},{1,0},{2,3},{3,2},{4,5},{5,4},{6,7},{7,6},{8,9},{9,8},{10,11... | collective-permute-start | bytes 3538952 | tf_op jit(solution)/shard_map/ppermute | solution.py:279
  134.7 16.4 %collective-permute-start.48 = (bf16[1536,384]{1,0:T(8,128)(2,1)}, bf16[1536,384]{1,0:T(8,128)(2,1)}, u32[]{:S(2)}, u32[]{:S(2)}) collective-permute-start(bf16[1536,384]{1,0:T(8,128)(2,1)} %convolution_convert_fusion.2), channel_id=1, source_target_pairs={{0,1},{1,0},{2,3},{3,2},{4,5},{5,4},{6,7},{7,6},{8,9},{9,8},{10,11... | collective-permute-start | bytes 3538952 | tf_op jit(solution)/shard_map/ppermute | solution.py:279
  138.8 18.8 %all-to-all-start.3 = ((bf16[16,10,768]{2,1,0:T(8,128)(2,1)}), bf16[16,10,768]{2,1,0:T(8,128)(2,1)}, u32[]{:S(2)}, u32[]{:S(2)}) async-start(bf16[16,10,768]{2,1,0:T(8,128)(2,1)} %all_to_all.38), calls=%async_computation.3 | async-start | bytes 786432 | tf_op jit(solution)/shard_map/all_to_all | solution.py:386
  149.0 98.8 %collective-permute-start.47 = (bf16[384,3072]{1,0:T(8,128)(2,1)}, bf16[384,3072]{1,0:T(8,128)(2,1)}, u32[]{:S(2)}, u32[]{:S(2)}) collective-permute-start(bf16[384,3072]{1,0:T(8,128)(2,1)} %fusion.2), channel_id=1, source_target_pairs={{1,16},{3,18},{5,20},{7,22},{9,24},{11,26},{13,28},{15,30},{16,1},... | collective-permute-start | bytes 7077896 | tf_op jit(solution)/shard_map/ppermute | solution.py:491
  157.6 60.8 %all-to-all-start.2 = ((bf16[16,10,768]{2,1,0:T(8,128)(2,1)}), bf16[16,10,768]{2,1,0:T(8,128)(2,1)}, u32[]{:S(2)}, u32[]{:S(2)}) async-start(bf16[16,10,768]{2,1,0:T(8,128)(2,1)} %convert_element_type.272), calls=%async_computation.2 | async-start | bytes 786432 | tf_op jit(solution)/shard_map/all_to_all | solution.py:386
  179.9 35.0 %collective-permute-start.41 = (f32[17,768]{1,0:T(8,128)S(1)}, f32[17,768]{1,0:T(8,128)}, u32[]{:S(2)}, u32[]{:S(2)}) collective-permute-start(f32[17,768]{1,0:T(8,128)S(1)} %pad_maximum_fusion.16), channel_id=1, source_target_pairs={{0,1},{1,0},{2,3},{3,2},{4,5},{5,4},{6,7},{7,6},{8,9},{9,8},{10,11... | collective-permute-start | bytes 156680 | tf_op jit(solution)/shard_map/ppermute | solution.py:279
  188.5 10.9 %copy-start.21 = (bf16[2,1,64,768]{3,2,1,0:T(8,128)(2,1)S(1)}, bf16[2,1,64,768]{3,2,1,0:T(8,128)(2,1)}, u32[]{:S(2)}) copy-start(bf16[2,1,64,768]{3,2,1,0:T(8,128)(2,1)} %param.12) | copy-start | bytes 589828
  203.7 2.0 collective-permute-start.36
  205.7 3.7 %collective-permute-start.37 = (f32[1,1152]{1,0:T(1,128)S(1)}, f32[1,1152]{1,0:T(1,128)S(1)}, u32[]{:S(2)}, u32[]{:S(2)}) collective-permute-start(f32[1,1152]{1,0:T(1,128)S(1)} %reshape_add_fusion), channel_id=1, source_target_pairs={{0,2},{1,3},{2,0},{3,1},{4,6},{5,7},{6,4},{7,5},{8,10},{9,11},{10,... | collective-permute-start | bytes 13832 | tf_op jit(solution)/shard_map/ppermute | solution.py:279
  208.8 34.6 %collective-permute-start.22 = (bf16[1152,768]{1,0:T(8,128)(2,1)}, bf16[1152,768]{1,0:T(8,128)(2,1)}, u32[]{:S(2)}, u32[]{:S(2)}) collective-permute-start(bf16[1152,768]{1,0:T(8,128)(2,1)} %convolution_convert_fusion.1), channel_id=1, source_target_pairs={{0,1},{1,0},{2,3},{3,2},{4,5},{5,4},{6,7},{7,6},{8,9},{9,8},{10,11... | collective-permute-start | bytes 5308424 | tf_op jit(solution)/shard_map/ppermute | solution.py:279
  209.4 3.6 %collective-permute-start.38 = (f32[1,1152]{1,0:T(1,128)S(1)}, f32[1,1152]{1,0:T(1,128)S(1)}, u32[]{:S(2)}, u32[]{:S(2)}) collective-permute-start(f32[1,1152]{1,0:T(1,128)S(1)} %add.349), channel_id=1, source_target_pairs={{0,16},{16,0},{1,17},{17,1},{2,18},{18,2},{3,19},{19,3},{4,20},{20... | collective-permute-start | bytes 13832 | tf_op jit(solution)/shard_map/ppermute | solution.py:277
  211.3 30.7 %collective-permute-start.23 = (bf16[384,768]{1,0:T(8,128)(2,1)}, bf16[384,768]{1,0:T(8,128)(2,1)}, u32[]{:S(2)}, u32[]{:S(2)}) collective-permute-start(bf16[384,768]{1,0:T(8,128)(2,1)} %convolution_convert_fusion.4), channel_id=1, source_target_pairs={{0,1},{1,0},{2,3},{3,2},{4,5},{5,4},{6,7},{7,6},{8,9},{9,8},{10,11... | collective-permute-start | bytes 1769480 | tf_op jit(solution)/shard_map/ppermute | solution.py:279
  213.1 7.1 %collective-permute-start.39 = (f32[1,1152]{1,0:T(1,128)S(1)}, f32[1,1152]{1,0:T(1,128)S(1)}, u32[]{:S(2)}, u32[]{:S(2)}) collective-permute-start(f32[1,1152]{1,0:T(1,128)S(1)} %add.350), channel_id=1, source_target_pairs={{0,4},{1,5},{2,6},{3,7},{4,0},{5,1},{6,2},{7,3},{8,12},{9,13},{10,... | collective-permute-start | bytes 13832 | tf_op jit(solution)/shard_map/ppermute | solution.py:279
  215.8 6.8 %collective-permute-start.42 = (f32[17,768]{1,0:T(8,128)S(1)}, f32[17,768]{1,0:T(8,128)}, u32[]{:S(2)}, u32[]{:S(2)}) collective-permute-start(f32[17,768]{1,0:T(8,128)S(1)} %fusion.100), channel_id=1, source_target_pairs={{0,2},{1,3},{2,0},{3,1},{4,6},{5,7},{6,4},{7,5},{8,10},{9,11},{10,... | collective-permute-start | bytes 156680 | tf_op jit(solution)/shard_map/ppermute | solution.py:279
  218.3 23.7 %copy-start.32 = (bf16[128,768]{0,1:T(8,128)(2,1)S(1)}, bf16[128,768]{0,1:T(8,128)(2,1)}, u32[]{:S(2)}) copy-start(bf16[128,768]{0,1:T(8,128)(2,1)} %copy-done.30) | copy-start | bytes 589828
  220.2 23.3 %copy-start.29 = (bf16[2,1,64,768]{3,2,1,0:T(8,128)(2,1)S(1)}, bf16[2,1,64,768]{3,2,1,0:T(8,128)(2,1)}, u32[]{:S(2)}) copy-start(bf16[2,1,64,768]{3,2,1,0:T(8,128)(2,1)} %multiply_convert_fusion.2) | copy-start | bytes 589828
  220.2 23.3 %copy-start.33 = (bf16[12,1,96,128]{3,2,1,0:T(8,128)(2,1)S(1)}, bf16[12,1,96,128]{3,2,1,0:T(8,128)(2,1)}, u32[]{:S(2)}) copy-start(bf16[12,1,96,128]{3,2,1,0:T(8,128)(2,1)} %get-tuple-element.73) | copy-start | bytes 884740
  220.2 6.7 %collective-permute-start.40 = (f32[1,1152]{1,0:T(1,128)S(1)}, f32[1,1152]{1,0:T(1,128)S(1)}, u32[]{:S(2)}, u32[]{:S(2)}) collective-permute-start(f32[1,1152]{1,0:T(1,128)S(1)} %add.351), channel_id=1, source_target_pairs={{0,8},{1,9},{2,10},{3,11},{4,12},{5,13},{6,14},{7,15},{8,0},{9,1},... | collective-permute-start | bytes 13832 | tf_op jit(solution)/shard_map/ppermute | solution.py:279
  223.5 5.4 %collective-permute-start.43 = (f32[17,768]{1,0:T(8,128)S(1)}, f32[17,768]{1,0:T(8,128)S(1)}, u32[]{:S(2)}, u32[]{:S(2)}) collective-permute-start(f32[17,768]{1,0:T(8,128)S(1)} %add.354), channel_id=1, source_target_pairs={{0,16},{16,0},{1,17},{17,1},{2,18},{18,2},{3,19},{19,3},{4,20},{20... | collective-permute-start | bytes 156680 | tf_op jit(solution)/shard_map/ppermute | solution.py:277
  226.9 26.3 %collective-permute-start.49 = (bf16[3072,384]{1,0:T(8,128)(2,1)}, bf16[3072,384]{1,0:T(8,128)(2,1)}, u32[]{:S(2)}, u32[]{:S(2)}) collective-permute-start(bf16[3072,384]{1,0:T(8,128)(2,1)} %fusion.1), channel_id=1, source_target_pairs={{1,16},{3,18},{5,20},{7,22},{9,24},{11,26},{13,28},{15,30},{16,1},... | collective-permute-start | bytes 7077896 | tf_op jit(solution)/shard_map/ppermute | solution.py:494
  229.0 5.1 %collective-permute-start.44 = (f32[17,768]{1,0:T(8,128)S(1)}, f32[17,768]{1,0:T(8,128)S(1)}, u32[]{:S(2)}, u32[]{:S(2)}) collective-permute-start(f32[17,768]{1,0:T(8,128)S(1)} %add.355), channel_id=1, source_target_pairs={{0,4},{1,5},{2,6},{3,7},{4,0},{5,1},{6,2},{7,3},{8,12},{9,13},{10,... | collective-permute-start | bytes 156680 | tf_op jit(solution)/shard_map/ppermute | solution.py:279
  234.1 6.7 %collective-permute-start.45 = (f32[17,768]{1,0:T(8,128)S(1)}, f32[17,768]{1,0:T(8,128)S(1)}, u32[]{:S(2)}, u32[]{:S(2)}) collective-permute-start(f32[17,768]{1,0:T(8,128)S(1)} %add.356), channel_id=1, source_target_pairs={{0,8},{1,9},{2,10},{3,11},{4,12},{5,13},{6,14},{7,15},{8,0},{9,1},... | collective-permute-start | bytes 156680 | tf_op jit(solution)/shard_map/ppermute | solution.py:279
  246.5 18.3 %collective-permute-start.28 = (bf16[1,2,2,2,1,96,256]{6,5,4,3,2,1,0:T(8,128)(2,1)S(1)}, bf16[1,2,2,2,1,96,256]{6,5,4,3,2,1,0:T(8,128)(2,1)S(1)}, u32[]{:S(2)}, u32[]{:S(2)}) collective-permute-start(bf16[1,2,2,2,1,96,256]{6,5,4,3,2,1,0:T(8,128)(2,1)S(1)} %dynamic-slice_convert_fusion.1), channel_id=1, source_target_pairs={{0,16},{16,0},{1,17},{17,1},{2,18},{18,2},{3,19},{19,3},{4,20},{20... | collective-permute-start | bytes 1179656 | tf_op jit(solution)/shard_map/ppermute | solution.py:277
  246.7 19.5 %collective-permute-start.32 = (bf16[2,1,2,2,1,96,256]{6,5,4,3,2,1,0:T(8,128)(2,1)S(1)}, bf16[2,1,2,2,1,96,256]{6,5,4,3,2,1,0:T(8,128)(2,1)S(1)}, u32[]{:S(2)}, u32[]{:S(2)}) collective-permute-start(bf16[2,1,2,2,1,96,256]{6,5,4,3,2,1,0:T(8,128)(2,1)S(1)} %dynamic-slice_convert_fusion), channel_id=1, source_target_pairs={{0,8},{1,9},{2,10},{3,11},{4,12},{5,13},{6,14},{7,15},{8,0},{9,1},... | collective-permute-start | bytes 1179656 | tf_op jit(solution)/shard_map/ppermute | solution.py:279
  247.2 19.7 %collective-permute-start.24 = (bf16[2,2,2,1,1,96,256]{6,5,4,3,2,1,0:T(8,128)(2,1)S(1)}, bf16[2,2,2,1,1,96,256]{6,5,4,3,2,1,0:T(8,128)(2,1)S(1)}, u32[]{:S(2)}, u32[]{:S(2)}) collective-permute-start(bf16[2,2,2,1,1,96,256]{6,5,4,3,2,1,0:T(8,128)(2,1)S(1)} %dynamic-slice_convert_fusion.2), channel_id=1, source_target_pairs={{0,2},{1,3},{2,0},{3,1},{4,6},{5,7},{6,4},{7,5},{8,10},{9,11},{10,... | collective-permute-start | bytes 1179656 | tf_op jit(solution)/shard_map/ppermute | solution.py:279
  265.0 12.2 %collective-permute-start.29 = (bf16[1,1,2,2,1,96,256]{6,5,4,3,2,1,0:T(8,128)(2,1)S(1)}, bf16[1,1,2,2,1,96,256]{6,5,4,3,2,1,0:T(8,128)(2,1)S(1)}, u32[]{:S(2)}, u32[]{:S(2)}) collective-permute-start(bf16[1,1,2,2,1,96,256]{6,5,4,3,2,1,0:T(8,128)(2,1)S(1)} %dynamic-slice_convert_fusion.4), channel_id=1, source_target_pairs={{0,8},{1,9},{2,10},{3,11},{4,12},{5,13},{6,14},{7,15},{8,0},{9,1},... | collective-permute-start | bytes 589832 | tf_op jit(solution)/shard_map/ppermute | solution.py:279
  266.3 11.1 %collective-permute-start.33 = (bf16[2,1,1,2,1,96,256]{6,5,4,3,2,1,0:T(8,128)(2,1)S(1)}, bf16[2,1,1,2,1,96,256]{6,5,4,3,2,1,0:T(8,128)(2,1)S(1)}, u32[]{:S(2)}, u32[]{:S(2)}) collective-permute-start(bf16[2,1,1,2,1,96,256]{6,5,4,3,2,1,0:T(8,128)(2,1)S(1)} %dynamic-slice_convert_fusion.3), channel_id=1, source_target_pairs={{0,4},{1,5},{2,6},{3,7},{4,0},{5,1},{6,2},{7,3},{8,12},{9,13},{10,... | collective-permute-start | bytes 589832 | tf_op jit(solution)/shard_map/ppermute | solution.py:279
  267.0 11.0 %collective-permute-start.25 = (bf16[1,2,2,1,1,96,256]{6,5,4,3,2,1,0:T(8,128)(2,1)S(1)}, bf16[1,2,2,1,1,96,256]{6,5,4,3,2,1,0:T(8,128)(2,1)S(1)}, u32[]{:S(2)}, u32[]{:S(2)}) collective-permute-start(bf16[1,2,2,1,1,96,256]{6,5,4,3,2,1,0:T(8,128)(2,1)S(1)} %dynamic-slice_convert_fusion.5), channel_id=1, source_target_pairs={{0,16},{16,0},{1,17},{17,1},{2,18},{18,2},{3,19},{19,3},{4,20},{20... | collective-permute-start | bytes 589832 | tf_op jit(solution)/shard_map/ppermute | solution.py:277
  277.2 5.8 %collective-permute-start.30 = (bf16[1,1,1,2,1,96,256]{6,5,4,3,2,1,0:T(8,128)(2,1)S(1)}, bf16[1,1,1,2,1,96,256]{6,5,4,3,2,1,0:T(8,128)(2,1)S(1)}, u32[]{:S(2)}, u32[]{:S(2)}) collective-permute-start(bf16[1,1,1,2,1,96,256]{6,5,4,3,2,1,0:T(8,128)(2,1)S(1)} %dynamic-slice_convert_fusion.7), channel_id=1, source_target_pairs={{0,4},{1,5},{2,6},{3,7},{4,0},{5,1},{6,2},{7,3},{8,12},{9,13},{10,... | collective-permute-start | bytes 294920 | tf_op jit(solution)/shard_map/ppermute | solution.py:279
  277.4 13.3 %copy-start.1 = (bf16[768,16]{0,1:T(8,128)(2,1)S(1)}, bf16[768,16]{0,1:T(8,128)(2,1)}, u32[]{:S(2)}) copy-start(bf16[768,16]{0,1:T(8,128)(2,1)} %param.17) | copy-start | bytes 73732
  277.4 5.8 %collective-permute-start.34 = (bf16[2,1,1,1,1,96,256]{6,5,4,3,2,1,0:T(8,128)(2,1)S(1)}, bf16[2,1,1,1,1,96,256]{6,5,4,3,2,1,0:T(8,128)(2,1)S(1)}, u32[]{:S(2)}, u32[]{:S(2)}) collective-permute-start(bf16[2,1,1,1,1,96,256]{6,5,4,3,2,1,0:T(8,128)(2,1)S(1)} %dynamic-slice_convert_fusion.6), channel_id=1, source_target_pairs={{0,2},{1,3},{2,0},{3,1},{4,6},{5,7},{6,4},{7,5},{8,10},{9,11},{10,... | collective-permute-start | bytes 294920 | tf_op jit(solution)/shard_map/ppermute | solution.py:279
  278.1 7.6 %collective-permute-start.26 = (bf16[1,1,2,1,1,96,256]{6,5,4,3,2,1,0:T(8,128)(2,1)S(1)}, bf16[1,1,2,1,1,96,256]{6,5,4,3,2,1,0:T(8,128)(2,1)S(1)}, u32[]{:S(2)}, u32[]{:S(2)}) collective-permute-start(bf16[1,1,2,1,1,96,256]{6,5,4,3,2,1,0:T(8,128)(2,1)S(1)} %dynamic-slice_convert_fusion.8), channel_id=1, source_target_pairs={{0,8},{1,9},{2,10},{3,11},{4,12},{5,13},{6,14},{7,15},{8,0},{9,1},... | collective-permute-start | bytes 294920 | tf_op jit(solution)/shard_map/ppermute | solution.py:279
  283.1 4.2 %collective-permute-start.31 = (bf16[1,1,1,1,1,96,256]{6,5,4,3,2,1,0:T(8,128)(2,1)S(1)}, bf16[1,1,1,1,1,96,256]{6,5,4,3,2,1,0:T(8,128)(2,1)S(1)}, u32[]{:S(2)}, u32[]{:S(2)}) collective-permute-start(bf16[1,1,1,1,1,96,256]{6,5,4,3,2,1,0:T(8,128)(2,1)S(1)} %dynamic-slice_convert_fusion.10), channel_id=1, source_target_pairs={{0,2},{1,3},{2,0},{3,1},{4,6},{5,7},{6,4},{7,5},{8,10},{9,11},{10,... | collective-permute-start | bytes 147464 | tf_op jit(solution)/shard_map/ppermute | solution.py:279
  283.3 4.2 %collective-permute-start.35 = (bf16[1,1,1,1,1,96,256]{6,5,4,3,2,1,0:T(8,128)(2,1)S(1)}, bf16[1,1,1,1,1,96,256]{6,5,4,3,2,1,0:T(8,128)(2,1)S(1)}, u32[]{:S(2)}, u32[]{:S(2)}) collective-permute-start(bf16[1,1,1,1,1,96,256]{6,5,4,3,2,1,0:T(8,128)(2,1)S(1)} %dynamic-slice_convert_fusion.9), channel_id=1, source_target_pairs={{0,16},{16,0},{1,17},{17,1},{2,18},{18,2},{3,19},{19,3},{4,20},{20... | collective-permute-start | bytes 147464 | tf_op jit(solution)/shard_map/ppermute | solution.py:277
  285.8 4.2 %collective-permute-start.27 = (bf16[1,1,1,1,1,96,256]{6,5,4,3,2,1,0:T(8,128)(2,1)S(1)}, bf16[1,1,1,1,1,96,256]{6,5,4,3,2,1,0:T(8,128)(2,1)S(1)}, u32[]{:S(2)}, u32[]{:S(2)}) collective-permute-start(bf16[1,1,1,1,1,96,256]{6,5,4,3,2,1,0:T(8,128)(2,1)S(1)} %dynamic-slice_convert_fusion.11), channel_id=1, source_target_pairs={{0,4},{1,5},{2,6},{3,7},{4,0},{5,1},{6,2},{7,3},{8,12},{9,13},{10,... | collective-permute-start | bytes 147464 | tf_op jit(solution)/shard_map/ppermute | solution.py:279
  (32 other events, 137.3 us)

commit v2 on v0

--- a/solution.py
+++ b/solution.py
@@ -1,6 +1,9 @@
+import functools
 import jax
 import jax.numpy as jnp
 from jax import lax
+from jax.experimental import pallas as pl
+from jax.experimental.pallas import tpu as pltpu
 from jax.sharding import PartitionSpec as P
 
 EPSILON = 1e-06
@@ -269,7 +272,633 @@
     )
 
 
+BOTH = ("dp", "expert")
+
+
+def flip(tensor, bit):
+    if bit == "y":
+        return lax.ppermute(tensor, "dp", [(0, 1), (1, 0)])
+    count = lax.axis_size("expert")
+    return lax.ppermute(tensor, "expert", [(i, i ^ bit) for i in range(count)])
+
+
+def own_bit(bit):
+    if bit == "y":
+        return lax.axis_index("dp")
+    return (lax.axis_index("expert") // bit) % 2
+
+
+ORDERS = ((8, 4, "y", 2), (2, 8, 4, "y"), ("y", 2, 8, 4))
+RS_ORDERS = ((2, "y", 8, 4), ("y", 8, 4, 2), (8, 4, 2, "y"))
+PLACE = {"y": 0, 8: 1, 4: 2, 2: 3, 1: 4}
+
+
+def gather_rows(shard, soon, later, prepare, waiting):
+    rows, width = shard.shape
+    third = width // 3
+    pieces = [
+        shard[:, i * third : (i + 1) * third].reshape(1, 1, 1, 1, rows, third) for i in range(3)
+    ]
+
+    def grow(piece, bit):
+        got = flip(piece, bit)
+        low = own_bit(bit) == 0
+        return jnp.concatenate(
+            [jnp.where(low, piece, got), jnp.where(low, got, piece)], axis=PLACE[bit]
+        )
+
+    for step in range(4):
+        if step == 1:
+            pieces, waiting = lax.optimization_barrier((pieces, waiting))
+            ready = prepare(*waiting)
+        if step == 2:
+            pieces, soon = lax.optimization_barrier((pieces, soon))
+        pieces = [grow(piece, ORDERS[i][step]) for i, piece in enumerate(pieces)]
+    pieces, later, ready = lax.optimization_barrier((pieces, later, ready))
+    pieces = [piece.reshape(-1, rows, third) for piece in pieces]
+    return pieces + [flip(piece, 1) for piece in pieces], soon, later, ready
+
+
+def reduce_step(total, bit):
+    mine = own_bit(bit)
+    axis = PLACE[bit]
+    send = lax.dynamic_index_in_dim(total, 1 - mine, axis, keepdims=True).astype(jnp.bfloat16)
+    keep = lax.dynamic_index_in_dim(total, mine, axis, keepdims=True)
+    return keep + flip(send, bit).astype(jnp.float32)
+
+
+def scatter_rows(leaves, stays, small, late):
+    late = list(late)
+    pieces = []
+    for index, (leave, stay) in enumerate(zip(leaves, stays)):
+        bit = RS_ORDERS[index][0]
+        shape = [2, 2, 2, 2, 1] + list(stay.shape[1:])
+        shape[PLACE[bit]] = 1
+        pieces.append((stay + flip(leave, bit).astype(jnp.float32)).reshape(shape))
+    for bit in (1, 2):
+        small = small + flip(small, bit)
+    for step in range(1, 4):
+        pieces, late[step], small = lax.optimization_barrier((pieces, late[step], small))
+        pieces = [reduce_step(piece, RS_ORDERS[i][step]) for i, piece in enumerate(pieces)]
+        small = small + flip(small, ("y", 8, 4)[step - 1])
+    whole = jnp.concatenate(pieces, axis=-1)
+    return whole.reshape(whole.shape[-2], whole.shape[-1]), small, late
+
+
+def dot(left, right, dims, **more):
+    return lax.dot_general(
+        left, right, (dims, ((), ())), preferred_element_type=jnp.float32, **more
+    )
+
+
+def call(kernel, mib, outs, scratch, *operands, plain_in=(), plain_out=()):
+    def spec(shape):
+        return pl.BlockSpec(
+            shape, lambda i: (0,) * len(shape), pipeline_mode=pl.Buffered(1)
+        )
+
+    left = pl.BlockSpec(memory_space=pl.ANY)
+    operands = operands[:1] + tuple(
+        pltpu.with_memory_space_constraint(operand, pltpu.HBM) for operand in operands[1:]
+    )
+    return pl.pallas_call(
+        kernel,
+        grid=(1,),
+        out_shape=tuple(pltpu.HBM(*out) for out in outs),
+        in_specs=[pl.BlockSpec(memory_space=pltpu.SMEM)]
+        + [left if i in plain_in else spec(operand.shape) for i, operand in enumerate(operands) if i],
+        out_specs=tuple(left if i in plain_out else spec(out[0]) for i, out in enumerate(outs)),
+        scratch_shapes=scratch,
+        compiler_params=pltpu.CompilerParams(vmem_limit_bytes=mib * 2**20),
+    )(*operands)
+
+
+def bias_kernel(table_ref, buckets_ref, square_ref):
+    heads, count, _ = square_ref.shape
+    row = lax.broadcasted_iota(jnp.int32, (count, count), 0)
+    column = lax.broadcasted_iota(jnp.int32, (count, count), 1)
+    half = count // 2
+    same = (row < half) == (column < half)
+    buckets = buckets_ref[...]
+    for head in range(heads):
+        total = jnp.where(same, 0.0, -jnp.inf)
+        for bucket in range(table_ref.shape[0]):
+            total = jnp.where(same & (buckets == bucket), table_ref[bucket, head], total)
+        square_ref[head] = total
+
+
+def attend_kernel(
+    place_ref, x_ref, *rest,
+):
+    pieces, rest = rest[:6], rest[6:]
+    (
+        gain_one_ref, gain_two_ref, bias_ref, dispatch_ref, dy_ref,
+        wt_qkv_ref, wt_o_ref, n1b_ref, qkv_ref, probs_ref, mixed_ref, resid_ref, n2b_ref, rows_ref,
+        mixed_t, wt_ref, come, go_qkv, go_o,
+    ) = rest
+    core = place_ref[0]
+    pairs, block, third = pieces[0].shape
+    for side, part in ((core, pieces[:3]), (1 - core, pieces[3:])):
+        for index in range(3):
+            pltpu.make_async_copy(
+                part[index], wt_ref.at[:, side, :, pl.ds(index * third, third)], come
+            ).start()
+    heads = probs_ref.shape[0]
+    width = x_ref.shape[1]
+    size = width // heads
+    x = x_ref[...].astype(jnp.float32)
+    n1b_ref[...] = (x * rms_scale(x) * gain_one_ref[...]).astype(jnp.bfloat16)
+    pltpu.make_async_copy(wt_ref, wt_ref, come).wait()
+    most = pairs * 3 // 4
+    leave_qkv = pltpu.make_async_copy(wt_ref.at[pl.ds(0, most)], wt_qkv_ref, go_qkv)
+    leave_o = pltpu.make_async_copy(wt_ref.at[pl.ds(most, pairs - most)], wt_o_ref, go_o)
+    leave_qkv.start()
+    leave_o.start()
+    qkv_ref[...] = dot(wt_ref[:most].reshape(3 * width, width), n1b_ref[...], ((1,), (1,))).astype(jnp.bfloat16)
+    for head in range(heads):
+        query = qkv_ref[head * size : (head + 1) * size]
+        keys = qkv_ref[width + head * size : width + (head + 1) * size]
+        values = qkv_ref[2 * width + head * size : 2 * width + (head + 1) * size]
+        scores = dot(keys, query, ((0,), (0,))) + bias_ref[head]
+        raised = jnp.exp(scores - jnp.max(scores, axis=0, keepdims=True))
+        probs = raised / jnp.sum(raised, axis=0, keepdims=True)
+        probs_ref[head] = probs
+        mixed_t[head * size : (head + 1) * size] = dot(
+            values, probs.astype(jnp.bfloat16), ((1,), (0,))
+        )
+    mixed_ref[...] = mixed_t[...].T.astype(jnp.bfloat16)
+    resid = x + dot(
+        mixed_ref[...], wt_ref[most:].reshape(width, width), ((1,), (1,))
+    )
+    resid_ref[...] = resid
+    n2b_ref[...] = (resid * rms_scale(resid) * gain_two_ref[...]).astype(jnp.bfloat16)
+    rows = dot(dispatch_ref[...], n2b_ref[...], ((1,), (0,)))
+    rows_ref[:, :width] = rows.astype(jnp.bfloat16)
+    dy_rows = dot(dispatch_ref[...], dy_ref[...], ((1,), (0,)))
+    rows_ref[:, width:] = dy_rows.astype(jnp.bfloat16)
+    leave_qkv.wait()
+    leave_o.wait()
+
+
+def attend_back_kernel(
+    core_ref, dn2_ref, dispatch_ref, resid_ref, dy_ref, gain_two_ref, wt_ref, qkv_ref, probs_ref,
+    n1b_ref, mixed_ref, dresid_ref, gain_ref, dqkv_ref, fold_ref, send_ref, keep_ref, columns,
+):
+    heads = probs_ref.shape[0]
+    count, width = resid_ref.shape
+    size = width // heads
+    core = core_ref[0]
+    resid = resid_ref[...]
+    scale = rms_scale(resid)
+    n2hat = resid * scale
+    dn2 = dot(dispatch_ref[...], dn2_ref[:, :width], ((0,), (0,)))
+    gain_ref[...] = jnp.sum(dn2 * n2hat, axis=0, keepdims=True)
+    dhat = dn2 * gain_two_ref[...]
+    dresid = dy_ref[...].astype(jnp.float32) + scale * (
+        dhat - n2hat * jnp.mean(dhat * n2hat, axis=-1, keepdims=True)
+    )
+    dresid_ref[...] = dresid
+    dattn = dresid.astype(jnp.bfloat16)
+    dab = dot(dattn, wt_ref[...], ((1,), (0,)))
+    dab_t = dab.T.astype(jnp.bfloat16)
+    columns[3 * width :] = dresid.T.astype(jnp.bfloat16)
+    for head in range(heads):
+        at = slice(head * size, (head + 1) * size)
+        query = qkv_ref[head * size : (head + 1) * size]
+        keys = qkv_ref[width + head * size : width + (head + 1) * size]
+        values = qkv_ref[2 * width + head * size : 2 * width + (head + 1) * size]
+        dab_head = dab_t[at]
+        probs = probs_ref[head]
+        dvalue = dot(dab_head, probs.astype(jnp.bfloat16), ((1,), (1,)))
+        dprobs = dot(values, dab_head, ((0,), (0,)))
+        dscores = probs * (dprobs - jnp.sum(probs * dprobs, axis=0, keepdims=True))
+        half = count // 2
+        fold_ref[head] = dscores[:half] + dscores[half:]
+        dscores_b = dscores.astype(jnp.bfloat16)
+        dquery = dot(keys, dscores_b, ((1,), (0,)))
+        dkey = dot(query, dscores_b, ((1,), (1,)))
+        columns[head * size : (head + 1) * size] = dquery.astype(jnp.bfloat16)
+        columns[width + head * size : width + (head + 1) * size] = dkey.astype(jnp.bfloat16)
+        columns[2 * width + head * size : 2 * width + (head + 1) * size] = dvalue.astype(
+            jnp.bfloat16
+        )
+    dqkv_ref[...] = columns[: 3 * width]
+    block = width // 8
+    sent = []
+    for pair in range(16):
+        theirs = pl.multiple_of((2 * pair + 1 - core) * block, block)
+        mine = pl.multiple_of((2 * pair + core) * block, block)
+        keep_ref[pair * block : (pair + 1) * block] = columns[pl.ds(mine, block), :]
+        sent.append(columns[pl.ds(theirs, block), :])
+    sent = jnp.concatenate(sent, axis=0)
+    split = 12 * block
+    send_ref[:split] = dot(sent[:split], n1b_ref[...], ((1,), (0,))).astype(jnp.bfloat16)
+    send_ref[split:] = dot(sent[split:], mixed_ref[...], ((1,), (0,))).astype(jnp.bfloat16)
+
+
+def token_back_kernel(
+    bucket_count, _, x_ref, dqkv_ref, wt_ref, gain_one_ref, dresid_ref, fold_ref, buckets_ref, gain_part_ref,
+    router_part_ref, grad_ref, small_ref,
+):
+    x = x_ref[...].astype(jnp.float32)
+    scale = rms_scale(x)
+    n1hat = x * scale
+    width = x.shape[1]
+    dn1 = dot(dqkv_ref[...], wt_ref[...], ((0,), (0,)))
+    gain_part = jnp.sum(dn1 * n1hat, axis=0, keepdims=True)
+    dhat = dn1 * gain_one_ref[...]
+    grad_ref[...] = dresid_ref[...] + scale * (
+        dhat - n1hat * jnp.mean(dhat * n1hat, axis=-1, keepdims=True)
+    )
+    experts = router_part_ref.shape[0]
+    tiles = width // 128
+    small_ref[...] = jnp.zeros(small_ref.shape, jnp.float32)
+    for tile in range(tiles):
+        at = slice(tile * 128, (tile + 1) * 128)
+        small_ref[tile * experts : (tile + 1) * experts] = router_part_ref[:, at]
+        base = tiles * experts + tile
+        small_ref[base : base + 1] = gain_part[:, at]
+        small_ref[base + 8 : base + 9] = gain_part_ref[:, at]
+    heads = fold_ref.shape[0]
+    lane = lax.broadcasted_iota(jnp.int32, (1, 128), 1)
+    table = jnp.zeros((heads, 128), jnp.float32)
+    buckets = buckets_ref[: fold_ref.shape[1]]
+    fold = fold_ref[...]
+    for bucket in range(bucket_count):
+        column = jnp.sum(jnp.where((buckets == bucket)[None], fold, 0.0), axis=1)
+        column = jnp.sum(column, axis=-1, keepdims=True)
+        table = table + jnp.where(lane == bucket, column, 0.0)
+    start = tiles * experts + 16
+    small_ref[start : start + heads] = table
+
+
+def split_kernel(
+    place_ref, keep_ref, n1b_ref, mixed_ref, got_ref,
+    send_a, send_b, send_c, keep_a, keep_b, keep_c, total,
+):
+    split = keep_ref.shape[0] * 3 // 4
+    blocks, block, width = total.shape
+    first = dot(keep_ref[:split], n1b_ref[...], ((1,), (0,)))
+    first = first + got_ref[:split].astype(jnp.float32)
+    total[: blocks * 3 // 4] = first.reshape(blocks * 3 // 4, block, width)
+    last = dot(keep_ref[split:], mixed_ref[...], ((1,), (0,)))
+    last = last + got_ref[split:].astype(jnp.float32)
+    total[blocks * 3 // 4 :] = last.reshape(blocks // 4, block, width)
+    begin = 0
+    for index, (send, keep) in enumerate(((send_a, keep_a), (send_b, keep_b), (send_c, keep_c))):
+        mine = place_ref[3 + index]
+        stride = {2: 1, 4: 2, 8: 4, "y": 8}[RS_ORDERS[index][0]]
+        columns = slice(begin, begin + send.shape[2])
+        begin += send.shape[2]
+        for j in range(blocks // 2):
+            low = j // stride * 2 * stride + j % stride
+            send[j] = total[low + (1 - mine) * stride, :, columns].astype(jnp.bfloat16)
+            keep[j] = total[low + mine * stride, :, columns]
+
+
+def expert_kernel(
+    place_ref, own_ref, got_ref, router_ref,
+    in_near_ref, in_arrived_ref, in_far_ref, out_near_ref, out_arrived_ref, out_far_ref,
+    rows_ref, hidden_ref, du_ref, dmade_ref, mine_ref, theirs_ref, probs_ref, in_full, out_full,
+):
+    core, host = place_ref[0], place_ref[1]
+    half, units = in_far_ref.shape
+    own, width = got_ref.shape[0], got_ref.shape[1] // 2
+    for side in range(2):
+
+        at, other = slice(side * half, (side + 1) * half), slice((1 - side) * half, (2 - side) * half)
+
+        @pl.when(core == side)
+        def _():
+            in_full[other] = in_far_ref[...]
+            out_full[:, other] = out_far_ref[...]
+
+        @pl.when((core == side) & (place_ref[2] == 1))
+        def _():
+            in_full[at] = in_near_ref[...]
+            out_full[:, at] = out_near_ref[...]
+
+        @pl.when((core == side) & (place_ref[2] == 0))
+        def _():
+            in_full[at] = in_arrived_ref[...]
+            out_full[:, at] = out_arrived_ref[...]
+
+    rows = jnp.concatenate([own_ref[:, :width], got_ref[:, :width]], axis=0)
+    dy = jnp.concatenate([own_ref[:, width:], got_ref[:, width:]], axis=0)
+    rows_ref[...] = rows
+    logits = dot(rows, router_ref[...], ((1,), (0,)))
+    raised = jnp.exp(logits - jnp.max(logits, axis=-1, keepdims=True))
+    probs = raised / jnp.sum(raised, axis=-1, keepdims=True)
+    probs_ref[...] = probs[:own]
+    chosen = lax.broadcasted_iota(jnp.int32, probs.shape, 1) == host
+    gate = jnp.sum(jnp.where(chosen, probs, 0.0), axis=-1, keepdims=True)
+    dmade_ref[...] = (gate * dy.astype(jnp.float32)).astype(jnp.bfloat16)
+    dmade = dmade_ref[...]
+    made = jnp.zeros(rows.shape, jnp.float32)
+    drows = jnp.zeros(rows.shape, jnp.float32)
+    step = units // 3
+    for begin in range(0, units, step):
+        at = slice(begin, begin + step)
+        upre = dot(rows, in_full[:, at], ((1,), (0,)))
+        square = upre * upre
+        bent = jnp.tanh(0.7978845608028654 * (upre + 0.044715 * upre * square))
+        hidden = (0.5 * upre * (1.0 + bent)).astype(jnp.bfloat16)
+        slope = 0.5 * (1.0 + bent) + 0.5 * upre * (1.0 - bent * bent) * (
+            0.7978845608028654 * (1.0 + 3.0 * 0.044715 * square)
+        )
+        dhidden = dot(dmade, out_full[at, :], ((1,), (1,)))
+        du = (dhidden * slope).astype(jnp.bfloat16)
+        hidden_ref[:, at] = hidden
+        du_ref[:, at] = du
+        made = made + dot(hidden, out_full[at, :], ((1,), (0,)))
+        drows = drows + dot(du, in_full[:, at], ((1,), (1,)))
+    mine_ref[0] = made[:own]
+    mine_ref[1] = drows[:own]
+    theirs_ref[0] = made[own:]
+    theirs_ref[1] = drows[own:]
+
+
+def settle_kernel(
+    place_ref, mine_ref, got_ref, own_ref, probs_ref, router_ref, back_ref, router_part_ref
+):
+    width = own_ref.shape[1] // 2
+    made = (mine_ref[0] + got_ref[0]).astype(jnp.bfloat16)
+    back_ref[:, width:] = made
+    drows = (mine_ref[1] + got_ref[1]).astype(jnp.bfloat16).astype(jnp.float32)
+    probs = probs_ref[...]
+    chosen = (lax.broadcasted_iota(jnp.int32, probs.shape, 1) == place_ref[1]).astype(jnp.float32)
+    gate = jnp.sum(probs * chosen, axis=-1, keepdims=True)
+    dgate = jnp.sum(
+        own_ref[:, width:].astype(jnp.float32) * made.astype(jnp.float32),
+        axis=-1,
+        keepdims=True,
+    )
+    dlogits = probs * dgate * (chosen - gate)
+    router_part_ref[...] = dot(
+        dlogits, own_ref[:, :width].astype(jnp.float32), ((0,), (0,)), precision=HIGH
+    )
+    dn2 = drows + dot(dlogits, router_ref[...].astype(jnp.float32), ((1,), (1,)), precision=HIGH)
+    back_ref[:, :width] = dn2.astype(jnp.bfloat16)
+
+
+def paired_body(
+    tokens,
+    attn_weight,
+    gain_attn,
+    gain_expert,
+    bias_table,
+    router_weight,
+    expert_in,
+    expert_out,
+    routes,
+    slots,
+    buckets,
+    cotangent,
+):
+    f32, bf16 = jnp.float32, jnp.bfloat16
+    micro, _, seq_len, width = tokens.shape
+    count = micro * seq_len
+    heads = bias_table.shape[1]
+    head_size = width // heads
+    bucket_count = bias_table.shape[0]
+    experts = lax.axis_size("expert")
+    capacity = (5 * seq_len + 4 * experts - 1) // (4 * experts)
+    places = micro * capacity
+    hidden_half = expert_in.shape[2] // 2
+    width_half = width // 2
+    dp_at, expert_at = lax.axis_index("dp"), lax.axis_index("expert")
+    core = expert_at % 2
+    home = core == dp_at
+    host = expert_at - core + dp_at
+    gain_one, gain_two = gain_attn.astype(f32), gain_expert.astype(f32)
+
+    across, first = [], []
+    for dp in range(2):
+        for e in range(experts):
+            here = dp * experts + e
+            if e % 2 == dp:
+                first.append((here, dp * experts + (e ^ 1), (1 - dp) * experts + e))
+            else:
+                across.append((here, (1 - dp) * experts + (e ^ 1)))
+                first.append((here, (1 - dp) * experts + e, dp * experts + (e ^ 1)))
+    outward = [(here, there) for here, there, _ in first]
+    homeward = [(here, there) for here, _, there in first]
+
+    groups = [
+        [dp * experts + 2 * pair + side for dp in range(2) for pair in range(experts // 2)]
+        for side in range(2)
+    ]
+
+    def to_chips(tensor):
+        return lax.all_to_all(
+            tensor, BOTH, split_axis=0, concat_axis=0, tiled=True, axis_index_groups=groups
+        )
+
+    route_ids, slot_ids = routes[:, 0], slots[:, 0]
+    chip = (route_ids % 2) * (experts // 2) + route_ids // 2
+    flat = chip * places + jnp.arange(micro)[:, None] * capacity + slot_ids
+    flat = jnp.where(slot_ids < capacity, flat, -1).reshape(1, count)
+    dispatch = (flat == jnp.arange(experts * places)[:, None]).astype(bf16)
+    upstream_b = cotangent.reshape(count, width)
+    def parts_of(local, axis):
+        near = lax.dynamic_slice_in_dim(local, dp_at * hidden_half, hidden_half, axis)
+        far = lax.dynamic_slice_in_dim(local, (1 - dp_at) * hidden_half, hidden_half, axis)
+        return near, far
+
+    in_near, in_far = parts_of(expert_in[0], 1)
+    in_arrived = lax.ppermute(in_near, BOTH, across)
+
+    def halves(tensor):
+        return (
+            lax.dynamic_slice_in_dim(tensor, core * width_half, width_half, 1),
+            lax.dynamic_slice_in_dim(tensor, (1 - core) * width_half, width_half, 1),
+        )
+
+    def whole(keep, got, axis):
+        low = core == 0
+        return jnp.concatenate(
+            [jnp.where(low, keep, got), jnp.where(low, got, keep)], axis=axis
+        )
+
+    def prepare(table, ids, out_local):
+        tiled = jnp.tile(ids.T, (micro, micro))
+        (square,) = call(bias_kernel, 10, (((heads, count, count), f32),), [], table, tiled)
+        return (square, tiled, in_far) + parts_of(out_local, 0)
+
+    pieces, in_arrived, dispatch, ready = gather_rows(
+        attn_weight.T,
+        in_arrived,
+        dispatch,
+        prepare,
+        (bias_table.astype(f32), buckets, expert_out[0]),
+    )
+    square, tiled, in_far, out_near, out_far = ready
+    out_arrived = lax.ppermute(out_near, BOTH, across)
+    place = jnp.stack(
+        [core, host, home.astype(jnp.int32)] + [own_bit(order[0]) for order in RS_ORDERS]
+    ).astype(jnp.int32)
+    gain_one, gain_two = gain_one[None], gain_two[None]
+    local = tokens.reshape(count, width)
+    row_count = dispatch.shape[0]
+    wt_qkv, wt_o, n1b, qkv, probs, mixed_b, resid, n2b, outgoing = call(
+        attend_kernel,
+        26,
+        (
+            ((12, 2, width // 8, width), bf16),
+            ((4, 2, width // 8, width), bf16),
+            ((count, width), bf16),
+            ((3 * width, count), bf16),
+            ((heads, count, count), f32),
+            ((count, width), bf16),
+            ((count, width), f32),
+            ((count, width), bf16),
+            ((row_count, 2 * width), bf16),
+        ),
+        [
+            pltpu.VMEM((width, count), f32),
+            pltpu.VMEM((16, 2, width // 8, width), bf16),
+            pltpu.SemaphoreType.DMA,
+            pltpu.SemaphoreType.DMA,
+            pltpu.SemaphoreType.DMA,
+        ],
+        place, local, *pieces, gain_one, gain_two, square, dispatch, upstream_b,
+        plain_in=range(2, 8),
+        plain_out=(0, 1),
+    )
+    wt_qkv, wt_o = wt_qkv.reshape(3 * width, width), wt_o.reshape(width, width)
+    outgoing, out_arrived, in_far, out_far = lax.optimization_barrier(
+        (outgoing, out_arrived, lax.ppermute(in_far, BOTH, outward), out_far)
+    )
+    own_rows = to_chips(outgoing)
+    in_parts = (in_near, in_arrived, in_far)
+    out_parts = (out_near, out_arrived, lax.ppermute(out_far, BOTH, outward))
+    rows, hidden, du, dmade, mine, theirs, row_probs = call(
+        expert_kernel,
+        34,
+        (
+            ((2 * row_count, width), bf16),
+            ((2 * row_count, hidden_half), bf16),
+            ((2 * row_count, hidden_half), bf16),
+            ((2 * row_count, width), bf16),
+            ((2, row_count, width), f32),
+            ((2, row_count, width), f32),
+            ((row_count, experts), f32),
+        ),
+        [pltpu.VMEM((width, hidden_half), bf16), pltpu.VMEM((hidden_half, width), bf16)],
+        place, own_rows, flip(own_rows, 1), router_weight, *in_parts, *out_parts,
+    )
+    back_rows, router_part = call(
+        settle_kernel,
+        10,
+        (
+            ((row_count, 2 * width), bf16),
+            ((experts, width), f32),
+        ),
+        [],
+        place, mine, flip(theirs, 1), own_rows, row_probs, router_weight,
+    )
+    in_other = dot(halves(rows)[1], du, ((0,), (0,))).astype(bf16)
+    back_rows, rows, hidden, du, dmade = lax.optimization_barrier(
+        (back_rows, rows, hidden, du, dmade)
+    )
+    home_rows = to_chips(back_rows)
+    rows_keep, _ = halves(rows)
+    dmade_keep, dmade_got = halves(dmade)
+
+    in_homely = lax.ppermute(in_other, BOTH, homeward)
+    in_mine = dot(rows_keep, du, ((0,), (0,)))
+    out_other = dot(hidden, dmade_got, ((0,), (0,))).astype(bf16)
+    out_homely = lax.ppermute(out_other, BOTH, homeward)
+    out_mine = dot(hidden, dmade_keep, ((0,), (0,)))
+    home_rows, in_homely, out_homely, in_leave, out_leave = lax.optimization_barrier(
+        (home_rows, in_homely, out_homely, in_mine.astype(bf16), out_mine.astype(bf16))
+    )
+    in_arrived = lax.ppermute(in_leave, BOTH, across)
+    out_arrived = lax.ppermute(out_leave, BOTH, across)
+
+    dresid, gain_two_part, dqkv, fold, send, keep = call(
+        attend_back_kernel,
+        26,
+        (
+            ((count, width), f32),
+            ((1, width), f32),
+            ((3 * width, count), bf16),
+            ((heads, count // 2, count), f32),
+            ((2 * width, width), bf16),
+            ((2 * width, count), bf16),
+        ),
+        [pltpu.VMEM((4 * width, count), bf16)],
+        place, home_rows, dispatch, resid, upstream_b, gain_two, wt_o, qkv, probs, n1b, mixed_b,
+    )
+    got = flip(send, 1)
+    small_rows = (width // 128) * experts + 16 + (heads + 7) // 8 * 8
+    token_grad, small = call(
+        functools.partial(token_back_kernel, bucket_count),
+        26,
+        (
+            ((count, width), f32),
+            ((small_rows, 128), f32),
+        ),
+        [],
+        place, local, dqkv, wt_qkv, gain_one, dresid, fold, tiled, gain_two_part,
+        router_part,
+    )
+    block = width // 8
+    pieces = (width // 2, width // 3, width // 6)
+    cut = call(
+        split_kernel,
+        30,
+        tuple(((8, block, piece), bf16) for piece in pieces)
+        + tuple(((8, block, piece), f32) for piece in pieces),
+        [pltpu.VMEM((16, block, width), f32)],
+        place, keep, n1b, mixed_b, got,
+    )
+    attn_share, small, late = scatter_rows(
+        cut[:3],
+        cut[3:],
+        small,
+        (
+            (),
+            (in_arrived, in_mine, in_homely),
+            (out_arrived, out_mine, out_homely),
+            home_rows,
+        ),
+    )
+    _, (in_arrived, in_mine, in_homely), (out_arrived, out_mine, out_homely), home_rows = late
+    in_back = (in_mine, in_homely, in_arrived)
+    out_back = (out_mine, out_homely, out_arrived)
+
+    def settled(parts, axis):
+        near, homely, arrived = parts
+        mine = jnp.where(home, near, homely.astype(f32))
+        other = jnp.where(home, homely.astype(f32), arrived.astype(f32))
+        return whole(mine, other, axis)
+
+    in_share, out_share = settled(in_back, 1), settled(out_back, 0)
+    router_probs = jax.nn.softmax(dot(n2b, router_weight, ((1,), (0,))), axis=-1)
+    picked = (route_ids.reshape(count, 1) == jnp.arange(experts)).astype(f32)
+    gate = jnp.sum(router_probs * picked, axis=-1, keepdims=True)
+    returned = dot(dispatch, home_rows[:, width:], ((0,), (0,)))
+    output = (resid + gate * returned).astype(bf16)
+
+    attn_share = attn_share.T
+    routed = (width // 128) * experts
+    return (
+        output.reshape(tokens.shape),
+        token_grad.reshape(tokens.shape),
+        attn_share,
+        small[routed : routed + width // 128].reshape(width),
+        small[routed + 8 : routed + 8 + width // 128].reshape(width),
+        small[routed + 16 : routed + 16 + heads, :bucket_count].T,
+        jnp.transpose(small[:routed].reshape(-1, experts, 128), (0, 2, 1)).reshape(width, experts),
+        in_share[None],
+        out_share[None],
+    )
+
+
 def solution(mesh):
+    paired = mesh.shape["dp"] == 2 and mesh.shape["expert"] == 16
+    chosen = paired_body if paired else body
     placed = (
         P(None, ("dp", "expert"), None, None),
         P(None, ("dp", "expert")),
@@ -285,7 +914,7 @@
         P(None, ("dp", "expert"), None, None),
     )
     return jax.shard_map(
-        body,
+        chosen,
         mesh=mesh,
         in_specs=placed,
         out_specs=(

time: 546 us -> 248 us (0.45)
  waiting for transfers between devices: 317 us -> 81.4 us
  matrix products: 72.2 us -> 13.2 us
  Pallas kernels: 0 us -> 44.4 us
  blocking collectives: 38.4 us -> 0 us
  starting transfers between devices: 32.4 us -> 64.5 us
  local copies, waits for them, and re-layouts: 39 us -> 21.5 us
  between operations: 16.4 us -> 1.34 us
  other arithmetic: 27.9 us -> 20.8 us
    all_gather x3 -> x0, waiting for transfers between devices: 158 us -> none  [the longest x1 66.2 us: body(): lax.all_gather(attn_weight, ('dp', 'expert'), axis=1, tiled=True)]
    unnamed x7 -> x0, waiting for transfers between devices: 118 us -> none
    dot_general x49 -> x6, matrix products: 72.2 us -> 13.2 us  [dot(): lax.dot_general(left, right, (dims, ((), ())), preferred_element_type=jnp...]
    ppermute x0 -> x43, waiting for transfers between devices: none -> 46.6 us  [the longest x28 41.9 us: flip(): return lax.ppermute(tensor, 'expert', [(i, i ^ bit) for i in range(count)])]
    ppermute x0 -> x43, starting transfers between devices: none -> 45.6 us  [the longest x28 30.5 us: flip(): return lax.ppermute(tensor, 'expert', [(i, i ^ bit) for i in range(count)])]
    pallas_call x0 -> x7, Pallas kernels: none -> 44.4 us  [call(): pl.pallas_call(kernel, grid=(1,), out_shape=tuple((pltpu.HBM(*out) for ou...]
    psum x1 -> x0, blocking collectives: 38.4 us -> none  [body(): lax.psum((gain_one_total, gain_two_total, bias_total, router_total), ('dp...]
    unnamed x276 -> x68, local copies, waits for them, and re-layouts: 20.7 us -> 3.97 us
  transfers between devices with their start and end apart: 14 -> 45, of which waited for: 11 -> 22; matrix products, arithmetic and copies ran while one was open for 23% -> 19% of each run, Pallas kernels for 0% -> 11%
where the time goes in v2:
time: 248 us; the launch traced here: 247 us
  waiting for transfers between devices  81.4 us (33%)
  starting transfers between devices  64.5 us (26%)
  Pallas kernels  44.4 us (18%)
  local copies, waits for them, and re-layouts  21.5 us (9%)
  other arithmetic  20.8 us (8%)
  matrix products  13.2 us (5%)
    pallas_call x7, Pallas kernels, call(): pl.pallas_call(kernel, grid=(1,), out_shape=tuple((pltpu.HBM(*out) for ou...  44.4 us
    ppermute x28, waiting for transfers between devices, flip(): return lax.ppermute(tensor, 'expert', [(i, i ^ bit) for i in range(count)])  41.9 us
    all_to_all x2, waiting for transfers between devices, to_chips(): lax.all_to_all(tensor, BOTH, split_axis=0, concat_axis=0, tiled=True, axi...  34.8 us
    ppermute x28, starting transfers between devices, flip(): return lax.ppermute(tensor, 'expert', [(i, i ^ bit) for i in range(count)])  30.5 us
    all_to_all x2, starting transfers between devices, to_chips(): lax.all_to_all(tensor, BOTH, split_axis=0, concat_axis=0, tiled=True, axi...  18.9 us
    dot_general x6, matrix products, dot(): lax.dot_general(left, right, (dims, ((), ())), preferred_element_type=jnp...  13.2 us
    ppermute x7, starting transfers between devices, flip(): return lax.ppermute(tensor, 'dp', [(0, 1), (1, 0)])  7.98 us
  transfers between devices with their start and end apart: 45, of which 22 were waited for; matrix products, arithmetic and copies ran while one was open for 19% of the time, Pallas kernels for 11%

profile of v2, /device:TPU:0, one launch (start us, length us, event | category | flops | bytes accessed | tf_op | source)
XLA Modules:
  0.0 247.1 jit_solution(600315126643301492)
XLA Ops:
  0.6 1.5 slice_bitcast_fusion
  2.1 3.0 %collective-permute-start.2 = (bf16[1,1,1,1,96,256]{5,4,3,2,1,0:T(8,128)(2,1)}, bf16[1,1,1,1,96,256]{5,4,3,2,1,0:T(8,128)(2,1)}, u32[]{:S(2)}, u32[]{:S(2)}) collective-permute-start(bf16[1,1,1,1,96,256]{5,4,3,2,1,0:T(8,128)(2,1)} %get-tuple-element.231), channel_id=1, source_target_pairs={{0,16},{16,0},{1,17},{17,1},{2,18},{18,2},{3,19},{19,3},{4,20},{20... | collective-permute-start | bytes 147464 | tf_op jit(solution)/shard_map/ppermute | solution.py:280
  5.1 1.5 collective-permute-start.1
  6.6 2.6 %collective-permute-start = (bf16[1,1,1,1,96,256]{5,4,3,2,1,0:T(8,128)(2,1)}, bf16[1,1,1,1,96,256]{5,4,3,2,1,0:T(8,128)(2,1)}, u32[]{:S(2)}, u32[]{:S(2)}) collective-permute-start(bf16[1,1,1,1,96,256]{5,4,3,2,1,0:T(8,128)(2,1)} %get-tuple-element.233), channel_id=1, source_target_pairs={{0,8},{1,9},{2,10},{3,11},{4,12},{5,13},{6,14},{7,15},{8,0},{9,1},... | collective-permute-start | bytes 147464 | tf_op jit(solution)/shard_map/ppermute | solution.py:282
  9.2 2.8 %dynamic-slice_bitcast_fusion = (bf16[384,1536]{1,0:T(8,128)(2,1)}, bf16[384,1536]{1,0:T(8,128)(2,1)S(1)}) fusion(bf16[1,384,3072]{2,1,0:T(8,128)(2,1)} %param.18, s32[]{:T(128)S(6)} %select_n.391, s32[]{:T(128)S(6)} %select_n.371), kind=kLoop, calls=%fused_computation.15 | loop fusion | bytes 4718600 | tf_op jit(solution)/shard_map/dynamic_slice | solution.py:705
  12.0 1.7 collective-permute-start.6
  16.6 1.1 broadcast_select_fusion.19
  19.7 1.6 collective-permute-start.3
  21.2 1.3 fusion.13.rest_9_.dispatch_ref
  22.5 1.5 copy.35
  24.0 1.4 tile.4
  25.4 1.7 tile.10.buckets_ref
  27.9 3.5 %shard_map.187.rest_8_ = f32[12,128,128]{2,1,0:T(8,128)} custom-call(f32[32,12]{1,0:T(8,128)S(1)} %convert_element_type.102.table_ref, s32[128,128]{1,0:T(8,128)} %tile.10.buckets_ref), custom_call_target="tpu_custom_call" | custom-call | tf_op jit(solution)/shard_map/pallas_call | solution.py:364
  32.4 3.0 %collective-permute-done.4 = bf16[1,1,1,2,96,256]{5,4,3,2,1,0:T(8,128)(2,1)S(1)} collective-permute-done((bf16[1,1,1,2,96,256]{5,4,3,2,1,0:T(8,128)(2,1)}, bf16[1,1,1,2,96,256]{5,4,3,2,1,0:T(8,128)(2,1)S(1)}, u32[]{:S(2)}, u32[]{:S(2)}) %collective-permute-start.4) | collective-permute-done | bytes 98336 | tf_op jit(solution)/shard_map/ppermute | solution.py:282
  36.5 1.3 constant_dynamic-slice_fusion
  38.8 7.5 %collective-permute-done.11 = bf16[2,1,1,2,96,256]{5,4,3,2,1,0:T(8,128)(2,1)S(1)} collective-permute-done((bf16[2,1,1,2,96,256]{5,4,3,2,1,0:T(8,128)(2,1)S(1)}, bf16[2,1,1,2,96,256]{5,4,3,2,1,0:T(8,128)(2,1)S(1)}, u32[]{:S(2)}, u32[]{:S(2)}) %collective-permute-start.11) | collective-permute-done | bytes 196640 | tf_op jit(solution)/shard_map/ppermute | solution.py:282
  47.3 1.7 collective-permute-done.9
  49.1 8.3 %collective-permute-done.12 = bf16[2,2,1,2,96,256]{5,4,3,2,1,0:T(8,128)(2,1)S(1)} collective-permute-done((bf16[2,2,1,2,96,256]{5,4,3,2,1,0:T(8,128)(2,1)S(1)}, bf16[2,2,1,2,96,256]{5,4,3,2,1,0:T(8,128)(2,1)S(1)}, u32[]{:S(2)}, u32[]{:S(2)}) %collective-permute-start.12) | collective-permute-done | bytes 393248 | tf_op jit(solution)/shard_map/ppermute | solution.py:282
  57.6 1.3 collective-permute-done.10
  59.2 1.7 collective-permute-start.16
  60.9 2.4 collective-permute-start.14
  65.3 1.1 collective-permute-done.13.rest_3_
  66.4 1.1 collective-permute-done.15.rest_5_
  67.6 10.3 %shard_map.188 = (bf16[12,2,96,768]{3,2,1,0:T(8,128)(2,1)}, bf16[4,2,96,768]{3,2,1,0:T(8,128)(2,1)}, bf16[128,768]{1,0:T(8,128)(2,1)}, bf16[2304,128]{1,0:T(8,12...) custom-call(s32[6]{0:T(128)S(1)} %stack.31.place_ref.core_ref._, ...), custom_call_target="tpu_custom_call" | custom-call | tf_op jit(solution)/shard_map/pallas_call | solution.py:364
  77.9 2.2 all_to_all.15
  80.1 12.3 %all-to-all-start = ((bf16[16,10,1536]{2,1,0:T(8,128)(2,1)}), bf16[16,10,1536]{2,1,0:T(8,128)(2,1)S(1)}, u32[]{:S(2)}, u32[]{:S(2)}) async-start(bf16[16,10,1536]{2,1,0:T(8,128)(2,1)} %all_to_all.15), calls=%async_computation | async-start | bytes 1572864 | tf_op jit(solution)/shard_map/all_to_all | solution.py:693
  92.4 1.4 collective-permute-start.19
  93.8 19.9 %all-to-all-done = bf16[16,10,1536]{2,1,0:T(8,128)(2,1)S(1)} async-done(((bf16[16,10,1536]{2,1,0:T(8,128)(2,1)}), bf16[16,10,1536]{2,1,0:T(8,128)(2,1)S(1)}, u32[]{:S(2)}, u32[]{:S(2)}) %all-to-all-start) | async-done | bytes 491552 | tf_op jit(solution)/shard_map/all_to_all | solution.py:693
  115.3 1.9 collective-permute-done.19.out_far_ref
  118.0 9.7 %shard_map.189 = (bf16[320,768]{1,0:T(8,128)(2,1)}, bf16[320,1536]{1,0:T(8,128)(2,1)}, bf16[320,1536]{1,0:T(8,128)(2,1)}, bf16[320,768]{1,0:T(8,128)(2,1)}, f32[...) custom-call(s32[6]{0:T(128)S(1)} %stack.31.place_ref.core_ref._, bf16[160,1536]{1,0:T(8,128)(2,1)} %copy-done.3, ...), custom_call_target="tpu_custom_call" | custom-call | tf_op jit(solution)/shard_map/pallas_call | solution.py:364
  127.8 3.2 %convolution_convert_fusion.1 = bf16[384,1536]{1,0:T(8,128)(2,1)} fusion(bf16[320,1536]{1,0:T(8,128)(2,1)} %get-tuple-element.130, bf16[320,768]{1,0:T(8,128)(2,1)} %get-tuple-element.129, s32[]{:T(128)S(6)} %select_n.392), kind=kOutput, calls=%fused_computation.7 | convolution fusion | flops 378077184 | bytes 2408452 | tf_op jit(solution)/shard_map/dot_general | solution.py:349
  132.5 3.4 %shard_map.190 = (bf16[160,1536]{1,0:T(8,128)(2,1)}, f32[16,768]{1,0:T(8,128)}) custom-call(s32[6]{0:T(128)S(1)} %stack.31.place_ref.core_ref._, f32[2,160,768]{2,1,0:T(8,128)} %get-tuple-element.118.mine_ref, f32[2,160,768]{2,1,0:T(8,128)} %copy-done.16, bf16[160,1536]{1,0:T(8,128)(2,1)} %copy-done.3, f32[160,16]{1,0:T(8,128)} %get-tuple-element.120.probs_ref, ...), custom_call_target="tpu_custom_call" | custom-call | tf_op jit(solution)/shard_map/pallas_call | solution.py:364
  135.9 2.0 convolution_convert_fusion
  138.0 1.0 all_to_all.18
  139.1 6.6 %all-to-all-start.1 = ((bf16[16,10,1536]{2,1,0:T(8,128)(2,1)}), bf16[16,10,1536]{2,1,0:T(8,128)(2,1)S(1)}, u32[]{:S(2)}, u32[]{:S(2)}) async-start(bf16[16,10,1536]{2,1,0:T(8,128)(2,1)} %all_to_all.18), calls=%async_computation.1 | async-start | bytes 1572864 | tf_op jit(solution)/shard_map/all_to_all | solution.py:693
  145.7 3.4 %fusion.22 = (bf16[1536,384]{1,0:T(8,128)(2,1)}, f32[1536,384]{1,0:T(8,128)S(1)}) fusion(bf16[320,1536]{1,0:T(8,128)(2,1)} %get-tuple-element.127, bf16[320,768]{1,0:T(8,128)(2,1)} %get-tuple-element.128, s32[]{:T(128)S(6)} %select_n.393), kind=kOutput, calls=%fused_computation.111 | convolution fusion | flops 378077184 | bytes 4767748 | tf_op jit(solution)/shard_map/dot_general | solution.py:349
  149.1 2.6 %fusion.21 = (bf16[384,1536]{1,0:T(8,128)(2,1)}, f32[384,1536]{1,0:T(8,128)}) fusion(bf16[320,1536]{1,0:T(8,128)(2,1)S(1)} %copy-done.4, bf16[320,768]{1,0:T(8,128)(2,1)S(1)} %copy-done.20, s32[]{:T(128)S(6)} %select_n.393), kind=kOutput, calls=%fused_computation.110 | convolution fusion | flops 378077184 | bytes 4767748 | tf_op jit(solution)/shard_map/dot_general | solution.py:349
  151.7 14.9 %all-to-all-done.1 = bf16[16,10,1536]{2,1,0:T(8,128)(2,1)S(1)} async-done(((bf16[16,10,1536]{2,1,0:T(8,128)(2,1)}), bf16[16,10,1536]{2,1,0:T(8,128)(2,1)S(1)}, u32[]{:S(2)}, u32[]{:S(2)}) %all-to-all-start.1) | async-done | bytes 491552 | tf_op jit(solution)/shard_map/all_to_all | solution.py:693
  167.5 7.8 %shard_map.191 = (f32[128,768]{1,0:T(8,128)}, f32[1,768]{1,0:T(1,128)}, bf16[2304,128]{1,0:T(8,128)(2,1)}, f32[12,64,128]{2,1,0:T(8,128)}, bf16[1536,768]{1,0:T(8,128)(2,1)}, /*index=5*/bf16[1536,128]{1,0:T(8,128)(2,1)}) custom-call(s32[6]{0:T(128)S(1)} %stack.31.place_ref.core_ref._, bf16[160,1536]{1,0:T(8,128)(2,1)} %all_to_all.20.dn2_ref, ...), custom_call_target="tpu_custom_call" | custom-call | tf_op jit(solution)/shard_map/pallas_call | solution.py:364
  175.3 1.3 collective-permute-start.23
  177.5 1.1 fusion.23
  178.6 5.1 %shard_map.193 = (f32[128,768]{1,0:T(8,128)}, f32[128,128]{1,0:T(8,128)}) custom-call(s32[6]{0:T(128)S(1)} %stack.31.place_ref.core_ref._, bf16[128,768]{1,0:T(8,128)(2,1)} %bitcast.100, bf16[2304,128]{1,0:T(8,128)(2,1)} %get-tuple-element.147.dqkv_ref, bf16[2304,768]{1,0:T(8,128)(2,1)} %bitcast.84, f32[1,768]{1,0:T(1,128)} %reshape.184.rest_6_.gain_one_ref, ...), custom_call_target="tpu_custom_call" | custom-call | tf_op jit(solution)/shard_map/pallas_call | solution.py:364
  183.8 2.5 %collective-permute-start.28 = (f32[128,128]{1,0:T(8,128)}, f32[128,128]{1,0:T(8,128)S(1)}, u32[]{:S(2)}, u32[]{:S(2)}) collective-permute-start(f32[128,128]{1,0:T(8,128)} %get-tuple-element.154), channel_id=1, source_target_pairs={{0,1},{1,0},{2,3},{3,2},{4,5},{5,4},{6,7},{7,6},{8,9},{9,8},{10,11... | collective-permute-start | bytes 196616 | tf_op jit(solution)/shard_map/ppermute | solution.py:282
  186.3 4.6 %shard_map.192 = (bf16[8,96,384]{2,1,0:T(8,128)(2,1)}, bf16[8,96,256]{2,1,0:T(8,128)(2,1)}, bf16[8,96,128]{2,1,0:T(8,128)(2,1)}, f32[8,96,384]{2,1,0:T(8,128)}, ...) custom-call(s32[6]{0:T(128)S(1)} %stack.31.place_ref.core_ref._, bf16[1536,128]{1,0:T(8,128)(2,1)} %get-tuple-element.137.keep_ref, ...), custom_call_target="tpu_custom_call" | custom-call | tf_op jit(solution)/shard_map/pallas_call | solution.py:364
  190.9 2.3 collective-permute-start.26
  193.8 1.5 collective-permute-start.29
  195.9 2.6 %collective-permute-done.29 = f32[128,128]{1,0:T(8,128)S(1)} collective-permute-done((f32[128,128]{1,0:T(8,128)S(1)}, f32[128,128]{1,0:T(8,128)S(1)}, u32[]{:S(2)}, u32[]{:S(2)}) %collective-permute-start.29) | collective-permute-done | bytes 65568 | tf_op jit(solution)/shard_map/ppermute | solution.py:282
  199.3 3.8 %collective-permute-done.26 = bf16[8,96,128]{2,1,0:T(8,128)(2,1)S(1)} collective-permute-done((bf16[8,96,128]{2,1,0:T(8,128)(2,1)}, bf16[8,96,128]{2,1,0:T(8,128)(2,1)S(1)}, u32[]{:S(2)}, u32[]{:S(2)}) %collective-permute-start.26) | collective-permute-done | bytes 196640 | tf_op jit(solution)/shard_map/ppermute | solution.py:282
  204.2 1.2 convert_add_fusion.1
  205.4 5.3 %collective-permute-done.24 = bf16[8,96,384]{2,1,0:T(8,128)(2,1)S(1)} collective-permute-done((bf16[8,96,384]{2,1,0:T(8,128)(2,1)}, bf16[8,96,384]{2,1,0:T(8,128)(2,1)S(1)}, u32[]{:S(2)}, u32[]{:S(2)}) %collective-permute-start.24) | collective-permute-done | bytes 589856 | tf_op jit(solution)/shard_map/ppermute | solution.py:282
  210.9 1.4 collective-permute-start.34
  212.3 1.5 collective-permute-start.32
  215.3 1.9 fusion.1
  217.2 2.5 %maximum_bitcast_fusion = f32[1,384,3072]{2,1,0:T(8,128)} fusion(f32[384,1536]{1,0:T(8,128)S(1)} %get-tuple-element.198, f32[384,1536]{1,0:T(8,128)S(1)} %get-tuple-element.197), kind=kLoop, calls=%fused_computation | loop fusion | flops 1179648 | bytes 9437184 | tf_op jit(solution)/shard_map/broadcast_in_dim | solution.py:894
  219.7 1.3 collective-permute-done.34
  221.0 3.3 %collective-permute-done.31 = bf16[1,1,2,2,1,96,256]{6,5,4,3,2,1,0:T(8,128)(2,1)S(1)} collective-permute-done((bf16[1,1,2,2,1,96,256]{6,5,4,3,2,1,0:T(8,128)(2,1)S(1)}, bf16[1,1,2,2,1,96,256]{6,5,4,3,2,1,0:T(8,128)(2,1)S(1)}, u32[]{:S(2)}, u32[]{:S(2)}) %collective-permute-start.31) | collective-permute-done | bytes 196640 | tf_op jit(solution)/shard_map/ppermute | solution.py:282
  224.6 1.5 collective-permute-start.37
  227.2 1.5 collective-permute-start.36
  228.7 2.0 collective-permute-start.35
  230.7 1.8 fusion.3
  232.5 2.5 %maximum_bitcast_fusion.1 = f32[1,3072,384]{2,1,0:T(8,128)} fusion(f32[1536,384]{1,0:T(8,128)S(1)} %get-tuple-element.196, f32[1536,384]{1,0:T(8,128)S(1)} %get-tuple-element.195), kind=kLoop, calls=%fused_computation.1 | loop fusion | flops 1179648 | bytes 9437184 | tf_op jit(solution)/shard_map/broadcast_in_dim | solution.py:895
  235.9 1.8 collective-permute-done.35
  237.7 1.8 collective-permute-start.41
  240.3 2.0 collective-permute-start.39
  (188 shorter events, 30.5 us)
Async XLA Ops:
  2.1 14.4 %collective-permute-start.2 = (bf16[1,1,1,1,96,256]{5,4,3,2,1,0:T(8,128)(2,1)}, bf16[1,1,1,1,96,256]{5,4,3,2,1,0:T(8,128)(2,1)}, u32[]{:S(2)}, u32[]{:S(2)}) collective-permute-start(bf16[1,1,1,1,96,256]{5,4,3,2,1,0:T(8,128)(2,1)} %get-tuple-element.231), channel_id=1, source_target_pairs={{0,16},{16,0},{1,17},{17,1},{2,18},{18,2},{3,19},{19,3},{4,20},{20... | collective-permute-start | bytes 147464 | tf_op jit(solution)/shard_map/ppermute | solution.py:280
  5.1 11.5 %collective-permute-start.1 = (bf16[1,1,1,1,96,256]{5,4,3,2,1,0:T(8,128)(2,1)}, bf16[1,1,1,1,96,256]{5,4,3,2,1,0:T(8,128)(2,1)}, u32[]{:S(2)}, u32[]{:S(2)}) collective-permute-start(bf16[1,1,1,1,96,256]{5,4,3,2,1,0:T(8,128)(2,1)} %get-tuple-element.232), channel_id=1, source_target_pairs={{0,2},{1,3},{2,0},{3,1},{4,6},{5,7},{6,4},{7,5},{8,10},{9,11},{10,... | collective-permute-start | bytes 147464 | tf_op jit(solution)/shard_map/ppermute | solution.py:282
  6.6 10.0 %collective-permute-start = (bf16[1,1,1,1,96,256]{5,4,3,2,1,0:T(8,128)(2,1)}, bf16[1,1,1,1,96,256]{5,4,3,2,1,0:T(8,128)(2,1)}, u32[]{:S(2)}, u32[]{:S(2)}) collective-permute-start(bf16[1,1,1,1,96,256]{5,4,3,2,1,0:T(8,128)(2,1)} %get-tuple-element.233), channel_id=1, source_target_pairs={{0,8},{1,9},{2,10},{3,11},{4,12},{5,13},{6,14},{7,15},{8,0},{9,1},... | collective-permute-start | bytes 147464 | tf_op jit(solution)/shard_map/ppermute | solution.py:282
  12.0 24.4 %copy-start.1 = (bf16[384,1536]{1,0:T(8,128)(2,1)}, bf16[384,1536]{1,0:T(8,128)(2,1)S(1)}, u32[]{:S(2)}) copy-start(bf16[384,1536]{1,0:T(8,128)(2,1)S(1)} %get-tuple-element.202.in_near_ref) | copy-start | bytes 3538948
  12.0 24.4 %collective-permute-start.6 = (bf16[384,1536]{1,0:T(8,128)(2,1)S(1)}, bf16[384,1536]{1,0:T(8,128)(2,1)}, u32[]{:S(2)}, u32[]{:S(2)}) collective-permute-start(bf16[384,1536]{1,0:T(8,128)(2,1)S(1)} %get-tuple-element.202.in_near_ref), channel_id=1, source_target_pairs={{1,16},{3,18},{5,20},{7,22},{9,24},{11,26},{13,28},{15,30},{16,1},... | collective-permute-start | bytes 3538952 | tf_op jit(solution)/shard_map/ppermute | solution.py:709
  16.6 20.0 %copy-start.9 = (bf16[1,3072,384]{2,1,0:T(8,128)(2,1)S(1)}, bf16[1,3072,384]{2,1,0:T(8,128)(2,1)}, u32[]{:S(2)}) copy-start(bf16[1,3072,384]{2,1,0:T(8,128)(2,1)} %param.19) | copy-start | bytes 7077892
  19.7 11.8 %collective-permute-start.3 = (bf16[1,2,1,1,96,256]{5,4,3,2,1,0:T(8,128)(2,1)}, bf16[1,2,1,1,96,256]{5,4,3,2,1,0:T(8,128)(2,1)}, u32[]{:S(2)}, u32[]{:S(2)}) collective-permute-start(bf16[1,2,1,1,96,256]{5,4,3,2,1,0:T(8,128)(2,1)} %pad_maximum_fusion.9), channel_id=1, source_target_pairs={{0,4},{1,5},{2,6},{3,7},{4,0},{5,1},{6,2},{7,3},{8,12},{9,13},{10,... | collective-permute-start | bytes 294920 | tf_op jit(solution)/shard_map/ppermute | solution.py:282
  27.1 9.3 %copy-start.21 = (bf16[2,1,1,1,96,256]{5,4,3,2,1,0:T(8,128)(2,1)S(1)}, bf16[2,1,1,1,96,256]{5,4,3,2,1,0:T(8,128)(2,1)}, u32[]{:S(2)}) copy-start(bf16[2,1,1,1,96,256]{5,4,3,2,1,0:T(8,128)(2,1)} %pad_maximum_fusion.11) | copy-start | bytes 294916
  27.1 8.3 %collective-permute-start.4 = (bf16[1,1,1,2,96,256]{5,4,3,2,1,0:T(8,128)(2,1)}, bf16[1,1,1,2,96,256]{5,4,3,2,1,0:T(8,128)(2,1)S(1)}, u32[]{:S(2)}, u32[]{:S(2)}) collective-permute-start(bf16[1,1,1,2,96,256]{5,4,3,2,1,0:T(8,128)(2,1)} %pad_maximum_fusion.10), channel_id=1, source_target_pairs={{0,8},{1,9},{2,10},{3,11},{4,12},{5,13},{6,14},{7,15},{8,0},{9,1},... | collective-permute-start | bytes 294920 | tf_op jit(solution)/shard_map/ppermute | solution.py:282
  27.4 9.0 %collective-permute-start.5 = (bf16[2,1,1,1,96,256]{5,4,3,2,1,0:T(8,128)(2,1)}, bf16[2,1,1,1,96,256]{5,4,3,2,1,0:T(8,128)(2,1)S(1)}, u32[]{:S(2)}, u32[]{:S(2)}) collective-permute-start(bf16[2,1,1,1,96,256]{5,4,3,2,1,0:T(8,128)(2,1)} %pad_maximum_fusion.11), channel_id=1, source_target_pairs={{0,2},{1,3},{2,0},{3,1},{4,6},{5,7},{6,4},{7,5},{8,10},{9,11},{10,... | collective-permute-start | bytes 294920 | tf_op jit(solution)/shard_map/ppermute | solution.py:282
  36.5 9.8 %collective-permute-start.11 = (bf16[2,1,1,2,96,256]{5,4,3,2,1,0:T(8,128)(2,1)S(1)}, bf16[2,1,1,2,96,256]{5,4,3,2,1,0:T(8,128)(2,1)S(1)}, u32[]{:S(2)}, u32[]{:S(2)}) collective-permute-start(bf16[2,1,1,2,96,256]{5,4,3,2,1,0:T(8,128)(2,1)S(1)} %pad_maximum_fusion.8), channel_id=1, source_target_pairs={{0,8},{1,9},{2,10},{3,11},{4,12},{5,13},{6,14},{7,15},{8,0},{9,1},... | collective-permute-start | bytes 589832 | tf_op jit(solution)/shard_map/ppermute | solution.py:282
  37.9 21.3 %copy-start.2 = (bf16[1536,384]{1,0:T(8,128)(2,1)}, bf16[1536,384]{1,0:T(8,128)(2,1)S(1)}, u32[]{:S(2)}) copy-start(bf16[1536,384]{1,0:T(8,128)(2,1)S(1)} %get-tuple-element.110.out_near_ref) | copy-start | bytes 3538948
  37.9 8.5 %collective-permute-start.7 = (bf16[1,2,2,1,96,256]{5,4,3,2,1,0:T(8,128)(2,1)S(1)}, bf16[1,2,2,1,96,256]{5,4,3,2,1,0:T(8,128)(2,1)S(1)}, u32[]{:S(2)}, u32[]{:S(2)}) collective-permute-start(bf16[1,2,2,1,96,256]{5,4,3,2,1,0:T(8,128)(2,1)S(1)} %pad_maximum_fusion.6), channel_id=1, source_target_pairs={{0,16},{16,0},{1,17},{17,1},{2,18},{18,2},{3,19},{19,3},{4,20},{20... | collective-permute-start | bytes 589832 | tf_op jit(solution)/shard_map/ppermute | solution.py:280
  38.3 10.6 %collective-permute-start.9 = (bf16[1,2,1,2,96,256]{5,4,3,2,1,0:T(8,128)(2,1)S(1)}, bf16[1,2,1,2,96,256]{5,4,3,2,1,0:T(8,128)(2,1)S(1)}, u32[]{:S(2)}, u32[]{:S(2)}) collective-permute-start(bf16[1,2,1,2,96,256]{5,4,3,2,1,0:T(8,128)(2,1)S(1)} %pad_maximum_fusion.7), channel_id=1, source_target_pairs={{0,4},{1,5},{2,6},{3,7},{4,0},{5,1},{6,2},{7,3},{8,12},{9,13},{10,... | collective-permute-start | bytes 589832 | tf_op jit(solution)/shard_map/ppermute | solution.py:282
  46.3 11.1 %collective-permute-start.12 = (bf16[2,2,1,2,96,256]{5,4,3,2,1,0:T(8,128)(2,1)S(1)}, bf16[2,2,1,2,96,256]{5,4,3,2,1,0:T(8,128)(2,1)S(1)}, u32[]{:S(2)}, u32[]{:S(2)}) collective-permute-start(bf16[2,2,1,2,96,256]{5,4,3,2,1,0:T(8,128)(2,1)S(1)} %pad_maximum_fusion.5), channel_id=1, source_target_pairs={{0,4},{1,5},{2,6},{3,7},{4,0},{5,1},{6,2},{7,3},{8,12},{9,13},{10,... | collective-permute-start | bytes 1179656 | tf_op jit(solution)/shard_map/ppermute | solution.py:282
  46.5 11.1 %collective-permute-start.8 = (bf16[2,2,2,1,96,256]{5,4,3,2,1,0:T(8,128)(2,1)S(1)}, bf16[2,2,2,1,96,256]{5,4,3,2,1,0:T(8,128)(2,1)S(1)}, u32[]{:S(2)}, u32[]{:S(2)}) collective-permute-start(bf16[2,2,2,1,96,256]{5,4,3,2,1,0:T(8,128)(2,1)S(1)} %pad_maximum_fusion.3), channel_id=1, source_target_pairs={{0,2},{1,3},{2,0},{3,1},{4,6},{5,7},{6,4},{7,5},{8,10},{9,11},{10,... | collective-permute-start | bytes 1179656 | tf_op jit(solution)/shard_map/ppermute | solution.py:282
  49.0 9.9 %collective-permute-start.10 = (bf16[1,2,2,2,96,256]{5,4,3,2,1,0:T(8,128)(2,1)S(1)}, bf16[1,2,2,2,96,256]{5,4,3,2,1,0:T(8,128)(2,1)S(1)}, u32[]{:S(2)}, u32[]{:S(2)}) collective-permute-start(bf16[1,2,2,2,96,256]{5,4,3,2,1,0:T(8,128)(2,1)S(1)} %pad_maximum_fusion.4), channel_id=1, source_target_pairs={{0,16},{16,0},{1,17},{17,1},{2,18},{18,2},{3,19},{19,3},{4,20},{20... | collective-permute-start | bytes 1179656 | tf_op jit(solution)/shard_map/ppermute | solution.py:280
  59.1 8.4 %copy-start.6 = (bf16[2,2,2,2,96,256]{5,4,3,2,1,0:T(8,128)(2,1)}, bf16[2,2,2,2,96,256]{5,4,3,2,1,0:T(8,128)(2,1)S(1)}, u32[]{:S(2)}) copy-start(bf16[2,2,2,2,96,256]{5,4,3,2,1,0:T(8,128)(2,1)S(1)} %get-tuple-element.102) | copy-start | bytes 2359300
  59.1 8.4 %copy-start.7 = (bf16[2,2,2,2,96,256]{5,4,3,2,1,0:T(8,128)(2,1)}, bf16[2,2,2,2,96,256]{5,4,3,2,1,0:T(8,128)(2,1)S(1)}, u32[]{:S(2)}) copy-start(bf16[2,2,2,2,96,256]{5,4,3,2,1,0:T(8,128)(2,1)S(1)} %get-tuple-element.103) | copy-start | bytes 2359300
  59.1 18.8 %collective-permute-start.17 = (bf16[384,1536]{1,0:T(8,128)(2,1)}, bf16[384,1536]{1,0:T(8,128)(2,1)}, u32[]{:S(2)}, u32[]{:S(2)}) collective-permute-start(bf16[384,1536]{1,0:T(8,128)(2,1)} %get-tuple-element.111), channel_id=1, source_target_pairs={{0,1},{1,17},{2,3},{3,19},{4,5},{5,21},{6,7},{7,23},{8,9},{9,25},{... | collective-permute-start | bytes 3538952 | tf_op jit(solution)/shard_map/ppermute | solution.py:770
  59.2 18.7 %collective-permute-start.16 = (bf16[1536,384]{1,0:T(8,128)(2,1)S(1)}, bf16[1536,384]{1,0:T(8,128)(2,1)}, u32[]{:S(2)}, u32[]{:S(2)}) collective-permute-start(bf16[1536,384]{1,0:T(8,128)(2,1)S(1)} %get-tuple-element.110.out_near_ref), channel_id=1, source_target_pairs={{1,16},{3,18},{5,20},{7,22},{9,24},{11,26},{13,28},{15,30},{16,1},... | collective-permute-start | bytes 3538952 | tf_op jit(solution)/shard_map/ppermute | solution.py:736
  60.9 4.4 %collective-permute-start.14 = (bf16[16,96,256]{2,1,0:T(8,128)(2,1)S(1)}, bf16[16,96,256]{2,1,0:T(8,128)(2,1)}, u32[]{:S(2)}, u32[]{:S(2)}) collective-permute-start(bf16[16,96,256]{2,1,0:T(8,128)(2,1)S(1)} %bitcast.89), channel_id=1, source_target_pairs={{0,1},{1,0},{2,3},{3,2},{4,5},{5,4},{6,7},{7,6},{8,9},{9,8},{10,11... | collective-permute-start | bytes 2359304 | tf_op jit(solution)/shard_map/ppermute | solution.py:282
  63.3 3.2 %collective-permute-start.13 = (bf16[16,96,256]{2,1,0:T(8,128)(2,1)S(1)}, bf16[16,96,256]{2,1,0:T(8,128)(2,1)}, u32[]{:S(2)}, u32[]{:S(2)}) collective-permute-start(bf16[16,96,256]{2,1,0:T(8,128)(2,1)S(1)} %bitcast.87), channel_id=1, source_target_pairs={{0,1},{1,0},{2,3},{3,2},{4,5},{5,4},{6,7},{7,6},{8,9},{9,8},{10,11... | collective-permute-start | bytes 2359304 | tf_op jit(solution)/shard_map/ppermute | solution.py:282
  63.3 4.2 %collective-permute-start.15 = (bf16[16,96,256]{2,1,0:T(8,128)(2,1)S(1)}, bf16[16,96,256]{2,1,0:T(8,128)(2,1)}, u32[]{:S(2)}, u32[]{:S(2)}) collective-permute-start(bf16[16,96,256]{2,1,0:T(8,128)(2,1)S(1)} %bitcast.85), channel_id=1, source_target_pairs={{0,1},{1,0},{2,3},{3,2},{4,5},{5,4},{6,7},{7,6},{8,9},{9,8},{10,11... | collective-permute-start | bytes 2359304 | tf_op jit(solution)/shard_map/ppermute | solution.py:282
  77.9 14.5 %copy-start.12 = (bf16[1536,384]{1,0:T(8,128)(2,1)S(1)}, bf16[1536,384]{1,0:T(8,128)(2,1)}, u32[]{:S(2)}) copy-start(bf16[1536,384]{1,0:T(8,128)(2,1)} %get-tuple-element.117) | copy-start | bytes 3538948
  77.9 36.6 %copy-start.23 = (bf16[768,16]{0,1:T(8,128)(2,1)S(1)}, bf16[768,16]{0,1:T(8,128)(2,1)}, u32[]{:S(2)}) copy-start(bf16[768,16]{0,1:T(8,128)(2,1)} %param.17) | copy-start | bytes 73732
  80.1 33.7 %all-to-all-start = ((bf16[16,10,1536]{2,1,0:T(8,128)(2,1)}), bf16[16,10,1536]{2,1,0:T(8,128)(2,1)S(1)}, u32[]{:S(2)}, u32[]{:S(2)}) async-start(bf16[16,10,1536]{2,1,0:T(8,128)(2,1)} %all_to_all.15), calls=%async_computation | async-start | bytes 1572864 | tf_op jit(solution)/shard_map/all_to_all | solution.py:693
  92.4 24.8 %collective-permute-start.19 = (bf16[1536,384]{1,0:T(8,128)(2,1)S(1)}, bf16[1536,384]{1,0:T(8,128)(2,1)}, u32[]{:S(2)}, u32[]{:S(2)}) collective-permute-start(bf16[1536,384]{1,0:T(8,128)(2,1)S(1)} %copy-done.12), channel_id=1, source_target_pairs={{0,1},{1,17},{2,3},{3,19},{4,5},{5,21},{6,7},{7,23},{8,9},{9,25},{... | collective-permute-start | bytes 3538952 | tf_op jit(solution)/shard_map/ppermute | solution.py:774
  113.9 3.3 %collective-permute-start.18 = (bf16[160,1536]{1,0:T(8,128)(2,1)S(1)}, bf16[160,1536]{1,0:T(8,128)(2,1)S(1)}, u32[]{:S(2)}, u32[]{:S(2)}) collective-permute-start(bf16[160,1536]{1,0:T(8,128)(2,1)S(1)} %all_to_all.17.own_ref), channel_id=1, source_target_pairs={{0,1},{1,0},{2,3},{3,2},{4,5},{5,4},{6,7},{7,6},{8,9},{9,8},{10,11... | collective-permute-start | bytes 1474568 | tf_op jit(solution)/shard_map/ppermute | solution.py:282
  127.7 3.7 %collective-permute-start.20 = (f32[2,160,768]{2,1,0:T(8,128)}, f32[2,160,768]{2,1,0:T(8,128)S(1)}, u32[]{:S(2)}, u32[]{:S(2)}) collective-permute-start(f32[2,160,768]{2,1,0:T(8,128)} %get-tuple-element.119), channel_id=1, source_target_pairs={{0,1},{1,0},{2,3},{3,2},{4,5},{5,4},{6,7},{7,6},{8,9},{9,8},{10,11... | collective-permute-start | bytes 2949128 | tf_op jit(solution)/shard_map/ppermute | solution.py:282
  127.7 8.1 %copy-start.15 = (bf16[320,1536]{1,0:T(8,128)(2,1)S(1)}, bf16[320,1536]{1,0:T(8,128)(2,1)}, u32[]{:S(2)}) copy-start(bf16[320,1536]{1,0:T(8,128)(2,1)} %get-tuple-element.127) | copy-start | bytes 2949124
  127.8 8.1 %copy-start.22 = (bf16[320,768]{1,0:T(8,128)(2,1)S(1)}, bf16[320,768]{1,0:T(8,128)(2,1)}, u32[]{:S(2)}) copy-start(bf16[320,768]{1,0:T(8,128)(2,1)} %get-tuple-element.128) | copy-start | bytes 1474564
  131.0 36.5 %collective-permute-start.21 = (bf16[384,1536]{1,0:T(8,128)(2,1)}, bf16[384,1536]{1,0:T(8,128)(2,1)}, u32[]{:S(2)}, u32[]{:S(2)}) collective-permute-start(bf16[384,1536]{1,0:T(8,128)(2,1)} %convolution_convert_fusion.1), channel_id=1, source_target_pairs={{0,16},{1,0},{2,18},{3,2},{4,20},{5,4},{6,22},{7,6},{8,24},{9,8},{... | collective-permute-start | bytes 3538952 | tf_op jit(solution)/shard_map/ppermute | solution.py:808
  137.9 29.7 %collective-permute-start.22 = (bf16[1536,384]{1,0:T(8,128)(2,1)}, bf16[1536,384]{1,0:T(8,128)(2,1)}, u32[]{:S(2)}, u32[]{:S(2)}) collective-permute-start(bf16[1536,384]{1,0:T(8,128)(2,1)} %convolution_convert_fusion), channel_id=1, source_target_pairs={{0,16},{1,0},{2,18},{3,2},{4,20},{5,4},{6,22},{7,6},{8,24},{9,8},{... | collective-permute-start | bytes 3538952 | tf_op jit(solution)/shard_map/ppermute | solution.py:811
  139.1 27.5 %all-to-all-start.1 = ((bf16[16,10,1536]{2,1,0:T(8,128)(2,1)}), bf16[16,10,1536]{2,1,0:T(8,128)(2,1)S(1)}, u32[]{:S(2)}, u32[]{:S(2)}) async-start(bf16[16,10,1536]{2,1,0:T(8,128)(2,1)} %all_to_all.18), calls=%async_computation.1 | async-start | bytes 1572864 | tf_op jit(solution)/shard_map/all_to_all | solution.py:693
  167.5 9.1 %copy-start.13 = (bf16[384,1536]{1,0:T(8,128)(2,1)S(1)}, bf16[384,1536]{1,0:T(8,128)(2,1)}, u32[]{:S(2)}) copy-start(bf16[384,1536]{1,0:T(8,128)(2,1)} %get-tuple-element.145) | copy-start | bytes 3538948
  175.3 11.0 %collective-permute-start.23 = (bf16[1536,768]{1,0:T(8,128)(2,1)}, bf16[1536,768]{1,0:T(8,128)(2,1)}, u32[]{:S(2)}, u32[]{:S(2)}) collective-permute-start(bf16[1536,768]{1,0:T(8,128)(2,1)} %get-tuple-element.138), channel_id=1, source_target_pairs={{0,1},{1,0},{2,3},{3,2},{4,5},{5,4},{6,7},{7,6},{8,9},{9,8},{10,11... | collective-permute-start | bytes 7077896 | tf_op jit(solution)/shard_map/ppermute | solution.py:282
  176.6 34.3 %collective-permute-start.27 = (bf16[384,1536]{1,0:T(8,128)(2,1)S(1)}, bf16[384,1536]{1,0:T(8,128)(2,1)S(1)}, u32[]{:S(2)}, u32[]{:S(2)}) collective-permute-start(bf16[384,1536]{1,0:T(8,128)(2,1)S(1)} %copy-done.13), channel_id=1, source_target_pairs={{1,16},{3,18},{5,20},{7,22},{9,24},{11,26},{13,28},{15,30},{16,1},... | collective-permute-start | bytes 3538952 | tf_op jit(solution)/shard_map/ppermute | solution.py:816
  183.7 10.0 %copy-start.24 = (f32[128,128]{1,0:T(8,128)S(1)}, f32[128,128]{1,0:T(8,128)}, u32[]{:S(2)}) copy-start(f32[128,128]{1,0:T(8,128)} %get-tuple-element.154) | copy-start | bytes 196612
  183.7 12.1 %copy-start.29 = (s32[128]{0:T(128)S(1)}, s32[128]{0:T(128)}, u32[]{:S(2)}) copy-start(s32[128]{0:T(128)} %copy-done.28) | copy-start | bytes 1540
  183.7 14.8 %copy-start.11 = (bf16[1536,384]{1,0:T(8,128)(2,1)S(1)}, bf16[1536,384]{1,0:T(8,128)(2,1)}, u32[]{:S(2)}) copy-start(bf16[1536,384]{1,0:T(8,128)(2,1)} %get-tuple-element.158) | copy-start | bytes 3538948
  183.8 10.0 %collective-permute-start.28 = (f32[128,128]{1,0:T(8,128)}, f32[128,128]{1,0:T(8,128)S(1)}, u32[]{:S(2)}, u32[]{:S(2)}) collective-permute-start(f32[128,128]{1,0:T(8,128)} %get-tuple-element.154), channel_id=1, source_target_pairs={{0,1},{1,0},{2,3},{3,2},{4,5},{5,4},{6,7},{7,6},{8,9},{9,8},{10,11... | collective-permute-start | bytes 196616 | tf_op jit(solution)/shard_map/ppermute | solution.py:282
  190.9 19.9 %copy-start.14 = (f32[8,96,384]{2,1,0:T(8,128)S(1)}, f32[8,96,384]{2,1,0:T(8,128)}, u32[]{:S(2)}) copy-start(f32[8,96,384]{2,1,0:T(8,128)} %get-tuple-element.139) | copy-start | bytes 3538948
  190.9 12.2 %collective-permute-start.26 = (bf16[8,96,128]{2,1,0:T(8,128)(2,1)}, bf16[8,96,128]{2,1,0:T(8,128)(2,1)S(1)}, u32[]{:S(2)}, u32[]{:S(2)}) collective-permute-start(bf16[8,96,128]{2,1,0:T(8,128)(2,1)} %get-tuple-element.144), channel_id=1, source_target_pairs={{0,8},{1,9},{2,10},{3,11},{4,12},{5,13},{6,14},{7,15},{8,0},{9,1},... | collective-permute-start | bytes 589832 | tf_op jit(solution)/shard_map/ppermute | solution.py:282
  193.2 11.0 %collective-permute-start.25 = (bf16[8,96,256]{2,1,0:T(8,128)(2,1)}, bf16[8,96,256]{2,1,0:T(8,128)(2,1)S(1)}, u32[]{:S(2)}, u32[]{:S(2)}) collective-permute-start(bf16[8,96,256]{2,1,0:T(8,128)(2,1)} %get-tuple-element.142), channel_id=1, source_target_pairs={{0,16},{16,0},{1,17},{17,1},{2,18},{18,2},{3,19},{19,3},{4,20},{20... | collective-permute-start | bytes 1179656 | tf_op jit(solution)/shard_map/ppermute | solution.py:280
  193.8 4.7 %collective-permute-start.29 = (f32[128,128]{1,0:T(8,128)S(1)}, f32[128,128]{1,0:T(8,128)S(1)}, u32[]{:S(2)}, u32[]{:S(2)}) collective-permute-start(f32[128,128]{1,0:T(8,128)S(1)} %add.212), channel_id=1, source_target_pairs={{0,2},{1,3},{2,0},{3,1},{4,6},{5,7},{6,4},{7,5},{8,10},{9,11},{10,... | collective-permute-start | bytes 196616 | tf_op jit(solution)/shard_map/ppermute | solution.py:282
  195.3 15.4 %collective-permute-start.24 = (bf16[8,96,384]{2,1,0:T(8,128)(2,1)}, bf16[8,96,384]{2,1,0:T(8,128)(2,1)S(1)}, u32[]{:S(2)}, u32[]{:S(2)}) collective-permute-start(bf16[8,96,384]{2,1,0:T(8,128)(2,1)} %get-tuple-element.140), channel_id=1, source_target_pairs={{0,2},{1,3},{2,0},{3,1},{4,6},{5,7},{6,4},{7,5},{8,10},{9,11},{10,... | collective-permute-start | bytes 1769480 | tf_op jit(solution)/shard_map/ppermute | solution.py:282
  198.5 26.1 %collective-permute-start.33 = (bf16[1536,384]{1,0:T(8,128)(2,1)S(1)}, bf16[1536,384]{1,0:T(8,128)(2,1)S(1)}, u32[]{:S(2)}, u32[]{:S(2)}) collective-permute-start(bf16[1536,384]{1,0:T(8,128)(2,1)S(1)} %copy-done.11), channel_id=1, source_target_pairs={{1,16},{3,18},{5,20},{7,22},{9,24},{11,26},{13,28},{15,30},{16,1},... | collective-permute-start | bytes 3538952 | tf_op jit(solution)/shard_map/ppermute | solution.py:817
  205.4 9.9 %copy-start = (f32[384,1536]{1,0:T(8,128)S(1)}, f32[384,1536]{1,0:T(8,128)}, u32[]{:S(2)}) copy-start(f32[384,1536]{1,0:T(8,128)} %get-tuple-element.171) | copy-start | bytes 7077892
  210.9 10.1 %collective-permute-start.34 = (f32[128,128]{1,0:T(8,128)S(1)}, f32[128,128]{1,0:T(8,128)S(1)}, u32[]{:S(2)}, u32[]{:S(2)}) collective-permute-start(f32[128,128]{1,0:T(8,128)S(1)} %add.213), channel_id=1, source_target_pairs={{0,16},{16,0},{1,17},{17,1},{2,18},{18,2},{3,19},{19,3},{4,20},{20... | collective-permute-start | bytes 196616 | tf_op jit(solution)/shard_map/ppermute | solution.py:280
  212.3 8.6 %collective-permute-start.32 = (bf16[2,1,1,2,1,96,128]{6,5,4,3,2,1,0:T(8,128)(2,1)S(1)}, bf16[2,1,1,2,1,96,128]{6,5,4,3,2,1,0:T(8,128)(2,1)S(1)}, u32[]{:S(2)}, u32[]{:S(2)}) collective-permute-start(bf16[2,1,1,2,1,96,128]{6,5,4,3,2,1,0:T(8,128)(2,1)S(1)} %dynamic-slice_convert_fusion.4), channel_id=1, source_target_pairs={{0,4},{1,5},{2,6},{3,7},{4,0},{5,1},{6,2},{7,3},{8,12},{9,13},{10,... | collective-permute-start | bytes 294920 | tf_op jit(solution)/shard_map/ppermute | solution.py:282
  213.9 10.4 %collective-permute-start.31 = (bf16[1,1,2,2,1,96,256]{6,5,4,3,2,1,0:T(8,128)(2,1)S(1)}, bf16[1,1,2,2,1,96,256]{6,5,4,3,2,1,0:T(8,128)(2,1)S(1)}, u32[]{:S(2)}, u32[]{:S(2)}) collective-permute-start(bf16[1,1,2,2,1,96,256]{6,5,4,3,2,1,0:T(8,128)(2,1)S(1)} %dynamic-slice_convert_fusion.1), channel_id=1, source_target_pairs={{0,8},{1,9},{2,10},{3,11},{4,12},{5,13},{6,14},{7,15},{8,0},{9,1},... | collective-permute-start | bytes 589832 | tf_op jit(solution)/shard_map/ppermute | solution.py:282
  214.6 10.0 %collective-permute-start.30 = (bf16[1,2,2,1,1,96,384]{6,5,4,3,2,1,0:T(8,128)(2,1)S(1)}, bf16[1,2,2,1,1,96,384]{6,5,4,3,2,1,0:T(8,128)(2,1)S(1)}, u32[]{:S(2)}, u32[]{:S(2)}) collective-permute-start(bf16[1,2,2,1,1,96,384]{6,5,4,3,2,1,0:T(8,128)(2,1)S(1)} %dynamic-slice_convert_fusion), channel_id=1, source_target_pairs={{0,16},{16,0},{1,17},{17,1},{2,18},{18,2},{3,19},{19,3},{4,20},{20... | collective-permute-start | bytes 884744 | tf_op jit(solution)/shard_map/ppermute | solution.py:280
  224.6 10.4 %collective-permute-start.37 = (bf16[2,1,1,1,1,96,128]{6,5,4,3,2,1,0:T(8,128)(2,1)S(1)}, bf16[2,1,1,1,1,96,128]{6,5,4,3,2,1,0:T(8,128)(2,1)S(1)}, u32[]{:S(2)}, u32[]{:S(2)}) collective-permute-start(bf16[2,1,1,1,1,96,128]{6,5,4,3,2,1,0:T(8,128)(2,1)S(1)} %dynamic-slice_convert_fusion.7), channel_id=1, source_target_pairs={{0,2},{1,3},{2,0},{3,1},{4,6},{5,7},{6,4},{7,5},{8,10},{9,11},{10,... | collective-permute-start | bytes 147464 | tf_op jit(solution)/shard_map/ppermute | solution.py:282
  226.2 9.7 %collective-permute-start.38 = (f32[128,128]{1,0:T(8,128)S(1)}, f32[128,128]{1,0:T(8,128)S(1)}, u32[]{:S(2)}, u32[]{:S(2)}) collective-permute-start(f32[128,128]{1,0:T(8,128)S(1)} %add.223), channel_id=1, source_target_pairs={{0,8},{1,9},{2,10},{3,11},{4,12},{5,13},{6,14},{7,15},{8,0},{9,1},... | collective-permute-start | bytes 196616 | tf_op jit(solution)/shard_map/ppermute | solution.py:282
  227.2 8.7 %collective-permute-start.36 = (bf16[1,1,1,2,1,96,256]{6,5,4,3,2,1,0:T(8,128)(2,1)S(1)}, bf16[1,1,1,2,1,96,256]{6,5,4,3,2,1,0:T(8,128)(2,1)S(1)}, u32[]{:S(2)}, u32[]{:S(2)}) collective-permute-start(bf16[1,1,1,2,1,96,256]{6,5,4,3,2,1,0:T(8,128)(2,1)S(1)} %dynamic-slice_convert_fusion.3), channel_id=1, source_target_pairs={{0,4},{1,5},{2,6},{3,7},{4,0},{5,1},{6,2},{7,3},{8,12},{9,13},{10,... | collective-permute-start | bytes 294920 | tf_op jit(solution)/shard_map/ppermute | solution.py:282
  228.7 9.0 %collective-permute-start.35 = (bf16[1,1,2,1,1,96,384]{6,5,4,3,2,1,0:T(8,128)(2,1)S(1)}, bf16[1,1,2,1,1,96,384]{6,5,4,3,2,1,0:T(8,128)(2,1)S(1)}, u32[]{:S(2)}, u32[]{:S(2)}) collective-permute-start(bf16[1,1,2,1,1,96,384]{6,5,4,3,2,1,0:T(8,128)(2,1)S(1)} %dynamic-slice_convert_fusion.2), channel_id=1, source_target_pairs={{0,8},{1,9},{2,10},{3,11},{4,12},{5,13},{6,14},{7,15},{8,0},{9,1},... | collective-permute-start | bytes 442376 | tf_op jit(solution)/shard_map/ppermute | solution.py:282
  232.5 9.8 %copy-start.8 = (bf16[160,1536]{1,0:T(8,128)(2,1)S(1)}, bf16[160,1536]{1,0:T(8,128)(2,1)}, u32[]{:S(2)}) copy-start(bf16[160,1536]{1,0:T(8,128)(2,1)} %all_to_all.20.dn2_ref) | copy-start | bytes 1474564
  232.5 9.8 %copy-start.10 = (f32[128,768]{1,0:T(8,128)S(1)}, f32[128,768]{1,0:T(8,128)}, u32[]{:S(2)}) copy-start(f32[128,768]{1,0:T(8,128)} %get-tuple-element.107.resid_ref) | copy-start | bytes 1179652
  232.5 9.8 %copy-start.17 = (bf16[160,128]{1,0:T(8,128)(2,1)S(1)}, bf16[160,128]{1,0:T(8,128)(2,1)}, u32[]{:S(2)}) copy-start(bf16[160,128]{1,0:T(8,128)(2,1)} %fusion.13.rest_9_.dispatch_ref) | copy-start | bytes 122884
  237.7 5.5 %collective-permute-start.41 = (bf16[1,1,1,1,1,96,128]{6,5,4,3,2,1,0:T(8,128)(2,1)S(1)}, bf16[1,1,1,1,1,96,128]{6,5,4,3,2,1,0:T(8,128)(2,1)S(1)}, u32[]{:S(2)}, u32[]{:S(2)}) collective-permute-start(bf16[1,1,1,1,1,96,128]{6,5,4,3,2,1,0:T(8,128)(2,1)S(1)} %dynamic-slice_convert_fusion.8), channel_id=1, source_target_pairs={{0,16},{16,0},{1,17},{17,1},{2,18},{18,2},{3,19},{19,3},{4,20},{20... | collective-permute-start | bytes 73736 | tf_op jit(solution)/shard_map/ppermute | solution.py:280
  239.5 4.1 %collective-permute-start.40 = (bf16[1,1,1,1,1,96,256]{6,5,4,3,2,1,0:T(8,128)(2,1)S(1)}, bf16[1,1,1,1,1,96,256]{6,5,4,3,2,1,0:T(8,128)(2,1)S(1)}, u32[]{:S(2)}, u32[]{:S(2)}) collective-permute-start(bf16[1,1,1,1,1,96,256]{6,5,4,3,2,1,0:T(8,128)(2,1)S(1)} %dynamic-slice_convert_fusion.6), channel_id=1, source_target_pairs={{0,2},{1,3},{2,0},{3,1},{4,6},{5,7},{6,4},{7,5},{8,10},{9,11},{10,... | collective-permute-start | bytes 147464 | tf_op jit(solution)/shard_map/ppermute | solution.py:282
  240.2 4.3 %collective-permute-start.42 = (f32[128,128]{1,0:T(8,128)S(1)}, f32[128,128]{1,0:T(8,128)S(1)}, u32[]{:S(2)}, u32[]{:S(2)}) collective-permute-start(f32[128,128]{1,0:T(8,128)S(1)} %add.229), channel_id=1, source_target_pairs={{0,4},{1,5},{2,6},{3,7},{4,0},{5,1},{6,2},{7,3},{8,12},{9,13},{10,... | collective-permute-start | bytes 196616 | tf_op jit(solution)/shard_map/ppermute | solution.py:282
  240.3 6.1 %collective-permute-start.39 = (bf16[1,1,1,1,1,96,384]{6,5,4,3,2,1,0:T(8,128)(2,1)S(1)}, bf16[1,1,1,1,1,96,384]{6,5,4,3,2,1,0:T(8,128)(2,1)S(1)}, u32[]{:S(2)}, u32[]{:S(2)}) collective-permute-start(bf16[1,1,1,1,1,96,384]{6,5,4,3,2,1,0:T(8,128)(2,1)S(1)} %dynamic-slice_convert_fusion.5), channel_id=1, source_target_pairs={{0,4},{1,5},{2,6},{3,7},{4,0},{5,1},{6,2},{7,3},{8,12},{9,13},{10,... | collective-permute-start | bytes 221192 | tf_op jit(solution)/shard_map/ppermute | solution.py:282
  (13 other events, 52.6 us)

commit v3 on v2

--- a/solution.py
+++ b/solution.py
@@ -288,17 +288,18 @@
     return (lax.axis_index("expert") // bit) % 2
 
 
-ORDERS = ((8, 4, "y", 2), (2, 8, 4, "y"), ("y", 2, 8, 4))
+ORDERS = ((8, "y", 4, 2), (2, "y", 8, 4), ("y", 2, 8, 4))
 RS_ORDERS = ((2, "y", 8, 4), ("y", 8, 4, 2), (8, 4, 2, "y"))
 PLACE = {"y": 0, 8: 1, 4: 2, 2: 3, 1: 4}
 
 
-def gather_rows(shard, soon, later, prepare, waiting):
+def gather_rows(shard, prepare, waiting):
     rows, width = shard.shape
-    third = width // 3
-    pieces = [
-        shard[:, i * third : (i + 1) * third].reshape(1, 1, 1, 1, rows, third) for i in range(3)
-    ]
+    pieces, begin = [], 0
+    for size in (width // 2, width // 6, width // 3):
+        piece = shard[:, begin : begin + size]
+        pieces.append(piece.reshape(1, 1, 1, 1, rows, size))
+        begin += size
 
     def grow(piece, bit):
         got = flip(piece, bit)
@@ -308,15 +309,13 @@
         )
 
     for step in range(4):
-        if step == 1:
+        if step == 2:
             pieces, waiting = lax.optimization_barrier((pieces, waiting))
             ready = prepare(*waiting)
-        if step == 2:
-            pieces, soon = lax.optimization_barrier((pieces, soon))
         pieces = [grow(piece, ORDERS[i][step]) for i, piece in enumerate(pieces)]
-    pieces, later, ready = lax.optimization_barrier((pieces, later, ready))
-    pieces = [piece.reshape(-1, rows, third) for piece in pieces]
-    return pieces + [flip(piece, 1) for piece in pieces], soon, later, ready
+    pieces, ready = lax.optimization_barrier((pieces, ready))
+    pieces = [piece.reshape(-1, rows, piece.shape[-1]) for piece in pieces]
+    return pieces + [flip(piece, 1) for piece in pieces], ready
 
 
 def reduce_step(total, bit):
@@ -373,18 +372,33 @@
     )(*operands)
 
 
-def bias_kernel(table_ref, buckets_ref, square_ref):
+def prepare_kernel(
+    places, capacity, table_ref, buckets_ref, routes_ref, slots_ref,
+    square_ref, tiled_ref, dispatch_ref, padded_ref,
+):
     heads, count, _ = square_ref.shape
+    turned = buckets_ref[...].astype(jnp.float32).T.astype(jnp.int32)
+    wide = jnp.concatenate([turned, turned], axis=1)
+    tiled_ref[...] = wide
+    buckets = jnp.concatenate([wide, wide], axis=0)
     row = lax.broadcasted_iota(jnp.int32, (count, count), 0)
     column = lax.broadcasted_iota(jnp.int32, (count, count), 1)
     half = count // 2
     same = (row < half) == (column < half)
-    buckets = buckets_ref[...]
     for head in range(heads):
         total = jnp.where(same, 0.0, -jnp.inf)
         for bucket in range(table_ref.shape[0]):
             total = jnp.where(same & (buckets == bucket), table_ref[bucket, head], total)
         square_ref[head] = total
+    routes = jnp.concatenate([routes_ref[0], routes_ref[1]], axis=1)
+    slots = jnp.concatenate([slots_ref[0], slots_ref[1]], axis=1)
+    second = lax.broadcasted_iota(jnp.int32, (1, count), 1) >= half
+    at = slots + jnp.where(second, capacity, 0)
+    chip = (routes & 1) * 8 + (routes >> 1)
+    for ref, size in ((dispatch_ref, places), (padded_ref, 16)):
+        flat = jnp.where(slots < capacity, chip * size + at, -1)
+        rows = lax.broadcasted_iota(jnp.int32, ref.shape, 0)
+        ref[...] = jnp.where(rows == flat, 1.0, 0.0).astype(jnp.bfloat16)
 
 
 def attend_kernel(
@@ -397,12 +411,15 @@
         mixed_t, wt_ref, come, go_qkv, go_o,
     ) = rest
     core = place_ref[0]
-    pairs, block, third = pieces[0].shape
+    pairs = pieces[0].shape[0]
     for side, part in ((core, pieces[:3]), (1 - core, pieces[3:])):
-        for index in range(3):
+        begin = 0
+        for piece in part:
+            size = piece.shape[2]
             pltpu.make_async_copy(
-                part[index], wt_ref.at[:, side, :, pl.ds(index * third, third)], come
+                piece, wt_ref.at[:, side, :, pl.ds(begin, size)], come
             ).start()
+            begin += size
     heads = probs_ref.shape[0]
     width = x_ref.shape[1]
     size = width // heads
@@ -432,10 +449,11 @@
     )
     resid_ref[...] = resid
     n2b_ref[...] = (resid * rms_scale(resid) * gain_two_ref[...]).astype(jnp.bfloat16)
-    rows = dot(dispatch_ref[...], n2b_ref[...], ((1,), (0,)))
-    rows_ref[:, :width] = rows.astype(jnp.bfloat16)
-    dy_rows = dot(dispatch_ref[...], dy_ref[...], ((1,), (0,)))
-    rows_ref[:, width:] = dy_rows.astype(jnp.bfloat16)
+    chips, places, _ = rows_ref.shape
+    rows = dot(dispatch_ref[...], n2b_ref[...], ((1,), (0,))).reshape(chips, -1, width)
+    rows_ref[:, :, :width] = rows[:, :places].astype(jnp.bfloat16)
+    dy_rows = dot(dispatch_ref[...], dy_ref[...], ((1,), (0,))).reshape(chips, -1, width)
+    rows_ref[:, :, width:] = dy_rows[:, :places].astype(jnp.bfloat16)
     leave_qkv.wait()
     leave_o.wait()
 
@@ -622,8 +640,21 @@
     place_ref, mine_ref, got_ref, own_ref, probs_ref, router_ref, back_ref, router_part_ref
 ):
     width = own_ref.shape[1] // 2
+    chips, places, _ = back_ref.shape
     made = (mine_ref[0] + got_ref[0]).astype(jnp.bfloat16)
-    back_ref[:, width:] = made
+    row = lax.broadcasted_iota(jnp.int32, (chips * 16, made.shape[0]), 0)
+    column = lax.broadcasted_iota(jnp.int32, row.shape, 1)
+    spread = jnp.zeros(row.shape, jnp.float32)
+    for chip in range(chips):
+        inside = (row >= chip * 16) & (row < chip * 16 + places)
+        spread = jnp.where(inside & (column == row - chip * (16 - places)), 1.0, spread)
+    spread = spread.astype(jnp.bfloat16)
+
+    def padded(values):
+        wide = dot(spread, values, ((1,), (0,))).reshape(chips, 16, width)
+        return wide[:, :places].astype(jnp.bfloat16)
+
+    back_ref[:, :, width:] = padded(made)
     drows = (mine_ref[1] + got_ref[1]).astype(jnp.bfloat16).astype(jnp.float32)
     probs = probs_ref[...]
     chosen = (lax.broadcasted_iota(jnp.int32, probs.shape, 1) == place_ref[1]).astype(jnp.float32)
@@ -638,7 +669,7 @@
         dlogits, own_ref[:, :width].astype(jnp.float32), ((0,), (0,)), precision=HIGH
     )
     dn2 = drows + dot(dlogits, router_ref[...].astype(jnp.float32), ((1,), (1,)), precision=HIGH)
-    back_ref[:, :width] = dn2.astype(jnp.bfloat16)
+    back_ref[:, :, :width] = padded(dn2.astype(jnp.bfloat16))
 
 
 def paired_body(
@@ -694,11 +725,7 @@
             tensor, BOTH, split_axis=0, concat_axis=0, tiled=True, axis_index_groups=groups
         )
 
-    route_ids, slot_ids = routes[:, 0], slots[:, 0]
-    chip = (route_ids % 2) * (experts // 2) + route_ids // 2
-    flat = chip * places + jnp.arange(micro)[:, None] * capacity + slot_ids
-    flat = jnp.where(slot_ids < capacity, flat, -1).reshape(1, count)
-    dispatch = (flat == jnp.arange(experts * places)[:, None]).astype(bf16)
+    row_count = experts * places
     upstream_b = cotangent.reshape(count, width)
     def parts_of(local, axis):
         near = lax.dynamic_slice_in_dim(local, dp_at * hidden_half, hidden_half, axis)
@@ -706,8 +733,6 @@
         return near, far
 
     in_near, in_far = parts_of(expert_in[0], 1)
-    in_arrived = lax.ppermute(in_near, BOTH, across)
-
     def halves(tensor):
         return (
             lax.dynamic_slice_in_dim(tensor, core * width_half, width_half, 1),
@@ -720,26 +745,35 @@
             [jnp.where(low, keep, got), jnp.where(low, got, keep)], axis=axis
         )
 
-    def prepare(table, ids, out_local):
-        tiled = jnp.tile(ids.T, (micro, micro))
-        (square,) = call(bias_kernel, 10, (((heads, count, count), f32),), [], table, tiled)
-        return (square, tiled, in_far) + parts_of(out_local, 0)
-
-    pieces, in_arrived, dispatch, ready = gather_rows(
+    def prepare(table, ids, route_ids, slot_ids, near, far, out_local):
+        made = call(
+            functools.partial(prepare_kernel, places, capacity),
+            16,
+            (
+                ((heads, count, count), f32),
+                ((seq_len, count), jnp.int32),
+                ((row_count, count), bf16),
+                ((experts * 16, count), bf16),
+            ),
+            [],
+            table, ids, route_ids, slot_ids,
+        )
+        in_arrived = lax.ppermute(near, BOTH, across)
+        in_far = lax.ppermute(far, BOTH, outward)
+        return tuple(made) + (in_arrived, in_far) + parts_of(out_local, 0)
+
+    pieces, ready = gather_rows(
         attn_weight.T,
-        in_arrived,
-        dispatch,
         prepare,
-        (bias_table.astype(f32), buckets, expert_out[0]),
-    )
-    square, tiled, in_far, out_near, out_far = ready
+        (bias_table.astype(f32), buckets, routes, slots, in_near, in_far, expert_out[0]),
+    )
+    square, tiled, dispatch, padded, in_arrived, in_far, out_near, out_far = ready
     out_arrived = lax.ppermute(out_near, BOTH, across)
     place = jnp.stack(
         [core, host, home.astype(jnp.int32)] + [own_bit(order[0]) for order in RS_ORDERS]
     ).astype(jnp.int32)
     gain_one, gain_two = gain_one[None], gain_two[None]
     local = tokens.reshape(count, width)
-    row_count = dispatch.shape[0]
     wt_qkv, wt_o, n1b, qkv, probs, mixed_b, resid, n2b, outgoing = call(
         attend_kernel,
         26,
@@ -752,7 +786,7 @@
             ((count, width), bf16),
             ((count, width), f32),
             ((count, width), bf16),
-            ((row_count, 2 * width), bf16),
+            ((experts, places, 2 * width), bf16),
         ),
         [
             pltpu.VMEM((width, count), f32),
@@ -761,15 +795,13 @@
             pltpu.SemaphoreType.DMA,
             pltpu.SemaphoreType.DMA,
         ],
-        place, local, *pieces, gain_one, gain_two, square, dispatch, upstream_b,
+        place, local, *pieces, gain_one, gain_two, square, padded, upstream_b,
         plain_in=range(2, 8),
         plain_out=(0, 1),
     )
     wt_qkv, wt_o = wt_qkv.reshape(3 * width, width), wt_o.reshape(width, width)
-    outgoing, out_arrived, in_far, out_far = lax.optimization_barrier(
-        (outgoing, out_arrived, lax.ppermute(in_far, BOTH, outward), out_far)
-    )
-    own_rows = to_chips(outgoing)
+    outgoing, out_arrived, out_far = lax.optimization_barrier((outgoing, out_arrived, out_far))
+    own_rows = to_chips(outgoing).reshape(row_count, 2 * width)
     in_parts = (in_near, in_arrived, in_far)
     out_parts = (out_near, out_arrived, lax.ppermute(out_far, BOTH, outward))
     rows, hidden, du, dmade, mine, theirs, row_probs = call(
@@ -791,7 +823,7 @@
         settle_kernel,
         10,
         (
-            ((row_count, 2 * width), bf16),
+            ((experts, places, 2 * width), bf16),
             ((experts, width), f32),
         ),
         [],
@@ -801,7 +833,7 @@
     back_rows, rows, hidden, du, dmade = lax.optimization_barrier(
         (back_rows, rows, hidden, du, dmade)
     )
-    home_rows = to_chips(back_rows)
+    home_rows = to_chips(back_rows).reshape(row_count, 2 * width)
     rows_keep, _ = halves(rows)
     dmade_keep, dmade_got = halves(dmade)
 
@@ -861,10 +893,13 @@
             (),
             (in_arrived, in_mine, in_homely),
             (out_arrived, out_mine, out_homely),
-            home_rows,
+            (home_rows, routes),
         ),
     )
-    _, (in_arrived, in_mine, in_homely), (out_arrived, out_mine, out_homely), home_rows = late
+    _, in_late, out_late, (home_rows, routes) = late
+    route_ids = routes[:, 0]
+    in_arrived, in_mine, in_homely = in_late
+    out_arrived, out_mine, out_homely = out_late
     in_back = (in_mine, in_homely, in_arrived)
     out_back = (out_mine, out_homely, out_arrived)
 

time: 248 us -> 232 us (0.935)
  other arithmetic: 20.8 us -> 15.3 us
  starting transfers between devices: 64.5 us -> 60.9 us
  local copies, waits for them, and re-layouts: 21.5 us -> 18 us
  waiting for transfers between devices: 81.4 us -> 78.1 us
    all_to_all x2, starting transfers between devices: 18.9 us -> 10.2 us  [to_chips(): lax.all_to_all(tensor, BOTH, split_axis=0, concat_axis=0, tiled=True, axi...]
    ppermute x28, waiting for transfers between devices: 41.9 us -> 33.6 us  [flip(): return lax.ppermute(tensor, 'expert', [(i, i ^ bit) for i in range(count)])]
    ppermute x28, starting transfers between devices: 30.5 us -> 35 us  [flip(): return lax.ppermute(tensor, 'expert', [(i, i ^ bit) for i in range(count)])]
    all_to_all x4 -> x0, local copies, waits for them, and re-layouts: 4.32 us -> none  [to_chips(): lax.all_to_all(tensor, BOTH, split_axis=0, concat_axis=0, tiled=True, axi...]
    another operation x2 -> x0, local copies, waits for them, and re-layouts: 3.1 us -> none  [prepare(): tiled = jnp.tile(ids.T, (micro, micro))]
    select_n x10 -> x12, other arithmetic: 3.26 us -> 0.45 us  [grow(): jnp.where(low, piece, got)]
    unnamed x68 -> x61, local copies, waits for them, and re-layouts: 3.97 us -> 5.43 us
  transfers between devices with their start and end apart: 45 -> 45, of which waited for: 22 -> 19; matrix products, arithmetic and copies ran while one was open for 19% -> 17% of each run, Pallas kernels for 11% -> 12%
where the time goes in v3:
time: 232 us; the launch traced here: 231 us
  waiting for transfers between devices  78.1 us (34%)
  starting transfers between devices  60.9 us (26%)
  Pallas kernels  45.1 us (19%)
  local copies, waits for them, and re-layouts  18 us (8%)
  other arithmetic  15.3 us (7%)
  matrix products  12.3 us (5%)
    pallas_call x7, Pallas kernels, call(): pl.pallas_call(kernel, grid=(1,), out_shape=tuple((pltpu.HBM(*out) for ou...  45.1 us
    all_to_all x2, waiting for transfers between devices, to_chips(): lax.all_to_all(tensor, BOTH, split_axis=0, concat_axis=0, tiled=True, axi...  36.9 us
    ppermute x28, starting transfers between devices, flip(): return lax.ppermute(tensor, 'expert', [(i, i ^ bit) for i in range(count)])  35 us
    ppermute x28, waiting for transfers between devices, flip(): return lax.ppermute(tensor, 'expert', [(i, i ^ bit) for i in range(count)])  33.6 us
    dot_general x6, matrix products, dot(): lax.dot_general(left, right, (dims, ((), ())), preferred_element_type=jnp...  12.3 us
    all_to_all x2, starting transfers between devices, to_chips(): lax.all_to_all(tensor, BOTH, split_axis=0, concat_axis=0, tiled=True, axi...  10.2 us
    ppermute x7, starting transfers between devices, flip(): return lax.ppermute(tensor, 'dp', [(0, 1), (1, 0)])  7.8 us
    dynamic_slice x2, local copies, waits for them, and re-layouts, parts_of(): lax.dynamic_slice_in_dim(local, (1 - dp_at) * hidden_half, hidden_half, a...  5.79 us
  transfers between devices with their start and end apart: 45, of which 19 were waited for; matrix products, arithmetic and copies ran while one was open for 17% of the time, Pallas kernels for 12%

profile of v3, /device:TPU:0, one launch (start us, length us, event | category | flops | bytes accessed | tf_op | source)
XLA Modules:
  0.0 231.0 jit_solution(9515632014404162021)
XLA Ops:
  1.4 2.9 %collective-permute-start.2 = (bf16[1,1,1,1,96,128]{5,4,3,2,1,0:T(8,128)(2,1)S(1)}, bf16[1,1,1,1,96,128]{5,4,3,2,1,0:T(8,128)(2,1)S(1)}, u32[]{:S(2)}, u32[]{:S(2)}) collective-permute-start(bf16[1,1,1,1,96,128]{5,4,3,2,1,0:T(8,128)(2,1)S(1)} %slice_bitcast_fusion.2), channel_id=1, source_target_pairs={{0,2},{1,3},{2,0},{3,1},{4,6},{5,7},{6,4},{7,5},{8,10},{9,11},{10,... | collective-permute-start | bytes 73736 | tf_op jit(solution)/shard_map/ppermute | solution.py:282
  5.1 1.5 collective-permute-start.4
  7.5 2.6 %collective-permute-start = (bf16[1,1,1,1,96,384]{5,4,3,2,1,0:T(8,128)(2,1)S(1)}, bf16[1,1,1,1,96,384]{5,4,3,2,1,0:T(8,128)(2,1)S(1)}, u32[]{:S(2)}, u32[]{:S(2)}) collective-permute-start(bf16[1,1,1,1,96,384]{5,4,3,2,1,0:T(8,128)(2,1)S(1)} %slice_bitcast_fusion), channel_id=1, source_target_pairs={{0,8},{1,9},{2,10},{3,11},{4,12},{5,13},{6,14},{7,15},{8,0},{9,1},... | collective-permute-start | bytes 221192 | tf_op jit(solution)/shard_map/ppermute | solution.py:282
  10.1 2.8 %dynamic-slice_bitcast_fusion = (bf16[384,1536]{1,0:T(8,128)(2,1)}, bf16[384,1536]{1,0:T(8,128)(2,1)S(1)}) fusion(bf16[1,384,3072]{2,1,0:T(8,128)(2,1)} %param.18, s32[]{:T(128)S(6)} %select_n.349, s32[]{:T(128)S(6)} %select_n.348), kind=kLoop, calls=%fused_computation.16 | loop fusion | bytes 4718600 | tf_op jit(solution)/shard_map/dynamic_slice | solution.py:732
  14.4 1.6 collective-permute-start.1
  16.0 1.6 collective-permute-done.3
  18.5 1.1 collective-permute-done.1
  19.7 1.2 collective-permute-start.8
  20.9 1.8 collective-permute-start.10
  22.7 1.6 collective-permute-start.6
  25.0 2.8 %collective-permute-start.13 = (bf16[384,1536]{1,0:T(8,128)(2,1)}, bf16[384,1536]{1,0:T(8,128)(2,1)S(1)}, u32[]{:S(2)}, u32[]{:S(2)}) collective-permute-start(bf16[384,1536]{1,0:T(8,128)(2,1)} %get-tuple-element.111), channel_id=1, source_target_pairs={{0,1},{1,17},{2,3},{3,19},{4,5},{5,21},{6,7},{7,23},{8,9},{9,25},{... | collective-permute-start | bytes 3538952 | tf_op jit(solution)/shard_map/ppermute | solution.py:762
  27.8 3.0 %constant_dynamic-slice_fusion = (bf16[1536,384]{1,0:T(8,128)(2,1)}, bf16[1536,384]{1,0:T(8,128)(2,1)S(1)}) fusion(bf16[3072,384]{1,0:T(8,128)(2,1)} %bitcast.88, s32[]{:T(128)S(6)} %select_n.349, s32[]{:T(128)S(6)} %select_n.348), kind=kLoop, calls=%fused_computation.95 | loop fusion | bytes 4718600 | tf_op jit(solution)/shard_map/dynamic_slice | solution.py:732
  30.8 3.7 %shard_map.187 = (f32[12,128,128]{2,1,0:T(8,128)}, s32[64,128]{1,0:T(8,128)}, bf16[160,128]{1,0:T(8,128)(2,1)}, bf16[256,128]{1,0:T(8,128)(2,1)}) custom-call(f32[32,12]{1,0:T(8,128)S(1)} %convert_element_type.99.table_ref, s32[64,64]{1,0:T(8,128)} %buckets_ref, s32[2,1,64]{2,1,0:T(1,128)} %routes_ref, s32[2,1,64]{2,1,0:T(1,128)} %slots_ref), custom_call_target="tpu_custom_call" | custom-call | tf_op jit(solution)/shard_map/pallas_call | solution.py:363
  35.2 1.6 collective-permute-start.11
  37.0 1.6 collective-permute-start.7
  38.5 3.9 %collective-permute-done.9 = bf16[2,2,1,2,96,128]{5,4,3,2,1,0:T(8,128)(2,1)S(1)} collective-permute-done((bf16[2,2,1,2,96,128]{5,4,3,2,1,0:T(8,128)(2,1)S(1)}, bf16[2,2,1,2,96,128]{5,4,3,2,1,0:T(8,128)(2,1)S(1)}, u32[]{:S(2)}, u32[]{:S(2)}) %collective-permute-start.9) | collective-permute-done | bytes 196640 | tf_op jit(solution)/shard_map/ppermute | solution.py:282
  43.2 6.7 %collective-permute-done.11 = bf16[2,2,1,2,96,256]{5,4,3,2,1,0:T(8,128)(2,1)S(1)} collective-permute-done((bf16[2,2,1,2,96,256]{5,4,3,2,1,0:T(8,128)(2,1)S(1)}, bf16[2,2,1,2,96,256]{5,4,3,2,1,0:T(8,128)(2,1)S(1)}, u32[]{:S(2)}, u32[]{:S(2)}) %collective-permute-start.11) | collective-permute-done | bytes 393248 | tf_op jit(solution)/shard_map/ppermute | solution.py:282
  49.9 1.0 pad_maximum_fusion.1
  52.0 2.4 %collective-permute-done.13.in_far_ref = bf16[384,1536]{1,0:T(8,128)(2,1)S(1)} collective-permute-done((bf16[384,1536]{1,0:T(8,128)(2,1)}, bf16[384,1536]{1,0:T(8,128)(2,1)S(1)}, u32[]{:S(2)}, u32[]{:S(2)}) %collective-permute-start.13) | collective-permute-done | bytes 1179680 | tf_op jit(solution)/shard_map/ppermute | solution.py:762
  54.5 1.7 collective-permute-start.17
  56.2 1.6 collective-permute-start.16
  59.2 1.5 collective-permute-done.15.rest_4_
  60.7 1.0 copy-done.9
  61.7 10.6 %shard_map.188 = (bf16[12,2,96,768]{3,2,1,0:T(8,128)(2,1)}, bf16[4,2,96,768]{3,2,1,0:T(8,128)(2,1)}, bf16[128,768]{1,0:T(8,128)(2,1)}, bf16[2304,128]{1,0:T(8,12...) custom-call(s32[6]{0:T(128)S(1)} %stack.31.place_ref.core_ref._, ...), custom_call_target="tpu_custom_call" | custom-call | tf_op jit(solution)/shard_map/pallas_call | solution.py:363
  72.4 3.6 %all-to-all-start = ((bf16[16,10,1536]{2,1,0:T(8,128)(2,1)}), bf16[16,10,1536]{2,1,0:T(8,128)(2,1)S(1)}, u32[]{:S(2)}, u32[]{:S(2)}) async-start(bf16[16,10,1536]{2,1,0:T(8,128)(2,1)} %get-tuple-element.122), calls=%async_computation | async-start | bytes 1572864 | tf_op jit(solution)/shard_map/all_to_all | solution.py:724
  76.4 21.2 %all-to-all-done = bf16[16,10,1536]{2,1,0:T(8,128)(2,1)S(1)} async-done(((bf16[16,10,1536]{2,1,0:T(8,128)(2,1)}), bf16[16,10,1536]{2,1,0:T(8,128)(2,1)S(1)}, u32[]{:S(2)}, u32[]{:S(2)}) %all-to-all-start) | async-done | bytes 491552 | tf_op jit(solution)/shard_map/all_to_all | solution.py:724
  98.7 1.5 collective-permute-done.19.out_far_ref
  100.2 1.0 copy-done.13
  101.9 9.6 %shard_map.189 = (bf16[320,768]{1,0:T(8,128)(2,1)}, bf16[320,1536]{1,0:T(8,128)(2,1)}, bf16[320,1536]{1,0:T(8,128)(2,1)}, bf16[320,768]{1,0:T(8,128)(2,1)}, f32[...) custom-call(s32[6]{0:T(128)S(1)} %stack.31.place_ref.core_ref._, bf16[160,1536]{1,0:T(8,128)(2,1)} %copy-done.4, ...), custom_call_target="tpu_custom_call" | custom-call | tf_op jit(solution)/shard_map/pallas_call | solution.py:363
  111.5 3.2 %convolution_convert_fusion.1 = bf16[384,1536]{1,0:T(8,128)(2,1)} fusion(bf16[320,1536]{1,0:T(8,128)(2,1)} %get-tuple-element.139, bf16[320,768]{1,0:T(8,128)(2,1)} %get-tuple-element.138, s32[]{:T(128)S(6)} %select_n.366), kind=kOutput, calls=%fused_computation.7 | convolution fusion | flops 378077184 | bytes 2408452 | tf_op jit(solution)/shard_map/dot_general | solution.py:348
  115.3 1.0 copy-done.15
  116.3 3.8 %shard_map.190 = (bf16[16,10,1536]{2,1,0:T(8,128)(2,1)}, f32[16,768]{1,0:T(8,128)}) custom-call(s32[6]{0:T(128)S(1)} %stack.31.place_ref.core_ref._, f32[2,160,768]{2,1,0:T(8,128)} %get-tuple-element.127.mine_ref, f32[2,160,768]{2,1,0:T(8,128)} %copy-done.15, bf16[160,1536]{1,0:T(8,128)(2,1)} %copy-done.4, f32[160,16]{1,0:T(8,128)} %get-tuple-element.129.probs_ref, ...), custom_call_target="tpu_custom_call" | custom-call | tf_op jit(solution)/shard_map/pallas_call | solution.py:363
  120.1 2.0 convolution_convert_fusion
  122.1 6.6 %all-to-all-start.1 = ((bf16[16,10,1536]{2,1,0:T(8,128)(2,1)}), bf16[16,10,1536]{2,1,0:T(8,128)(2,1)S(1)}, u32[]{:S(2)}, u32[]{:S(2)}) async-start(bf16[16,10,1536]{2,1,0:T(8,128)(2,1)} %get-tuple-element.135), calls=%async_computation.1 | async-start | bytes 1572864 | tf_op jit(solution)/shard_map/all_to_all | solution.py:724
  128.7 3.3 %fusion.19 = (bf16[1536,384]{1,0:T(8,128)(2,1)}, f32[1536,384]{1,0:T(8,128)S(1)}) fusion(bf16[320,1536]{1,0:T(8,128)(2,1)} %get-tuple-element.136, bf16[320,768]{1,0:T(8,128)(2,1)} %get-tuple-element.137, s32[]{:T(128)S(6)} %select_n.367), kind=kOutput, calls=%fused_computation.100 | convolution fusion | flops 378077184 | bytes 4767748 | tf_op jit(solution)/shard_map/dot_general | solution.py:348
  132.1 2.7 %fusion.18 = (bf16[384,1536]{1,0:T(8,128)(2,1)}, f32[384,1536]{1,0:T(8,128)}) fusion(bf16[320,1536]{1,0:T(8,128)(2,1)S(1)} %copy-done.5, bf16[320,768]{1,0:T(8,128)(2,1)S(1)} %copy-done.18, s32[]{:T(128)S(6)} %select_n.367), kind=kOutput, calls=%fused_computation.99 | convolution fusion | flops 378077184 | bytes 4767748 | tf_op jit(solution)/shard_map/dot_general | solution.py:348
  134.7 15.7 %all-to-all-done.1 = bf16[16,10,1536]{2,1,0:T(8,128)(2,1)S(1)} async-done(((bf16[16,10,1536]{2,1,0:T(8,128)(2,1)}), bf16[16,10,1536]{2,1,0:T(8,128)(2,1)S(1)}, u32[]{:S(2)}, u32[]{:S(2)}) %all-to-all-start.1) | async-done | bytes 491552 | tf_op jit(solution)/shard_map/all_to_all | solution.py:724
  150.4 0.9 reshape.99.dn2_ref
  151.4 7.7 %shard_map.191 = (f32[128,768]{1,0:T(8,128)}, f32[1,768]{1,0:T(1,128)}, bf16[2304,128]{1,0:T(8,128)(2,1)}, f32[12,64,128]{2,1,0:T(8,128)}, bf16[1536,768]{1,0:T(8,128)(2,1)}, /*index=5*/bf16[1536,128]{1,0:T(8,128)(2,1)}) custom-call(s32[6]{0:T(128)S(1)} %stack.31.place_ref.core_ref._, bf16[160,1536]{1,0:T(8,128)(2,1)} %reshape.99.dn2_ref, ...), custom_call_target="tpu_custom_call" | custom-call | tf_op jit(solution)/shard_map/pallas_call | solution.py:363
  159.1 1.2 collective-permute-start.23
  160.3 0.9 collective-permute-start.27
  161.3 5.1 %shard_map.193 = (f32[128,768]{1,0:T(8,128)}, f32[128,128]{1,0:T(8,128)}) custom-call(s32[6]{0:T(128)S(1)} %stack.31.place_ref.core_ref._, bf16[128,768]{1,0:T(8,128)(2,1)} %bitcast.95, bf16[2304,128]{1,0:T(8,128)(2,1)} %get-tuple-element.157.dqkv_ref, bf16[2304,768]{1,0:T(8,128)(2,1)} %bitcast.85, f32[1,768]{1,0:T(1,128)} %reshape.113.rest_6_.gain_one_ref, ...), custom_call_target="tpu_custom_call" | custom-call | tf_op jit(solution)/shard_map/pallas_call | solution.py:363
  166.4 2.6 %collective-permute-start.28 = (f32[128,128]{1,0:T(8,128)}, f32[128,128]{1,0:T(8,128)S(1)}, u32[]{:S(2)}, u32[]{:S(2)}) collective-permute-start(f32[128,128]{1,0:T(8,128)} %get-tuple-element.164), channel_id=1, source_target_pairs={{0,1},{1,0},{2,3},{3,2},{4,5},{5,4},{6,7},{7,6},{8,9},{9,8},{10,11... | collective-permute-start | bytes 196616 | tf_op jit(solution)/shard_map/ppermute | solution.py:282
  168.9 4.6 %shard_map.192 = (bf16[8,96,384]{2,1,0:T(8,128)(2,1)}, bf16[8,96,256]{2,1,0:T(8,128)(2,1)}, bf16[8,96,128]{2,1,0:T(8,128)(2,1)}, f32[8,96,384]{2,1,0:T(8,128)}, ...) custom-call(s32[6]{0:T(128)S(1)} %stack.31.place_ref.core_ref._, bf16[1536,128]{1,0:T(8,128)(2,1)} %get-tuple-element.147.keep_ref, ...), custom_call_target="tpu_custom_call" | custom-call | tf_op jit(solution)/shard_map/pallas_call | solution.py:363
  173.5 2.2 collective-permute-start.26
  176.6 1.5 collective-permute-start.29
  178.7 2.8 %collective-permute-done.29 = f32[128,128]{1,0:T(8,128)S(1)} collective-permute-done((f32[128,128]{1,0:T(8,128)S(1)}, f32[128,128]{1,0:T(8,128)S(1)}, u32[]{:S(2)}, u32[]{:S(2)}) %collective-permute-start.29) | collective-permute-done | bytes 65568 | tf_op jit(solution)/shard_map/ppermute | solution.py:282
  182.2 3.5 %collective-permute-done.26 = bf16[8,96,128]{2,1,0:T(8,128)(2,1)S(1)} collective-permute-done((bf16[8,96,128]{2,1,0:T(8,128)(2,1)}, bf16[8,96,128]{2,1,0:T(8,128)(2,1)S(1)}, u32[]{:S(2)}, u32[]{:S(2)}) %collective-permute-start.26) | collective-permute-done | bytes 196640 | tf_op jit(solution)/shard_map/ppermute | solution.py:282
  185.7 1.0 convert_add_fusion.4
  186.8 1.2 convert_add_fusion.1
  188.0 5.5 %collective-permute-done.24 = bf16[8,96,384]{2,1,0:T(8,128)(2,1)S(1)} collective-permute-done((bf16[8,96,384]{2,1,0:T(8,128)(2,1)}, bf16[8,96,384]{2,1,0:T(8,128)(2,1)S(1)}, u32[]{:S(2)}, u32[]{:S(2)}) %collective-permute-start.24) | collective-permute-done | bytes 589856 | tf_op jit(solution)/shard_map/ppermute | solution.py:282
  193.7 1.3 collective-permute-start.34
  195.0 1.5 collective-permute-start.32
  198.1 1.9 fusion.1
  200.0 2.5 %maximum_bitcast_fusion = f32[1,384,3072]{2,1,0:T(8,128)} fusion(f32[384,1536]{1,0:T(8,128)S(1)} %get-tuple-element.210, f32[384,1536]{1,0:T(8,128)S(1)} %get-tuple-element.209), kind=kLoop, calls=%fused_computation | loop fusion | flops 1179648 | bytes 9437184 | tf_op jit(solution)/shard_map/broadcast_in_dim | solution.py:929
  203.5 3.6 %collective-permute-done.31 = bf16[1,1,2,2,1,96,256]{6,5,4,3,2,1,0:T(8,128)(2,1)S(1)} collective-permute-done((bf16[1,1,2,2,1,96,256]{6,5,4,3,2,1,0:T(8,128)(2,1)S(1)}, bf16[1,1,2,2,1,96,256]{6,5,4,3,2,1,0:T(8,128)(2,1)S(1)}, u32[]{:S(2)}, u32[]{:S(2)}) %collective-permute-start.31) | collective-permute-done | bytes 196640 | tf_op jit(solution)/shard_map/ppermute | solution.py:282
  207.2 1.4 collective-permute-start.37
  208.6 2.3 collective-permute-start.38
  210.9 1.5 collective-permute-start.36
  213.2 1.8 fusion.3
  215.0 2.5 %maximum_bitcast_fusion.1 = f32[1,3072,384]{2,1,0:T(8,128)} fusion(f32[1536,384]{1,0:T(8,128)S(1)} %get-tuple-element.208, f32[1536,384]{1,0:T(8,128)S(1)} %get-tuple-element.207), kind=kLoop, calls=%fused_computation.1 | loop fusion | flops 1179648 | bytes 9437184 | tf_op jit(solution)/shard_map/broadcast_in_dim | solution.py:930
  217.6 3.3 %collective-permute-done.35 = bf16[1,1,2,1,1,96,384]{6,5,4,3,2,1,0:T(8,128)(2,1)S(1)} collective-permute-done((bf16[1,1,2,1,1,96,384]{6,5,4,3,2,1,0:T(8,128)(2,1)S(1)}, bf16[1,1,2,1,1,96,384]{6,5,4,3,2,1,0:T(8,128)(2,1)S(1)}, u32[]{:S(2)}, u32[]{:S(2)}) %collective-permute-start.35) | collective-permute-done | bytes 147488 | tf_op jit(solution)/shard_map/ppermute | solution.py:282
  222.1 1.3 collective-permute-start.41
  224.1 2.0 collective-permute-start.39
  (175 shorter events, 25.0 us)
Async XLA Ops:
  1.4 11.7 %collective-permute-start.2 = (bf16[1,1,1,1,96,128]{5,4,3,2,1,0:T(8,128)(2,1)S(1)}, bf16[1,1,1,1,96,128]{5,4,3,2,1,0:T(8,128)(2,1)S(1)}, u32[]{:S(2)}, u32[]{:S(2)}) collective-permute-start(bf16[1,1,1,1,96,128]{5,4,3,2,1,0:T(8,128)(2,1)S(1)} %slice_bitcast_fusion.2), channel_id=1, source_target_pairs={{0,2},{1,3},{2,0},{3,1},{4,6},{5,7},{6,4},{7,5},{8,10},{9,11},{10,... | collective-permute-start | bytes 73736 | tf_op jit(solution)/shard_map/ppermute | solution.py:282
  5.1 8.6 %collective-permute-start.4 = (bf16[1,1,1,1,96,256]{5,4,3,2,1,0:T(8,128)(2,1)S(1)}, bf16[1,1,1,1,96,256]{5,4,3,2,1,0:T(8,128)(2,1)S(1)}, u32[]{:S(2)}, u32[]{:S(2)}) collective-permute-start(bf16[1,1,1,1,96,256]{5,4,3,2,1,0:T(8,128)(2,1)S(1)} %slice_bitcast_fusion.1), channel_id=1, source_target_pairs={{0,16},{16,0},{1,17},{17,1},{2,18},{18,2},{3,19},{19,3},{4,20},{20... | collective-permute-start | bytes 147464 | tf_op jit(solution)/shard_map/ppermute | solution.py:280
  7.5 6.8 %collective-permute-start = (bf16[1,1,1,1,96,384]{5,4,3,2,1,0:T(8,128)(2,1)S(1)}, bf16[1,1,1,1,96,384]{5,4,3,2,1,0:T(8,128)(2,1)S(1)}, u32[]{:S(2)}, u32[]{:S(2)}) collective-permute-start(bf16[1,1,1,1,96,384]{5,4,3,2,1,0:T(8,128)(2,1)S(1)} %slice_bitcast_fusion), channel_id=1, source_target_pairs={{0,8},{1,9},{2,10},{3,11},{4,12},{5,13},{6,14},{7,15},{8,0},{9,1},... | collective-permute-start | bytes 221192 | tf_op jit(solution)/shard_map/ppermute | solution.py:282
  13.0 17.8 %copy-start.2 = (bf16[384,1536]{1,0:T(8,128)(2,1)}, bf16[384,1536]{1,0:T(8,128)(2,1)S(1)}, u32[]{:S(2)}) copy-start(bf16[384,1536]{1,0:T(8,128)(2,1)S(1)} %get-tuple-element.110.in_near_ref) | copy-start | bytes 3538948
  13.1 4.5 %collective-permute-start.3 = (bf16[1,1,1,2,96,128]{5,4,3,2,1,0:T(8,128)(2,1)S(1)}, bf16[1,1,1,2,96,128]{5,4,3,2,1,0:T(8,128)(2,1)S(1)}, u32[]{:S(2)}, u32[]{:S(2)}) collective-permute-start(bf16[1,1,1,2,96,128]{5,4,3,2,1,0:T(8,128)(2,1)S(1)} %pad_maximum_fusion.11), channel_id=1, source_target_pairs={{0,16},{16,0},{1,17},{17,1},{2,18},{18,2},{3,19},{19,3},{4,20},{20... | collective-permute-start | bytes 147464 | tf_op jit(solution)/shard_map/ppermute | solution.py:280
  13.7 4.7 %collective-permute-start.5 = (bf16[2,1,1,1,96,256]{5,4,3,2,1,0:T(8,128)(2,1)S(1)}, bf16[2,1,1,1,96,256]{5,4,3,2,1,0:T(8,128)(2,1)S(1)}, u32[]{:S(2)}, u32[]{:S(2)}) collective-permute-start(bf16[2,1,1,1,96,256]{5,4,3,2,1,0:T(8,128)(2,1)S(1)} %pad_maximum_fusion.10), channel_id=1, source_target_pairs={{0,2},{1,3},{2,0},{3,1},{4,6},{5,7},{6,4},{7,5},{8,10},{9,11},{10,... | collective-permute-start | bytes 294920 | tf_op jit(solution)/shard_map/ppermute | solution.py:282
  14.4 5.2 %collective-permute-start.1 = (bf16[1,2,1,1,96,384]{5,4,3,2,1,0:T(8,128)(2,1)S(1)}, bf16[1,2,1,1,96,384]{5,4,3,2,1,0:T(8,128)(2,1)S(1)}, u32[]{:S(2)}, u32[]{:S(2)}) collective-permute-start(bf16[1,2,1,1,96,384]{5,4,3,2,1,0:T(8,128)(2,1)S(1)} %pad_maximum_fusion.8), channel_id=1, source_target_pairs={{0,16},{16,0},{1,17},{17,1},{2,18},{18,2},{3,19},{19,3},{4,20},{20... | collective-permute-start | bytes 442376 | tf_op jit(solution)/shard_map/ppermute | solution.py:280
  19.7 14.8 %collective-permute-start.8 = (bf16[2,1,1,2,96,128]{5,4,3,2,1,0:T(8,128)(2,1)S(1)}, bf16[2,1,1,2,96,128]{5,4,3,2,1,0:T(8,128)(2,1)S(1)}, u32[]{:S(2)}, u32[]{:S(2)}) collective-permute-start(bf16[2,1,1,2,96,128]{5,4,3,2,1,0:T(8,128)(2,1)S(1)} %pad_maximum_fusion.9), channel_id=1, source_target_pairs={{0,8},{1,9},{2,10},{3,11},{4,12},{5,13},{6,14},{7,15},{8,0},{9,1},... | collective-permute-start | bytes 294920 | tf_op jit(solution)/shard_map/ppermute | solution.py:282
  20.9 14.2 %collective-permute-start.10 = (bf16[2,1,1,2,96,256]{5,4,3,2,1,0:T(8,128)(2,1)S(1)}, bf16[2,1,1,2,96,256]{5,4,3,2,1,0:T(8,128)(2,1)S(1)}, u32[]{:S(2)}, u32[]{:S(2)}) collective-permute-start(bf16[2,1,1,2,96,256]{5,4,3,2,1,0:T(8,128)(2,1)S(1)} %pad_maximum_fusion.6), channel_id=1, source_target_pairs={{0,8},{1,9},{2,10},{3,11},{4,12},{5,13},{6,14},{7,15},{8,0},{9,1},... | collective-permute-start | bytes 589832 | tf_op jit(solution)/shard_map/ppermute | solution.py:282
  22.7 14.1 %collective-permute-start.6 = (bf16[2,2,1,1,96,384]{5,4,3,2,1,0:T(8,128)(2,1)S(1)}, bf16[2,2,1,1,96,384]{5,4,3,2,1,0:T(8,128)(2,1)S(1)}, u32[]{:S(2)}, u32[]{:S(2)}) collective-permute-start(bf16[2,2,1,1,96,384]{5,4,3,2,1,0:T(8,128)(2,1)S(1)} %pad_maximum_fusion.5), channel_id=1, source_target_pairs={{0,4},{1,5},{2,6},{3,7},{4,0},{5,1},{6,2},{7,3},{8,12},{9,13},{10,... | collective-permute-start | bytes 884744 | tf_op jit(solution)/shard_map/ppermute | solution.py:282
  24.2 27.8 %collective-permute-start.12 = (bf16[384,1536]{1,0:T(8,128)(2,1)S(1)}, bf16[384,1536]{1,0:T(8,128)(2,1)S(1)}, u32[]{:S(2)}, u32[]{:S(2)}) collective-permute-start(bf16[384,1536]{1,0:T(8,128)(2,1)S(1)} %get-tuple-element.110.in_near_ref), channel_id=1, source_target_pairs={{1,16},{3,18},{5,20},{7,22},{9,24},{11,26},{13,28},{15,30},{16,1},... | collective-permute-start | bytes 3538952 | tf_op jit(solution)/shard_map/ppermute | solution.py:761
  25.0 29.5 %collective-permute-start.13 = (bf16[384,1536]{1,0:T(8,128)(2,1)}, bf16[384,1536]{1,0:T(8,128)(2,1)S(1)}, u32[]{:S(2)}, u32[]{:S(2)}) collective-permute-start(bf16[384,1536]{1,0:T(8,128)(2,1)} %get-tuple-element.111), channel_id=1, source_target_pairs={{0,1},{1,17},{2,3},{3,19},{4,5},{5,21},{6,7},{7,23},{8,9},{9,25},{... | collective-permute-start | bytes 3538952 | tf_op jit(solution)/shard_map/ppermute | solution.py:762
  30.8 23.7 %copy-start.3 = (bf16[1536,384]{1,0:T(8,128)(2,1)}, bf16[1536,384]{1,0:T(8,128)(2,1)S(1)}, u32[]{:S(2)}) copy-start(bf16[1536,384]{1,0:T(8,128)(2,1)S(1)} %get-tuple-element.120.out_near_ref) | copy-start | bytes 3538948
  34.6 7.8 %collective-permute-start.9 = (bf16[2,2,1,2,96,128]{5,4,3,2,1,0:T(8,128)(2,1)S(1)}, bf16[2,2,1,2,96,128]{5,4,3,2,1,0:T(8,128)(2,1)S(1)}, u32[]{:S(2)}, u32[]{:S(2)}) collective-permute-start(bf16[2,2,1,2,96,128]{5,4,3,2,1,0:T(8,128)(2,1)S(1)} %pad_maximum_fusion.7), channel_id=1, source_target_pairs={{0,4},{1,5},{2,6},{3,7},{4,0},{5,1},{6,2},{7,3},{8,12},{9,13},{10,... | collective-permute-start | bytes 589832 | tf_op jit(solution)/shard_map/ppermute | solution.py:282
  35.2 14.7 %collective-permute-start.11 = (bf16[2,2,1,2,96,256]{5,4,3,2,1,0:T(8,128)(2,1)S(1)}, bf16[2,2,1,2,96,256]{5,4,3,2,1,0:T(8,128)(2,1)S(1)}, u32[]{:S(2)}, u32[]{:S(2)}) collective-permute-start(bf16[2,2,1,2,96,256]{5,4,3,2,1,0:T(8,128)(2,1)S(1)} %pad_maximum_fusion.4), channel_id=1, source_target_pairs={{0,4},{1,5},{2,6},{3,7},{4,0},{5,1},{6,2},{7,3},{8,12},{9,13},{10,... | collective-permute-start | bytes 1179656 | tf_op jit(solution)/shard_map/ppermute | solution.py:282
  37.0 14.8 %collective-permute-start.7 = (bf16[2,2,2,1,96,384]{5,4,3,2,1,0:T(8,128)(2,1)S(1)}, bf16[2,2,2,1,96,384]{5,4,3,2,1,0:T(8,128)(2,1)S(1)}, u32[]{:S(2)}, u32[]{:S(2)}) collective-permute-start(bf16[2,2,2,1,96,384]{5,4,3,2,1,0:T(8,128)(2,1)S(1)} %pad_maximum_fusion.2), channel_id=1, source_target_pairs={{0,2},{1,3},{2,0},{3,1},{4,6},{5,7},{6,4},{7,5},{8,10},{9,11},{10,... | collective-permute-start | bytes 1769480 | tf_op jit(solution)/shard_map/ppermute | solution.py:282
  50.9 7.0 %copy-start.27 = (bf16[768]{0:T(1024)(128)(2,1)S(1)}, bf16[768]{0:T(1024)(128)(2,1)}, u32[]{:S(2)}) copy-start(bf16[768]{0:T(1024)(128)(2,1)} %param.14) | copy-start | bytes 4612
  50.9 7.6 %copy-start.28 = (bf16[768]{0:T(1024)(128)(2,1)S(1)}, bf16[768]{0:T(1024)(128)(2,1)}, u32[]{:S(2)}) copy-start(bf16[768]{0:T(1024)(128)(2,1)} %param.15) | copy-start | bytes 4612
  52.0 8.7 %copy-start.1 = (bf16[2,2,2,2,96,384]{5,4,3,2,1,0:T(8,128)(2,1)}, bf16[2,2,2,2,96,384]{5,4,3,2,1,0:T(8,128)(2,1)S(1)}, u32[]{:S(2)}) copy-start(bf16[2,2,2,2,96,384]{5,4,3,2,1,0:T(8,128)(2,1)S(1)} %pad_maximum_fusion) | copy-start | bytes 3538948
  52.0 4.2 %copy-start.10 = (bf16[384,1536]{1,0:T(8,128)(2,1)}, bf16[384,1536]{1,0:T(8,128)(2,1)S(1)}, u32[]{:S(2)}) copy-start(bf16[384,1536]{1,0:T(8,128)(2,1)S(1)} %collective-permute-done.12.in_arrived_ref) | copy-start | bytes 3538948
  54.5 6.2 %collective-permute-start.14 = (bf16[16,96,384]{2,1,0:T(8,128)(2,1)S(1)}, bf16[16,96,384]{2,1,0:T(8,128)(2,1)S(1)}, u32[]{:S(2)}, u32[]{:S(2)}) collective-permute-start(bf16[16,96,384]{2,1,0:T(8,128)(2,1)S(1)} %bitcast.81), channel_id=1, source_target_pairs={{0,1},{1,0},{2,3},{3,2},{4,5},{5,4},{6,7},{7,6},{8,9},{9,8},{10,11... | collective-permute-start | bytes 3538952 | tf_op jit(solution)/shard_map/ppermute | solution.py:282
  54.5 17.9 %collective-permute-start.17 = (bf16[1536,384]{1,0:T(8,128)(2,1)S(1)}, bf16[1536,384]{1,0:T(8,128)(2,1)}, u32[]{:S(2)}, u32[]{:S(2)}) collective-permute-start(bf16[1536,384]{1,0:T(8,128)(2,1)S(1)} %get-tuple-element.120.out_near_ref), channel_id=1, source_target_pairs={{1,16},{3,18},{5,20},{7,22},{9,24},{11,26},{13,28},{15,30},{16,1},... | collective-permute-start | bytes 3538952 | tf_op jit(solution)/shard_map/ppermute | solution.py:771
  56.2 4.5 %collective-permute-start.16 = (bf16[16,96,256]{2,1,0:T(8,128)(2,1)}, bf16[16,96,256]{2,1,0:T(8,128)(2,1)}, u32[]{:S(2)}, u32[]{:S(2)}) collective-permute-start(bf16[16,96,256]{2,1,0:T(8,128)(2,1)} %bitcast.16.rest_2_), channel_id=1, source_target_pairs={{0,1},{1,0},{2,3},{3,2},{4,5},{5,4},{6,7},{7,6},{8,9},{9,8},{10,11... | collective-permute-start | bytes 2359304 | tf_op jit(solution)/shard_map/ppermute | solution.py:282
  57.8 2.8 %collective-permute-start.15 = (bf16[16,96,128]{2,1,0:T(8,128)(2,1)}, bf16[16,96,128]{2,1,0:T(8,128)(2,1)}, u32[]{:S(2)}, u32[]{:S(2)}) collective-permute-start(bf16[16,96,128]{2,1,0:T(8,128)(2,1)} %bitcast.15.rest_1_), channel_id=1, source_target_pairs={{0,1},{1,0},{2,3},{3,2},{4,5},{5,4},{6,7},{7,6},{8,9},{9,8},{10,11... | collective-permute-start | bytes 1179656 | tf_op jit(solution)/shard_map/ppermute | solution.py:282
  72.4 25.5 %copy-start.22 = (bf16[768,16]{0,1:T(8,128)(2,1)S(1)}, bf16[768,16]{0,1:T(8,128)(2,1)}, u32[]{:S(2)}) copy-start(bf16[768,16]{0,1:T(8,128)(2,1)} %param.17) | copy-start | bytes 73732
  72.4 25.2 %all-to-all-start = ((bf16[16,10,1536]{2,1,0:T(8,128)(2,1)}), bf16[16,10,1536]{2,1,0:T(8,128)(2,1)S(1)}, u32[]{:S(2)}, u32[]{:S(2)}) async-start(bf16[16,10,1536]{2,1,0:T(8,128)(2,1)} %get-tuple-element.122), calls=%async_computation | async-start | bytes 1572864 | tf_op jit(solution)/shard_map/all_to_all | solution.py:724
  76.0 24.1 %collective-permute-start.19 = (bf16[1536,384]{1,0:T(8,128)(2,1)}, bf16[1536,384]{1,0:T(8,128)(2,1)S(1)}, u32[]{:S(2)}, u32[]{:S(2)}) collective-permute-start(bf16[1536,384]{1,0:T(8,128)(2,1)} %get-tuple-element.126), channel_id=1, source_target_pairs={{0,1},{1,17},{2,3},{3,19},{4,5},{5,21},{6,7},{7,23},{8,9},{9,25},{... | collective-permute-start | bytes 3538952 | tf_op jit(solution)/shard_map/ppermute | solution.py:806
  97.8 2.4 %collective-permute-start.18 = (bf16[160,1536]{1,0:T(8,128)(2,1)S(1)}, bf16[160,1536]{1,0:T(8,128)(2,1)S(1)}, u32[]{:S(2)}, u32[]{:S(2)}) collective-permute-start(bf16[160,1536]{1,0:T(8,128)(2,1)S(1)} %reshape.98.own_ref), channel_id=1, source_target_pairs={{0,1},{1,0},{2,3},{3,2},{4,5},{5,4},{6,7},{7,6},{8,9},{9,8},{10,11... | collective-permute-start | bytes 1474568 | tf_op jit(solution)/shard_map/ppermute | solution.py:282
  111.5 3.8 %collective-permute-start.20 = (f32[2,160,768]{2,1,0:T(8,128)}, f32[2,160,768]{2,1,0:T(8,128)S(1)}, u32[]{:S(2)}, u32[]{:S(2)}) collective-permute-start(f32[2,160,768]{2,1,0:T(8,128)} %get-tuple-element.128), channel_id=1, source_target_pairs={{0,1},{1,0},{2,3},{3,2},{4,5},{5,4},{6,7},{7,6},{8,9},{9,8},{10,11... | collective-permute-start | bytes 2949128 | tf_op jit(solution)/shard_map/ppermute | solution.py:282
  111.5 8.6 %copy-start.14 = (bf16[320,1536]{1,0:T(8,128)(2,1)S(1)}, bf16[320,1536]{1,0:T(8,128)(2,1)}, u32[]{:S(2)}) copy-start(bf16[320,1536]{1,0:T(8,128)(2,1)} %get-tuple-element.136) | copy-start | bytes 2949124
  111.5 8.6 %copy-start.21 = (bf16[320,768]{1,0:T(8,128)(2,1)S(1)}, bf16[320,768]{1,0:T(8,128)(2,1)}, u32[]{:S(2)}) copy-start(bf16[320,768]{1,0:T(8,128)(2,1)} %get-tuple-element.137) | copy-start | bytes 1474564
  114.8 36.6 %collective-permute-start.21 = (bf16[384,1536]{1,0:T(8,128)(2,1)}, bf16[384,1536]{1,0:T(8,128)(2,1)}, u32[]{:S(2)}, u32[]{:S(2)}) collective-permute-start(bf16[384,1536]{1,0:T(8,128)(2,1)} %convolution_convert_fusion.1), channel_id=1, source_target_pairs={{0,16},{1,0},{2,18},{3,2},{4,20},{5,4},{6,22},{7,6},{8,24},{9,8},{... | collective-permute-start | bytes 3538952 | tf_op jit(solution)/shard_map/ppermute | solution.py:840
  122.1 29.3 %collective-permute-start.22 = (bf16[1536,384]{1,0:T(8,128)(2,1)}, bf16[1536,384]{1,0:T(8,128)(2,1)}, u32[]{:S(2)}, u32[]{:S(2)}) collective-permute-start(bf16[1536,384]{1,0:T(8,128)(2,1)} %convolution_convert_fusion), channel_id=1, source_target_pairs={{0,16},{1,0},{2,18},{3,2},{4,20},{5,4},{6,22},{7,6},{8,24},{9,8},{... | collective-permute-start | bytes 3538952 | tf_op jit(solution)/shard_map/ppermute | solution.py:843
  122.1 28.3 %all-to-all-start.1 = ((bf16[16,10,1536]{2,1,0:T(8,128)(2,1)}), bf16[16,10,1536]{2,1,0:T(8,128)(2,1)S(1)}, u32[]{:S(2)}, u32[]{:S(2)}) async-start(bf16[16,10,1536]{2,1,0:T(8,128)(2,1)} %get-tuple-element.135), calls=%async_computation.1 | async-start | bytes 1572864 | tf_op jit(solution)/shard_map/all_to_all | solution.py:724
  159.1 9.8 %collective-permute-start.23 = (bf16[1536,768]{1,0:T(8,128)(2,1)}, bf16[1536,768]{1,0:T(8,128)(2,1)}, u32[]{:S(2)}, u32[]{:S(2)}) collective-permute-start(bf16[1536,768]{1,0:T(8,128)(2,1)} %get-tuple-element.148), channel_id=1, source_target_pairs={{0,1},{1,0},{2,3},{3,2},{4,5},{5,4},{6,7},{7,6},{8,9},{9,8},{10,11... | collective-permute-start | bytes 7077896 | tf_op jit(solution)/shard_map/ppermute | solution.py:282
  160.3 33.4 %collective-permute-start.27 = (bf16[384,1536]{1,0:T(8,128)(2,1)}, bf16[384,1536]{1,0:T(8,128)(2,1)S(1)}, u32[]{:S(2)}, u32[]{:S(2)}) collective-permute-start(bf16[384,1536]{1,0:T(8,128)(2,1)} %get-tuple-element.155), channel_id=1, source_target_pairs={{1,16},{3,18},{5,20},{7,22},{9,24},{11,26},{13,28},{15,30},{16,1},... | collective-permute-start | bytes 3538952 | tf_op jit(solution)/shard_map/ppermute | solution.py:848
  166.3 10.0 %copy-start.19 = (bf16[128,768]{1,0:T(8,128)(2,1)S(1)}, bf16[128,768]{1,0:T(8,128)(2,1)}, u32[]{:S(2)}) copy-start(bf16[128,768]{1,0:T(8,128)(2,1)} %get-tuple-element.176) | copy-start | bytes 589828
  166.3 10.0 %copy-start.23 = (bf16[768,16]{0,1:T(8,128)(2,1)S(1)}, bf16[768,16]{0,1:T(8,128)(2,1)}, u32[]{:S(2)}) copy-start(bf16[768,16]{0,1:T(8,128)(2,1)} %param.17) | copy-start | bytes 73732
  166.3 10.2 %copy-start.24 = (f32[128,128]{1,0:T(8,128)S(1)}, f32[128,128]{1,0:T(8,128)}, u32[]{:S(2)}) copy-start(f32[128,128]{1,0:T(8,128)} %get-tuple-element.164) | copy-start | bytes 196612
  166.3 15.1 %copy-start.8 = (bf16[1536,384]{1,0:T(8,128)(2,1)S(1)}, bf16[1536,384]{1,0:T(8,128)(2,1)}, u32[]{:S(2)}) copy-start(bf16[1536,384]{1,0:T(8,128)(2,1)} %get-tuple-element.168) | copy-start | bytes 3538948
  166.4 10.2 %collective-permute-start.28 = (f32[128,128]{1,0:T(8,128)}, f32[128,128]{1,0:T(8,128)S(1)}, u32[]{:S(2)}, u32[]{:S(2)}) collective-permute-start(f32[128,128]{1,0:T(8,128)} %get-tuple-element.164), channel_id=1, source_target_pairs={{0,1},{1,0},{2,3},{3,2},{4,5},{5,4},{6,7},{7,6},{8,9},{9,8},{10,11... | collective-permute-start | bytes 196616 | tf_op jit(solution)/shard_map/ppermute | solution.py:282
  173.5 20.1 %copy-start.12 = (f32[8,96,384]{2,1,0:T(8,128)S(1)}, f32[8,96,384]{2,1,0:T(8,128)}, u32[]{:S(2)}) copy-start(f32[8,96,384]{2,1,0:T(8,128)} %get-tuple-element.149) | copy-start | bytes 3538948
  173.5 12.2 %collective-permute-start.26 = (bf16[8,96,128]{2,1,0:T(8,128)(2,1)}, bf16[8,96,128]{2,1,0:T(8,128)(2,1)S(1)}, u32[]{:S(2)}, u32[]{:S(2)}) collective-permute-start(bf16[8,96,128]{2,1,0:T(8,128)(2,1)} %get-tuple-element.154), channel_id=1, source_target_pairs={{0,8},{1,9},{2,10},{3,11},{4,12},{5,13},{6,14},{7,15},{8,0},{9,1},... | collective-permute-start | bytes 589832 | tf_op jit(solution)/shard_map/ppermute | solution.py:282
  175.7 11.1 %collective-permute-start.25 = (bf16[8,96,256]{2,1,0:T(8,128)(2,1)}, bf16[8,96,256]{2,1,0:T(8,128)(2,1)S(1)}, u32[]{:S(2)}, u32[]{:S(2)}) collective-permute-start(bf16[8,96,256]{2,1,0:T(8,128)(2,1)} %get-tuple-element.152), channel_id=1, source_target_pairs={{0,16},{16,0},{1,17},{17,1},{2,18},{18,2},{3,19},{19,3},{4,20},{20... | collective-permute-start | bytes 1179656 | tf_op jit(solution)/shard_map/ppermute | solution.py:280
  176.6 4.9 %collective-permute-start.29 = (f32[128,128]{1,0:T(8,128)S(1)}, f32[128,128]{1,0:T(8,128)S(1)}, u32[]{:S(2)}, u32[]{:S(2)}) collective-permute-start(f32[128,128]{1,0:T(8,128)S(1)} %add.163), channel_id=1, source_target_pairs={{0,2},{1,3},{2,0},{3,1},{4,6},{5,7},{6,4},{7,5},{8,10},{9,11},{10,... | collective-permute-start | bytes 196616 | tf_op jit(solution)/shard_map/ppermute | solution.py:282
  178.0 15.5 %collective-permute-start.24 = (bf16[8,96,384]{2,1,0:T(8,128)(2,1)}, bf16[8,96,384]{2,1,0:T(8,128)(2,1)S(1)}, u32[]{:S(2)}, u32[]{:S(2)}) collective-permute-start(bf16[8,96,384]{2,1,0:T(8,128)(2,1)} %get-tuple-element.150), channel_id=1, source_target_pairs={{0,2},{1,3},{2,0},{3,1},{4,6},{5,7},{6,4},{7,5},{8,10},{9,11},{10,... | collective-permute-start | bytes 1769480 | tf_op jit(solution)/shard_map/ppermute | solution.py:282
  181.5 25.7 %collective-permute-start.33 = (bf16[1536,384]{1,0:T(8,128)(2,1)S(1)}, bf16[1536,384]{1,0:T(8,128)(2,1)S(1)}, u32[]{:S(2)}, u32[]{:S(2)}) collective-permute-start(bf16[1536,384]{1,0:T(8,128)(2,1)S(1)} %copy-done.8), channel_id=1, source_target_pairs={{1,16},{3,18},{5,20},{7,22},{9,24},{11,26},{13,28},{15,30},{16,1},... | collective-permute-start | bytes 3538952 | tf_op jit(solution)/shard_map/ppermute | solution.py:849
  188.0 10.1 %copy-start = (f32[384,1536]{1,0:T(8,128)S(1)}, f32[384,1536]{1,0:T(8,128)}, u32[]{:S(2)}) copy-start(f32[384,1536]{1,0:T(8,128)} %get-tuple-element.183) | copy-start | bytes 7077892
  193.7 9.7 %collective-permute-start.34 = (f32[128,128]{1,0:T(8,128)S(1)}, f32[128,128]{1,0:T(8,128)S(1)}, u32[]{:S(2)}, u32[]{:S(2)}) collective-permute-start(f32[128,128]{1,0:T(8,128)S(1)} %add.164), channel_id=1, source_target_pairs={{0,16},{16,0},{1,17},{17,1},{2,18},{18,2},{3,19},{19,3},{4,20},{20... | collective-permute-start | bytes 196616 | tf_op jit(solution)/shard_map/ppermute | solution.py:280
  195.0 8.4 %collective-permute-start.32 = (bf16[2,1,1,2,1,96,128]{6,5,4,3,2,1,0:T(8,128)(2,1)S(1)}, bf16[2,1,1,2,1,96,128]{6,5,4,3,2,1,0:T(8,128)(2,1)S(1)}, u32[]{:S(2)}, u32[]{:S(2)}) collective-permute-start(bf16[2,1,1,2,1,96,128]{6,5,4,3,2,1,0:T(8,128)(2,1)S(1)} %dynamic-slice_convert_fusion.4), channel_id=1, source_target_pairs={{0,4},{1,5},{2,6},{3,7},{4,0},{5,1},{6,2},{7,3},{8,12},{9,13},{10,... | collective-permute-start | bytes 294920 | tf_op jit(solution)/shard_map/ppermute | solution.py:282
  196.5 10.5 %collective-permute-start.31 = (bf16[1,1,2,2,1,96,256]{6,5,4,3,2,1,0:T(8,128)(2,1)S(1)}, bf16[1,1,2,2,1,96,256]{6,5,4,3,2,1,0:T(8,128)(2,1)S(1)}, u32[]{:S(2)}, u32[]{:S(2)}) collective-permute-start(bf16[1,1,2,2,1,96,256]{6,5,4,3,2,1,0:T(8,128)(2,1)S(1)} %dynamic-slice_convert_fusion.1), channel_id=1, source_target_pairs={{0,8},{1,9},{2,10},{3,11},{4,12},{5,13},{6,14},{7,15},{8,0},{9,1},... | collective-permute-start | bytes 589832 | tf_op jit(solution)/shard_map/ppermute | solution.py:282
  197.2 9.9 %collective-permute-start.30 = (bf16[1,2,2,1,1,96,384]{6,5,4,3,2,1,0:T(8,128)(2,1)S(1)}, bf16[1,2,2,1,1,96,384]{6,5,4,3,2,1,0:T(8,128)(2,1)S(1)}, u32[]{:S(2)}, u32[]{:S(2)}) collective-permute-start(bf16[1,2,2,1,1,96,384]{6,5,4,3,2,1,0:T(8,128)(2,1)S(1)} %dynamic-slice_convert_fusion), channel_id=1, source_target_pairs={{0,16},{16,0},{1,17},{17,1},{2,18},{18,2},{3,19},{19,3},{4,20},{20... | collective-permute-start | bytes 884744 | tf_op jit(solution)/shard_map/ppermute | solution.py:280
  207.2 10.3 %collective-permute-start.37 = (bf16[2,1,1,1,1,96,128]{6,5,4,3,2,1,0:T(8,128)(2,1)S(1)}, bf16[2,1,1,1,1,96,128]{6,5,4,3,2,1,0:T(8,128)(2,1)S(1)}, u32[]{:S(2)}, u32[]{:S(2)}) collective-permute-start(bf16[2,1,1,1,1,96,128]{6,5,4,3,2,1,0:T(8,128)(2,1)S(1)} %dynamic-slice_convert_fusion.7), channel_id=1, source_target_pairs={{0,2},{1,3},{2,0},{3,1},{4,6},{5,7},{6,4},{7,5},{8,10},{9,11},{10,... | collective-permute-start | bytes 147464 | tf_op jit(solution)/shard_map/ppermute | solution.py:282
  208.6 8.9 %collective-permute-start.38 = (f32[128,128]{1,0:T(8,128)S(1)}, f32[128,128]{1,0:T(8,128)S(1)}, u32[]{:S(2)}, u32[]{:S(2)}) collective-permute-start(f32[128,128]{1,0:T(8,128)S(1)} %add.174), channel_id=1, source_target_pairs={{0,8},{1,9},{2,10},{3,11},{4,12},{5,13},{6,14},{7,15},{8,0},{9,1},... | collective-permute-start | bytes 196616 | tf_op jit(solution)/shard_map/ppermute | solution.py:282
  210.9 6.6 %collective-permute-start.36 = (bf16[1,1,1,2,1,96,256]{6,5,4,3,2,1,0:T(8,128)(2,1)S(1)}, bf16[1,1,1,2,1,96,256]{6,5,4,3,2,1,0:T(8,128)(2,1)S(1)}, u32[]{:S(2)}, u32[]{:S(2)}) collective-permute-start(bf16[1,1,1,2,1,96,256]{6,5,4,3,2,1,0:T(8,128)(2,1)S(1)} %dynamic-slice_convert_fusion.3), channel_id=1, source_target_pairs={{0,4},{1,5},{2,6},{3,7},{4,0},{5,1},{6,2},{7,3},{8,12},{9,13},{10,... | collective-permute-start | bytes 294920 | tf_op jit(solution)/shard_map/ppermute | solution.py:282
  212.5 8.4 %collective-permute-start.35 = (bf16[1,1,2,1,1,96,384]{6,5,4,3,2,1,0:T(8,128)(2,1)S(1)}, bf16[1,1,2,1,1,96,384]{6,5,4,3,2,1,0:T(8,128)(2,1)S(1)}, u32[]{:S(2)}, u32[]{:S(2)}) collective-permute-start(bf16[1,1,2,1,1,96,384]{6,5,4,3,2,1,0:T(8,128)(2,1)S(1)} %dynamic-slice_convert_fusion.2), channel_id=1, source_target_pairs={{0,8},{1,9},{2,10},{3,11},{4,12},{5,13},{6,14},{7,15},{8,0},{9,1},... | collective-permute-start | bytes 442376 | tf_op jit(solution)/shard_map/ppermute | solution.py:282
  214.9 6.4 %copy-start.26 = (s32[2,1,64]{2,1,0:T(1,128)S(1)}, s32[2,1,64]{2,1,0:T(1,128)}, u32[]{:S(2)}) copy-start(s32[2,1,64]{2,1,0:T(1,128)} %routes_ref) | copy-start | bytes 1540
  215.0 11.2 %copy-start.6 = (bf16[160,1536]{1,0:T(8,128)(2,1)S(1)}, bf16[160,1536]{1,0:T(8,128)(2,1)}, u32[]{:S(2)}) copy-start(bf16[160,1536]{1,0:T(8,128)(2,1)} %reshape.99.dn2_ref) | copy-start | bytes 1474564
  215.0 11.2 %copy-start.7 = (f32[128,768]{1,0:T(8,128)S(1)}, f32[128,768]{1,0:T(8,128)}, u32[]{:S(2)}) copy-start(f32[128,768]{1,0:T(8,128)} %get-tuple-element.118.resid_ref) | copy-start | bytes 1179652
  215.0 11.2 %copy-start.20 = (bf16[160,128]{1,0:T(8,128)(2,1)S(1)}, bf16[160,128]{1,0:T(8,128)(2,1)}, u32[]{:S(2)}) copy-start(bf16[160,128]{1,0:T(8,128)(2,1)} %get-tuple-element.141.dispatch_ref) | copy-start | bytes 122884
  222.1 5.0 %collective-permute-start.41 = (bf16[1,1,1,1,1,96,128]{6,5,4,3,2,1,0:T(8,128)(2,1)S(1)}, bf16[1,1,1,1,1,96,128]{6,5,4,3,2,1,0:T(8,128)(2,1)S(1)}, u32[]{:S(2)}, u32[]{:S(2)}) collective-permute-start(bf16[1,1,1,1,1,96,128]{6,5,4,3,2,1,0:T(8,128)(2,1)S(1)} %dynamic-slice_convert_fusion.8), channel_id=1, source_target_pairs={{0,16},{16,0},{1,17},{17,1},{2,18},{18,2},{3,19},{19,3},{4,20},{20... | collective-permute-start | bytes 73736 | tf_op jit(solution)/shard_map/ppermute | solution.py:280
  223.4 4.1 %collective-permute-start.40 = (bf16[1,1,1,1,1,96,256]{6,5,4,3,2,1,0:T(8,128)(2,1)S(1)}, bf16[1,1,1,1,1,96,256]{6,5,4,3,2,1,0:T(8,128)(2,1)S(1)}, u32[]{:S(2)}, u32[]{:S(2)}) collective-permute-start(bf16[1,1,1,1,1,96,256]{6,5,4,3,2,1,0:T(8,128)(2,1)S(1)} %dynamic-slice_convert_fusion.6), channel_id=1, source_target_pairs={{0,2},{1,3},{2,0},{3,1},{4,6},{5,7},{6,4},{7,5},{8,10},{9,11},{10,... | collective-permute-start | bytes 147464 | tf_op jit(solution)/shard_map/ppermute | solution.py:282
  224.0 4.3 %collective-permute-start.42 = (f32[128,128]{1,0:T(8,128)S(1)}, f32[128,128]{1,0:T(8,128)S(1)}, u32[]{:S(2)}, u32[]{:S(2)}) collective-permute-start(f32[128,128]{1,0:T(8,128)S(1)} %add.180), channel_id=1, source_target_pairs={{0,4},{1,5},{2,6},{3,7},{4,0},{5,1},{6,2},{7,3},{8,12},{9,13},{10,... | collective-permute-start | bytes 196616 | tf_op jit(solution)/shard_map/ppermute | solution.py:282
  224.1 6.1 %collective-permute-start.39 = (bf16[1,1,1,1,1,96,384]{6,5,4,3,2,1,0:T(8,128)(2,1)S(1)}, bf16[1,1,1,1,1,96,384]{6,5,4,3,2,1,0:T(8,128)(2,1)S(1)}, u32[]{:S(2)}, u32[]{:S(2)}) collective-permute-start(bf16[1,1,1,1,1,96,384]{6,5,4,3,2,1,0:T(8,128)(2,1)S(1)} %dynamic-slice_convert_fusion.5), channel_id=1, source_target_pairs={{0,4},{1,5},{2,6},{3,7},{4,0},{5,1},{6,2},{7,3},{8,12},{9,13},{10,... | collective-permute-start | bytes 221192 | tf_op jit(solution)/shard_map/ppermute | solution.py:282
  (10 other events, 20.4 us)

commit v4 on v3

--- a/solution.py
+++ b/solution.py
@@ -288,15 +288,15 @@
     return (lax.axis_index("expert") // bit) % 2
 
 
-ORDERS = ((8, "y", 4, 2), (2, "y", 8, 4), ("y", 2, 8, 4))
-RS_ORDERS = ((2, "y", 8, 4), ("y", 8, 4, 2), (8, 4, 2, "y"))
+ORDERS = (("y", 2, 8, 4), (2, "y", 8, 4), (8, "y", 4, 2))
+RS_ORDERS = ((8, 4, 2, "y"), ("y", 8, 4, 2), (2, "y", 8, 4))
 PLACE = {"y": 0, 8: 1, 4: 2, 2: 3, 1: 4}
 
 
-def gather_rows(shard, prepare, waiting):
+def gather_rows(shard, prepare, waiting, divide, last):
     rows, width = shard.shape
     pieces, begin = [], 0
-    for size in (width // 2, width // 6, width // 3):
+    for size in (width // 3, width // 6, width // 2):
         piece = shard[:, begin : begin + size]
         pieces.append(piece.reshape(1, 1, 1, 1, rows, size))
         begin += size
@@ -312,10 +312,13 @@
         if step == 2:
             pieces, waiting = lax.optimization_barrier((pieces, waiting))
             ready = prepare(*waiting)
+        if step == 3:
+            pieces, last = lax.optimization_barrier((pieces, last))
+            last = divide(last, 0)
         pieces = [grow(piece, ORDERS[i][step]) for i, piece in enumerate(pieces)]
-    pieces, ready = lax.optimization_barrier((pieces, ready))
+    pieces, ready, last = lax.optimization_barrier((pieces, ready, last))
     pieces = [piece.reshape(-1, rows, piece.shape[-1]) for piece in pieces]
-    return pieces + [flip(piece, 1) for piece in pieces], ready
+    return pieces + [flip(piece, 1) for piece in pieces], ready, last
 
 
 def reduce_step(total, bit):
@@ -350,7 +353,7 @@
     )
 
 
-def call(kernel, mib, outs, scratch, *operands, plain_in=(), plain_out=()):
+def call(kernel, mib, outs, scratch, *operands, plain_in=(), plain_out=(), free=()):
     def spec(shape):
         return pl.BlockSpec(
             shape, lambda i: (0,) * len(shape), pipeline_mode=pl.Buffered(1)
@@ -358,7 +361,9 @@
 
     left = pl.BlockSpec(memory_space=pl.ANY)
     operands = operands[:1] + tuple(
-        pltpu.with_memory_space_constraint(operand, pltpu.HBM) for operand in operands[1:]
+        operand if i in free else pltpu.with_memory_space_constraint(operand, pltpu.HBM)
+        for i, operand in enumerate(operands)
+        if i
     )
     return pl.pallas_call(
         kernel,
@@ -578,33 +583,34 @@
     place_ref, own_ref, got_ref, router_ref,
     in_near_ref, in_arrived_ref, in_far_ref, out_near_ref, out_arrived_ref, out_far_ref,
     rows_ref, hidden_ref, du_ref, dmade_ref, mine_ref, theirs_ref, probs_ref, in_full, out_full,
+    come_in, come_out,
 ):
     core, host = place_ref[0], place_ref[1]
     half, units = in_far_ref.shape
     own, width = got_ref.shape[0], got_ref.shape[1] // 2
     for side in range(2):
 
-        at, other = slice(side * half, (side + 1) * half), slice((1 - side) * half, (2 - side) * half)
+        at, other = pl.ds(side * half, half), pl.ds((1 - side) * half, half)
 
         @pl.when(core == side)
         def _():
-            in_full[other] = in_far_ref[...]
-            out_full[:, other] = out_far_ref[...]
+            pltpu.make_async_copy(in_far_ref, in_full.at[other], come_in).start()
+            pltpu.make_async_copy(out_far_ref, out_full.at[:, other], come_out).start()
 
         @pl.when((core == side) & (place_ref[2] == 1))
         def _():
-            in_full[at] = in_near_ref[...]
-            out_full[:, at] = out_near_ref[...]
+            pltpu.make_async_copy(in_near_ref, in_full.at[at], come_in).start()
+            pltpu.make_async_copy(out_near_ref, out_full.at[:, at], come_out).start()
 
         @pl.when((core == side) & (place_ref[2] == 0))
         def _():
-            in_full[at] = in_arrived_ref[...]
-            out_full[:, at] = out_arrived_ref[...]
+            pltpu.make_async_copy(in_arrived_ref, in_full.at[at], come_in).start()
+            pltpu.make_async_copy(out_arrived_ref, out_full.at[:, at], come_out).start()
 
     rows = jnp.concatenate([own_ref[:, :width], got_ref[:, :width]], axis=0)
     dy = jnp.concatenate([own_ref[:, width:], got_ref[:, width:]], axis=0)
     rows_ref[...] = rows
-    logits = dot(rows, router_ref[...], ((1,), (0,)))
+    logits = dot(rows, router_ref[...], ((1,), (1,)))
     raised = jnp.exp(logits - jnp.max(logits, axis=-1, keepdims=True))
     probs = raised / jnp.sum(raised, axis=-1, keepdims=True)
     probs_ref[...] = probs[:own]
@@ -612,6 +618,8 @@
     gate = jnp.sum(jnp.where(chosen, probs, 0.0), axis=-1, keepdims=True)
     dmade_ref[...] = (gate * dy.astype(jnp.float32)).astype(jnp.bfloat16)
     dmade = dmade_ref[...]
+    pltpu.make_async_copy(in_full, in_full, come_in).wait()
+    pltpu.make_async_copy(out_full, out_full, come_out).wait()
     made = jnp.zeros(rows.shape, jnp.float32)
     drows = jnp.zeros(rows.shape, jnp.float32)
     step = units // 3
@@ -644,10 +652,8 @@
     made = (mine_ref[0] + got_ref[0]).astype(jnp.bfloat16)
     row = lax.broadcasted_iota(jnp.int32, (chips * 16, made.shape[0]), 0)
     column = lax.broadcasted_iota(jnp.int32, row.shape, 1)
-    spread = jnp.zeros(row.shape, jnp.float32)
-    for chip in range(chips):
-        inside = (row >= chip * 16) & (row < chip * 16 + places)
-        spread = jnp.where(inside & (column == row - chip * (16 - places)), 1.0, spread)
+    inside = (row & 15) < places
+    spread = jnp.where(inside & (column == (row >> 4) * places + (row & 15)), 1.0, 0.0)
     spread = spread.astype(jnp.bfloat16)
 
     def padded(values):
@@ -668,7 +674,7 @@
     router_part_ref[...] = dot(
         dlogits, own_ref[:, :width].astype(jnp.float32), ((0,), (0,)), precision=HIGH
     )
-    dn2 = drows + dot(dlogits, router_ref[...].astype(jnp.float32), ((1,), (1,)), precision=HIGH)
+    dn2 = drows + dot(dlogits, router_ref[...].astype(jnp.float32), ((1,), (0,)), precision=HIGH)
     back_ref[:, :, :width] = padded(dn2.astype(jnp.bfloat16))
 
 
@@ -745,7 +751,9 @@
             [jnp.where(low, keep, got), jnp.where(low, got, keep)], axis=axis
         )
 
-    def prepare(table, ids, route_ids, slot_ids, near, far, out_local):
+    moved = []
+
+    def prepare(table, ids, route_ids, slot_ids, near, far):
         made = call(
             functools.partial(prepare_kernel, places, capacity),
             16,
@@ -759,15 +767,18 @@
             table, ids, route_ids, slot_ids,
         )
         in_arrived = lax.ppermute(near, BOTH, across)
-        in_far = lax.ppermute(far, BOTH, outward)
-        return tuple(made) + (in_arrived, in_far) + parts_of(out_local, 0)
-
-    pieces, ready = gather_rows(
+        moved.append(lax.ppermute(far, BOTH, outward))
+        return tuple(made) + (in_arrived,)
+
+    pieces, ready, (out_near, out_far) = gather_rows(
         attn_weight.T,
         prepare,
-        (bias_table.astype(f32), buckets, routes, slots, in_near, in_far, expert_out[0]),
-    )
-    square, tiled, dispatch, padded, in_arrived, in_far, out_near, out_far = ready
+        (bias_table.astype(f32), buckets, routes, slots, in_near, in_far),
+        parts_of,
+        expert_out[0],
+    )
+    square, tiled, dispatch, padded, in_arrived = ready
+    pieces, in_far = lax.optimization_barrier((pieces, moved[0]))
     out_arrived = lax.ppermute(out_near, BOTH, across)
     place = jnp.stack(
         [core, host, home.astype(jnp.int32)] + [own_bit(order[0]) for order in RS_ORDERS]
@@ -816,8 +827,15 @@
             ((2, row_count, width), f32),
             ((row_count, experts), f32),
         ),
-        [pltpu.VMEM((width, hidden_half), bf16), pltpu.VMEM((hidden_half, width), bf16)],
-        place, own_rows, flip(own_rows, 1), router_weight, *in_parts, *out_parts,
+        [
+            pltpu.VMEM((width, hidden_half), bf16),
+            pltpu.VMEM((hidden_half, width), bf16),
+            pltpu.SemaphoreType.DMA,
+            pltpu.SemaphoreType.DMA,
+        ],
+        place, own_rows, flip(own_rows, 1), router_weight.T, *in_parts, *out_parts,
+        plain_in=range(4, 10),
+        free=(2,),
     )
     back_rows, router_part = call(
         settle_kernel,
@@ -827,7 +845,8 @@
             ((experts, width), f32),
         ),
         [],
-        place, mine, flip(theirs, 1), own_rows, row_probs, router_weight,
+        place, mine, flip(theirs, 1), own_rows, row_probs, router_weight.T,
+        free=(2,),
     )
     in_other = dot(halves(rows)[1], du, ((0,), (0,))).astype(bf16)
     back_rows, rows, hidden, du, dmade = lax.optimization_barrier(
@@ -876,7 +895,7 @@
         router_part,
     )
     block = width // 8
-    pieces = (width // 2, width // 3, width // 6)
+    pieces = (width // 6, width // 3, width // 2)
     cut = call(
         split_kernel,
         30,
@@ -884,6 +903,7 @@
         + tuple(((8, block, piece), f32) for piece in pieces),
         [pltpu.VMEM((16, block, width), f32)],
         place, keep, n1b, mixed_b, got,
+        free=(4,),
     )
     attn_share, small, late = scatter_rows(
         cut[:3],

time: 232 us -> 227 us (0.978)
  local copies, waits for them, and re-layouts: 18 us -> 13.4 us
    ppermute x7, waiting for transfers between devices: 3.7 us -> 7.17 us  [flip(): return lax.ppermute(tensor, 'dp', [(0, 1), (1, 0)])]
    unnamed x61 -> x62, local copies, waits for them, and re-layouts: 5.43 us -> 2.61 us
    ppermute x1, waiting for transfers between devices: 2.44 us -> 0.01 us  [prepare(): moved.append(lax.ppermute(far, BOTH, outward))]
  transfers between devices with their start and end apart: 45 -> 45, of which waited for: 19 -> 22; matrix products, arithmetic and copies ran while one was open for 17% -> 16% of each run, Pallas kernels for 12% -> 12%
where the time goes in v4:
time: 227 us
  waiting for transfers between devices  79.4 us (35%)
  starting transfers between devices  61.8 us (27%)
  Pallas kernels  43.5 us (19%)
  other arithmetic  14.2 us (6%)
  local copies, waits for them, and re-layouts  13.4 us (6%)
  matrix products  13 us (6%)
    pallas_call x7, Pallas kernels, call(): pl.pallas_call(kernel, grid=(1,), out_shape=tuple((pltpu.HBM(*out) for ou...  43.5 us
    all_to_all x2, waiting for transfers between devices, to_chips(): lax.all_to_all(tensor, BOTH, split_axis=0, concat_axis=0, tiled=True, axi...  36.7 us
    ppermute x28, starting transfers between devices, flip(): return lax.ppermute(tensor, 'expert', [(i, i ^ bit) for i in range(count)])  36.2 us
    ppermute x28, waiting for transfers between devices, flip(): return lax.ppermute(tensor, 'expert', [(i, i ^ bit) for i in range(count)])  32.4 us
    dot_general x6, matrix products, dot(): lax.dot_general(left, right, (dims, ((), ())), preferred_element_type=jnp...  13 us
    all_to_all x2, starting transfers between devices, to_chips(): lax.all_to_all(tensor, BOTH, split_axis=0, concat_axis=0, tiled=True, axi...  10.6 us
    ppermute x7, starting transfers between devices, flip(): return lax.ppermute(tensor, 'dp', [(0, 1), (1, 0)])  7.95 us
    ppermute x7, waiting for transfers between devices, flip(): return lax.ppermute(tensor, 'dp', [(0, 1), (1, 0)])  7.17 us
  transfers between devices with their start and end apart: 45, of which 22 were waited for; matrix products, arithmetic and copies ran while one was open for 16% of the time, Pallas kernels for 12%

profile of v4, /device:TPU:0, one launch (start us, length us, event | category | flops | bytes accessed | tf_op | source)
XLA Modules:
  0.0 226.6 jit_solution(9649080935704825881)
XLA Ops:
  1.4 2.9 %collective-permute-start.2 = (bf16[1,1,1,1,96,128]{5,4,3,2,1,0:T(8,128)(2,1)S(1)}, bf16[1,1,1,1,96,128]{5,4,3,2,1,0:T(8,128)(2,1)S(1)}, u32[]{:S(2)}, u32[]{:S(2)}) collective-permute-start(bf16[1,1,1,1,96,128]{5,4,3,2,1,0:T(8,128)(2,1)S(1)} %slice_bitcast_fusion.2), channel_id=1, source_target_pairs={{0,2},{1,3},{2,0},{3,1},{4,6},{5,7},{6,4},{7,5},{8,10},{9,11},{10,... | collective-permute-start | bytes 73736 | tf_op jit(solution)/shard_map/ppermute | solution.py:282
  5.1 1.5 collective-permute-start
  7.5 2.6 %collective-permute-start.4 = (bf16[1,1,1,1,96,384]{5,4,3,2,1,0:T(8,128)(2,1)S(1)}, bf16[1,1,1,1,96,384]{5,4,3,2,1,0:T(8,128)(2,1)S(1)}, u32[]{:S(2)}, u32[]{:S(2)}) collective-permute-start(bf16[1,1,1,1,96,384]{5,4,3,2,1,0:T(8,128)(2,1)S(1)} %slice_bitcast_fusion), channel_id=1, source_target_pairs={{0,8},{1,9},{2,10},{3,11},{4,12},{5,13},{6,14},{7,15},{8,0},{9,1},... | collective-permute-start | bytes 221192 | tf_op jit(solution)/shard_map/ppermute | solution.py:282
  10.1 2.8 %dynamic-slice_bitcast_fusion = (bf16[384,1536]{1,0:T(8,128)(2,1)}, bf16[384,1536]{1,0:T(8,128)(2,1)S(1)}) fusion(bf16[1,384,3072]{2,1,0:T(8,128)(2,1)} %param.18, s32[]{:T(128)S(6)} %select_n.349, s32[]{:T(128)S(6)} %select_n.348), kind=kLoop, calls=%fused_computation.16 | loop fusion | bytes 4718600 | tf_op jit(solution)/shard_map/dynamic_slice | solution.py:738
  14.4 1.6 collective-permute-start.5
  16.0 1.6 collective-permute-done.3
  18.5 1.1 collective-permute-done.5
  19.7 1.2 collective-permute-start.7
  20.9 1.8 collective-permute-start.6
  22.7 1.6 collective-permute-start.8
  25.0 2.8 %collective-permute-start.16 = (bf16[384,1536]{1,0:T(8,128)(2,1)}, bf16[384,1536]{1,0:T(8,128)(2,1)}, u32[]{:S(2)}, u32[]{:S(2)}) collective-permute-start(bf16[384,1536]{1,0:T(8,128)(2,1)} %get-tuple-element.127), channel_id=1, source_target_pairs={{0,1},{1,17},{2,3},{3,19},{4,5},{5,21},{6,7},{7,23},{8,9},{9,25},{... | collective-permute-start | bytes 3538952 | tf_op jit(solution)/shard_map/ppermute | solution.py:770
  27.8 3.7 %shard_map.187 = (f32[12,128,128]{2,1,0:T(8,128)}, s32[64,128]{1,0:T(8,128)}, bf16[160,128]{1,0:T(8,128)(2,1)}, bf16[256,128]{1,0:T(8,128)(2,1)}) custom-call(f32[32,12]{1,0:T(8,128)S(1)} %convert_element_type.99.table_ref, s32[64,64]{1,0:T(8,128)} %buckets_ref, s32[2,1,64]{2,1,0:T(1,128)} %routes_ref, s32[2,1,64]{2,1,0:T(1,128)} %slots_ref), custom_call_target="tpu_custom_call" | custom-call | tf_op jit(solution)/shard_map/pallas_call | solution.py:368
  31.6 2.2 collective-permute-done.6
  34.7 1.8 collective-permute-start.9
  36.4 1.6 collective-permute-start.11
  38.1 1.2 constant_dynamic-slice_fusion
  39.3 3.0 %collective-permute-done.10 = bf16[2,2,1,2,96,128]{5,4,3,2,1,0:T(8,128)(2,1)S(1)} collective-permute-done((bf16[2,2,1,2,96,128]{5,4,3,2,1,0:T(8,128)(2,1)S(1)}, bf16[2,2,1,2,96,128]{5,4,3,2,1,0:T(8,128)(2,1)S(1)}, u32[]{:S(2)}, u32[]{:S(2)}) %collective-permute-start.10) | collective-permute-done | bytes 196640 | tf_op jit(solution)/shard_map/ppermute | solution.py:282
  43.1 5.1 %collective-permute-done.9 = bf16[2,2,1,2,96,256]{5,4,3,2,1,0:T(8,128)(2,1)S(1)} collective-permute-done((bf16[2,2,1,2,96,256]{5,4,3,2,1,0:T(8,128)(2,1)S(1)}, bf16[2,2,1,2,96,256]{5,4,3,2,1,0:T(8,128)(2,1)S(1)}, u32[]{:S(2)}, u32[]{:S(2)}) %collective-permute-start.9) | collective-permute-done | bytes 393248 | tf_op jit(solution)/shard_map/ppermute | solution.py:282
  48.4 1.3 collective-permute-done.11
  49.8 1.1 pad_maximum_fusion
  51.7 3.2 %collective-permute-start.13 = (bf16[16,96,256]{2,1,0:T(8,128)(2,1)S(1)}, bf16[16,96,256]{2,1,0:T(8,128)(2,1)}, u32[]{:S(2)}, u32[]{:S(2)}) collective-permute-start(bf16[16,96,256]{2,1,0:T(8,128)(2,1)S(1)} %bitcast.85), channel_id=1, source_target_pairs={{0,1},{1,0},{2,3},{3,2},{4,5},{5,4},{6,7},{7,6},{8,9},{9,8},{10,11... | collective-permute-start | bytes 2359304 | tf_op jit(solution)/shard_map/ppermute | solution.py:282
  56.2 1.3 collective-permute-done.14.rest_4_
  58.3 10.7 %shard_map.188 = (bf16[12,2,96,768]{3,2,1,0:T(8,128)(2,1)}, bf16[4,2,96,768]{3,2,1,0:T(8,128)(2,1)}, bf16[128,768]{1,0:T(8,128)(2,1)}, bf16[2304,128]{1,0:T(8,12...) custom-call(s32[6]{0:T(128)S(1)} %stack.31.place_ref.core_ref._, ...), custom_call_target="tpu_custom_call" | custom-call | tf_op jit(solution)/shard_map/pallas_call | solution.py:368
  69.0 3.9 %all-to-all-start = ((bf16[16,10,1536]{2,1,0:T(8,128)(2,1)}), bf16[16,10,1536]{2,1,0:T(8,128)(2,1)S(1)}, u32[]{:S(2)}, u32[]{:S(2)}) async-start(bf16[16,10,1536]{2,1,0:T(8,128)(2,1)} %get-tuple-element.140), calls=%async_computation | async-start | bytes 1572864 | tf_op jit(solution)/shard_map/all_to_all | solution.py:730
  73.2 20.5 %all-to-all-done = bf16[16,10,1536]{2,1,0:T(8,128)(2,1)S(1)} async-done(((bf16[16,10,1536]{2,1,0:T(8,128)(2,1)}), bf16[16,10,1536]{2,1,0:T(8,128)(2,1)S(1)}, u32[]{:S(2)}, u32[]{:S(2)}) %all-to-all-start) | async-done | bytes 491552 | tf_op jit(solution)/shard_map/all_to_all | solution.py:730
  94.0 3.1 %collective-permute-done.19.out_far_ref = bf16[1536,384]{1,0:T(8,128)(2,1)S(1)} collective-permute-done((bf16[1536,384]{1,0:T(8,128)(2,1)}, bf16[1536,384]{1,0:T(8,128)(2,1)S(1)}, u32[]{:S(2)}, u32[]{:S(2)}) %collective-permute-start.19) | collective-permute-done | bytes 1179680 | tf_op jit(solution)/shard_map/ppermute | solution.py:817
  97.1 1.0 copy-done.14
  98.1 8.7 %shard_map.189 = (bf16[320,768]{1,0:T(8,128)(2,1)}, bf16[320,1536]{1,0:T(8,128)(2,1)}, bf16[320,1536]{1,0:T(8,128)(2,1)}, bf16[320,768]{1,0:T(8,128)(2,1)}, f32[...) custom-call(s32[6]{0:T(128)S(1)} %stack.31.place_ref.core_ref._, bf16[160,1536]{1,0:T(8,128)(2,1)} %copy-done.4, ...), custom_call_target="tpu_custom_call" | custom-call | tf_op jit(solution)/shard_map/pallas_call | solution.py:368
  107.0 3.2 %convolution_convert_fusion.1 = bf16[384,1536]{1,0:T(8,128)(2,1)} fusion(bf16[320,1536]{1,0:T(8,128)(2,1)} %get-tuple-element.157, bf16[320,768]{1,0:T(8,128)(2,1)} %get-tuple-element.156, s32[]{:T(128)S(6)} %select_n.366), kind=kOutput, calls=%fused_computation.7 | convolution fusion | flops 378077184 | bytes 2408452 | tf_op jit(solution)/shard_map/dot_general | solution.py:351
  110.2 3.4 %shard_map.190 = (bf16[16,10,1536]{2,1,0:T(8,128)(2,1)}, f32[16,768]{1,0:T(8,128)}) custom-call(s32[6]{0:T(128)S(1)} %stack.31.place_ref.core_ref._, f32[2,160,768]{2,1,0:T(8,128)} %get-tuple-element.145.mine_ref, f32[2,160,768]{2,1,0:T(8,128)S(1)} %collective-permute-done.20.got_ref, bf16[160,1536]{1,0:T(8,128)(2,1)} %copy-done.4, ...), custom_call_target="tpu_custom_call" | custom-call | tf_op jit(solution)/shard_map/pallas_call | solution.py:368
  113.7 2.0 convolution_convert_fusion
  115.7 6.7 %all-to-all-start.1 = ((bf16[16,10,1536]{2,1,0:T(8,128)(2,1)}), bf16[16,10,1536]{2,1,0:T(8,128)(2,1)S(1)}, u32[]{:S(2)}, u32[]{:S(2)}) async-start(bf16[16,10,1536]{2,1,0:T(8,128)(2,1)} %get-tuple-element.153), calls=%async_computation.1 | async-start | bytes 1572864 | tf_op jit(solution)/shard_map/all_to_all | solution.py:730
  122.5 4.1 %fusion.19 = (bf16[1536,384]{1,0:T(8,128)(2,1)}, f32[1536,384]{1,0:T(8,128)}) fusion(bf16[320,1536]{1,0:T(8,128)(2,1)} %get-tuple-element.154, bf16[320,768]{1,0:T(8,128)(2,1)} %get-tuple-element.155, s32[]{:T(128)S(6)} %select_n.367), kind=kOutput, calls=%fused_computation.100 | convolution fusion | flops 378077184 | bytes 4767748 | tf_op jit(solution)/shard_map/dot_general | solution.py:351
  126.6 2.6 %fusion.18 = (bf16[384,1536]{1,0:T(8,128)(2,1)}, f32[384,1536]{1,0:T(8,128)}) fusion(bf16[320,1536]{1,0:T(8,128)(2,1)S(1)} %copy-done.5, bf16[320,768]{1,0:T(8,128)(2,1)S(1)} %copy-done.19, s32[]{:T(128)S(6)} %select_n.367), kind=kOutput, calls=%fused_computation.99 | convolution fusion | flops 378077184 | bytes 4767748 | tf_op jit(solution)/shard_map/dot_general | solution.py:351
  129.2 16.1 %all-to-all-done.1 = bf16[16,10,1536]{2,1,0:T(8,128)(2,1)S(1)} async-done(((bf16[16,10,1536]{2,1,0:T(8,128)(2,1)}), bf16[16,10,1536]{2,1,0:T(8,128)(2,1)S(1)}, u32[]{:S(2)}, u32[]{:S(2)}) %all-to-all-start.1) | async-done | bytes 491552 | tf_op jit(solution)/shard_map/all_to_all | solution.py:730
  146.3 8.1 %shard_map.191 = (f32[128,768]{1,0:T(8,128)}, f32[1,768]{1,0:T(1,128)}, bf16[2304,128]{1,0:T(8,128)(2,1)}, f32[12,64,128]{2,1,0:T(8,128)}, bf16[1536,768]{1,0:T(8,128)(2,1)}, /*index=5*/bf16[1536,128]{1,0:T(8,128)(2,1)}) custom-call(s32[6]{0:T(128)S(1)} %stack.31.place_ref.core_ref._, bf16[160,1536]{1,0:T(8,128)(2,1)} %reshape.99.dn2_ref, ...), custom_call_target="tpu_custom_call" | custom-call | tf_op jit(solution)/shard_map/pallas_call | solution.py:368
  154.4 1.8 collective-permute-start.23
  156.2 1.7 collective-permute-start.27
  157.9 5.1 %shard_map.193 = (f32[128,768]{1,0:T(8,128)}, f32[128,128]{1,0:T(8,128)}) custom-call(s32[6]{0:T(128)S(1)} %stack.31.place_ref.core_ref._, bf16[128,768]{1,0:T(8,128)(2,1)} %bitcast.96, bf16[2304,128]{1,0:T(8,128)(2,1)} %get-tuple-element.175.dqkv_ref, bf16[2304,768]{1,0:T(8,128)(2,1)} %bitcast.84, f32[1,768]{1,0:T(1,128)} %reshape.113.rest_6_.gain_one_ref, ...), custom_call_target="tpu_custom_call" | custom-call | tf_op jit(solution)/shard_map/pallas_call | solution.py:368
  163.0 1.4 collective-permute-start.28
  164.3 3.7 %shard_map.192 = (bf16[8,96,128]{2,1,0:T(8,128)(2,1)}, bf16[8,96,256]{2,1,0:T(8,128)(2,1)}, bf16[8,96,384]{2,1,0:T(8,128)(2,1)}, f32[8,96,128]{2,1,0:T(8,128)}, ...) custom-call(s32[6]{0:T(128)S(1)} %stack.31.place_ref.core_ref._, bf16[1536,128]{1,0:T(8,128)(2,1)} %get-tuple-element.165.keep_ref, ...), custom_call_target="tpu_custom_call" | custom-call | tf_op jit(solution)/shard_map/pallas_call | solution.py:368
  168.1 2.7 %collective-permute-start.24 = (bf16[8,96,128]{2,1,0:T(8,128)(2,1)}, bf16[8,96,128]{2,1,0:T(8,128)(2,1)S(1)}, u32[]{:S(2)}, u32[]{:S(2)}) collective-permute-start(bf16[8,96,128]{2,1,0:T(8,128)(2,1)} %get-tuple-element.168), channel_id=1, source_target_pairs={{0,8},{1,9},{2,10},{3,11},{4,12},{5,13},{6,14},{7,15},{8,0},{9,1},... | collective-permute-start | bytes 589832 | tf_op jit(solution)/shard_map/ppermute | solution.py:282
  171.7 1.1 collective-permute-start.29
  173.8 2.9 %collective-permute-done.29 = f32[128,128]{1,0:T(8,128)S(1)} collective-permute-done((f32[128,128]{1,0:T(8,128)S(1)}, f32[128,128]{1,0:T(8,128)S(1)}, u32[]{:S(2)}, u32[]{:S(2)}) %collective-permute-start.29) | collective-permute-done | bytes 65568 | tf_op jit(solution)/shard_map/ppermute | solution.py:282
  177.5 2.9 %collective-permute-done.24 = bf16[8,96,128]{2,1,0:T(8,128)(2,1)S(1)} collective-permute-done((bf16[8,96,128]{2,1,0:T(8,128)(2,1)}, bf16[8,96,128]{2,1,0:T(8,128)(2,1)S(1)}, u32[]{:S(2)}, u32[]{:S(2)}) %collective-permute-start.24) | collective-permute-done | bytes 196640 | tf_op jit(solution)/shard_map/ppermute | solution.py:282
  180.4 1.0 convert_add_fusion.4
  181.4 1.1 collective-permute-done.25
  182.5 1.2 convert_add_fusion.1
  183.8 4.7 %collective-permute-done.26 = bf16[8,96,384]{2,1,0:T(8,128)(2,1)S(1)} collective-permute-done((bf16[8,96,384]{2,1,0:T(8,128)(2,1)}, bf16[8,96,384]{2,1,0:T(8,128)(2,1)S(1)}, u32[]{:S(2)}, u32[]{:S(2)}) %collective-permute-start.26) | collective-permute-done | bytes 589856 | tf_op jit(solution)/shard_map/ppermute | solution.py:282
  188.6 1.2 collective-permute-start.34
  189.8 1.5 collective-permute-start.30
  192.0 1.0 collective-permute-start.32
  193.0 1.9 fusion.1
  194.9 2.5 %maximum_bitcast_fusion = f32[1,384,3072]{2,1,0:T(8,128)} fusion(f32[384,1536]{1,0:T(8,128)S(1)} %get-tuple-element.228, f32[384,1536]{1,0:T(8,128)S(1)} %get-tuple-element.227), kind=kLoop, calls=%fused_computation | loop fusion | flops 1179648 | bytes 9437184 | tf_op jit(solution)/shard_map/broadcast_in_dim | solution.py:949
  197.4 2.3 %collective-permute-done.34 = f32[128,128]{1,0:T(8,128)S(1)} collective-permute-done((f32[128,128]{1,0:T(8,128)S(1)}, f32[128,128]{1,0:T(8,128)S(1)}, u32[]{:S(2)}, u32[]{:S(2)}) %collective-permute-start.34) | collective-permute-done | bytes 65568 | tf_op jit(solution)/shard_map/ppermute | solution.py:280
  199.8 2.0 collective-permute-done.31
  201.9 1.0 collective-permute-done.32
  203.0 1.1 collective-permute-start.35
  204.1 2.4 %collective-permute-start.38 = (f32[128,128]{1,0:T(8,128)S(1)}, f32[128,128]{1,0:T(8,128)S(1)}, u32[]{:S(2)}, u32[]{:S(2)}) collective-permute-start(f32[128,128]{1,0:T(8,128)S(1)} %add.174), channel_id=1, source_target_pairs={{0,8},{1,9},{2,10},{3,11},{4,12},{5,13},{6,14},{7,15},{8,0},{9,1},... | collective-permute-start | bytes 196616 | tf_op jit(solution)/shard_map/ppermute | solution.py:282
  206.5 1.5 collective-permute-start.36
  209.2 2.5 %maximum_bitcast_fusion.1 = f32[1,3072,384]{2,1,0:T(8,128)} fusion(f32[1536,384]{1,0:T(8,128)S(1)} %get-tuple-element.226, f32[1536,384]{1,0:T(8,128)S(1)} %get-tuple-element.225), kind=kLoop, calls=%fused_computation.1 | loop fusion | flops 1179648 | bytes 9437184 | tf_op jit(solution)/shard_map/broadcast_in_dim | solution.py:950
  211.8 4.5 %collective-permute-done.37 = bf16[1,1,2,1,1,96,384]{6,5,4,3,2,1,0:T(8,128)(2,1)S(1)} collective-permute-done((bf16[1,1,2,1,1,96,384]{6,5,4,3,2,1,0:T(8,128)(2,1)S(1)}, bf16[1,1,2,1,1,96,384]{6,5,4,3,2,1,0:T(8,128)(2,1)S(1)}, u32[]{:S(2)}, u32[]{:S(2)}) %collective-permute-start.37) | collective-permute-done | bytes 147488 | tf_op jit(solution)/shard_map/ppermute | solution.py:282
  217.6 1.4 collective-permute-start.39
  219.7 2.0 collective-permute-start.41
  (176 shorter events, 23.5 us)
Async XLA Ops:
  1.4 11.7 %collective-permute-start.2 = (bf16[1,1,1,1,96,128]{5,4,3,2,1,0:T(8,128)(2,1)S(1)}, bf16[1,1,1,1,96,128]{5,4,3,2,1,0:T(8,128)(2,1)S(1)}, u32[]{:S(2)}, u32[]{:S(2)}) collective-permute-start(bf16[1,1,1,1,96,128]{5,4,3,2,1,0:T(8,128)(2,1)S(1)} %slice_bitcast_fusion.2), channel_id=1, source_target_pairs={{0,2},{1,3},{2,0},{3,1},{4,6},{5,7},{6,4},{7,5},{8,10},{9,11},{10,... | collective-permute-start | bytes 73736 | tf_op jit(solution)/shard_map/ppermute | solution.py:282
  5.1 8.6 %collective-permute-start = (bf16[1,1,1,1,96,256]{5,4,3,2,1,0:T(8,128)(2,1)S(1)}, bf16[1,1,1,1,96,256]{5,4,3,2,1,0:T(8,128)(2,1)S(1)}, u32[]{:S(2)}, u32[]{:S(2)}) collective-permute-start(bf16[1,1,1,1,96,256]{5,4,3,2,1,0:T(8,128)(2,1)S(1)} %slice_bitcast_fusion.1), channel_id=1, source_target_pairs={{0,16},{16,0},{1,17},{17,1},{2,18},{18,2},{3,19},{19,3},{4,20},{20... | collective-permute-start | bytes 147464 | tf_op jit(solution)/shard_map/ppermute | solution.py:280
  7.5 6.8 %collective-permute-start.4 = (bf16[1,1,1,1,96,384]{5,4,3,2,1,0:T(8,128)(2,1)S(1)}, bf16[1,1,1,1,96,384]{5,4,3,2,1,0:T(8,128)(2,1)S(1)}, u32[]{:S(2)}, u32[]{:S(2)}) collective-permute-start(bf16[1,1,1,1,96,384]{5,4,3,2,1,0:T(8,128)(2,1)S(1)} %slice_bitcast_fusion), channel_id=1, source_target_pairs={{0,8},{1,9},{2,10},{3,11},{4,12},{5,13},{6,14},{7,15},{8,0},{9,1},... | collective-permute-start | bytes 221192 | tf_op jit(solution)/shard_map/ppermute | solution.py:282
  13.0 20.9 %copy-start.2 = (bf16[384,1536]{1,0:T(8,128)(2,1)}, bf16[384,1536]{1,0:T(8,128)(2,1)S(1)}, u32[]{:S(2)}) copy-start(bf16[384,1536]{1,0:T(8,128)(2,1)S(1)} %get-tuple-element.122.in_near_ref) | copy-start | bytes 3538948
  13.1 4.5 %collective-permute-start.3 = (bf16[1,1,1,2,96,128]{5,4,3,2,1,0:T(8,128)(2,1)S(1)}, bf16[1,1,1,2,96,128]{5,4,3,2,1,0:T(8,128)(2,1)S(1)}, u32[]{:S(2)}, u32[]{:S(2)}) collective-permute-start(bf16[1,1,1,2,96,128]{5,4,3,2,1,0:T(8,128)(2,1)S(1)} %pad_maximum_fusion.11), channel_id=1, source_target_pairs={{0,16},{16,0},{1,17},{17,1},{2,18},{18,2},{3,19},{19,3},{4,20},{20... | collective-permute-start | bytes 147464 | tf_op jit(solution)/shard_map/ppermute | solution.py:280
  13.7 4.7 %collective-permute-start.1 = (bf16[2,1,1,1,96,256]{5,4,3,2,1,0:T(8,128)(2,1)S(1)}, bf16[2,1,1,1,96,256]{5,4,3,2,1,0:T(8,128)(2,1)S(1)}, u32[]{:S(2)}, u32[]{:S(2)}) collective-permute-start(bf16[2,1,1,1,96,256]{5,4,3,2,1,0:T(8,128)(2,1)S(1)} %pad_maximum_fusion.9), channel_id=1, source_target_pairs={{0,2},{1,3},{2,0},{3,1},{4,6},{5,7},{6,4},{7,5},{8,10},{9,11},{10,... | collective-permute-start | bytes 294920 | tf_op jit(solution)/shard_map/ppermute | solution.py:282
  14.4 5.2 %collective-permute-start.5 = (bf16[1,2,1,1,96,384]{5,4,3,2,1,0:T(8,128)(2,1)S(1)}, bf16[1,2,1,1,96,384]{5,4,3,2,1,0:T(8,128)(2,1)S(1)}, u32[]{:S(2)}, u32[]{:S(2)}) collective-permute-start(bf16[1,2,1,1,96,384]{5,4,3,2,1,0:T(8,128)(2,1)S(1)} %pad_maximum_fusion.8), channel_id=1, source_target_pairs={{0,16},{16,0},{1,17},{17,1},{2,18},{18,2},{3,19},{19,3},{4,20},{20... | collective-permute-start | bytes 442376 | tf_op jit(solution)/shard_map/ppermute | solution.py:280
  19.7 11.9 %collective-permute-start.7 = (bf16[2,1,1,2,96,128]{5,4,3,2,1,0:T(8,128)(2,1)S(1)}, bf16[2,1,1,2,96,128]{5,4,3,2,1,0:T(8,128)(2,1)S(1)}, u32[]{:S(2)}, u32[]{:S(2)}) collective-permute-start(bf16[2,1,1,2,96,128]{5,4,3,2,1,0:T(8,128)(2,1)S(1)} %pad_maximum_fusion.10), channel_id=1, source_target_pairs={{0,8},{1,9},{2,10},{3,11},{4,12},{5,13},{6,14},{7,15},{8,0},{9,1},... | collective-permute-start | bytes 294920 | tf_op jit(solution)/shard_map/ppermute | solution.py:282
  20.9 13.0 %collective-permute-start.6 = (bf16[2,1,1,2,96,256]{5,4,3,2,1,0:T(8,128)(2,1)S(1)}, bf16[2,1,1,2,96,256]{5,4,3,2,1,0:T(8,128)(2,1)S(1)}, u32[]{:S(2)}, u32[]{:S(2)}) collective-permute-start(bf16[2,1,1,2,96,256]{5,4,3,2,1,0:T(8,128)(2,1)S(1)} %pad_maximum_fusion.6), channel_id=1, source_target_pairs={{0,8},{1,9},{2,10},{3,11},{4,12},{5,13},{6,14},{7,15},{8,0},{9,1},... | collective-permute-start | bytes 589832 | tf_op jit(solution)/shard_map/ppermute | solution.py:282
  22.7 11.5 %collective-permute-start.8 = (bf16[2,2,1,1,96,384]{5,4,3,2,1,0:T(8,128)(2,1)S(1)}, bf16[2,2,1,1,96,384]{5,4,3,2,1,0:T(8,128)(2,1)S(1)}, u32[]{:S(2)}, u32[]{:S(2)}) collective-permute-start(bf16[2,2,1,1,96,384]{5,4,3,2,1,0:T(8,128)(2,1)S(1)} %pad_maximum_fusion.5), channel_id=1, source_target_pairs={{0,4},{1,5},{2,6},{3,7},{4,0},{5,1},{6,2},{7,3},{8,12},{9,13},{10,... | collective-permute-start | bytes 884744 | tf_op jit(solution)/shard_map/ppermute | solution.py:282
  24.2 26.7 %collective-permute-start.12 = (bf16[384,1536]{1,0:T(8,128)(2,1)S(1)}, bf16[384,1536]{1,0:T(8,128)(2,1)S(1)}, u32[]{:S(2)}, u32[]{:S(2)}) collective-permute-start(bf16[384,1536]{1,0:T(8,128)(2,1)S(1)} %get-tuple-element.122.in_near_ref), channel_id=1, source_target_pairs={{1,16},{3,18},{5,20},{7,22},{9,24},{11,26},{13,28},{15,30},{16,1},... | collective-permute-start | bytes 3538952 | tf_op jit(solution)/shard_map/ppermute | solution.py:769
  25.0 31.3 %collective-permute-start.16 = (bf16[384,1536]{1,0:T(8,128)(2,1)}, bf16[384,1536]{1,0:T(8,128)(2,1)}, u32[]{:S(2)}, u32[]{:S(2)}) collective-permute-start(bf16[384,1536]{1,0:T(8,128)(2,1)} %get-tuple-element.127), channel_id=1, source_target_pairs={{0,1},{1,17},{2,3},{3,19},{4,5},{5,21},{6,7},{7,23},{8,9},{9,25},{... | collective-permute-start | bytes 3538952 | tf_op jit(solution)/shard_map/ppermute | solution.py:770
  34.3 7.9 %collective-permute-start.10 = (bf16[2,2,1,2,96,128]{5,4,3,2,1,0:T(8,128)(2,1)S(1)}, bf16[2,2,1,2,96,128]{5,4,3,2,1,0:T(8,128)(2,1)S(1)}, u32[]{:S(2)}, u32[]{:S(2)}) collective-permute-start(bf16[2,2,1,2,96,128]{5,4,3,2,1,0:T(8,128)(2,1)S(1)} %pad_maximum_fusion.7), channel_id=1, source_target_pairs={{0,4},{1,5},{2,6},{3,7},{4,0},{5,1},{6,2},{7,3},{8,12},{9,13},{10,... | collective-permute-start | bytes 589832 | tf_op jit(solution)/shard_map/ppermute | solution.py:282
  34.7 13.5 %collective-permute-start.9 = (bf16[2,2,1,2,96,256]{5,4,3,2,1,0:T(8,128)(2,1)S(1)}, bf16[2,2,1,2,96,256]{5,4,3,2,1,0:T(8,128)(2,1)S(1)}, u32[]{:S(2)}, u32[]{:S(2)}) collective-permute-start(bf16[2,2,1,2,96,256]{5,4,3,2,1,0:T(8,128)(2,1)S(1)} %pad_maximum_fusion.3), channel_id=1, source_target_pairs={{0,4},{1,5},{2,6},{3,7},{4,0},{5,1},{6,2},{7,3},{8,12},{9,13},{10,... | collective-permute-start | bytes 1179656 | tf_op jit(solution)/shard_map/ppermute | solution.py:282
  36.4 13.2 %collective-permute-start.11 = (bf16[2,2,2,1,96,384]{5,4,3,2,1,0:T(8,128)(2,1)S(1)}, bf16[2,2,2,1,96,384]{5,4,3,2,1,0:T(8,128)(2,1)S(1)}, u32[]{:S(2)}, u32[]{:S(2)}) collective-permute-start(bf16[2,2,2,1,96,384]{5,4,3,2,1,0:T(8,128)(2,1)S(1)} %pad_maximum_fusion.2), channel_id=1, source_target_pairs={{0,2},{1,3},{2,0},{3,1},{4,6},{5,7},{6,4},{7,5},{8,10},{9,11},{10,... | collective-permute-start | bytes 1769480 | tf_op jit(solution)/shard_map/ppermute | solution.py:282
  39.3 11.7 %copy-start.3 = (bf16[1536,384]{1,0:T(8,128)(2,1)}, bf16[1536,384]{1,0:T(8,128)(2,1)S(1)}, u32[]{:S(2)}) copy-start(bf16[1536,384]{1,0:T(8,128)(2,1)S(1)} %get-tuple-element.138.out_near_ref) | copy-start | bytes 3538948
  48.4 6.6 %copy-start.28 = (bf16[768]{0:T(1024)(128)(2,1)S(1)}, bf16[768]{0:T(1024)(128)(2,1)}, u32[]{:S(2)}) copy-start(bf16[768]{0:T(1024)(128)(2,1)} %param.14) | copy-start | bytes 4612
  48.4 7.2 %copy-start.29 = (bf16[768]{0:T(1024)(128)(2,1)S(1)}, bf16[768]{0:T(1024)(128)(2,1)}, u32[]{:S(2)}) copy-start(bf16[768]{0:T(1024)(128)(2,1)} %param.15) | copy-start | bytes 4612
  51.0 6.6 %collective-permute-start.15 = (bf16[16,96,384]{2,1,0:T(8,128)(2,1)}, bf16[16,96,384]{2,1,0:T(8,128)(2,1)}, u32[]{:S(2)}, u32[]{:S(2)}) collective-permute-start(bf16[16,96,384]{2,1,0:T(8,128)(2,1)} %bitcast.16.rest_2_), channel_id=1, source_target_pairs={{0,1},{1,0},{2,3},{3,2},{4,5},{5,4},{6,7},{7,6},{8,9},{9,8},{10,11... | collective-permute-start | bytes 3538952 | tf_op jit(solution)/shard_map/ppermute | solution.py:282
  51.0 18.0 %collective-permute-start.17 = (bf16[1536,384]{1,0:T(8,128)(2,1)S(1)}, bf16[1536,384]{1,0:T(8,128)(2,1)S(1)}, u32[]{:S(2)}, u32[]{:S(2)}) collective-permute-start(bf16[1536,384]{1,0:T(8,128)(2,1)S(1)} %get-tuple-element.138.out_near_ref), channel_id=1, source_target_pairs={{1,16},{3,18},{5,20},{7,22},{9,24},{11,26},{13,28},{15,30},{16,1},... | collective-permute-start | bytes 3538952 | tf_op jit(solution)/shard_map/ppermute | solution.py:782
  51.7 5.9 %collective-permute-start.13 = (bf16[16,96,256]{2,1,0:T(8,128)(2,1)S(1)}, bf16[16,96,256]{2,1,0:T(8,128)(2,1)}, u32[]{:S(2)}, u32[]{:S(2)}) collective-permute-start(bf16[16,96,256]{2,1,0:T(8,128)(2,1)S(1)} %bitcast.85), channel_id=1, source_target_pairs={{0,1},{1,0},{2,3},{3,2},{4,5},{5,4},{6,7},{7,6},{8,9},{9,8},{10,11... | collective-permute-start | bytes 2359304 | tf_op jit(solution)/shard_map/ppermute | solution.py:282
  54.9 2.7 %collective-permute-start.14 = (bf16[16,96,128]{2,1,0:T(8,128)(2,1)}, bf16[16,96,128]{2,1,0:T(8,128)(2,1)S(1)}, u32[]{:S(2)}, u32[]{:S(2)}) collective-permute-start(bf16[16,96,128]{2,1,0:T(8,128)(2,1)} %bitcast.15.rest_1_), channel_id=1, source_target_pairs={{0,1},{1,0},{2,3},{3,2},{4,5},{5,4},{6,7},{7,6},{8,9},{9,8},{10,11... | collective-permute-start | bytes 1179656 | tf_op jit(solution)/shard_map/ppermute | solution.py:282
  69.0 24.7 %all-to-all-start = ((bf16[16,10,1536]{2,1,0:T(8,128)(2,1)}), bf16[16,10,1536]{2,1,0:T(8,128)(2,1)S(1)}, u32[]{:S(2)}, u32[]{:S(2)}) async-start(bf16[16,10,1536]{2,1,0:T(8,128)(2,1)} %get-tuple-element.140), calls=%async_computation | async-start | bytes 1572864 | tf_op jit(solution)/shard_map/all_to_all | solution.py:730
  73.0 24.2 %collective-permute-start.19 = (bf16[1536,384]{1,0:T(8,128)(2,1)}, bf16[1536,384]{1,0:T(8,128)(2,1)S(1)}, u32[]{:S(2)}, u32[]{:S(2)}) collective-permute-start(bf16[1536,384]{1,0:T(8,128)(2,1)} %get-tuple-element.144), channel_id=1, source_target_pairs={{0,1},{1,17},{2,3},{3,19},{4,5},{5,21},{6,7},{7,23},{8,9},{9,25},{... | collective-permute-start | bytes 3538952 | tf_op jit(solution)/shard_map/ppermute | solution.py:817
  94.0 3.2 %collective-permute-start.18 = (bf16[160,1536]{1,0:T(8,128)(2,1)S(1)}, bf16[160,1536]{1,0:T(8,128)(2,1)S(1)}, u32[]{:S(2)}, u32[]{:S(2)}) collective-permute-start(bf16[160,1536]{1,0:T(8,128)(2,1)S(1)} %reshape.98.own_ref), channel_id=1, source_target_pairs={{0,1},{1,0},{2,3},{3,2},{4,5},{5,4},{6,7},{7,6},{8,9},{9,8},{10,11... | collective-permute-start | bytes 1474568 | tf_op jit(solution)/shard_map/ppermute | solution.py:282
  106.9 3.4 %collective-permute-start.20 = (f32[2,160,768]{2,1,0:T(8,128)}, f32[2,160,768]{2,1,0:T(8,128)S(1)}, u32[]{:S(2)}, u32[]{:S(2)}) collective-permute-start(f32[2,160,768]{2,1,0:T(8,128)} %get-tuple-element.146), channel_id=1, source_target_pairs={{0,1},{1,0},{2,3},{3,2},{4,5},{5,4},{6,7},{7,6},{8,9},{9,8},{10,11... | collective-permute-start | bytes 2949128 | tf_op jit(solution)/shard_map/ppermute | solution.py:282
  107.0 6.7 %copy-start.17 = (bf16[320,1536]{1,0:T(8,128)(2,1)S(1)}, bf16[320,1536]{1,0:T(8,128)(2,1)}, u32[]{:S(2)}) copy-start(bf16[320,1536]{1,0:T(8,128)(2,1)} %get-tuple-element.154) | copy-start | bytes 2949124
  107.0 6.7 %copy-start.24 = (bf16[320,768]{1,0:T(8,128)(2,1)S(1)}, bf16[320,768]{1,0:T(8,128)(2,1)}, u32[]{:S(2)}) copy-start(bf16[320,768]{1,0:T(8,128)(2,1)} %get-tuple-element.155) | copy-start | bytes 1474564
  110.2 36.1 %collective-permute-start.21 = (bf16[384,1536]{1,0:T(8,128)(2,1)}, bf16[384,1536]{1,0:T(8,128)(2,1)S(1)}, u32[]{:S(2)}, u32[]{:S(2)}) collective-permute-start(bf16[384,1536]{1,0:T(8,128)(2,1)} %convolution_convert_fusion.1), channel_id=1, source_target_pairs={{0,16},{1,0},{2,18},{3,2},{4,20},{5,4},{6,22},{7,6},{8,24},{9,8},{... | collective-permute-start | bytes 3538952 | tf_op jit(solution)/shard_map/ppermute | solution.py:859
  115.6 30.7 %collective-permute-start.22 = (bf16[1536,384]{1,0:T(8,128)(2,1)}, bf16[1536,384]{1,0:T(8,128)(2,1)S(1)}, u32[]{:S(2)}, u32[]{:S(2)}) collective-permute-start(bf16[1536,384]{1,0:T(8,128)(2,1)} %convolution_convert_fusion), channel_id=1, source_target_pairs={{0,16},{1,0},{2,18},{3,2},{4,20},{5,4},{6,22},{7,6},{8,24},{9,8},{... | collective-permute-start | bytes 3538952 | tf_op jit(solution)/shard_map/ppermute | solution.py:862
  115.7 29.6 %all-to-all-start.1 = ((bf16[16,10,1536]{2,1,0:T(8,128)(2,1)}), bf16[16,10,1536]{2,1,0:T(8,128)(2,1)S(1)}, u32[]{:S(2)}, u32[]{:S(2)}) async-start(bf16[16,10,1536]{2,1,0:T(8,128)(2,1)} %get-tuple-element.153), calls=%async_computation.1 | async-start | bytes 1572864 | tf_op jit(solution)/shard_map/all_to_all | solution.py:730
  146.3 8.1 %copy-start.10 = (bf16[384,1536]{1,0:T(8,128)(2,1)}, bf16[384,1536]{1,0:T(8,128)(2,1)S(1)}, u32[]{:S(2)}) copy-start(bf16[384,1536]{1,0:T(8,128)(2,1)S(1)} %collective-permute-done.21) | copy-start | bytes 3538948
  154.4 9.9 %collective-permute-start.23 = (bf16[1536,768]{1,0:T(8,128)(2,1)}, bf16[1536,768]{1,0:T(8,128)(2,1)S(1)}, u32[]{:S(2)}, u32[]{:S(2)}) collective-permute-start(bf16[1536,768]{1,0:T(8,128)(2,1)} %get-tuple-element.166), channel_id=1, source_target_pairs={{0,1},{1,0},{2,3},{3,2},{4,5},{5,4},{6,7},{7,6},{8,9},{9,8},{10,11... | collective-permute-start | bytes 7077896 | tf_op jit(solution)/shard_map/ppermute | solution.py:282
  156.2 32.4 %collective-permute-start.27 = (bf16[384,1536]{1,0:T(8,128)(2,1)}, bf16[384,1536]{1,0:T(8,128)(2,1)}, u32[]{:S(2)}, u32[]{:S(2)}) collective-permute-start(bf16[384,1536]{1,0:T(8,128)(2,1)} %get-tuple-element.173), channel_id=1, source_target_pairs={{1,16},{3,18},{5,20},{7,22},{9,24},{11,26},{13,28},{15,30},{16,1},... | collective-permute-start | bytes 3538952 | tf_op jit(solution)/shard_map/ppermute | solution.py:867
  162.9 8.5 %copy-start.21 = (bf16[768,16]{0,1:T(8,128)(2,1)S(1)}, bf16[768,16]{0,1:T(8,128)(2,1)}, u32[]{:S(2)}) copy-start(bf16[768,16]{0,1:T(8,128)(2,1)} %param.17) | copy-start | bytes 73732
  162.9 8.5 %copy-start.22 = (bf16[128,768]{1,0:T(8,128)(2,1)S(1)}, bf16[128,768]{1,0:T(8,128)(2,1)}, u32[]{:S(2)}) copy-start(bf16[128,768]{1,0:T(8,128)(2,1)} %get-tuple-element.194) | copy-start | bytes 589828
  162.9 8.7 %copy-start.25 = (f32[128,128]{1,0:T(8,128)S(1)}, f32[128,128]{1,0:T(8,128)}, u32[]{:S(2)}) copy-start(f32[128,128]{1,0:T(8,128)} %get-tuple-element.182) | copy-start | bytes 196612
  162.9 13.8 %copy-start.15 = (bf16[1536,384]{1,0:T(8,128)(2,1)S(1)}, bf16[1536,384]{1,0:T(8,128)(2,1)}, u32[]{:S(2)}) copy-start(bf16[1536,384]{1,0:T(8,128)(2,1)} %get-tuple-element.186) | copy-start | bytes 3538948
  163.0 8.7 %collective-permute-start.28 = (f32[128,128]{1,0:T(8,128)}, f32[128,128]{1,0:T(8,128)S(1)}, u32[]{:S(2)}, u32[]{:S(2)}) collective-permute-start(f32[128,128]{1,0:T(8,128)} %get-tuple-element.182), channel_id=1, source_target_pairs={{0,1},{1,0},{2,3},{3,2},{4,5},{5,4},{6,7},{7,6},{8,9},{9,8},{10,11... | collective-permute-start | bytes 196616 | tf_op jit(solution)/shard_map/ppermute | solution.py:282
  168.1 20.4 %copy-start.16 = (f32[8,96,384]{2,1,0:T(8,128)S(1)}, f32[8,96,384]{2,1,0:T(8,128)}, u32[]{:S(2)}) copy-start(f32[8,96,384]{2,1,0:T(8,128)} %get-tuple-element.171) | copy-start | bytes 3538948
  168.1 12.3 %collective-permute-start.24 = (bf16[8,96,128]{2,1,0:T(8,128)(2,1)}, bf16[8,96,128]{2,1,0:T(8,128)(2,1)S(1)}, u32[]{:S(2)}, u32[]{:S(2)}) collective-permute-start(bf16[8,96,128]{2,1,0:T(8,128)(2,1)} %get-tuple-element.168), channel_id=1, source_target_pairs={{0,8},{1,9},{2,10},{3,11},{4,12},{5,13},{6,14},{7,15},{8,0},{9,1},... | collective-permute-start | bytes 589832 | tf_op jit(solution)/shard_map/ppermute | solution.py:282
  170.8 11.8 %collective-permute-start.25 = (bf16[8,96,256]{2,1,0:T(8,128)(2,1)}, bf16[8,96,256]{2,1,0:T(8,128)(2,1)S(1)}, u32[]{:S(2)}, u32[]{:S(2)}) collective-permute-start(bf16[8,96,256]{2,1,0:T(8,128)(2,1)} %get-tuple-element.170), channel_id=1, source_target_pairs={{0,16},{16,0},{1,17},{17,1},{2,18},{18,2},{3,19},{19,3},{4,20},{20... | collective-permute-start | bytes 1179656 | tf_op jit(solution)/shard_map/ppermute | solution.py:280
  171.7 5.0 %collective-permute-start.29 = (f32[128,128]{1,0:T(8,128)S(1)}, f32[128,128]{1,0:T(8,128)S(1)}, u32[]{:S(2)}, u32[]{:S(2)}) collective-permute-start(f32[128,128]{1,0:T(8,128)S(1)} %add.163), channel_id=1, source_target_pairs={{0,2},{1,3},{2,0},{3,1},{4,6},{5,7},{6,4},{7,5},{8,10},{9,11},{10,... | collective-permute-start | bytes 196616 | tf_op jit(solution)/shard_map/ppermute | solution.py:282
  172.8 15.7 %collective-permute-start.26 = (bf16[8,96,384]{2,1,0:T(8,128)(2,1)}, bf16[8,96,384]{2,1,0:T(8,128)(2,1)S(1)}, u32[]{:S(2)}, u32[]{:S(2)}) collective-permute-start(bf16[8,96,384]{2,1,0:T(8,128)(2,1)} %get-tuple-element.172), channel_id=1, source_target_pairs={{0,2},{1,3},{2,0},{3,1},{4,6},{5,7},{6,4},{7,5},{8,10},{9,11},{10,... | collective-permute-start | bytes 1769480 | tf_op jit(solution)/shard_map/ppermute | solution.py:282
  176.7 26.2 %collective-permute-start.33 = (bf16[1536,384]{1,0:T(8,128)(2,1)S(1)}, bf16[1536,384]{1,0:T(8,128)(2,1)S(1)}, u32[]{:S(2)}, u32[]{:S(2)}) collective-permute-start(bf16[1536,384]{1,0:T(8,128)(2,1)S(1)} %copy-done.15), channel_id=1, source_target_pairs={{1,16},{3,18},{5,20},{7,22},{9,24},{11,26},{13,28},{15,30},{16,1},... | collective-permute-start | bytes 3538952 | tf_op jit(solution)/shard_map/ppermute | solution.py:868
  183.8 9.3 %copy-start.1 = (f32[384,1536]{1,0:T(8,128)S(1)}, f32[384,1536]{1,0:T(8,128)}, u32[]{:S(2)}) copy-start(f32[384,1536]{1,0:T(8,128)} %get-tuple-element.201) | copy-start | bytes 7077892
  183.8 9.2 %copy-start.11 = (bf16[384,1536]{1,0:T(8,128)(2,1)S(1)}, bf16[384,1536]{1,0:T(8,128)(2,1)}, u32[]{:S(2)}) copy-start(bf16[384,1536]{1,0:T(8,128)(2,1)} %copy-done.10) | copy-start | bytes 3538948
  188.6 11.1 %collective-permute-start.34 = (f32[128,128]{1,0:T(8,128)S(1)}, f32[128,128]{1,0:T(8,128)S(1)}, u32[]{:S(2)}, u32[]{:S(2)}) collective-permute-start(f32[128,128]{1,0:T(8,128)S(1)} %add.164), channel_id=1, source_target_pairs={{0,16},{16,0},{1,17},{17,1},{2,18},{18,2},{3,19},{19,3},{4,20},{20... | collective-permute-start | bytes 196616 | tf_op jit(solution)/shard_map/ppermute | solution.py:280
  189.8 9.9 %collective-permute-start.30 = (bf16[2,1,1,2,1,96,128]{6,5,4,3,2,1,0:T(8,128)(2,1)S(1)}, bf16[2,1,1,2,1,96,128]{6,5,4,3,2,1,0:T(8,128)(2,1)S(1)}, u32[]{:S(2)}, u32[]{:S(2)}) collective-permute-start(bf16[2,1,1,2,1,96,128]{6,5,4,3,2,1,0:T(8,128)(2,1)S(1)} %dynamic-slice_convert_fusion.4), channel_id=1, source_target_pairs={{0,4},{1,5},{2,6},{3,7},{4,0},{5,1},{6,2},{7,3},{8,12},{9,13},{10,... | collective-permute-start | bytes 294920 | tf_op jit(solution)/shard_map/ppermute | solution.py:282
  191.4 10.5 %collective-permute-start.31 = (bf16[1,1,2,2,1,96,256]{6,5,4,3,2,1,0:T(8,128)(2,1)S(1)}, bf16[1,1,2,2,1,96,256]{6,5,4,3,2,1,0:T(8,128)(2,1)S(1)}, u32[]{:S(2)}, u32[]{:S(2)}) collective-permute-start(bf16[1,1,2,2,1,96,256]{6,5,4,3,2,1,0:T(8,128)(2,1)S(1)} %dynamic-slice_convert_fusion.1), channel_id=1, source_target_pairs={{0,8},{1,9},{2,10},{3,11},{4,12},{5,13},{6,14},{7,15},{8,0},{9,1},... | collective-permute-start | bytes 589832 | tf_op jit(solution)/shard_map/ppermute | solution.py:282
  192.0 10.9 %collective-permute-start.32 = (bf16[1,2,2,1,1,96,384]{6,5,4,3,2,1,0:T(8,128)(2,1)S(1)}, bf16[1,2,2,1,1,96,384]{6,5,4,3,2,1,0:T(8,128)(2,1)S(1)}, u32[]{:S(2)}, u32[]{:S(2)}) collective-permute-start(bf16[1,2,2,1,1,96,384]{6,5,4,3,2,1,0:T(8,128)(2,1)S(1)} %dynamic-slice_convert_fusion), channel_id=1, source_target_pairs={{0,16},{16,0},{1,17},{17,1},{2,18},{18,2},{3,19},{19,3},{4,20},{20... | collective-permute-start | bytes 884744 | tf_op jit(solution)/shard_map/ppermute | solution.py:280
  197.4 11.3 %copy-start = (f32[1536,384]{1,0:T(8,128)S(1)}, f32[1536,384]{1,0:T(8,128)}, u32[]{:S(2)}) copy-start(f32[1536,384]{1,0:T(8,128)} %get-tuple-element.204) | copy-start | bytes 7077892
  203.0 8.7 %collective-permute-start.35 = (bf16[2,1,1,1,1,96,128]{6,5,4,3,2,1,0:T(8,128)(2,1)S(1)}, bf16[2,1,1,1,1,96,128]{6,5,4,3,2,1,0:T(8,128)(2,1)S(1)}, u32[]{:S(2)}, u32[]{:S(2)}) collective-permute-start(bf16[2,1,1,1,1,96,128]{6,5,4,3,2,1,0:T(8,128)(2,1)S(1)} %dynamic-slice_convert_fusion.7), channel_id=1, source_target_pairs={{0,2},{1,3},{2,0},{3,1},{4,6},{5,7},{6,4},{7,5},{8,10},{9,11},{10,... | collective-permute-start | bytes 147464 | tf_op jit(solution)/shard_map/ppermute | solution.py:282
  204.1 7.6 %collective-permute-start.38 = (f32[128,128]{1,0:T(8,128)S(1)}, f32[128,128]{1,0:T(8,128)S(1)}, u32[]{:S(2)}, u32[]{:S(2)}) collective-permute-start(f32[128,128]{1,0:T(8,128)S(1)} %add.174), channel_id=1, source_target_pairs={{0,8},{1,9},{2,10},{3,11},{4,12},{5,13},{6,14},{7,15},{8,0},{9,1},... | collective-permute-start | bytes 196616 | tf_op jit(solution)/shard_map/ppermute | solution.py:282
  206.5 5.2 %collective-permute-start.36 = (bf16[1,1,1,2,1,96,256]{6,5,4,3,2,1,0:T(8,128)(2,1)S(1)}, bf16[1,1,1,2,1,96,256]{6,5,4,3,2,1,0:T(8,128)(2,1)S(1)}, u32[]{:S(2)}, u32[]{:S(2)}) collective-permute-start(bf16[1,1,1,2,1,96,256]{6,5,4,3,2,1,0:T(8,128)(2,1)S(1)} %dynamic-slice_convert_fusion.3), channel_id=1, source_target_pairs={{0,4},{1,5},{2,6},{3,7},{4,0},{5,1},{6,2},{7,3},{8,12},{9,13},{10,... | collective-permute-start | bytes 294920 | tf_op jit(solution)/shard_map/ppermute | solution.py:282
  208.1 8.2 %collective-permute-start.37 = (bf16[1,1,2,1,1,96,384]{6,5,4,3,2,1,0:T(8,128)(2,1)S(1)}, bf16[1,1,2,1,1,96,384]{6,5,4,3,2,1,0:T(8,128)(2,1)S(1)}, u32[]{:S(2)}, u32[]{:S(2)}) collective-permute-start(bf16[1,1,2,1,1,96,384]{6,5,4,3,2,1,0:T(8,128)(2,1)S(1)} %dynamic-slice_convert_fusion.2), channel_id=1, source_target_pairs={{0,8},{1,9},{2,10},{3,11},{4,12},{5,13},{6,14},{7,15},{8,0},{9,1},... | collective-permute-start | bytes 442376 | tf_op jit(solution)/shard_map/ppermute | solution.py:282
  209.2 7.7 %copy-start.27 = (s32[2,1,64]{2,1,0:T(1,128)S(1)}, s32[2,1,64]{2,1,0:T(1,128)}, u32[]{:S(2)}) copy-start(s32[2,1,64]{2,1,0:T(1,128)} %routes_ref) | copy-start | bytes 1540
  209.2 12.5 %copy-start.7 = (bf16[160,1536]{1,0:T(8,128)(2,1)S(1)}, bf16[160,1536]{1,0:T(8,128)(2,1)}, u32[]{:S(2)}) copy-start(bf16[160,1536]{1,0:T(8,128)(2,1)} %reshape.99.dn2_ref) | copy-start | bytes 1474564
  209.2 12.5 %copy-start.9 = (f32[128,768]{1,0:T(8,128)S(1)}, f32[128,768]{1,0:T(8,128)}, u32[]{:S(2)}) copy-start(f32[128,768]{1,0:T(8,128)} %get-tuple-element.136.resid_ref) | copy-start | bytes 1179652
  209.2 12.5 %copy-start.23 = (bf16[160,128]{1,0:T(8,128)(2,1)S(1)}, bf16[160,128]{1,0:T(8,128)(2,1)}, u32[]{:S(2)}) copy-start(bf16[160,128]{1,0:T(8,128)(2,1)} %get-tuple-element.159.dispatch_ref) | copy-start | bytes 122884
  217.6 5.1 %collective-permute-start.39 = (bf16[1,1,1,1,1,96,128]{6,5,4,3,2,1,0:T(8,128)(2,1)S(1)}, bf16[1,1,1,1,1,96,128]{6,5,4,3,2,1,0:T(8,128)(2,1)S(1)}, u32[]{:S(2)}, u32[]{:S(2)}) collective-permute-start(bf16[1,1,1,1,1,96,128]{6,5,4,3,2,1,0:T(8,128)(2,1)S(1)} %dynamic-slice_convert_fusion.8), channel_id=1, source_target_pairs={{0,16},{16,0},{1,17},{17,1},{2,18},{18,2},{3,19},{19,3},{4,20},{20... | collective-permute-start | bytes 73736 | tf_op jit(solution)/shard_map/ppermute | solution.py:280
  219.1 4.1 %collective-permute-start.40 = (bf16[1,1,1,1,1,96,256]{6,5,4,3,2,1,0:T(8,128)(2,1)S(1)}, bf16[1,1,1,1,1,96,256]{6,5,4,3,2,1,0:T(8,128)(2,1)S(1)}, u32[]{:S(2)}, u32[]{:S(2)}) collective-permute-start(bf16[1,1,1,1,1,96,256]{6,5,4,3,2,1,0:T(8,128)(2,1)S(1)} %dynamic-slice_convert_fusion.6), channel_id=1, source_target_pairs={{0,2},{1,3},{2,0},{3,1},{4,6},{5,7},{6,4},{7,5},{8,10},{9,11},{10,... | collective-permute-start | bytes 147464 | tf_op jit(solution)/shard_map/ppermute | solution.py:282
  219.6 4.3 %collective-permute-start.42 = (f32[128,128]{1,0:T(8,128)S(1)}, f32[128,128]{1,0:T(8,128)S(1)}, u32[]{:S(2)}, u32[]{:S(2)}) collective-permute-start(f32[128,128]{1,0:T(8,128)S(1)} %add.180), channel_id=1, source_target_pairs={{0,4},{1,5},{2,6},{3,7},{4,0},{5,1},{6,2},{7,3},{8,12},{9,13},{10,... | collective-permute-start | bytes 196616 | tf_op jit(solution)/shard_map/ppermute | solution.py:282
  219.7 6.1 %collective-permute-start.41 = (bf16[1,1,1,1,1,96,384]{6,5,4,3,2,1,0:T(8,128)(2,1)S(1)}, bf16[1,1,1,1,1,96,384]{6,5,4,3,2,1,0:T(8,128)(2,1)S(1)}, u32[]{:S(2)}, u32[]{:S(2)}) collective-permute-start(bf16[1,1,1,1,1,96,384]{6,5,4,3,2,1,0:T(8,128)(2,1)S(1)} %dynamic-slice_convert_fusion.5), channel_id=1, source_target_pairs={{0,4},{1,5},{2,6},{3,7},{4,0},{5,1},{6,2},{7,3},{8,12},{9,13},{10,... | collective-permute-start | bytes 221192 | tf_op jit(solution)/shard_map/ppermute | solution.py:282
  (11 other events, 37.1 us)

commit v5 on v4

--- a/solution.py
+++ b/solution.py
@@ -865,7 +865,6 @@
         (home_rows, in_homely, out_homely, in_mine.astype(bf16), out_mine.astype(bf16))
     )
     in_arrived = lax.ppermute(in_leave, BOTH, across)
-    out_arrived = lax.ppermute(out_leave, BOTH, across)
 
     dresid, gain_two_part, dqkv, fold, send, keep = call(
         attend_back_kernel,
@@ -905,6 +904,8 @@
         place, keep, n1b, mixed_b, got,
         free=(4,),
     )
+    cut, out_leave = lax.optimization_barrier((cut, out_leave))
+    out_arrived = lax.ppermute(out_leave, BOTH, across)
     attn_share, small, late = scatter_rows(
         cut[:3],
         cut[3:],

time: 227 us -> 227 us (level)
  no operation moved by 1% of the time
where the time goes in v5:
time: 227 us
  waiting for transfers between devices  79.4 us (35%)
  starting transfers between devices  61.8 us (27%)
  Pallas kernels  43.5 us (19%)
  other arithmetic  14.1 us (6%)
  local copies, waits for them, and re-layouts  13.4 us (6%)
  matrix products  13 us (6%)
    pallas_call x7, Pallas kernels, call(): pl.pallas_call(kernel, grid=(1,), out_shape=tuple((pltpu.HBM(*out) for ou...  43.5 us
    all_to_all x2, waiting for transfers between devices, to_chips(): lax.all_to_all(tensor, BOTH, split_axis=0, concat_axis=0, tiled=True, axi...  36.7 us
    ppermute x28, starting transfers between devices, flip(): return lax.ppermute(tensor, 'expert', [(i, i ^ bit) for i in range(count)])  36.2 us
    ppermute x28, waiting for transfers between devices, flip(): return lax.ppermute(tensor, 'expert', [(i, i ^ bit) for i in range(count)])  32.4 us
    dot_general x6, matrix products, dot(): lax.dot_general(left, right, (dims, ((), ())), preferred_element_type=jnp...  13 us
    all_to_all x2, starting transfers between devices, to_chips(): lax.all_to_all(tensor, BOTH, split_axis=0, concat_axis=0, tiled=True, axi...  10.6 us
    ppermute x7, starting transfers between devices, flip(): return lax.ppermute(tensor, 'dp', [(0, 1), (1, 0)])  7.95 us
    ppermute x7, waiting for transfers between devices, flip(): return lax.ppermute(tensor, 'dp', [(0, 1), (1, 0)])  7.18 us
  transfers between devices with their start and end apart: 45, of which 22 were waited for; matrix products, arithmetic and copies ran while one was open for 16% of the time, Pallas kernels for 12%

profile of v5, /device:TPU:0, one launch (start us, length us, event | category | flops | bytes accessed | tf_op | source)
XLA Modules:
  0.0 226.6 jit_solution(3335269570912336164)
XLA Ops:
  1.4 2.9 %collective-permute-start.2 = (bf16[1,1,1,1,96,128]{5,4,3,2,1,0:T(8,128)(2,1)S(1)}, bf16[1,1,1,1,96,128]{5,4,3,2,1,0:T(8,128)(2,1)S(1)}, u32[]{:S(2)}, u32[]{:S(2)}) collective-permute-start(bf16[1,1,1,1,96,128]{5,4,3,2,1,0:T(8,128)(2,1)S(1)} %slice_bitcast_fusion.2), channel_id=1, source_target_pairs={{0,2},{1,3},{2,0},{3,1},{4,6},{5,7},{6,4},{7,5},{8,10},{9,11},{10,... | collective-permute-start | bytes 73736 | tf_op jit(solution)/shard_map/ppermute | solution.py:282
  5.1 1.5 collective-permute-start
  7.5 2.6 %collective-permute-start.4 = (bf16[1,1,1,1,96,384]{5,4,3,2,1,0:T(8,128)(2,1)S(1)}, bf16[1,1,1,1,96,384]{5,4,3,2,1,0:T(8,128)(2,1)S(1)}, u32[]{:S(2)}, u32[]{:S(2)}) collective-permute-start(bf16[1,1,1,1,96,384]{5,4,3,2,1,0:T(8,128)(2,1)S(1)} %slice_bitcast_fusion), channel_id=1, source_target_pairs={{0,8},{1,9},{2,10},{3,11},{4,12},{5,13},{6,14},{7,15},{8,0},{9,1},... | collective-permute-start | bytes 221192 | tf_op jit(solution)/shard_map/ppermute | solution.py:282
  10.1 2.8 %dynamic-slice_bitcast_fusion = (bf16[384,1536]{1,0:T(8,128)(2,1)}, bf16[384,1536]{1,0:T(8,128)(2,1)S(1)}) fusion(bf16[1,384,3072]{2,1,0:T(8,128)(2,1)} %param.18, s32[]{:T(128)S(6)} %select_n.349, s32[]{:T(128)S(6)} %select_n.348), kind=kLoop, calls=%fused_computation.16 | loop fusion | bytes 4718600 | tf_op jit(solution)/shard_map/dynamic_slice | solution.py:738
  14.4 1.6 collective-permute-start.5
  16.0 1.6 collective-permute-done.3
  18.5 1.1 collective-permute-done.5
  19.7 1.2 collective-permute-start.7
  20.9 1.8 collective-permute-start.6
  22.7 1.6 collective-permute-start.8
  25.0 2.8 %collective-permute-start.16 = (bf16[384,1536]{1,0:T(8,128)(2,1)}, bf16[384,1536]{1,0:T(8,128)(2,1)}, u32[]{:S(2)}, u32[]{:S(2)}) collective-permute-start(bf16[384,1536]{1,0:T(8,128)(2,1)} %get-tuple-element.134), channel_id=1, source_target_pairs={{0,1},{1,17},{2,3},{3,19},{4,5},{5,21},{6,7},{7,23},{8,9},{9,25},{... | collective-permute-start | bytes 3538952 | tf_op jit(solution)/shard_map/ppermute | solution.py:770
  27.8 3.7 %shard_map.187 = (f32[12,128,128]{2,1,0:T(8,128)}, s32[64,128]{1,0:T(8,128)}, bf16[160,128]{1,0:T(8,128)(2,1)}, bf16[256,128]{1,0:T(8,128)(2,1)}) custom-call(f32[32,12]{1,0:T(8,128)S(1)} %convert_element_type.99.table_ref, s32[64,64]{1,0:T(8,128)} %buckets_ref, s32[2,1,64]{2,1,0:T(1,128)} %routes_ref, s32[2,1,64]{2,1,0:T(1,128)} %slots_ref), custom_call_target="tpu_custom_call" | custom-call | tf_op jit(solution)/shard_map/pallas_call | solution.py:368
  31.6 2.2 collective-permute-done.6
  34.7 1.8 collective-permute-start.9
  36.4 1.6 collective-permute-start.11
  38.1 1.2 constant_dynamic-slice_fusion
  39.3 3.0 %collective-permute-done.10 = bf16[2,2,1,2,96,128]{5,4,3,2,1,0:T(8,128)(2,1)S(1)} collective-permute-done((bf16[2,2,1,2,96,128]{5,4,3,2,1,0:T(8,128)(2,1)S(1)}, bf16[2,2,1,2,96,128]{5,4,3,2,1,0:T(8,128)(2,1)S(1)}, u32[]{:S(2)}, u32[]{:S(2)}) %collective-permute-start.10) | collective-permute-done | bytes 196640 | tf_op jit(solution)/shard_map/ppermute | solution.py:282
  43.1 5.1 %collective-permute-done.9 = bf16[2,2,1,2,96,256]{5,4,3,2,1,0:T(8,128)(2,1)S(1)} collective-permute-done((bf16[2,2,1,2,96,256]{5,4,3,2,1,0:T(8,128)(2,1)S(1)}, bf16[2,2,1,2,96,256]{5,4,3,2,1,0:T(8,128)(2,1)S(1)}, u32[]{:S(2)}, u32[]{:S(2)}) %collective-permute-start.9) | collective-permute-done | bytes 393248 | tf_op jit(solution)/shard_map/ppermute | solution.py:282
  48.4 1.3 collective-permute-done.11
  49.8 1.1 pad_maximum_fusion
  51.7 3.2 %collective-permute-start.13 = (bf16[16,96,256]{2,1,0:T(8,128)(2,1)S(1)}, bf16[16,96,256]{2,1,0:T(8,128)(2,1)}, u32[]{:S(2)}, u32[]{:S(2)}) collective-permute-start(bf16[16,96,256]{2,1,0:T(8,128)(2,1)S(1)} %bitcast.85), channel_id=1, source_target_pairs={{0,1},{1,0},{2,3},{3,2},{4,5},{5,4},{6,7},{7,6},{8,9},{9,8},{10,11... | collective-permute-start | bytes 2359304 | tf_op jit(solution)/shard_map/ppermute | solution.py:282
  56.2 1.3 collective-permute-done.14.rest_4_
  58.3 10.7 %shard_map.188 = (bf16[12,2,96,768]{3,2,1,0:T(8,128)(2,1)}, bf16[4,2,96,768]{3,2,1,0:T(8,128)(2,1)}, bf16[128,768]{1,0:T(8,128)(2,1)}, bf16[2304,128]{1,0:T(8,12...) custom-call(s32[6]{0:T(128)S(1)} %stack.31.place_ref.core_ref._, ...), custom_call_target="tpu_custom_call" | custom-call | tf_op jit(solution)/shard_map/pallas_call | solution.py:368
  69.0 3.9 %all-to-all-start = ((bf16[16,10,1536]{2,1,0:T(8,128)(2,1)}), bf16[16,10,1536]{2,1,0:T(8,128)(2,1)S(1)}, u32[]{:S(2)}, u32[]{:S(2)}) async-start(bf16[16,10,1536]{2,1,0:T(8,128)(2,1)} %get-tuple-element.147), calls=%async_computation | async-start | bytes 1572864 | tf_op jit(solution)/shard_map/all_to_all | solution.py:730
  73.2 20.5 %all-to-all-done = bf16[16,10,1536]{2,1,0:T(8,128)(2,1)S(1)} async-done(((bf16[16,10,1536]{2,1,0:T(8,128)(2,1)}), bf16[16,10,1536]{2,1,0:T(8,128)(2,1)S(1)}, u32[]{:S(2)}, u32[]{:S(2)}) %all-to-all-start) | async-done | bytes 491552 | tf_op jit(solution)/shard_map/all_to_all | solution.py:730
  94.0 3.1 %collective-permute-done.19.out_far_ref = bf16[1536,384]{1,0:T(8,128)(2,1)S(1)} collective-permute-done((bf16[1536,384]{1,0:T(8,128)(2,1)}, bf16[1536,384]{1,0:T(8,128)(2,1)S(1)}, u32[]{:S(2)}, u32[]{:S(2)}) %collective-permute-start.19) | collective-permute-done | bytes 1179680 | tf_op jit(solution)/shard_map/ppermute | solution.py:817
  97.1 1.0 copy-done.14
  98.1 8.7 %shard_map.189 = (bf16[320,768]{1,0:T(8,128)(2,1)}, bf16[320,1536]{1,0:T(8,128)(2,1)}, bf16[320,1536]{1,0:T(8,128)(2,1)}, bf16[320,768]{1,0:T(8,128)(2,1)}, f32[...) custom-call(s32[6]{0:T(128)S(1)} %stack.31.place_ref.core_ref._, bf16[160,1536]{1,0:T(8,128)(2,1)} %copy-done.4, ...), custom_call_target="tpu_custom_call" | custom-call | tf_op jit(solution)/shard_map/pallas_call | solution.py:368
  107.0 3.2 %convolution_convert_fusion.1 = bf16[384,1536]{1,0:T(8,128)(2,1)} fusion(bf16[320,1536]{1,0:T(8,128)(2,1)} %get-tuple-element.164, bf16[320,768]{1,0:T(8,128)(2,1)} %get-tuple-element.163, s32[]{:T(128)S(6)} %select_n.366), kind=kOutput, calls=%fused_computation.7 | convolution fusion | flops 378077184 | bytes 2408452 | tf_op jit(solution)/shard_map/dot_general | solution.py:351
  110.2 3.4 %shard_map.190 = (bf16[16,10,1536]{2,1,0:T(8,128)(2,1)}, f32[16,768]{1,0:T(8,128)}) custom-call(s32[6]{0:T(128)S(1)} %stack.31.place_ref.core_ref._, f32[2,160,768]{2,1,0:T(8,128)} %get-tuple-element.152.mine_ref, f32[2,160,768]{2,1,0:T(8,128)S(1)} %collective-permute-done.20.got_ref, bf16[160,1536]{1,0:T(8,128)(2,1)} %copy-done.4, ...), custom_call_target="tpu_custom_call" | custom-call | tf_op jit(solution)/shard_map/pallas_call | solution.py:368
  113.7 2.0 convolution_convert_fusion
  115.7 6.7 %all-to-all-start.1 = ((bf16[16,10,1536]{2,1,0:T(8,128)(2,1)}), bf16[16,10,1536]{2,1,0:T(8,128)(2,1)S(1)}, u32[]{:S(2)}, u32[]{:S(2)}) async-start(bf16[16,10,1536]{2,1,0:T(8,128)(2,1)} %get-tuple-element.160), calls=%async_computation.1 | async-start | bytes 1572864 | tf_op jit(solution)/shard_map/all_to_all | solution.py:730
  122.5 4.1 %fusion.19 = (bf16[1536,384]{1,0:T(8,128)(2,1)}, f32[1536,384]{1,0:T(8,128)}) fusion(bf16[320,1536]{1,0:T(8,128)(2,1)} %get-tuple-element.161, bf16[320,768]{1,0:T(8,128)(2,1)} %get-tuple-element.162, s32[]{:T(128)S(6)} %select_n.367), kind=kOutput, calls=%fused_computation.100 | convolution fusion | flops 378077184 | bytes 4767748 | tf_op jit(solution)/shard_map/dot_general | solution.py:351
  126.6 2.6 %fusion.18 = (bf16[384,1536]{1,0:T(8,128)(2,1)}, f32[384,1536]{1,0:T(8,128)}) fusion(bf16[320,1536]{1,0:T(8,128)(2,1)S(1)} %copy-done.5, bf16[320,768]{1,0:T(8,128)(2,1)S(1)} %copy-done.19, s32[]{:T(128)S(6)} %select_n.367), kind=kOutput, calls=%fused_computation.99 | convolution fusion | flops 378077184 | bytes 4767748 | tf_op jit(solution)/shard_map/dot_general | solution.py:351
  129.2 16.1 %all-to-all-done.1 = bf16[16,10,1536]{2,1,0:T(8,128)(2,1)S(1)} async-done(((bf16[16,10,1536]{2,1,0:T(8,128)(2,1)}), bf16[16,10,1536]{2,1,0:T(8,128)(2,1)S(1)}, u32[]{:S(2)}, u32[]{:S(2)}) %all-to-all-start.1) | async-done | bytes 491552 | tf_op jit(solution)/shard_map/all_to_all | solution.py:730
  146.3 8.1 %shard_map.191 = (f32[128,768]{1,0:T(8,128)}, f32[1,768]{1,0:T(1,128)}, bf16[2304,128]{1,0:T(8,128)(2,1)}, f32[12,64,128]{2,1,0:T(8,128)}, bf16[1536,768]{1,0:T(8,128)(2,1)}, /*index=5*/bf16[1536,128]{1,0:T(8,128)(2,1)}) custom-call(s32[6]{0:T(128)S(1)} %stack.31.place_ref.core_ref._, bf16[160,1536]{1,0:T(8,128)(2,1)} %reshape.99.dn2_ref, ...), custom_call_target="tpu_custom_call" | custom-call | tf_op jit(solution)/shard_map/pallas_call | solution.py:368
  154.4 1.8 collective-permute-start.23
  156.2 1.7 collective-permute-start.27
  157.9 5.1 %shard_map.193 = (f32[128,768]{1,0:T(8,128)}, f32[128,128]{1,0:T(8,128)}) custom-call(s32[6]{0:T(128)S(1)} %stack.31.place_ref.core_ref._, bf16[128,768]{1,0:T(8,128)(2,1)} %bitcast.96, bf16[2304,128]{1,0:T(8,128)(2,1)} %get-tuple-element.189.dqkv_ref, bf16[2304,768]{1,0:T(8,128)(2,1)} %bitcast.84, f32[1,768]{1,0:T(1,128)} %reshape.113.rest_6_.gain_one_ref, ...), custom_call_target="tpu_custom_call" | custom-call | tf_op jit(solution)/shard_map/pallas_call | solution.py:368
  163.0 1.4 collective-permute-start.28
  164.3 3.7 %shard_map.192 = (bf16[8,96,128]{2,1,0:T(8,128)(2,1)}, bf16[8,96,256]{2,1,0:T(8,128)(2,1)}, bf16[8,96,384]{2,1,0:T(8,128)(2,1)}, f32[8,96,128]{2,1,0:T(8,128)}, ...) custom-call(s32[6]{0:T(128)S(1)} %stack.31.place_ref.core_ref._, bf16[1536,128]{1,0:T(8,128)(2,1)} %get-tuple-element.172.keep_ref, ...), custom_call_target="tpu_custom_call" | custom-call | tf_op jit(solution)/shard_map/pallas_call | solution.py:368
  168.1 2.7 %collective-permute-start.24 = (bf16[8,96,128]{2,1,0:T(8,128)(2,1)}, bf16[8,96,128]{2,1,0:T(8,128)(2,1)S(1)}, u32[]{:S(2)}, u32[]{:S(2)}) collective-permute-start(bf16[8,96,128]{2,1,0:T(8,128)(2,1)} %get-tuple-element.182), channel_id=1, source_target_pairs={{0,8},{1,9},{2,10},{3,11},{4,12},{5,13},{6,14},{7,15},{8,0},{9,1},... | collective-permute-start | bytes 589832 | tf_op jit(solution)/shard_map/ppermute | solution.py:282
  171.7 1.1 collective-permute-start.29
  173.8 2.9 %collective-permute-done.29 = f32[128,128]{1,0:T(8,128)S(1)} collective-permute-done((f32[128,128]{1,0:T(8,128)S(1)}, f32[128,128]{1,0:T(8,128)S(1)}, u32[]{:S(2)}, u32[]{:S(2)}) %collective-permute-start.29) | collective-permute-done | bytes 65568 | tf_op jit(solution)/shard_map/ppermute | solution.py:282
  177.5 2.9 %collective-permute-done.24 = bf16[8,96,128]{2,1,0:T(8,128)(2,1)S(1)} collective-permute-done((bf16[8,96,128]{2,1,0:T(8,128)(2,1)}, bf16[8,96,128]{2,1,0:T(8,128)(2,1)S(1)}, u32[]{:S(2)}, u32[]{:S(2)}) %collective-permute-start.24) | collective-permute-done | bytes 196640 | tf_op jit(solution)/shard_map/ppermute | solution.py:282
  180.4 1.0 convert_add_fusion.4
  181.4 1.1 collective-permute-done.25
  182.5 1.2 convert_add_fusion.1
  183.8 4.7 %collective-permute-done.26 = bf16[8,96,384]{2,1,0:T(8,128)(2,1)S(1)} collective-permute-done((bf16[8,96,384]{2,1,0:T(8,128)(2,1)}, bf16[8,96,384]{2,1,0:T(8,128)(2,1)S(1)}, u32[]{:S(2)}, u32[]{:S(2)}) %collective-permute-start.26) | collective-permute-done | bytes 589856 | tf_op jit(solution)/shard_map/ppermute | solution.py:282
  188.6 1.2 collective-permute-start.34
  189.8 1.5 collective-permute-start.30
  192.0 1.0 collective-permute-start.32
  193.0 1.9 fusion.1
  194.9 2.5 %maximum_bitcast_fusion = f32[1,384,3072]{2,1,0:T(8,128)} fusion(f32[384,1536]{1,0:T(8,128)S(1)} %get-tuple-element.242, f32[384,1536]{1,0:T(8,128)S(1)} %get-tuple-element.241), kind=kLoop, calls=%fused_computation | loop fusion | flops 1179648 | bytes 9437184 | tf_op jit(solution)/shard_map/broadcast_in_dim | solution.py:950
  197.4 2.3 %collective-permute-done.34 = f32[128,128]{1,0:T(8,128)S(1)} collective-permute-done((f32[128,128]{1,0:T(8,128)S(1)}, f32[128,128]{1,0:T(8,128)S(1)}, u32[]{:S(2)}, u32[]{:S(2)}) %collective-permute-start.34) | collective-permute-done | bytes 65568 | tf_op jit(solution)/shard_map/ppermute | solution.py:280
  199.8 2.0 collective-permute-done.31
  201.9 1.0 collective-permute-done.32
  203.0 1.1 collective-permute-start.35
  204.1 2.4 %collective-permute-start.38 = (f32[128,128]{1,0:T(8,128)S(1)}, f32[128,128]{1,0:T(8,128)S(1)}, u32[]{:S(2)}, u32[]{:S(2)}) collective-permute-start(f32[128,128]{1,0:T(8,128)S(1)} %add.174), channel_id=1, source_target_pairs={{0,8},{1,9},{2,10},{3,11},{4,12},{5,13},{6,14},{7,15},{8,0},{9,1},... | collective-permute-start | bytes 196616 | tf_op jit(solution)/shard_map/ppermute | solution.py:282
  206.5 1.5 collective-permute-start.36
  209.2 2.5 %maximum_bitcast_fusion.1 = f32[1,3072,384]{2,1,0:T(8,128)} fusion(f32[1536,384]{1,0:T(8,128)S(1)} %get-tuple-element.240, f32[1536,384]{1,0:T(8,128)S(1)} %get-tuple-element.239), kind=kLoop, calls=%fused_computation.1 | loop fusion | flops 1179648 | bytes 9437184 | tf_op jit(solution)/shard_map/broadcast_in_dim | solution.py:951
  211.8 4.5 %collective-permute-done.37 = bf16[1,1,2,1,1,96,384]{6,5,4,3,2,1,0:T(8,128)(2,1)S(1)} collective-permute-done((bf16[1,1,2,1,1,96,384]{6,5,4,3,2,1,0:T(8,128)(2,1)S(1)}, bf16[1,1,2,1,1,96,384]{6,5,4,3,2,1,0:T(8,128)(2,1)S(1)}, u32[]{:S(2)}, u32[]{:S(2)}) %collective-permute-start.37) | collective-permute-done | bytes 147488 | tf_op jit(solution)/shard_map/ppermute | solution.py:282
  217.6 1.4 collective-permute-start.39
  219.7 2.0 collective-permute-start.41
  (176 shorter events, 23.5 us)
Async XLA Ops:
  1.4 11.7 %collective-permute-start.2 = (bf16[1,1,1,1,96,128]{5,4,3,2,1,0:T(8,128)(2,1)S(1)}, bf16[1,1,1,1,96,128]{5,4,3,2,1,0:T(8,128)(2,1)S(1)}, u32[]{:S(2)}, u32[]{:S(2)}) collective-permute-start(bf16[1,1,1,1,96,128]{5,4,3,2,1,0:T(8,128)(2,1)S(1)} %slice_bitcast_fusion.2), channel_id=1, source_target_pairs={{0,2},{1,3},{2,0},{3,1},{4,6},{5,7},{6,4},{7,5},{8,10},{9,11},{10,... | collective-permute-start | bytes 73736 | tf_op jit(solution)/shard_map/ppermute | solution.py:282
  5.1 8.6 %collective-permute-start = (bf16[1,1,1,1,96,256]{5,4,3,2,1,0:T(8,128)(2,1)S(1)}, bf16[1,1,1,1,96,256]{5,4,3,2,1,0:T(8,128)(2,1)S(1)}, u32[]{:S(2)}, u32[]{:S(2)}) collective-permute-start(bf16[1,1,1,1,96,256]{5,4,3,2,1,0:T(8,128)(2,1)S(1)} %slice_bitcast_fusion.1), channel_id=1, source_target_pairs={{0,16},{16,0},{1,17},{17,1},{2,18},{18,2},{3,19},{19,3},{4,20},{20... | collective-permute-start | bytes 147464 | tf_op jit(solution)/shard_map/ppermute | solution.py:280
  7.5 6.8 %collective-permute-start.4 = (bf16[1,1,1,1,96,384]{5,4,3,2,1,0:T(8,128)(2,1)S(1)}, bf16[1,1,1,1,96,384]{5,4,3,2,1,0:T(8,128)(2,1)S(1)}, u32[]{:S(2)}, u32[]{:S(2)}) collective-permute-start(bf16[1,1,1,1,96,384]{5,4,3,2,1,0:T(8,128)(2,1)S(1)} %slice_bitcast_fusion), channel_id=1, source_target_pairs={{0,8},{1,9},{2,10},{3,11},{4,12},{5,13},{6,14},{7,15},{8,0},{9,1},... | collective-permute-start | bytes 221192 | tf_op jit(solution)/shard_map/ppermute | solution.py:282
  13.0 20.9 %copy-start.2 = (bf16[384,1536]{1,0:T(8,128)(2,1)}, bf16[384,1536]{1,0:T(8,128)(2,1)S(1)}, u32[]{:S(2)}) copy-start(bf16[384,1536]{1,0:T(8,128)(2,1)S(1)} %get-tuple-element.129.in_near_ref) | copy-start | bytes 3538948
  13.1 4.5 %collective-permute-start.3 = (bf16[1,1,1,2,96,128]{5,4,3,2,1,0:T(8,128)(2,1)S(1)}, bf16[1,1,1,2,96,128]{5,4,3,2,1,0:T(8,128)(2,1)S(1)}, u32[]{:S(2)}, u32[]{:S(2)}) collective-permute-start(bf16[1,1,1,2,96,128]{5,4,3,2,1,0:T(8,128)(2,1)S(1)} %pad_maximum_fusion.11), channel_id=1, source_target_pairs={{0,16},{16,0},{1,17},{17,1},{2,18},{18,2},{3,19},{19,3},{4,20},{20... | collective-permute-start | bytes 147464 | tf_op jit(solution)/shard_map/ppermute | solution.py:280
  13.7 4.7 %collective-permute-start.1 = (bf16[2,1,1,1,96,256]{5,4,3,2,1,0:T(8,128)(2,1)S(1)}, bf16[2,1,1,1,96,256]{5,4,3,2,1,0:T(8,128)(2,1)S(1)}, u32[]{:S(2)}, u32[]{:S(2)}) collective-permute-start(bf16[2,1,1,1,96,256]{5,4,3,2,1,0:T(8,128)(2,1)S(1)} %pad_maximum_fusion.9), channel_id=1, source_target_pairs={{0,2},{1,3},{2,0},{3,1},{4,6},{5,7},{6,4},{7,5},{8,10},{9,11},{10,... | collective-permute-start | bytes 294920 | tf_op jit(solution)/shard_map/ppermute | solution.py:282
  14.4 5.2 %collective-permute-start.5 = (bf16[1,2,1,1,96,384]{5,4,3,2,1,0:T(8,128)(2,1)S(1)}, bf16[1,2,1,1,96,384]{5,4,3,2,1,0:T(8,128)(2,1)S(1)}, u32[]{:S(2)}, u32[]{:S(2)}) collective-permute-start(bf16[1,2,1,1,96,384]{5,4,3,2,1,0:T(8,128)(2,1)S(1)} %pad_maximum_fusion.8), channel_id=1, source_target_pairs={{0,16},{16,0},{1,17},{17,1},{2,18},{18,2},{3,19},{19,3},{4,20},{20... | collective-permute-start | bytes 442376 | tf_op jit(solution)/shard_map/ppermute | solution.py:280
  19.7 11.9 %collective-permute-start.7 = (bf16[2,1,1,2,96,128]{5,4,3,2,1,0:T(8,128)(2,1)S(1)}, bf16[2,1,1,2,96,128]{5,4,3,2,1,0:T(8,128)(2,1)S(1)}, u32[]{:S(2)}, u32[]{:S(2)}) collective-permute-start(bf16[2,1,1,2,96,128]{5,4,3,2,1,0:T(8,128)(2,1)S(1)} %pad_maximum_fusion.10), channel_id=1, source_target_pairs={{0,8},{1,9},{2,10},{3,11},{4,12},{5,13},{6,14},{7,15},{8,0},{9,1},... | collective-permute-start | bytes 294920 | tf_op jit(solution)/shard_map/ppermute | solution.py:282
  20.9 13.0 %collective-permute-start.6 = (bf16[2,1,1,2,96,256]{5,4,3,2,1,0:T(8,128)(2,1)S(1)}, bf16[2,1,1,2,96,256]{5,4,3,2,1,0:T(8,128)(2,1)S(1)}, u32[]{:S(2)}, u32[]{:S(2)}) collective-permute-start(bf16[2,1,1,2,96,256]{5,4,3,2,1,0:T(8,128)(2,1)S(1)} %pad_maximum_fusion.6), channel_id=1, source_target_pairs={{0,8},{1,9},{2,10},{3,11},{4,12},{5,13},{6,14},{7,15},{8,0},{9,1},... | collective-permute-start | bytes 589832 | tf_op jit(solution)/shard_map/ppermute | solution.py:282
  22.7 11.5 %collective-permute-start.8 = (bf16[2,2,1,1,96,384]{5,4,3,2,1,0:T(8,128)(2,1)S(1)}, bf16[2,2,1,1,96,384]{5,4,3,2,1,0:T(8,128)(2,1)S(1)}, u32[]{:S(2)}, u32[]{:S(2)}) collective-permute-start(bf16[2,2,1,1,96,384]{5,4,3,2,1,0:T(8,128)(2,1)S(1)} %pad_maximum_fusion.5), channel_id=1, source_target_pairs={{0,4},{1,5},{2,6},{3,7},{4,0},{5,1},{6,2},{7,3},{8,12},{9,13},{10,... | collective-permute-start | bytes 884744 | tf_op jit(solution)/shard_map/ppermute | solution.py:282
  24.2 26.7 %collective-permute-start.12 = (bf16[384,1536]{1,0:T(8,128)(2,1)S(1)}, bf16[384,1536]{1,0:T(8,128)(2,1)S(1)}, u32[]{:S(2)}, u32[]{:S(2)}) collective-permute-start(bf16[384,1536]{1,0:T(8,128)(2,1)S(1)} %get-tuple-element.129.in_near_ref), channel_id=1, source_target_pairs={{1,16},{3,18},{5,20},{7,22},{9,24},{11,26},{13,28},{15,30},{16,1},... | collective-permute-start | bytes 3538952 | tf_op jit(solution)/shard_map/ppermute | solution.py:769
  25.0 31.3 %collective-permute-start.16 = (bf16[384,1536]{1,0:T(8,128)(2,1)}, bf16[384,1536]{1,0:T(8,128)(2,1)}, u32[]{:S(2)}, u32[]{:S(2)}) collective-permute-start(bf16[384,1536]{1,0:T(8,128)(2,1)} %get-tuple-element.134), channel_id=1, source_target_pairs={{0,1},{1,17},{2,3},{3,19},{4,5},{5,21},{6,7},{7,23},{8,9},{9,25},{... | collective-permute-start | bytes 3538952 | tf_op jit(solution)/shard_map/ppermute | solution.py:770
  34.3 7.9 %collective-permute-start.10 = (bf16[2,2,1,2,96,128]{5,4,3,2,1,0:T(8,128)(2,1)S(1)}, bf16[2,2,1,2,96,128]{5,4,3,2,1,0:T(8,128)(2,1)S(1)}, u32[]{:S(2)}, u32[]{:S(2)}) collective-permute-start(bf16[2,2,1,2,96,128]{5,4,3,2,1,0:T(8,128)(2,1)S(1)} %pad_maximum_fusion.7), channel_id=1, source_target_pairs={{0,4},{1,5},{2,6},{3,7},{4,0},{5,1},{6,2},{7,3},{8,12},{9,13},{10,... | collective-permute-start | bytes 589832 | tf_op jit(solution)/shard_map/ppermute | solution.py:282
  34.7 13.5 %collective-permute-start.9 = (bf16[2,2,1,2,96,256]{5,4,3,2,1,0:T(8,128)(2,1)S(1)}, bf16[2,2,1,2,96,256]{5,4,3,2,1,0:T(8,128)(2,1)S(1)}, u32[]{:S(2)}, u32[]{:S(2)}) collective-permute-start(bf16[2,2,1,2,96,256]{5,4,3,2,1,0:T(8,128)(2,1)S(1)} %pad_maximum_fusion.3), channel_id=1, source_target_pairs={{0,4},{1,5},{2,6},{3,7},{4,0},{5,1},{6,2},{7,3},{8,12},{9,13},{10,... | collective-permute-start | bytes 1179656 | tf_op jit(solution)/shard_map/ppermute | solution.py:282
  36.4 13.2 %collective-permute-start.11 = (bf16[2,2,2,1,96,384]{5,4,3,2,1,0:T(8,128)(2,1)S(1)}, bf16[2,2,2,1,96,384]{5,4,3,2,1,0:T(8,128)(2,1)S(1)}, u32[]{:S(2)}, u32[]{:S(2)}) collective-permute-start(bf16[2,2,2,1,96,384]{5,4,3,2,1,0:T(8,128)(2,1)S(1)} %pad_maximum_fusion.2), channel_id=1, source_target_pairs={{0,2},{1,3},{2,0},{3,1},{4,6},{5,7},{6,4},{7,5},{8,10},{9,11},{10,... | collective-permute-start | bytes 1769480 | tf_op jit(solution)/shard_map/ppermute | solution.py:282
  39.3 11.7 %copy-start.3 = (bf16[1536,384]{1,0:T(8,128)(2,1)}, bf16[1536,384]{1,0:T(8,128)(2,1)S(1)}, u32[]{:S(2)}) copy-start(bf16[1536,384]{1,0:T(8,128)(2,1)S(1)} %get-tuple-element.145.out_near_ref) | copy-start | bytes 3538948
  48.4 6.6 %copy-start.28 = (bf16[768]{0:T(1024)(128)(2,1)S(1)}, bf16[768]{0:T(1024)(128)(2,1)}, u32[]{:S(2)}) copy-start(bf16[768]{0:T(1024)(128)(2,1)} %param.14) | copy-start | bytes 4612
  48.4 7.2 %copy-start.29 = (bf16[768]{0:T(1024)(128)(2,1)S(1)}, bf16[768]{0:T(1024)(128)(2,1)}, u32[]{:S(2)}) copy-start(bf16[768]{0:T(1024)(128)(2,1)} %param.15) | copy-start | bytes 4612
  51.0 6.6 %collective-permute-start.15 = (bf16[16,96,384]{2,1,0:T(8,128)(2,1)}, bf16[16,96,384]{2,1,0:T(8,128)(2,1)}, u32[]{:S(2)}, u32[]{:S(2)}) collective-permute-start(bf16[16,96,384]{2,1,0:T(8,128)(2,1)} %bitcast.16.rest_2_), channel_id=1, source_target_pairs={{0,1},{1,0},{2,3},{3,2},{4,5},{5,4},{6,7},{7,6},{8,9},{9,8},{10,11... | collective-permute-start | bytes 3538952 | tf_op jit(solution)/shard_map/ppermute | solution.py:282
  51.0 18.0 %collective-permute-start.17 = (bf16[1536,384]{1,0:T(8,128)(2,1)S(1)}, bf16[1536,384]{1,0:T(8,128)(2,1)S(1)}, u32[]{:S(2)}, u32[]{:S(2)}) collective-permute-start(bf16[1536,384]{1,0:T(8,128)(2,1)S(1)} %get-tuple-element.145.out_near_ref), channel_id=1, source_target_pairs={{1,16},{3,18},{5,20},{7,22},{9,24},{11,26},{13,28},{15,30},{16,1},... | collective-permute-start | bytes 3538952 | tf_op jit(solution)/shard_map/ppermute | solution.py:782
  51.7 5.9 %collective-permute-start.13 = (bf16[16,96,256]{2,1,0:T(8,128)(2,1)S(1)}, bf16[16,96,256]{2,1,0:T(8,128)(2,1)}, u32[]{:S(2)}, u32[]{:S(2)}) collective-permute-start(bf16[16,96,256]{2,1,0:T(8,128)(2,1)S(1)} %bitcast.85), channel_id=1, source_target_pairs={{0,1},{1,0},{2,3},{3,2},{4,5},{5,4},{6,7},{7,6},{8,9},{9,8},{10,11... | collective-permute-start | bytes 2359304 | tf_op jit(solution)/shard_map/ppermute | solution.py:282
  54.9 2.7 %collective-permute-start.14 = (bf16[16,96,128]{2,1,0:T(8,128)(2,1)}, bf16[16,96,128]{2,1,0:T(8,128)(2,1)S(1)}, u32[]{:S(2)}, u32[]{:S(2)}) collective-permute-start(bf16[16,96,128]{2,1,0:T(8,128)(2,1)} %bitcast.15.rest_1_), channel_id=1, source_target_pairs={{0,1},{1,0},{2,3},{3,2},{4,5},{5,4},{6,7},{7,6},{8,9},{9,8},{10,11... | collective-permute-start | bytes 1179656 | tf_op jit(solution)/shard_map/ppermute | solution.py:282
  69.0 24.7 %all-to-all-start = ((bf16[16,10,1536]{2,1,0:T(8,128)(2,1)}), bf16[16,10,1536]{2,1,0:T(8,128)(2,1)S(1)}, u32[]{:S(2)}, u32[]{:S(2)}) async-start(bf16[16,10,1536]{2,1,0:T(8,128)(2,1)} %get-tuple-element.147), calls=%async_computation | async-start | bytes 1572864 | tf_op jit(solution)/shard_map/all_to_all | solution.py:730
  73.0 24.2 %collective-permute-start.19 = (bf16[1536,384]{1,0:T(8,128)(2,1)}, bf16[1536,384]{1,0:T(8,128)(2,1)S(1)}, u32[]{:S(2)}, u32[]{:S(2)}) collective-permute-start(bf16[1536,384]{1,0:T(8,128)(2,1)} %get-tuple-element.151), channel_id=1, source_target_pairs={{0,1},{1,17},{2,3},{3,19},{4,5},{5,21},{6,7},{7,23},{8,9},{9,25},{... | collective-permute-start | bytes 3538952 | tf_op jit(solution)/shard_map/ppermute | solution.py:817
  94.0 3.2 %collective-permute-start.18 = (bf16[160,1536]{1,0:T(8,128)(2,1)S(1)}, bf16[160,1536]{1,0:T(8,128)(2,1)S(1)}, u32[]{:S(2)}, u32[]{:S(2)}) collective-permute-start(bf16[160,1536]{1,0:T(8,128)(2,1)S(1)} %reshape.98.own_ref), channel_id=1, source_target_pairs={{0,1},{1,0},{2,3},{3,2},{4,5},{5,4},{6,7},{7,6},{8,9},{9,8},{10,11... | collective-permute-start | bytes 1474568 | tf_op jit(solution)/shard_map/ppermute | solution.py:282
  106.9 3.4 %collective-permute-start.20 = (f32[2,160,768]{2,1,0:T(8,128)}, f32[2,160,768]{2,1,0:T(8,128)S(1)}, u32[]{:S(2)}, u32[]{:S(2)}) collective-permute-start(f32[2,160,768]{2,1,0:T(8,128)} %get-tuple-element.153), channel_id=1, source_target_pairs={{0,1},{1,0},{2,3},{3,2},{4,5},{5,4},{6,7},{7,6},{8,9},{9,8},{10,11... | collective-permute-start | bytes 2949128 | tf_op jit(solution)/shard_map/ppermute | solution.py:282
  107.0 6.7 %copy-start.17 = (bf16[320,1536]{1,0:T(8,128)(2,1)S(1)}, bf16[320,1536]{1,0:T(8,128)(2,1)}, u32[]{:S(2)}) copy-start(bf16[320,1536]{1,0:T(8,128)(2,1)} %get-tuple-element.161) | copy-start | bytes 2949124
  107.0 6.7 %copy-start.24 = (bf16[320,768]{1,0:T(8,128)(2,1)S(1)}, bf16[320,768]{1,0:T(8,128)(2,1)}, u32[]{:S(2)}) copy-start(bf16[320,768]{1,0:T(8,128)(2,1)} %get-tuple-element.162) | copy-start | bytes 1474564
  110.2 36.1 %collective-permute-start.21 = (bf16[384,1536]{1,0:T(8,128)(2,1)}, bf16[384,1536]{1,0:T(8,128)(2,1)S(1)}, u32[]{:S(2)}, u32[]{:S(2)}) collective-permute-start(bf16[384,1536]{1,0:T(8,128)(2,1)} %convolution_convert_fusion.1), channel_id=1, source_target_pairs={{0,16},{1,0},{2,18},{3,2},{4,20},{5,4},{6,22},{7,6},{8,24},{9,8},{... | collective-permute-start | bytes 3538952 | tf_op jit(solution)/shard_map/ppermute | solution.py:859
  115.6 30.7 %collective-permute-start.22 = (bf16[1536,384]{1,0:T(8,128)(2,1)}, bf16[1536,384]{1,0:T(8,128)(2,1)S(1)}, u32[]{:S(2)}, u32[]{:S(2)}) collective-permute-start(bf16[1536,384]{1,0:T(8,128)(2,1)} %convolution_convert_fusion), channel_id=1, source_target_pairs={{0,16},{1,0},{2,18},{3,2},{4,20},{5,4},{6,22},{7,6},{8,24},{9,8},{... | collective-permute-start | bytes 3538952 | tf_op jit(solution)/shard_map/ppermute | solution.py:862
  115.7 29.6 %all-to-all-start.1 = ((bf16[16,10,1536]{2,1,0:T(8,128)(2,1)}), bf16[16,10,1536]{2,1,0:T(8,128)(2,1)S(1)}, u32[]{:S(2)}, u32[]{:S(2)}) async-start(bf16[16,10,1536]{2,1,0:T(8,128)(2,1)} %get-tuple-element.160), calls=%async_computation.1 | async-start | bytes 1572864 | tf_op jit(solution)/shard_map/all_to_all | solution.py:730
  146.3 8.1 %copy-start.10 = (bf16[384,1536]{1,0:T(8,128)(2,1)}, bf16[384,1536]{1,0:T(8,128)(2,1)S(1)}, u32[]{:S(2)}) copy-start(bf16[384,1536]{1,0:T(8,128)(2,1)S(1)} %collective-permute-done.21) | copy-start | bytes 3538948
  154.4 9.9 %collective-permute-start.23 = (bf16[1536,768]{1,0:T(8,128)(2,1)}, bf16[1536,768]{1,0:T(8,128)(2,1)S(1)}, u32[]{:S(2)}, u32[]{:S(2)}) collective-permute-start(bf16[1536,768]{1,0:T(8,128)(2,1)} %get-tuple-element.173), channel_id=1, source_target_pairs={{0,1},{1,0},{2,3},{3,2},{4,5},{5,4},{6,7},{7,6},{8,9},{9,8},{10,11... | collective-permute-start | bytes 7077896 | tf_op jit(solution)/shard_map/ppermute | solution.py:282
  156.2 32.4 %collective-permute-start.27 = (bf16[384,1536]{1,0:T(8,128)(2,1)}, bf16[384,1536]{1,0:T(8,128)(2,1)}, u32[]{:S(2)}, u32[]{:S(2)}) collective-permute-start(bf16[384,1536]{1,0:T(8,128)(2,1)} %get-tuple-element.187), channel_id=1, source_target_pairs={{1,16},{3,18},{5,20},{7,22},{9,24},{11,26},{13,28},{15,30},{16,1},... | collective-permute-start | bytes 3538952 | tf_op jit(solution)/shard_map/ppermute | solution.py:867
  162.9 8.5 %copy-start.21 = (bf16[768,16]{0,1:T(8,128)(2,1)S(1)}, bf16[768,16]{0,1:T(8,128)(2,1)}, u32[]{:S(2)}) copy-start(bf16[768,16]{0,1:T(8,128)(2,1)} %param.17) | copy-start | bytes 73732
  162.9 8.5 %copy-start.22 = (bf16[128,768]{1,0:T(8,128)(2,1)S(1)}, bf16[128,768]{1,0:T(8,128)(2,1)}, u32[]{:S(2)}) copy-start(bf16[128,768]{1,0:T(8,128)(2,1)} %get-tuple-element.208) | copy-start | bytes 589828
  162.9 8.7 %copy-start.25 = (f32[128,128]{1,0:T(8,128)S(1)}, f32[128,128]{1,0:T(8,128)}, u32[]{:S(2)}) copy-start(f32[128,128]{1,0:T(8,128)} %get-tuple-element.196) | copy-start | bytes 196612
  162.9 13.8 %copy-start.15 = (bf16[1536,384]{1,0:T(8,128)(2,1)S(1)}, bf16[1536,384]{1,0:T(8,128)(2,1)}, u32[]{:S(2)}) copy-start(bf16[1536,384]{1,0:T(8,128)(2,1)} %get-tuple-element.200) | copy-start | bytes 3538948
  163.0 8.7 %collective-permute-start.28 = (f32[128,128]{1,0:T(8,128)}, f32[128,128]{1,0:T(8,128)S(1)}, u32[]{:S(2)}, u32[]{:S(2)}) collective-permute-start(f32[128,128]{1,0:T(8,128)} %get-tuple-element.196), channel_id=1, source_target_pairs={{0,1},{1,0},{2,3},{3,2},{4,5},{5,4},{6,7},{7,6},{8,9},{9,8},{10,11... | collective-permute-start | bytes 196616 | tf_op jit(solution)/shard_map/ppermute | solution.py:282
  168.1 20.4 %copy-start.16 = (f32[8,96,384]{2,1,0:T(8,128)S(1)}, f32[8,96,384]{2,1,0:T(8,128)}, u32[]{:S(2)}) copy-start(f32[8,96,384]{2,1,0:T(8,128)} %get-tuple-element.185) | copy-start | bytes 3538948
  168.1 12.3 %collective-permute-start.24 = (bf16[8,96,128]{2,1,0:T(8,128)(2,1)}, bf16[8,96,128]{2,1,0:T(8,128)(2,1)S(1)}, u32[]{:S(2)}, u32[]{:S(2)}) collective-permute-start(bf16[8,96,128]{2,1,0:T(8,128)(2,1)} %get-tuple-element.182), channel_id=1, source_target_pairs={{0,8},{1,9},{2,10},{3,11},{4,12},{5,13},{6,14},{7,15},{8,0},{9,1},... | collective-permute-start | bytes 589832 | tf_op jit(solution)/shard_map/ppermute | solution.py:282
  170.8 11.8 %collective-permute-start.25 = (bf16[8,96,256]{2,1,0:T(8,128)(2,1)}, bf16[8,96,256]{2,1,0:T(8,128)(2,1)S(1)}, u32[]{:S(2)}, u32[]{:S(2)}) collective-permute-start(bf16[8,96,256]{2,1,0:T(8,128)(2,1)} %get-tuple-element.184), channel_id=1, source_target_pairs={{0,16},{16,0},{1,17},{17,1},{2,18},{18,2},{3,19},{19,3},{4,20},{20... | collective-permute-start | bytes 1179656 | tf_op jit(solution)/shard_map/ppermute | solution.py:280
  171.7 5.0 %collective-permute-start.29 = (f32[128,128]{1,0:T(8,128)S(1)}, f32[128,128]{1,0:T(8,128)S(1)}, u32[]{:S(2)}, u32[]{:S(2)}) collective-permute-start(f32[128,128]{1,0:T(8,128)S(1)} %add.163), channel_id=1, source_target_pairs={{0,2},{1,3},{2,0},{3,1},{4,6},{5,7},{6,4},{7,5},{8,10},{9,11},{10,... | collective-permute-start | bytes 196616 | tf_op jit(solution)/shard_map/ppermute | solution.py:282
  172.8 15.7 %collective-permute-start.26 = (bf16[8,96,384]{2,1,0:T(8,128)(2,1)}, bf16[8,96,384]{2,1,0:T(8,128)(2,1)S(1)}, u32[]{:S(2)}, u32[]{:S(2)}) collective-permute-start(bf16[8,96,384]{2,1,0:T(8,128)(2,1)} %get-tuple-element.186), channel_id=1, source_target_pairs={{0,2},{1,3},{2,0},{3,1},{4,6},{5,7},{6,4},{7,5},{8,10},{9,11},{10,... | collective-permute-start | bytes 1769480 | tf_op jit(solution)/shard_map/ppermute | solution.py:282
  176.8 26.2 %collective-permute-start.33 = (bf16[1536,384]{1,0:T(8,128)(2,1)S(1)}, bf16[1536,384]{1,0:T(8,128)(2,1)S(1)}, u32[]{:S(2)}, u32[]{:S(2)}) collective-permute-start(bf16[1536,384]{1,0:T(8,128)(2,1)S(1)} %copy-done.15), channel_id=1, source_target_pairs={{1,16},{3,18},{5,20},{7,22},{9,24},{11,26},{13,28},{15,30},{16,1},... | collective-permute-start | bytes 3538952 | tf_op jit(solution)/shard_map/ppermute | solution.py:908
  183.8 9.3 %copy-start.1 = (f32[384,1536]{1,0:T(8,128)S(1)}, f32[384,1536]{1,0:T(8,128)}, u32[]{:S(2)}) copy-start(f32[384,1536]{1,0:T(8,128)} %get-tuple-element.215) | copy-start | bytes 7077892
  183.8 9.2 %copy-start.11 = (bf16[384,1536]{1,0:T(8,128)(2,1)S(1)}, bf16[384,1536]{1,0:T(8,128)(2,1)}, u32[]{:S(2)}) copy-start(bf16[384,1536]{1,0:T(8,128)(2,1)} %copy-done.10) | copy-start | bytes 3538948
  188.6 11.1 %collective-permute-start.34 = (f32[128,128]{1,0:T(8,128)S(1)}, f32[128,128]{1,0:T(8,128)S(1)}, u32[]{:S(2)}, u32[]{:S(2)}) collective-permute-start(f32[128,128]{1,0:T(8,128)S(1)} %add.164), channel_id=1, source_target_pairs={{0,16},{16,0},{1,17},{17,1},{2,18},{18,2},{3,19},{19,3},{4,20},{20... | collective-permute-start | bytes 196616 | tf_op jit(solution)/shard_map/ppermute | solution.py:280
  189.8 9.9 %collective-permute-start.30 = (bf16[2,1,1,2,1,96,128]{6,5,4,3,2,1,0:T(8,128)(2,1)S(1)}, bf16[2,1,1,2,1,96,128]{6,5,4,3,2,1,0:T(8,128)(2,1)S(1)}, u32[]{:S(2)}, u32[]{:S(2)}) collective-permute-start(bf16[2,1,1,2,1,96,128]{6,5,4,3,2,1,0:T(8,128)(2,1)S(1)} %dynamic-slice_convert_fusion.4), channel_id=1, source_target_pairs={{0,4},{1,5},{2,6},{3,7},{4,0},{5,1},{6,2},{7,3},{8,12},{9,13},{10,... | collective-permute-start | bytes 294920 | tf_op jit(solution)/shard_map/ppermute | solution.py:282
  191.4 10.5 %collective-permute-start.31 = (bf16[1,1,2,2,1,96,256]{6,5,4,3,2,1,0:T(8,128)(2,1)S(1)}, bf16[1,1,2,2,1,96,256]{6,5,4,3,2,1,0:T(8,128)(2,1)S(1)}, u32[]{:S(2)}, u32[]{:S(2)}) collective-permute-start(bf16[1,1,2,2,1,96,256]{6,5,4,3,2,1,0:T(8,128)(2,1)S(1)} %dynamic-slice_convert_fusion.1), channel_id=1, source_target_pairs={{0,8},{1,9},{2,10},{3,11},{4,12},{5,13},{6,14},{7,15},{8,0},{9,1},... | collective-permute-start | bytes 589832 | tf_op jit(solution)/shard_map/ppermute | solution.py:282
  192.0 10.9 %collective-permute-start.32 = (bf16[1,2,2,1,1,96,384]{6,5,4,3,2,1,0:T(8,128)(2,1)S(1)}, bf16[1,2,2,1,1,96,384]{6,5,4,3,2,1,0:T(8,128)(2,1)S(1)}, u32[]{:S(2)}, u32[]{:S(2)}) collective-permute-start(bf16[1,2,2,1,1,96,384]{6,5,4,3,2,1,0:T(8,128)(2,1)S(1)} %dynamic-slice_convert_fusion), channel_id=1, source_target_pairs={{0,16},{16,0},{1,17},{17,1},{2,18},{18,2},{3,19},{19,3},{4,20},{20... | collective-permute-start | bytes 884744 | tf_op jit(solution)/shard_map/ppermute | solution.py:280
  197.4 11.3 %copy-start = (f32[1536,384]{1,0:T(8,128)S(1)}, f32[1536,384]{1,0:T(8,128)}, u32[]{:S(2)}) copy-start(f32[1536,384]{1,0:T(8,128)} %get-tuple-element.218) | copy-start | bytes 7077892
  203.0 8.7 %collective-permute-start.35 = (bf16[2,1,1,1,1,96,128]{6,5,4,3,2,1,0:T(8,128)(2,1)S(1)}, bf16[2,1,1,1,1,96,128]{6,5,4,3,2,1,0:T(8,128)(2,1)S(1)}, u32[]{:S(2)}, u32[]{:S(2)}) collective-permute-start(bf16[2,1,1,1,1,96,128]{6,5,4,3,2,1,0:T(8,128)(2,1)S(1)} %dynamic-slice_convert_fusion.7), channel_id=1, source_target_pairs={{0,2},{1,3},{2,0},{3,1},{4,6},{5,7},{6,4},{7,5},{8,10},{9,11},{10,... | collective-permute-start | bytes 147464 | tf_op jit(solution)/shard_map/ppermute | solution.py:282
  204.1 7.6 %collective-permute-start.38 = (f32[128,128]{1,0:T(8,128)S(1)}, f32[128,128]{1,0:T(8,128)S(1)}, u32[]{:S(2)}, u32[]{:S(2)}) collective-permute-start(f32[128,128]{1,0:T(8,128)S(1)} %add.174), channel_id=1, source_target_pairs={{0,8},{1,9},{2,10},{3,11},{4,12},{5,13},{6,14},{7,15},{8,0},{9,1},... | collective-permute-start | bytes 196616 | tf_op jit(solution)/shard_map/ppermute | solution.py:282
  206.5 5.2 %collective-permute-start.36 = (bf16[1,1,1,2,1,96,256]{6,5,4,3,2,1,0:T(8,128)(2,1)S(1)}, bf16[1,1,1,2,1,96,256]{6,5,4,3,2,1,0:T(8,128)(2,1)S(1)}, u32[]{:S(2)}, u32[]{:S(2)}) collective-permute-start(bf16[1,1,1,2,1,96,256]{6,5,4,3,2,1,0:T(8,128)(2,1)S(1)} %dynamic-slice_convert_fusion.3), channel_id=1, source_target_pairs={{0,4},{1,5},{2,6},{3,7},{4,0},{5,1},{6,2},{7,3},{8,12},{9,13},{10,... | collective-permute-start | bytes 294920 | tf_op jit(solution)/shard_map/ppermute | solution.py:282
  208.1 8.2 %collective-permute-start.37 = (bf16[1,1,2,1,1,96,384]{6,5,4,3,2,1,0:T(8,128)(2,1)S(1)}, bf16[1,1,2,1,1,96,384]{6,5,4,3,2,1,0:T(8,128)(2,1)S(1)}, u32[]{:S(2)}, u32[]{:S(2)}) collective-permute-start(bf16[1,1,2,1,1,96,384]{6,5,4,3,2,1,0:T(8,128)(2,1)S(1)} %dynamic-slice_convert_fusion.2), channel_id=1, source_target_pairs={{0,8},{1,9},{2,10},{3,11},{4,12},{5,13},{6,14},{7,15},{8,0},{9,1},... | collective-permute-start | bytes 442376 | tf_op jit(solution)/shard_map/ppermute | solution.py:282
  209.2 7.7 %copy-start.27 = (s32[2,1,64]{2,1,0:T(1,128)S(1)}, s32[2,1,64]{2,1,0:T(1,128)}, u32[]{:S(2)}) copy-start(s32[2,1,64]{2,1,0:T(1,128)} %routes_ref) | copy-start | bytes 1540
  209.2 12.5 %copy-start.7 = (bf16[160,1536]{1,0:T(8,128)(2,1)S(1)}, bf16[160,1536]{1,0:T(8,128)(2,1)}, u32[]{:S(2)}) copy-start(bf16[160,1536]{1,0:T(8,128)(2,1)} %reshape.99.dn2_ref) | copy-start | bytes 1474564
  209.2 12.5 %copy-start.9 = (f32[128,768]{1,0:T(8,128)S(1)}, f32[128,768]{1,0:T(8,128)}, u32[]{:S(2)}) copy-start(f32[128,768]{1,0:T(8,128)} %get-tuple-element.143.resid_ref) | copy-start | bytes 1179652
  209.2 12.5 %copy-start.23 = (bf16[160,128]{1,0:T(8,128)(2,1)S(1)}, bf16[160,128]{1,0:T(8,128)(2,1)}, u32[]{:S(2)}) copy-start(bf16[160,128]{1,0:T(8,128)(2,1)} %get-tuple-element.166.dispatch_ref) | copy-start | bytes 122884
  217.6 5.1 %collective-permute-start.39 = (bf16[1,1,1,1,1,96,128]{6,5,4,3,2,1,0:T(8,128)(2,1)S(1)}, bf16[1,1,1,1,1,96,128]{6,5,4,3,2,1,0:T(8,128)(2,1)S(1)}, u32[]{:S(2)}, u32[]{:S(2)}) collective-permute-start(bf16[1,1,1,1,1,96,128]{6,5,4,3,2,1,0:T(8,128)(2,1)S(1)} %dynamic-slice_convert_fusion.8), channel_id=1, source_target_pairs={{0,16},{16,0},{1,17},{17,1},{2,18},{18,2},{3,19},{19,3},{4,20},{20... | collective-permute-start | bytes 73736 | tf_op jit(solution)/shard_map/ppermute | solution.py:280
  219.1 4.1 %collective-permute-start.40 = (bf16[1,1,1,1,1,96,256]{6,5,4,3,2,1,0:T(8,128)(2,1)S(1)}, bf16[1,1,1,1,1,96,256]{6,5,4,3,2,1,0:T(8,128)(2,1)S(1)}, u32[]{:S(2)}, u32[]{:S(2)}) collective-permute-start(bf16[1,1,1,1,1,96,256]{6,5,4,3,2,1,0:T(8,128)(2,1)S(1)} %dynamic-slice_convert_fusion.6), channel_id=1, source_target_pairs={{0,2},{1,3},{2,0},{3,1},{4,6},{5,7},{6,4},{7,5},{8,10},{9,11},{10,... | collective-permute-start | bytes 147464 | tf_op jit(solution)/shard_map/ppermute | solution.py:282
  219.6 4.3 %collective-permute-start.42 = (f32[128,128]{1,0:T(8,128)S(1)}, f32[128,128]{1,0:T(8,128)S(1)}, u32[]{:S(2)}, u32[]{:S(2)}) collective-permute-start(f32[128,128]{1,0:T(8,128)S(1)} %add.180), channel_id=1, source_target_pairs={{0,4},{1,5},{2,6},{3,7},{4,0},{5,1},{6,2},{7,3},{8,12},{9,13},{10,... | collective-permute-start | bytes 196616 | tf_op jit(solution)/shard_map/ppermute | solution.py:282
  219.7 6.1 %collective-permute-start.41 = (bf16[1,1,1,1,1,96,384]{6,5,4,3,2,1,0:T(8,128)(2,1)S(1)}, bf16[1,1,1,1,1,96,384]{6,5,4,3,2,1,0:T(8,128)(2,1)S(1)}, u32[]{:S(2)}, u32[]{:S(2)}) collective-permute-start(bf16[1,1,1,1,1,96,384]{6,5,4,3,2,1,0:T(8,128)(2,1)S(1)} %dynamic-slice_convert_fusion.5), channel_id=1, source_target_pairs={{0,4},{1,5},{2,6},{3,7},{4,0},{5,1},{6,2},{7,3},{8,12},{9,13},{10,... | collective-permute-start | bytes 221192 | tf_op jit(solution)/shard_map/ppermute | solution.py:282
  (11 other events, 37.1 us)
